TPU v7x, 32 devices: a whole 2x2x4 slice. The times are simulated.
32 devices in a mesh: seq: 8 (over y, x, core), db: 4 (over z).
Axes of the slice: x: 2, y: 2, z: 4, core: 2. Of those that a mesh axis runs over, the one named last changes fastest.
Arguments:
- hidden_in: bfloat16 [2048, 4096], P('seq'), may hold values from -4 to 4
- query_rows: bfloat16 [2048, 4096], P('seq', 'db'), may hold values from -32 to 32
- key_rows: bfloat16 [2048, 4096], P('seq', 'db'), may hold values from -32 to 32
- value_rows: bfloat16 [2048, 4096], P('seq', 'db'), may hold values from -6 to 6
- w_self_out: bfloat16 [4096, 4096], P('db'), may hold values from -0.1796875 to 0.1796875
- norm_gain: bfloat16 [4096], replicated, may hold values from 0.099609375 to 1.8984375
- w_cross_q: bfloat16 [4096, 4096], P(None, 'db'), may hold values from -2 to 2
- w_cross_k: bfloat16 [1024, 4096], P(None, 'db'), may hold values from -1 to 1
- w_cross_v: bfloat16 [1024, 4096], P(None, 'db'), may hold values from -0.1875 to 0.1875
- w_cross_out: bfloat16 [4096, 4096], P('db'), may hold values from -0.09375 to 0.09375
- enc_table: bfloat16 [32, 128, 1024], P('db'), may hold values from -6 to 6
- nb_shard: int32 [32, 2], P('seq'), may hold values from 0 to 3, all different within a row; in each aligned block of 4 rows (0 to 3, 4 to 7, ...) at most 4 rows name the same one
- nb_row: int32 [32, 2], P('seq'), may hold values from 0 to 7
Outputs:
- block_out: float32 [2048, 4096], P(('seq', 'db'))
Inputs may be any that keep to these rules, and one draw needn't show every extreme that they name: `nb_shard`: the spans held by one index of seq name each shard at most 4 times, and in the spans of some indices one shard exactly 4 times; the 2 neighbours of a span lie in different shards.
All inputs are finite; a program needn't handle non-finite values.
Results may differ from a plain program's by a relative error of at most 0.038.
Values may be sent and summed in bfloat16 or wider, within the bound.
No kernel may reach another device: no remote copies, remote signals or barrier semaphores. Data moves between devices by JAX's collectives and lax.ppermute only.
A program may use at most 128 MiB of HBM per device.

v0:
```python
import math

import jax
import jax.numpy as jnp
from jax import lax
from jax.sharding import PartitionSpec as P

HD = 128
SPAN = 64
NEIGH = 2
NLEN = 128


NEG_BIG = -1e30


def from_behind(block, axis, distance):
    devices = range(lax.axis_size(axis))
    route = [(i - distance, i) for i in devices if i - distance in devices]
    return lax.ppermute(block, axis, route)


def attend_block(state, query_three, key_block, value_block, query_pos, key_pos, score_scale):
    run_max, run_sum, run_acc = state
    scores = (
        jnp.einsum("qhd,khd->hqk", query_three, key_block, preferred_element_type=jnp.float32)
        * score_scale
    )
    allowed = (key_pos[None, :] <= query_pos[:, None]) & (key_pos[None, :] >= 0)
    scores = jnp.where(allowed[None], scores, NEG_BIG)
    new_max = jnp.maximum(run_max, jnp.max(scores, axis=-1))
    rescale = jnp.exp(run_max - new_max)
    weights = jnp.exp(scores - new_max[..., None])
    new_sum = run_sum * rescale + jnp.sum(weights, axis=-1)
    added = jnp.einsum(
        "hqk,khd->hqd",
        weights.astype(jnp.bfloat16),
        value_block,
        preferred_element_type=jnp.float32,
    )
    return (new_max, new_sum, run_acc * rescale[..., None] + added)


def fold_piece(carried, query_three, pieces, query_pos, score_scale):
    key_piece, value_piece = pieces
    count_rows = key_piece.shape[0]
    heads_local = query_three.shape[1]
    block_rows = math.gcd(count_rows, 512)
    block_count = count_rows // block_rows
    last_query = query_pos[query_pos.shape[0] - 1]

    def one_block(block_index, state):
        key_first = block_index * block_rows

        def compute(inner):
            key_block = lax.dynamic_slice_in_dim(
                key_piece, block_index * block_rows, block_rows, 0
            ).reshape(block_rows, heads_local, HD)
            value_block = lax.dynamic_slice_in_dim(
                value_piece, block_index * block_rows, block_rows, 0
            ).reshape(block_rows, heads_local, HD)
            key_pos = key_first + jnp.arange(block_rows, dtype=jnp.int32)
            return attend_block(
                inner, query_three, key_block, value_block, query_pos, key_pos, score_scale
            )

        def unchanged(inner):
            return inner

        live = (key_first <= last_query) & (key_first + block_rows > 0)
        return lax.cond(live, compute, unchanged, state)

    return lax.fori_loop(0, block_count, one_block, carried)


def empty_state(heads_local, rows):
    return (
        jnp.full((heads_local, rows), NEG_BIG, jnp.float32),
        jnp.zeros((heads_local, rows), jnp.float32),
        jnp.zeros((heads_local, rows, HD), jnp.float32),
    )


def finish_state(state, rows, width_local):
    run_max, run_sum, run_acc = state
    return (
        (run_acc / run_sum[..., None])
        .transpose(1, 0, 2)
        .reshape(rows, width_local)
        .astype(jnp.bfloat16)
    )


def per_device(
    hidden_in,
    query_rows,
    key_rows,
    value_rows,
    w_self_out,
    norm_gain,
    w_cross_q,
    w_cross_k,
    w_cross_v,
    w_cross_out,
    enc_table,
    nb_shard,
    nb_row,
):
    tok_rows = hidden_in.shape[0]
    width_local = query_rows.shape[1]
    heads_local = width_local // HD
    db_count = lax.axis_size("db")
    seq_index = lax.axis_index("seq")
    db_index = lax.axis_index("db")
    score_scale = 1.0 / math.sqrt(HD)
    query_three = query_rows.reshape(tok_rows, heads_local, HD)
    query_pos = seq_index * tok_rows + jnp.arange(tok_rows, dtype=jnp.int32)
    initial = empty_state(heads_local, tok_rows)
    state = fold_piece(
        initial,
        query_three,
        (
            lax.all_gather(key_rows, "seq", axis=0, tiled=True),
            lax.all_gather(value_rows, "seq", axis=0, tiled=True),
        ),
        query_pos,
        score_scale,
    )
    attended = finish_state(state, tok_rows, width_local)
    share_rows = tok_rows // db_count
    attn_total = lax.psum(
        jnp.dot(attended, w_self_out, preferred_element_type=jnp.float32).astype(jnp.bfloat16), "db"
    ).astype(jnp.float32)
    residual = hidden_in.astype(jnp.float32) + attn_total
    mean_square = jnp.mean(residual * residual, axis=-1, keepdims=True)
    normed = (residual * lax.rsqrt(mean_square + 1e-05) * norm_gain.astype(jnp.float32)).astype(
        jnp.bfloat16
    )
    cross_query = jnp.dot(normed, w_cross_q, preferred_element_type=jnp.float32).astype(
        jnp.bfloat16
    )
    span_count = tok_rows // SPAN
    entry_count = span_count * NEIGH
    capacity = 2 * ((entry_count + db_count - 1) // db_count)
    shard_flat = nb_shard.reshape(entry_count)
    row_flat = nb_row.reshape(entry_count)
    entry_ids = jnp.arange(entry_count, dtype=jnp.int32)
    earlier = (shard_flat[:, None] == shard_flat[None, :]) & (
        entry_ids[None, :] < entry_ids[:, None]
    )
    rank_flat = jnp.sum(earlier.astype(jnp.int32), axis=1)
    slot_ids = jnp.arange(capacity, dtype=jnp.int32)
    chosen = ((shard_flat[None, :] == db_index) & (rank_flat[None, :] == slot_ids[:, None])).astype(
        jnp.int32
    )
    pick_rows = jnp.sum(chosen * row_flat[None, :], axis=1)
    live_slot = jnp.sum(chosen, axis=1) > 0
    picked = jnp.take(enc_table, pick_rows, axis=0)
    outgoing = jnp.where(live_slot[:, None, None], picked, jnp.zeros_like(picked))
    arrived = lax.all_gather(outgoing, "db", axis=0, tiled=True)
    wanted = jnp.take(arrived, shard_flat * capacity + rank_flat, axis=0).reshape(
        entry_count * NLEN, enc_table.shape[2]
    )
    cross_keys = jnp.dot(wanted, w_cross_k, preferred_element_type=jnp.float32).astype(jnp.bfloat16)
    cross_values = jnp.dot(wanted, w_cross_v, preferred_element_type=jnp.float32).astype(
        jnp.bfloat16
    )
    cross_pair = jnp.stack((cross_keys, cross_values)).reshape(
        2, span_count, NEIGH * NLEN, width_local
    )
    previous = from_behind(cross_pair[:, span_count - 1], "seq", 1)
    extended = jnp.concatenate((previous[:, None], cross_pair), axis=1).reshape(
        2, span_count + 1, NEIGH * NLEN, heads_local, HD
    )
    padded = jnp.pad(cross_query, ((1, SPAN - 1), (0, 0))).reshape(
        span_count + 1, SPAN, heads_local, HD
    )
    scores = (
        jnp.einsum("gqhd,gkhd->ghqk", padded, extended[0], preferred_element_type=jnp.float32)
        * score_scale
    )
    top_score = jnp.max(scores, axis=-1, keepdims=True)
    weights = jnp.exp(scores - top_score)
    totals = jnp.sum(weights, axis=-1, keepdims=True)
    mixed = (
        jnp.einsum(
            "ghqk,gkhd->ghqd",
            weights.astype(jnp.bfloat16),
            extended[1],
            preferred_element_type=jnp.float32,
        )
        / totals
    )
    cross_mixed = (
        mixed.transpose(0, 2, 1, 3)
        .reshape((span_count + 1) * SPAN, width_local)[1 : tok_rows + 1]
        .astype(jnp.bfloat16)
    )
    cross_share = lax.psum_scatter(
        jnp.dot(cross_mixed, w_cross_out, preferred_element_type=jnp.float32).astype(jnp.bfloat16),
        "db",
        scatter_dimension=0,
        tiled=True,
    ).astype(jnp.float32)
    own_residual = lax.dynamic_slice_in_dim(residual, db_index * share_rows, share_rows, 0)
    return own_residual + cross_share


def solution(mesh):
    placed = (
        P("seq", None),
        P("seq", "db"),
        P("seq", "db"),
        P("seq", "db"),
        P("db", None),
        P(),
        P(None, "db"),
        P(None, "db"),
        P(None, "db"),
        P("db", None),
        P("db", None, None),
        P("seq", None),
        P("seq", None),
    )
    return jax.shard_map(
        per_device, mesh=mesh, in_specs=placed, out_specs=P(("seq", "db"), None), check_vma=False
    )
```

profile of v0, /device:TPU:0, one launch (start us, length us, event | category | flops | bytes accessed | tf_op | source)
XLA Modules:
  0.0 372.9 jit_solution(9170992306960440199)
XLA Ops:
  6.5 0.9 copy.65
  7.5 0.1 mul.94
  7.5 0.8 copy.64
  8.3 0.1 reshape.166
  8.4 0.2 convert_reduce_fusion
  8.6 0.1 convert_reduce_fusion.1
  8.8 2.2 gather_fusion
  11.0 1.2 select_select_fusion
  12.2 0.0 all-gather.8.cloned.1.call-update
  12.2 0.0 all-gather.4.cloned.1.call-start
  12.2 2.1 copy.59
  14.3 0.0 all-gather.4.cloned.1.call-update
  14.3 0.0 all-gather.6.cloned.1.call-start
  14.4 1.0 copy.61
  15.4 0.0 all-gather.6.cloned.1.call-update
  15.4 0.0 all-reduce.3.cloned.1.call-start
  15.5 0.1 copy.66
  15.6 0.1 mul.98
  15.7 0.6 slice.18
  16.3 1.2 copy.60
  17.5 0.3 copy.62
  17.9 0.1 broadcast_bitcast_fusion
  17.9 77.9 %all-gather.8.cloned.1.call-done = bf16[16,128,1024]{2,1,0:T(8,128)(2,1)} async-done(((bf16[4,128,1024]{2,1,0:T(8,128)(2,1)}), bf16[16,128,1024]{2,1,0:T(8,128)(2,1)}) %all-gather.8.cloned.1.call-update) | async-done | bytes 4194320 | tf_op jit(solution)/shard_map/all_gather | solution.py:160
  95.8 4.2 %gather_fusion.1 = bf16[8,128,1024]{2,1,0:T(8,128)(2,1)} fusion(bf16[16,128,1024]{2,1,0:T(8,128)(2,1)} %all-gather.8.cloned.1.call-done, s32[1024]{0:T(1024)S(1)} %pad_clamp_fusion), kind=kCustom, calls=%fused_computation.1 | custom fusion | bytes 4194336 | tf_op jit(solution)/shard_map/jit(_take)/gather | solution.py:161
  100.0 1.9 bitcast_select_fusion.1
  101.9 1.3 copy-done.7
  103.2 3.7 convolution_convert_fusion.2
  106.9 26.8 %all-gather.4.cloned.1.call-done = bf16[2048,1024]{0,1:T(8,128)(2,1)} async-done(((bf16[256,1024]{0,1:T(8,128)(2,1)}), bf16[2048,1024]{0,1:T(8,128)(2,1)}) %all-gather.4.cloned.1.call-update) | async-done | bytes 4194320 | tf_op jit(solution)/shard_map/all_gather | solution.py:123
  133.7 39.4 %all-gather.6.cloned.1.call-done = bf16[2048,1024]{0,1:T(8,128)(2,1)} async-done(((bf16[256,1024]{0,1:T(8,128)(2,1)}), bf16[2048,1024]{0,1:T(8,128)(2,1)}) %all-gather.6.cloned.1.call-update) | async-done | bytes 4194320 | tf_op jit(solution)/shard_map/all_gather | solution.py:124
  173.0 1.1 broadcast_in_dim.77
  174.1 10.2 %while.18 = (s32[]{:T(128)}, f32[8,256]{1,0:T(8,128)S(1)}, f32[8,256]{1,0:T(8,128)S(1)}, f32[8,256,128]{2,1,0:T(8,128)}, s32[]{:T(128)}, /*index=5*/bf16[2048,10...) while((s32[]{:T(128)}, f32[8,256]{1,0:T(8,128)S(1)}, ...), condition=%wide.region_5.6_spmd.clone, body=%wide.region_0.5_spmd.clone.sunk | while | flops 549197568 | bytes 22160756 | solution.py:73
  174.7 7.5 %conditional.3 = ((f32[8,256]{1,0:T(8,128)S(1)}, f32[8,256]{1,0:T(8,128)S(1)}, f32[8,256,128]{2,1,0:T(8,128)})) conditional(s32[]{:T(128)} %convert_element_type.110, (f32[8,256]{1,0:T(8,128)S(1)}, f32[8,256]{1,0:T(8,128)S(1)}, f32[8,256,128]{2,1,0:T(8,128)}) %tuple.54, (s32[]{:T(128)}, s32[]{:T(128)}, s32[]{:T(128)}, bf16[2048,1024]{0,1:T(8,128)(2,1)}, ...), branch_computations={%region_1.0_spmd, %region_2.4_spmd} | conditional | flops 549197568 | bytes 22159454 | solution.py:71
  174.8 0.2 compare_and_fusion
  175.0 1.7 constant_dynamic-slice_fusion
  176.7 0.9 fusion.4
  177.6 0.9 fusion.3
  178.5 3.7 fusion.11
  184.3 1.6 copy.63
  185.9 0.1 divide_convert_fusion
  186.0 7.1 %convolution_convert_fusion.1 = bf16[256,4096]{1,0:T(8,128)(2,1)} fusion(bf16[256,1024]{0,1:T(8,128)(2,1)S(1)} %bitcast.73, bf16[1024,4096]{1,0:T(8,128)(2,1)} %param.21), kind=kOutput, calls=%fused_computation.26 | convolution fusion | flops 2148532224 | bytes 11010048 | tf_op jit(solution)/shard_map/dot_general | solution.py:132
  193.1 0.0 all-reduce.3.cloned.1.call-update
  193.1 0.2 reduce-scatter.2.cloned.1.call-start
  193.3 5.9 %convolution_convert_fusion.3 = bf16[1024,1024]{1,0:T(8,128)(2,1)} fusion(bf16[1024,1024]{1,0:T(8,128)(2,1)} %copy-done.7, bf16[1024,1024]{1,0:T(8,128)(2,1)} %param.24), kind=kOutput, calls=%fused_computation.39 | convolution fusion | flops 2148532224 | bytes 6291456 | tf_op jit(solution)/shard_map/dot_general | solution.py:164
  199.2 2.8 copy.67
  202.1 4.0 %copy.68 = bf16[1,4,256,1024]{2,3,1,0:T(8,128)(2,1)} copy(bf16[1,4,256,1024]{3,2,1,0:T(8,128)(2,1)} %bitcast.77) | data formatting | bytes 4194304 | tf_op jit(solution)/shard_map/stack | solution.py:168
  206.0 1.3 fusion.27
  207.3 2.2 collective-permute-start
  209.6 2.2 collective-permute-done
  211.8 0.7 maximum_maximum_fusion
  212.4 2.7 fusion.36
  215.1 87.1 %all-reduce.3.cloned.1.call-done = bf16[256,4096]{1,0:T(8,128)(2,1)} async-done(((bf16[256,4096]{1,0:T(8,128)(2,1)}), bf16[256,4096]{1,0:T(8,128)(2,1)}) %all-reduce.3.cloned.1.call-update) | async-done | bytes 2097168 | tf_op jit(solution)/shard_map/psum | solution.py:131
  302.2 4.4 %convert_add_fusion = (f32[256,4096]{1,0:T(8,128)}, f32[256]{0:T(256)S(1)}) fusion(bf16[256,4096]{1,0:T(8,128)(2,1)} %all-reduce.3.cloned.1.call-done, bf16[256,4096]{1,0:T(8,128)(2,1)S(1)} %copy-done.5), kind=kLoop, calls=%fused_computation.29 | loop fusion | flops 5242624 | bytes 8389632 | tf_op jit(solution)/shard_map/add | solution.py:134
  306.6 5.9 %fusion.26 = bf16[256,1024]{1,0:T(8,128)(2,1)S(1)} fusion(bf16[4096,1024]{1,0:T(8,128)(2,1)} %param.23, f32[4096]{0:T(1024)S(1)} %convert_element_type.67, f32[256]{0:T(256)S(1)} %add_rsqrt_fusion, bf16[256,4096]{1,0:T(8,128)(2,1)S(1)} %copy-done.6, bf16[256,4096]{1,0:T(8,128)(2,1)S(1)} %copy-done.5), kind=kOutput, calls=%fused_computation.45 | convolution fusion | flops 2154037248 | bytes 13124608 | tf_op jit(solution)/shard_map/dot_general | solution.py:139
  312.5 0.2 pad_bitcast_fusion
  312.7 0.1 copy.79
  312.8 0.7 multiply_reduce_fusion.1
  313.5 0.9 fusion.16
  314.4 0.8 copy-done.4
  315.3 1.3 fusion.22
  316.6 0.4 copy.73
  317.0 0.1 copy.86
  317.2 3.8 %convolution_convert_fusion = bf16[256,4096]{1,0:T(8,128)(2,1)} fusion(bf16[1024,4096]{1,0:T(8,128)(2,1)S(1)} %bitcast.84, bf16[320,1024]{1,0:T(8,128)(2,1)S(1)} %bitcast.81), kind=kOutput, calls=%fused_computation.25 | convolution fusion | flops 2148532224 | bytes 11010048 | tf_op jit(solution)/shard_map/dot_general | solution.py:200
  321.0 43.0 %reduce-scatter.2.cloned.1.call-done = bf16[64,4096]{1,0:T(8,128)(2,1)} async-done(((bf16[256,4096]{1,0:T(8,128)(2,1)}), bf16[64,4096]{1,0:T(8,128)(2,1)}) %reduce-scatter.2.cloned.1.call-update) | async-done | bytes 524304 | tf_op jit(solution)/shard_map/reduce_scatter | solution.py:199
  364.0 2.4 convert_add_fusion.1
  (52 shorter events, 0.2 us)
Async XLA Ops:
  6.5 96.6 %copy-start = (bf16[1024,1024]{1,0:T(8,128)(2,1)S(1)}, bf16[1024,1024]{1,0:T(8,128)(2,1)}, u32[]{:S(2)}) copy-start(bf16[1024,1024]{1,0:T(8,128)(2,1)} %param.25) | copy-start | bytes 6291460
  6.5 89.3 %all-gather.8.cloned.1.call-start = ((), (), s32[]{:S(2)}) async-start(), calls=%async_computation.4 | async-start | bytes 5242880 | tf_op jit(solution)/shard_map/all_gather | solution.py:160
  12.1 2.2 copy-start.8
  12.1 3.3 copy-start.10
  12.2 121.5 %all-gather.4.cloned.1.call-start = ((), (), s32[]{:S(2)}) async-start(), calls=%async_computation.1 | async-start | bytes 4718592 | tf_op jit(solution)/shard_map/all_gather | solution.py:123
  14.3 158.7 %all-gather.6.cloned.1.call-start = ((), (), s32[]{:S(2)}) async-start(), calls=%async_computation.2 | async-start | bytes 4718592 | tf_op jit(solution)/shard_map/all_gather | solution.py:124
  15.4 286.8 %all-reduce.3.cloned.1.call-start = ((), (), s32[]{:S(2)}) async-start(), calls=%async_computation.3 | async-start | bytes 4194304 | tf_op jit(solution)/shard_map/psum | solution.py:131
  101.8 1.3 copy-start.7
  193.1 170.9 %reduce-scatter.2.cloned.1.call-start = ((), (), s32[]{:S(2)}) async-start(), calls=%async_computation.5 | async-start | bytes 2621440 | tf_op jit(solution)/shard_map/reduce_scatter | solution.py:199
  206.0 3.5 copy-start.9
  206.0 5.7 %copy-start.2 = (bf16[1,4,256,1024]{2,3,1,0:T(8,128)(2,1)S(1)}, bf16[1,4,256,1024]{2,3,1,0:T(8,128)(2,1)}, u32[]{:S(2)}) copy-start(bf16[1,4,256,1024]{2,3,1,0:T(8,128)(2,1)} %copy.68) | copy-start | bytes 6291460
  207.3 4.4 %collective-permute-start = (bf16[2,256,1024]{1,2,0:T(8,128)(2,1)S(1)}, bf16[2,256,1024]{1,2,0:T(8,128)(2,1)S(1)}, u32[]{:S(2)}, u32[]{:S(2)}) collective-permute-start(bf16[2,256,1024]{1,2,0:T(8,128)(2,1)S(1)} %fusion.27), channel_id=1, source_target_pairs={{0,4},{4,8},{8,12},{12,16},{16,20},{20,24},{24,28},{1,5},{5,9},{9,... | collective-permute-start | bytes 3145736 | tf_op jit(solution)/shard_map/ppermute | solution.py:20
  212.4 89.8 %copy-start.5 = (bf16[256,4096]{1,0:T(8,128)(2,1)S(1)}, bf16[256,4096]{1,0:T(8,128)(2,1)}, u32[]{:S(2)}) copy-start(bf16[256,4096]{1,0:T(8,128)(2,1)} %param.17) | copy-start | bytes 6291460
  302.2 4.4 %copy-start.6 = (bf16[256,4096]{1,0:T(8,128)(2,1)S(1)}, bf16[256,4096]{1,0:T(8,128)(2,1)}, u32[]{:S(2)}) copy-start(bf16[256,4096]{1,0:T(8,128)(2,1)} %all-reduce.3.cloned.1.call-done) | copy-start | bytes 6291460
  302.2 15.0 %slice-start = ((s8[8388608]{0:T(1024)(128)(4,1)}), s8[4194304]{0:T(1024)(128)(4,1)S(1)}, s32[]{:S(2)}) async-start(s8[8388608]{0:T(1024)(128)(4,1)} %bitcast.83), calls=%async_computation.6 | async-start | bytes 8388608
  306.6 6.2 %copy-start.3 = (bf16[1,5,256,1024]{2,3,1,0:T(8,128)(2,1)S(1)}, bf16[1,5,256,1024]{2,3,1,0:T(8,128)(2,1)}, u32[]{:S(2)}) copy-start(bf16[1,5,256,1024]{2,3,1,0:T(8,128)(2,1)} %get-tuple-element.284) | copy-start | bytes 7864324
  306.6 10.6 %slice-start.1 = ((s8[8388608]{0:T(1024)(128)(4,1)}), s8[4194304]{0:T(1024)(128)(4,1)S(1)}, s32[]{:S(2)}) async-start(s8[8388608]{0:T(1024)(128)(4,1)} %bitcast.83), calls=%async_computation.7 | async-start | bytes 8388608
  313.5 1.7 copy-start.4
  317.2 49.2 %copy-start.1 = (bf16[1024,1024]{1,0:T(8,128)(2,1)S(1)}, bf16[1024,1024]{1,0:T(8,128)(2,1)}, u32[]{:S(2)}) copy-start(bf16[1024,1024]{1,0:T(8,128)(2,1)} %param.25) | copy-start | bytes 6291460
Sparse Core Ops, SparseCore 0:
  12.3 83.4 all-gather.7
  97.7 35.9 all-gather.3
  135.5 37.4 all-gather.5
  193.2 108.9 all-reduce.2
  321.1 42.7 reduce-scatter.1
where the time goes:
time: 374 us; the launch traced here: 373 us
  waiting for transfers between devices  276 us (74%)
  matrix products  33 us (9%)
  local copies, waits for them, and re-layouts  30.6 us (8%)
  other arithmetic  14.3 us (4%)
  between operations  13.5 us (4%)
    psum x1, waiting for transfers between devices, per_device(): lax.psum(jnp.dot(attended, w_self_out, preferred_element_type=jnp.float32...  87.1 us
    all_gather x1, waiting for transfers between devices, per_device(): arrived = lax.all_gather(outgoing, 'db', axis=0, tiled=True)  77.9 us
    reduce_scatter x1, waiting for transfers between devices, per_device(): lax.psum_scatter(jnp.dot(cross_mixed, w_cross_out, preferred_element_type...  43 us
    all_gather x1, waiting for transfers between devices, per_device(): lax.all_gather(value_rows, 'seq', axis=0, tiled=True)  39.4 us
    all_gather x1, waiting for transfers between devices, per_device(): lax.all_gather(key_rows, 'seq', axis=0, tiled=True)  26.8 us
    unnamed x35, local copies, waits for them, and re-layouts  8.9 us
  transfers between devices with their start and end apart: 6, of which 6 were waited for; matrix products, arithmetic and copies ran while one was open for 9% of the time, Pallas kernels for 0%

commit v1 on v0

v1 whole, which is shorter than its diff:
```python
import functools
import math

import jax
import jax.numpy as jnp
from jax import lax
from jax.experimental import pallas as pl
from jax.experimental.pallas import tpu as pltpu
from jax.sharding import PartitionSpec as P

HD = 128
SPAN = 64
NEIGH = 2
NLEN = 128
GROUP = NEIGH * NLEN

NEG_BIG = -1e30
LOG2E = 1.4426950408889634
VMEM_BYTES = 48 * 1024 * 1024


def shift(block, axis, distance, senders):
    size = lax.axis_size(axis)
    route = [(k, k + distance) for k in senders if 0 <= k + distance < size]
    return lax.ppermute(block, axis, route)


def add_rounded(first, second):
    return (first.astype(jnp.float32) + second.astype(jnp.float32)).astype(jnp.bfloat16)


def line_reduce_scatter(blocks):
    size = lax.axis_size("db")
    me = lax.axis_index("db")

    def pick(d):
        return lax.dynamic_index_in_dim(blocks, jnp.clip(d, 0, size - 1), 0, keepdims=False)

    up = down = None
    for step in range(size - 1):
        far = size - 1 - step
        up_block, down_block = pick(me + far), pick(me - far)
        if step:
            up_block, down_block = add_rounded(up_block, up), add_rounded(down_block, down)
        up = shift(up_block, "db", 1, range(step + 1))
        down = shift(down_block, "db", -1, range(size - 1 - step, size))
    total = pick(me).astype(jnp.float32)
    return total + up.astype(jnp.float32) + down.astype(jnp.float32)


def line_all_gather(block):
    size = lax.axis_size("db")
    me = lax.axis_index("db")
    whole = jnp.zeros((size,) + block.shape, block.dtype)
    whole = lax.dynamic_update_index_in_dim(whole, block, me, 0)
    up = down = block
    pieces = []
    for step in range(size - 1):
        up = shift(up, "db", 1, range(step, size))
        down = shift(down, "db", -1, range(0, size - step))
        pieces.append((step + 1, up, down))
    parts = []
    for owner in range(size):
        chosen = block
        for distance, from_low, from_high in pieces:
            chosen = jnp.where(me - owner == distance, from_low, chosen)
            chosen = jnp.where(owner - me == distance, from_high, chosen)
        parts.append(chosen)
    return jnp.stack(parts)


def self_kernel(qkv_ref, out_ref, *, blocks, rows, scale):
    for block in range(blocks):
        query = qkv_ref[block, 0]
        live = (block + 1) * rows
        keys = qkv_ref[0 : block + 1, 1].reshape(live, HD)
        values = qkv_ref[0 : block + 1, 2].reshape(live, HD)
        scores = lax.dot_general(
            query, keys, (((1,), (1,)), ((), ())), preferred_element_type=jnp.float32
        )
        query_pos = block * rows + lax.broadcasted_iota(jnp.int32, (rows, live), 0)
        key_pos = lax.broadcasted_iota(jnp.int32, (rows, live), 1)
        scores = jnp.where(key_pos <= query_pos, scores * (scale * LOG2E), NEG_BIG)
        top = jnp.max(scores, axis=-1, keepdims=True)
        weights = jnp.exp2(scores - top)
        total = jnp.sum(weights, axis=-1, keepdims=True)
        mixed = jnp.dot(weights.astype(jnp.bfloat16), values, preferred_element_type=jnp.float32)
        out_ref[block] = (mixed / total).astype(jnp.bfloat16)


def self_attend_head(qkv, scale):
    blocks, _, rows, _ = qkv.shape
    return pl.pallas_call(
        functools.partial(self_kernel, blocks=blocks, rows=rows, scale=scale),
        out_shape=jax.ShapeDtypeStruct((blocks, rows, HD), jnp.bfloat16),
        in_specs=[pl.BlockSpec(memory_space=pltpu.VMEM)],
        out_specs=pl.BlockSpec(memory_space=pltpu.VMEM),
        compiler_params=pltpu.CompilerParams(vmem_limit_bytes=VMEM_BYTES),
        cost_estimate=pl.CostEstimate(
            flops=2 * blocks * blocks * rows * rows * HD,
            bytes_accessed=8 * blocks * rows * HD,
            transcendentals=blocks * blocks * rows * rows // 2,
        ),
        name="self_attend",
    )(qkv)


def self_attention_by_head(query_rows, key_rows, value_rows, scale):
    rows, width = query_rows.shape
    count = lax.axis_size("seq")
    packed = jnp.stack((query_rows, key_rows, value_rows)).reshape(3, rows, count, HD)
    packed = packed.transpose(2, 0, 1, 3)
    held = lax.all_to_all(packed, "seq", 0, 0, tiled=True)
    mixed = self_attend_head(held, scale)
    back = lax.all_to_all(mixed, "seq", 0, 0, tiled=True)
    return back.transpose(1, 0, 2).reshape(rows, width)


def self_attention_gathered(query_rows, key_rows, value_rows, scale):
    rows, width = query_rows.shape
    heads = width // HD
    keys = lax.all_gather(key_rows, "seq", axis=0, tiled=True)
    values = lax.all_gather(value_rows, "seq", axis=0, tiled=True)
    count = keys.shape[0]
    query_pos = lax.axis_index("seq") * rows + jnp.arange(rows, dtype=jnp.int32)
    allowed = jnp.arange(count, dtype=jnp.int32)[None, :] <= query_pos[:, None]
    scores = (
        jnp.einsum(
            "qhd,khd->hqk",
            query_rows.reshape(rows, heads, HD),
            keys.reshape(count, heads, HD),
            preferred_element_type=jnp.float32,
        )
        * scale
    )
    scores = jnp.where(allowed[None], scores, NEG_BIG)
    weights = jnp.exp(scores - jnp.max(scores, axis=-1, keepdims=True))
    total = jnp.sum(weights, axis=-1)
    mixed = jnp.einsum(
        "hqk,khd->hqd",
        weights.astype(jnp.bfloat16),
        values.reshape(count, heads, HD),
        preferred_element_type=jnp.float32,
    )
    return (mixed / total[..., None]).transpose(1, 0, 2).reshape(rows, width).astype(jnp.bfloat16)


def project_kernel(where_ref, first_ref, second_ref, wk_ref, wv_ref, keys_ref, values_ref):
    depth = first_ref.shape[-1]
    rows = jnp.concatenate(
        (first_ref[...].reshape(NLEN, depth), second_ref[...].reshape(NLEN, depth)), axis=0
    )
    keys_ref[...] = jnp.dot(rows, wk_ref[...], preferred_element_type=jnp.float32).astype(
        jnp.bfloat16
    )
    values_ref[...] = jnp.dot(rows, wv_ref[...], preferred_element_type=jnp.float32).astype(
        jnp.bfloat16
    )


def project_encodings(where, table, w_cross_k, w_cross_v):
    groups = where.shape[0] // (2 * NEIGH)
    _, cuts, _, piece, depth = table.shape
    width = w_cross_k.shape[1]

    def entry(neighbour):
        def index(group, where_ref):
            at = 2 * (NEIGH * group + neighbour)
            return (where_ref[at], 0, where_ref[at + 1], 0, 0)

        return pl.BlockSpec((1, cuts, 1, piece, depth), index)

    fixed = pl.BlockSpec((depth, width), lambda group, where_ref: (0, 0))
    made = pl.BlockSpec((GROUP, width), lambda group, where_ref: (group, 0))
    return pl.pallas_call(
        project_kernel,
        out_shape=[jax.ShapeDtypeStruct((groups * GROUP, width), jnp.bfloat16)] * 2,
        grid_spec=pltpu.PrefetchScalarGridSpec(
            num_scalar_prefetch=1,
            grid=(groups,),
            in_specs=[entry(0), entry(1), fixed, fixed],
            out_specs=[made, made],
        ),
        compiler_params=pltpu.CompilerParams(
            vmem_limit_bytes=VMEM_BYTES, dimension_semantics=("arbitrary",)
        ),
        cost_estimate=pl.CostEstimate(
            flops=4 * groups * GROUP * depth * width,
            bytes_accessed=2 * (groups * GROUP * (depth + 2 * width) + 2 * depth * width),
            transcendentals=0,
        ),
        name="project_encodings",
    )(where, table, table, w_cross_k, w_cross_v)


def cross_kernel(live_ref, query_ref, keys_ref, values_ref, out_ref, *, spans, heads, scale):
    row = lax.broadcasted_iota(jnp.int32, (SPAN, 2 * GROUP), 0)
    column = lax.broadcasted_iota(jnp.int32, (SPAN, 2 * GROUP), 1)
    allowed = (column >= GROUP) == (row == SPAN - 1)
    for span in range(spans):
        for head in range(heads):
            lanes = slice(head * HD, (head + 1) * HD)
            query = query_ref[span * SPAN : (span + 1) * SPAN, lanes]
            keys = keys_ref[span * GROUP : (span + 2) * GROUP, lanes]
            values = values_ref[span * GROUP : (span + 2) * GROUP, lanes]
            scores = lax.dot_general(
                query, keys, (((1,), (1,)), ((), ())), preferred_element_type=jnp.float32
            )
            scores = jnp.where(allowed, scores * (scale * LOG2E), NEG_BIG)
            top = jnp.max(scores, axis=-1, keepdims=True)
            weights = jnp.exp2(scores - top)
            total = jnp.sum(weights, axis=-1, keepdims=True)
            mixed = jnp.dot(
                weights.astype(jnp.bfloat16), values, preferred_element_type=jnp.float32
            )
            mixed = mixed / total
            if span == 0:
                own = lax.broadcasted_iota(jnp.int32, (SPAN, HD), 0) == SPAN - 1
                mixed = jnp.where(own | (live_ref[0] > 0), mixed, 0.0)
            out_ref[span * SPAN : (span + 1) * SPAN, lanes] = mixed.astype(jnp.bfloat16)


def cross_attend(live, query, keys, values, scale):
    rows, width = query.shape
    vmem = pl.BlockSpec(memory_space=pltpu.VMEM)
    return pl.pallas_call(
        functools.partial(
            cross_kernel, spans=rows // SPAN, heads=width // HD, scale=scale
        ),
        out_shape=jax.ShapeDtypeStruct((rows, width), jnp.bfloat16),
        in_specs=[pl.BlockSpec(memory_space=pltpu.SMEM), vmem, vmem, vmem],
        out_specs=vmem,
        compiler_params=pltpu.CompilerParams(vmem_limit_bytes=VMEM_BYTES),
        cost_estimate=pl.CostEstimate(
            flops=8 * rows * GROUP * width,
            bytes_accessed=2 * (2 * rows + 2 * keys.shape[0]) * width,
            transcendentals=2 * rows * GROUP * width // HD,
        ),
        name="cross_attend",
    )(live, query, keys, values)


def per_device(
    hidden_in,
    query_rows,
    key_rows,
    value_rows,
    w_self_out,
    norm_gain,
    w_cross_q,
    w_cross_k,
    w_cross_v,
    w_cross_out,
    enc_table,
    nb_shard,
    nb_row,
):
    rows, features = hidden_in.shape
    width = query_rows.shape[1]
    heads = width // HD
    n_seq, n_db = lax.axis_size("seq"), lax.axis_size("db")
    seq_index, db_index = lax.axis_index("seq"), lax.axis_index("db")
    scale = 1.0 / math.sqrt(HD)
    share = rows // n_db

    rows_shard, _, depth = enc_table.shape
    piece = rows_shard * NLEN // n_seq
    part = lax.dynamic_slice_in_dim(
        enc_table.reshape(rows_shard * NLEN, depth), seq_index * piece, piece, 0
    )
    along_db = lax.all_gather(part, "db", axis=0)
    wanted = jnp.stack((nb_row, nb_shard), axis=-1).astype(jnp.int32)
    before = shift(wanted[-1], "seq", 1, range(n_seq))
    where = jnp.concatenate((before[None], wanted), axis=0).reshape(-1)

    if heads == n_seq:
        attended = self_attention_by_head(query_rows, key_rows, value_rows, scale)
    else:
        attended = self_attention_gathered(query_rows, key_rows, value_rows, scale)

    along_db, attended = lax.optimization_barrier((along_db, attended))
    table = lax.all_gather(along_db, "seq", axis=0).reshape(
        rows_shard, NLEN // piece, n_db, piece, depth
    )

    partial = jnp.dot(attended, w_self_out, preferred_element_type=jnp.float32).astype(jnp.bfloat16)
    attn_share = line_reduce_scatter(partial.reshape(n_db, share, features))
    residual = (
        lax.dynamic_slice_in_dim(hidden_in, db_index * share, share, 0).astype(jnp.float32)
        + attn_share
    )
    mean_square = jnp.mean(residual * residual, axis=-1, keepdims=True)
    normed_share = (
        residual * lax.rsqrt(mean_square + 1e-05) * norm_gain.astype(jnp.float32)
    ).astype(jnp.bfloat16)
    normed = line_all_gather(normed_share).reshape(rows, features)
    cross_query = jnp.dot(normed, w_cross_q, preferred_element_type=jnp.float32).astype(
        jnp.bfloat16
    )
    keys, values = project_encodings(where, table, w_cross_k, w_cross_v)
    live = (seq_index > 0).astype(jnp.int32).reshape(1)
    mixed = cross_attend(live, cross_query, keys, values, scale)
    out_partial = jnp.dot(mixed, w_cross_out, preferred_element_type=jnp.float32).astype(
        jnp.bfloat16
    )
    return residual + line_reduce_scatter(out_partial.reshape(n_db, share, features))


def solution(mesh):
    placed = (
        P("seq", None),
        P("seq", "db"),
        P("seq", "db"),
        P("seq", "db"),
        P("db", None),
        P(),
        P(None, "db"),
        P(None, "db"),
        P(None, "db"),
        P("db", None),
        P("db", None, None),
        P("seq", None),
        P("seq", None),
    )
    return jax.shard_map(
        per_device, mesh=mesh, in_specs=placed, out_specs=P(("seq", "db"), None), check_vma=False
    )
```

time: 374 us -> 273 us (0.73)
  waiting for transfers between devices: 276 us -> 130 us
  starting transfers between devices: 2.58 us -> 47 us
  Pallas kernels: 0 us -> 24.8 us
  local copies, waits for them, and re-layouts: 30.6 us -> 12.6 us
  matrix products: 33 us -> 17.4 us
  blocking collectives: 0 us -> 12.2 us
    all_gather x3 -> x2, waiting for transfers between devices: 144 us -> 0.04 us  [the longest x1 0.02 us: per_device(): along_db = lax.all_gather(part, 'db', axis=0)]
    ppermute x1 -> x19, waiting for transfers between devices: 2.18 us -> 110 us  [shift(): return lax.ppermute(block, axis, route)]
    psum x1 -> x0, waiting for transfers between devices: 87.1 us -> none  [per_device(): lax.psum(jnp.dot(attended, w_self_out, preferred_element_type=jnp.float32...]
    reduce_scatter x1 -> x0, waiting for transfers between devices: 43 us -> none  [per_device(): lax.psum_scatter(jnp.dot(cross_mixed, w_cross_out, preferred_element_type...]
    ppermute x1 -> x19, starting transfers between devices: 2.23 us -> 41.8 us  [shift(): return lax.ppermute(block, axis, route)]
    pallas_call x0 -> x3, Pallas kernels: none -> 24.8 us  [the longest x1 9.82 us: cross_attend(): pl.pallas_call(functools.partial(cross_kernel, spans=rows // SPAN, heads=...]
    all_to_all x0 -> x1, waiting for transfers between devices: none -> 20.3 us  [self_attention_by_head(): held = lax.all_to_all(packed, 'seq', 0, 0, tiled=True)]
    dot_general x7 -> x1, matrix products: 20 us -> 5.73 us  [per_device(): jnp.dot(mixed, w_cross_out, preferred_element_type=jnp.float32)]
  transfers between devices with their start and end apart: 6 -> 22, of which waited for: 6 -> 14; matrix products, arithmetic and copies ran while one was open for 9% -> 9% of each run, Pallas kernels for 0% -> 2%
where the time goes in v1:
time: 273 us; the launch traced here: 272 us
  waiting for transfers between devices  130 us (48%)
  starting transfers between devices  47 us (17%)
  Pallas kernels  24.8 us (9%)
  matrix products  17.4 us (6%)
  between operations  13.9 us (5%)
  other arithmetic  13.5 us (5%)
  local copies, waits for them, and re-layouts  12.6 us (5%)
  blocking collectives  12.2 us (4%)
    ppermute x19, waiting for transfers between devices, shift(): return lax.ppermute(block, axis, route)  110 us
    ppermute x19, starting transfers between devices, shift(): return lax.ppermute(block, axis, route)  41.8 us
    all_to_all x1, waiting for transfers between devices, self_attention_by_head(): held = lax.all_to_all(packed, 'seq', 0, 0, tiled=True)  20.3 us
    all_to_all x1, blocking collectives, self_attention_by_head(): back = lax.all_to_all(mixed, 'seq', 0, 0, tiled=True)  12.2 us
    pallas_call x1, Pallas kernels, cross_attend(): pl.pallas_call(functools.partial(cross_kernel, spans=rows // SPAN, heads=...  9.82 us
    pallas_call x1, Pallas kernels, project_encodings(): pl.pallas_call(project_kernel, out_shape=[jax.ShapeDtypeStruct((groups *...  8.9 us
    unnamed x25, local copies, waits for them, and re-layouts  8.05 us
    pallas_call x1, Pallas kernels, self_attend_head(): pl.pallas_call(functools.partial(self_kernel, blocks=blocks, rows=rows, s...  6.08 us
  transfers between devices with their start and end apart: 22, of which 14 were waited for; matrix products, arithmetic and copies ran while one was open for 9% of the time, Pallas kernels for 2%

profile of v1, /device:TPU:0, one launch (start us, length us, event | category | flops | bytes accessed | tf_op | source)
XLA Modules:
  0.0 271.8 jit_solution(4132120254521047994)
XLA Ops:
  6.5 1.4 copy.27
  7.9 0.3 copy.30
  8.2 1.2 copy.28
  9.5 1.0 copy.31
  10.5 1.2 copy.29
  11.7 1.0 copy.32
  12.7 2.5 maximum_bitcast_fusion
  15.2 5.2 %all-to-all-start = ((bf16[8,3,256,128]{3,2,1,0:T(8,128)(2,1)}), bf16[8,3,256,128]{3,2,1,0:T(8,128)(2,1)}, u32[]{:S(2)}, u32[]{:S(2)}) async-start(bf16[8,3,256,128]{3,2,1,0:T(8,128)(2,1)} %maximum_bitcast_fusion), calls=%async_computation | async-start | bytes 3145728 | tf_op jit(solution)/shard_map/all_to_all | solution.py:113
  20.5 0.7 constant_dynamic-slice_fusion
  21.3 20.3 %all-to-all-done.qkv_ref = bf16[8,3,256,128]{3,2,1,0:T(8,128)(2,1)} async-done(((bf16[8,3,256,128]{3,2,1,0:T(8,128)(2,1)}), bf16[8,3,256,128]{3,2,1,0:T(8,128)(2,1)}, u32[]{:S(2)}, u32[]{:S(2)}) %all-to-all-start) | async-done | bytes 1572896 | tf_op jit(solution)/shard_map/all_to_all | solution.py:113
  41.6 6.1 %self_attend.1 = bf16[8,256,128]{2,1,0:T(8,128)(2,1)S(1)} custom-call(bf16[8,3,256,128]{3,2,1,0:T(8,128)(2,1)} %all-to-all-done.qkv_ref), custom_call_target="tpu_custom_call" | custom-call | flops 1073741824 | bytes 2097152 | tf_op jit(solution)/shard_map/self_attend/pallas_call | solution.py:93
  47.6 12.2 %all_to_all.10 = bf16[8,256,128]{2,1,0:T(8,128)(2,1)S(1)} all-to-all(bf16[8,256,128]{2,1,0:T(8,128)(2,1)S(1)} %self_attend.1), channel_id=1, replica_groups=mesh['seq'=8,'db'=4] {'seq'}, dimensions={0} | all-to-all | bytes 1048576 | tf_op jit(solution)/shard_map/all_to_all | solution.py:115
  59.8 0.2 copy.33
  60.1 5.8 %convolution_convert_fusion.1 = bf16[256,4096]{1,0:T(8,128)(2,1)S(1)} fusion(bf16[256,1024]{0,1:T(8,128)(2,1)S(1)} %bitcast.84, bf16[1024,4096]{1,0:T(8,128)(2,1)} %param.17), kind=kOutput, calls=%fused_computation.1 | convolution fusion | flops 2148532224 | bytes 11010048 | tf_op jit(solution)/shard_map/dot_general | solution.py:286
  65.8 0.9 dynamic-slice_bitcast_fusion.3
  66.7 4.0 %collective-permute-start = (bf16[64,4096]{1,0:T(8,128)(2,1)S(1)}, bf16[64,4096]{1,0:T(8,128)(2,1)S(1)}, u32[]{:S(2)}, u32[]{:S(2)}) collective-permute-start(bf16[64,4096]{1,0:T(8,128)(2,1)S(1)} %get-tuple-element.25), channel_id=1, source_target_pairs={{0,1},{4,5},{8,9},{12,13},{16,17},{20,21},{24,25},{28,29}} | collective-permute-start | bytes 1572872 | tf_op jit(solution)/shard_map/ppermute | solution.py:25
  70.7 1.5 collective-permute-start.3
  72.2 9.0 %collective-permute-done = bf16[64,4096]{1,0:T(8,128)(2,1)S(1)} collective-permute-done((bf16[64,4096]{1,0:T(8,128)(2,1)S(1)}, bf16[64,4096]{1,0:T(8,128)(2,1)S(1)}, u32[]{:S(2)}, u32[]{:S(2)}) %collective-permute-start) | collective-permute-done | bytes 524320 | tf_op jit(solution)/shard_map/ppermute | solution.py:25
  81.3 4.4 %collective-permute-start.1 = (bf16[64,4096]{1,0:T(8,128)(2,1)S(1)}, bf16[64,4096]{1,0:T(8,128)(2,1)S(1)}, u32[]{:S(2)}, u32[]{:S(2)}) collective-permute-start(bf16[64,4096]{1,0:T(8,128)(2,1)S(1)} %fusion.8), channel_id=1, source_target_pairs={{0,1},{1,2},{4,5},{5,6},{8,9},{9,10},{12,13},{13,14},{16,17},{17,1... | collective-permute-start | bytes 1572872 | tf_op jit(solution)/shard_map/ppermute | solution.py:25
  85.8 9.6 %collective-permute-done.1 = bf16[64,4096]{1,0:T(8,128)(2,1)S(1)} collective-permute-done((bf16[64,4096]{1,0:T(8,128)(2,1)S(1)}, bf16[64,4096]{1,0:T(8,128)(2,1)S(1)}, u32[]{:S(2)}, u32[]{:S(2)}) %collective-permute-start.1) | collective-permute-done | bytes 524320 | tf_op jit(solution)/shard_map/ppermute | solution.py:25
  95.4 2.3 fusion.9
  97.6 1.5 collective-permute-start.4
  99.1 4.3 %collective-permute-start.2 = (bf16[64,4096]{1,0:T(8,128)(2,1)}, bf16[64,4096]{1,0:T(8,128)(2,1)S(1)}, u32[]{:S(2)}, u32[]{:S(2)}) collective-permute-start(bf16[64,4096]{1,0:T(8,128)(2,1)} %get-tuple-element.23), channel_id=1, source_target_pairs={{0,1},{1,2},{2,3},{4,5},{5,6},{6,7},{8,9},{9,10},{10,11},{12,13},{... | collective-permute-start | bytes 1572872 | tf_op jit(solution)/shard_map/ppermute | solution.py:25
  103.4 1.2 fusion.7
  104.6 1.3 collective-permute-start.5
  105.9 6.6 %collective-permute-done.2 = bf16[64,4096]{1,0:T(8,128)(2,1)S(1)} collective-permute-done((bf16[64,4096]{1,0:T(8,128)(2,1)}, bf16[64,4096]{1,0:T(8,128)(2,1)S(1)}, u32[]{:S(2)}, u32[]{:S(2)}) %collective-permute-start.2) | collective-permute-done | bytes 524320 | tf_op jit(solution)/shard_map/ppermute | solution.py:25
  112.5 0.8 copy-done.7
  113.3 12.3 %collective-permute-done.5 = bf16[64,4096]{1,0:T(8,128)(2,1)} collective-permute-done((bf16[64,4096]{1,0:T(8,128)(2,1)S(1)}, bf16[64,4096]{1,0:T(8,128)(2,1)}, u32[]{:S(2)}, u32[]{:S(2)}) %collective-permute-start.5) | collective-permute-done | bytes 524320 | tf_op jit(solution)/shard_map/ppermute | solution.py:25
  125.6 1.8 multiply_reduce_fusion
  127.4 0.2 multiply_convert_fusion
  127.6 3.7 %collective-permute-start.9 = (bf16[64,4096]{1,0:T(8,128)(2,1)S(1)}, bf16[64,4096]{1,0:T(8,128)(2,1)S(1)}, u32[]{:S(2)}, u32[]{:S(2)}) collective-permute-start(bf16[64,4096]{1,0:T(8,128)(2,1)S(1)} %multiply_convert_fusion), channel_id=1, source_target_pairs={{0,1},{1,2},{2,3},{4,5},{5,6},{6,7},{8,9},{9,10},{10,11},{12,13},{... | collective-permute-start | bytes 1572872 | tf_op jit(solution)/shard_map/ppermute | solution.py:25
  131.2 1.3 collective-permute-start.6
  132.5 5.7 %collective-permute-done.9 = bf16[64,4096]{1,0:T(8,128)(2,1)S(1)} collective-permute-done((bf16[64,4096]{1,0:T(8,128)(2,1)S(1)}, bf16[64,4096]{1,0:T(8,128)(2,1)S(1)}, u32[]{:S(2)}, u32[]{:S(2)}) %collective-permute-start.9) | collective-permute-done | bytes 524320 | tf_op jit(solution)/shard_map/ppermute | solution.py:25
  138.2 0.7 collective-permute-start.10
  138.9 4.3 %collective-permute-done.6 = bf16[64,4096]{1,0:T(8,128)(2,1)S(1)} collective-permute-done((bf16[64,4096]{1,0:T(8,128)(2,1)S(1)}, bf16[64,4096]{1,0:T(8,128)(2,1)S(1)}, u32[]{:S(2)}, u32[]{:S(2)}) %collective-permute-start.6) | collective-permute-done | bytes 524320 | tf_op jit(solution)/shard_map/ppermute | solution.py:25
  143.2 1.3 collective-permute-start.7
  144.5 1.5 collective-permute-start.11
  146.0 10.2 %collective-permute-done.7 = bf16[64,4096]{1,0:T(8,128)(2,1)S(1)} collective-permute-done((bf16[64,4096]{1,0:T(8,128)(2,1)S(1)}, bf16[64,4096]{1,0:T(8,128)(2,1)S(1)}, u32[]{:S(2)}, u32[]{:S(2)}) %collective-permute-start.7) | collective-permute-done | bytes 524320 | tf_op jit(solution)/shard_map/ppermute | solution.py:25
  156.2 1.3 collective-permute-start.8
  157.7 1.5 collective-permute-start.12
  159.2 0.6 collective-permute-done.12
  160.1 7.2 %collective-permute-done.8 = bf16[64,4096]{1,0:T(8,128)(2,1)} collective-permute-done((bf16[64,4096]{1,0:T(8,128)(2,1)S(1)}, bf16[64,4096]{1,0:T(8,128)(2,1)}, u32[]{:S(2)}, u32[]{:S(2)}) %collective-permute-start.8) | collective-permute-done | bytes 524320 | tf_op jit(solution)/shard_map/ppermute | solution.py:25
  167.3 1.6 select_bitcast_fusion.2
  169.0 1.6 select_bitcast_fusion.3
  170.6 0.3 pad_maximum_fusion
  170.9 5.9 %convolution_convert_fusion.2.query_ref = bf16[256,1024]{1,0:T(8,128)(2,1)S(1)} fusion(bf16[256,4096]{1,0:T(8,128)(2,1)S(1)} %bitcast.85, bf16[4096,1024]{1,0:T(8,128)(2,1)} %param.19), kind=kOutput, calls=%fused_computation.4 | convolution fusion | flops 2147745792 | bytes 11010048 | tf_op jit(solution)/shard_map/dot_general | solution.py:297
  176.9 1.6 copy-done.4
  178.5 8.9 %project_encodings.1 = (bf16[1280,1024]{1,0:T(8,128)(2,1)}, bf16[1280,1024]{1,0:T(8,128)(2,1)}) custom-call(s32[20]{0:T(128)S(1)} %reshape.68.where_ref, bf16[8,1,4,128,1024]{4,3,2,1,0:T(8,128)(2,1)} %bitcast.72, bf16[8,1,4,128,1024]{4,3,2,1,0:T(8,128)(2,1)} %bitcast.73, bf16[1024,1024]{1,0:T(8,128)(2,1)S(1)} %copy-done.3, bf16[1024,1024]{1,0:T(8,128)(2,1)S(1)} %copy-done.4), custom_call_target="tpu_custom_call" | custom-call | flops 5368709120 | bytes 12058624 | tf_op jit(solution)/shard_map/project_encodings/pallas_call | solution.py:175
  187.4 1.7 copy-done.2
  189.1 9.8 %cross_attend.1 = bf16[256,1024]{1,0:T(8,128)(2,1)S(1)} custom-call(s32[1]{0:T(128)} %bitcast.16.live_ref, bf16[256,1024]{1,0:T(8,128)(2,1)S(1)} %convolution_convert_fusion.2.query_ref, bf16[1280,1024]{1,0:T(8,128)(2,1)S(1)} %copy-done.2, bf16[1280,1024]{1,0:T(8,128)(2,1)} %get-tuple-element.12.values_ref), custom_call_target="tpu_custom_call" | custom-call | flops 536870912 | bytes 6291456 | tf_op jit(solution)/shard_map/cross_attend/pallas_call | solution.py:226
  199.0 5.7 %convolution_convert_fusion = bf16[256,4096]{1,0:T(8,128)(2,1)S(1)} fusion(bf16[256,1024]{1,0:T(8,128)(2,1)S(1)} %cross_attend.1, bf16[1024,4096]{1,0:T(8,128)(2,1)} %param.22), kind=kOutput, calls=%fused_computation | convolution fusion | flops 2148532224 | bytes 11010048 | tf_op jit(solution)/shard_map/dot_general | solution.py:303
  204.8 1.4 collective-permute-start.13
  206.2 0.7 collective-permute-start.16
  206.9 11.2 %collective-permute-done.13 = bf16[64,4096]{1,0:T(8,128)(2,1)S(1)} collective-permute-done((bf16[64,4096]{1,0:T(8,128)(2,1)S(1)}, bf16[64,4096]{1,0:T(8,128)(2,1)S(1)}, u32[]{:S(2)}, u32[]{:S(2)}) %collective-permute-start.13) | collective-permute-done | bytes 524320 | tf_op jit(solution)/shard_map/ppermute | solution.py:25
  218.2 4.5 %collective-permute-start.14 = (bf16[64,4096]{1,0:T(8,128)(2,1)S(1)}, bf16[64,4096]{1,0:T(8,128)(2,1)S(1)}, u32[]{:S(2)}, u32[]{:S(2)}) collective-permute-start(bf16[64,4096]{1,0:T(8,128)(2,1)S(1)} %fusion.2), channel_id=1, source_target_pairs={{0,1},{1,2},{4,5},{5,6},{8,9},{9,10},{12,13},{13,14},{16,17},{17,1... | collective-permute-start | bytes 1572872 | tf_op jit(solution)/shard_map/ppermute | solution.py:25
  222.8 11.1 %collective-permute-done.14 = bf16[64,4096]{1,0:T(8,128)(2,1)S(1)} collective-permute-done((bf16[64,4096]{1,0:T(8,128)(2,1)S(1)}, bf16[64,4096]{1,0:T(8,128)(2,1)S(1)}, u32[]{:S(2)}, u32[]{:S(2)}) %collective-permute-start.14) | collective-permute-done | bytes 524320 | tf_op jit(solution)/shard_map/ppermute | solution.py:25
  233.9 0.2 fusion.3
  234.2 0.7 collective-permute-start.17
  234.9 5.0 %collective-permute-start.15 = (bf16[64,4096]{1,0:T(8,128)(2,1)S(1)}, bf16[64,4096]{1,0:T(8,128)(2,1)S(1)}, u32[]{:S(2)}, u32[]{:S(2)}) collective-permute-start(bf16[64,4096]{1,0:T(8,128)(2,1)S(1)} %get-tuple-element.19), channel_id=1, source_target_pairs={{0,1},{1,2},{2,3},{4,5},{5,6},{6,7},{8,9},{9,10},{10,11},{12,13},{... | collective-permute-start | bytes 1572872 | tf_op jit(solution)/shard_map/ppermute | solution.py:25
  239.9 0.1 fusion.1
  240.1 1.4 collective-permute-start.18
  241.5 8.7 %collective-permute-done.15 = bf16[64,4096]{1,0:T(8,128)(2,1)S(1)} collective-permute-done((bf16[64,4096]{1,0:T(8,128)(2,1)S(1)}, bf16[64,4096]{1,0:T(8,128)(2,1)S(1)}, u32[]{:S(2)}, u32[]{:S(2)}) %collective-permute-start.15) | collective-permute-done | bytes 524320 | tf_op jit(solution)/shard_map/ppermute | solution.py:25
  250.2 13.5 %collective-permute-done.18 = bf16[64,4096]{1,0:T(8,128)(2,1)S(1)} collective-permute-done((bf16[64,4096]{1,0:T(8,128)(2,1)S(1)}, bf16[64,4096]{1,0:T(8,128)(2,1)S(1)}, u32[]{:S(2)}, u32[]{:S(2)}) %collective-permute-start.18) | collective-permute-done | bytes 524320 | tf_op jit(solution)/shard_map/ppermute | solution.py:25
  263.7 1.2 fusion.5
  (42 shorter events, 1.1 us)
Async XLA Ops:
  6.5 13.9 %copy-start = (bf16[8,128,1024]{2,1,0:T(8,128)(2,1)S(1)}, bf16[8,128,1024]{2,1,0:T(8,128)(2,1)}, u32[]{:S(2)}) copy-start(bf16[8,128,1024]{2,1,0:T(8,128)(2,1)} %param.23) | copy-start | bytes 6291460
  15.2 26.3 %all-to-all-start = ((bf16[8,3,256,128]{3,2,1,0:T(8,128)(2,1)}), bf16[8,3,256,128]{3,2,1,0:T(8,128)(2,1)}, u32[]{:S(2)}, u32[]{:S(2)}) async-start(bf16[8,3,256,128]{3,2,1,0:T(8,128)(2,1)} %maximum_bitcast_fusion), calls=%async_computation | async-start | bytes 3145728 | tf_op jit(solution)/shard_map/all_to_all | solution.py:113
  20.4 39.6 %all-gather.5.cloned.1.call-start = ((), (), s32[]{:S(2)}) async-start(), calls=%async_computation.2 | async-start | bytes 1310720 | tf_op jit(solution)/shard_map/all_gather | solution.py:271
  21.2 155.6 %all-gather.7.cloned.1.call-start = ((), (), s32[]{:S(2)}) async-start(), calls=%async_computation.3 | async-start | bytes 9437184 | tf_op jit(solution)/shard_map/all_gather | solution.py:282
  66.7 14.4 %collective-permute-start = (bf16[64,4096]{1,0:T(8,128)(2,1)S(1)}, bf16[64,4096]{1,0:T(8,128)(2,1)S(1)}, u32[]{:S(2)}, u32[]{:S(2)}) collective-permute-start(bf16[64,4096]{1,0:T(8,128)(2,1)S(1)} %get-tuple-element.25), channel_id=1, source_target_pairs={{0,1},{4,5},{8,9},{12,13},{16,17},{20,21},{24,25},{28,29}} | collective-permute-start | bytes 1572872 | tf_op jit(solution)/shard_map/ppermute | solution.py:25
  70.7 15.1 %collective-permute-start.3 = (bf16[64,4096]{1,0:T(8,128)(2,1)}, bf16[64,4096]{1,0:T(8,128)(2,1)}, u32[]{:S(2)}, u32[]{:S(2)}) collective-permute-start(bf16[64,4096]{1,0:T(8,128)(2,1)} %get-tuple-element.26), channel_id=1, source_target_pairs={{3,2},{7,6},{11,10},{15,14},{19,18},{23,22},{27,26},{31,30}} | collective-permute-start | bytes 1572872 | tf_op jit(solution)/shard_map/ppermute | solution.py:25
  81.3 14.1 %collective-permute-start.1 = (bf16[64,4096]{1,0:T(8,128)(2,1)S(1)}, bf16[64,4096]{1,0:T(8,128)(2,1)S(1)}, u32[]{:S(2)}, u32[]{:S(2)}) collective-permute-start(bf16[64,4096]{1,0:T(8,128)(2,1)S(1)} %fusion.8), channel_id=1, source_target_pairs={{0,1},{1,2},{4,5},{5,6},{8,9},{9,10},{12,13},{13,14},{16,17},{17,1... | collective-permute-start | bytes 1572872 | tf_op jit(solution)/shard_map/ppermute | solution.py:25
  85.7 20.1 %copy-start.8 = (bf16[4096]{0:T(1024)(128)(2,1)S(1)}, bf16[4096]{0:T(1024)(128)(2,1)}, u32[]{:S(2)}) copy-start(bf16[4096]{0:T(1024)(128)(2,1)} %param.18) | copy-start | bytes 24580
  97.6 5.7 %collective-permute-start.4 = (bf16[64,4096]{1,0:T(8,128)(2,1)}, bf16[64,4096]{1,0:T(8,128)(2,1)}, u32[]{:S(2)}, u32[]{:S(2)}) collective-permute-start(bf16[64,4096]{1,0:T(8,128)(2,1)} %get-tuple-element.24), channel_id=1, source_target_pairs={{2,1},{3,2},{6,5},{7,6},{10,9},{11,10},{14,13},{15,14},{18,17},{19... | collective-permute-start | bytes 1572872 | tf_op jit(solution)/shard_map/ppermute | solution.py:25
  99.1 13.4 %collective-permute-start.2 = (bf16[64,4096]{1,0:T(8,128)(2,1)}, bf16[64,4096]{1,0:T(8,128)(2,1)S(1)}, u32[]{:S(2)}, u32[]{:S(2)}) collective-permute-start(bf16[64,4096]{1,0:T(8,128)(2,1)} %get-tuple-element.23), channel_id=1, source_target_pairs={{0,1},{1,2},{2,3},{4,5},{5,6},{6,7},{8,9},{9,10},{10,11},{12,13},{... | collective-permute-start | bytes 1572872 | tf_op jit(solution)/shard_map/ppermute | solution.py:25
  104.6 21.0 %collective-permute-start.5 = (bf16[64,4096]{1,0:T(8,128)(2,1)S(1)}, bf16[64,4096]{1,0:T(8,128)(2,1)}, u32[]{:S(2)}, u32[]{:S(2)}) collective-permute-start(bf16[64,4096]{1,0:T(8,128)(2,1)S(1)} %fusion.7), channel_id=1, source_target_pairs={{1,0},{2,1},{3,2},{5,4},{6,5},{7,6},{9,8},{10,9},{11,10},{13,12},{... | collective-permute-start | bytes 1572872 | tf_op jit(solution)/shard_map/ppermute | solution.py:25
  105.9 51.6 %copy-start.9 = (s32[4,2]{0,1:T(2,128)S(1)}, s32[4,2]{0,1:T(2,128)}, u32[]{:S(2)}) copy-start(s32[4,2]{0,1:T(2,128)} %param.24) | copy-start | bytes 100
  105.9 51.6 %copy-start.10 = (s32[4,2]{0,1:T(2,128)S(1)}, s32[4,2]{0,1:T(2,128)}, u32[]{:S(2)}) copy-start(s32[4,2]{0,1:T(2,128)} %param.25) | copy-start | bytes 100
  112.5 0.8 copy-start.7
  127.3 41.6 %copy-start.5 = (f32[64,4096]{1,0:T(8,128)}, f32[64,4096]{1,0:T(8,128)S(1)}, u32[]{:S(2)}) copy-start(f32[64,4096]{1,0:T(8,128)S(1)} %get-tuple-element.14) | copy-start | bytes 3145732
  127.6 10.7 %collective-permute-start.9 = (bf16[64,4096]{1,0:T(8,128)(2,1)S(1)}, bf16[64,4096]{1,0:T(8,128)(2,1)S(1)}, u32[]{:S(2)}, u32[]{:S(2)}) collective-permute-start(bf16[64,4096]{1,0:T(8,128)(2,1)S(1)} %multiply_convert_fusion), channel_id=1, source_target_pairs={{0,1},{1,2},{2,3},{4,5},{5,6},{6,7},{8,9},{9,10},{10,11},{12,13},{... | collective-permute-start | bytes 1572872 | tf_op jit(solution)/shard_map/ppermute | solution.py:25
  131.2 12.0 %collective-permute-start.6 = (bf16[64,4096]{1,0:T(8,128)(2,1)S(1)}, bf16[64,4096]{1,0:T(8,128)(2,1)S(1)}, u32[]{:S(2)}, u32[]{:S(2)}) collective-permute-start(bf16[64,4096]{1,0:T(8,128)(2,1)S(1)} %multiply_convert_fusion), channel_id=1, source_target_pairs={{1,0},{2,1},{3,2},{5,4},{6,5},{7,6},{9,8},{10,9},{11,10},{13,12},{... | collective-permute-start | bytes 1572872 | tf_op jit(solution)/shard_map/ppermute | solution.py:25
  138.2 6.3 %collective-permute-start.10 = (bf16[64,4096]{1,0:T(8,128)(2,1)S(1)}, bf16[64,4096]{1,0:T(8,128)(2,1)S(1)}, u32[]{:S(2)}, u32[]{:S(2)}) collective-permute-start(bf16[64,4096]{1,0:T(8,128)(2,1)S(1)} %collective-permute-done.9), channel_id=1, source_target_pairs={{1,2},{2,3},{5,6},{6,7},{9,10},{10,11},{13,14},{14,15},{17,18},{18... | collective-permute-start | bytes 1572872 | tf_op jit(solution)/shard_map/ppermute | solution.py:25
  143.2 13.0 %collective-permute-start.7 = (bf16[64,4096]{1,0:T(8,128)(2,1)S(1)}, bf16[64,4096]{1,0:T(8,128)(2,1)S(1)}, u32[]{:S(2)}, u32[]{:S(2)}) collective-permute-start(bf16[64,4096]{1,0:T(8,128)(2,1)S(1)} %collective-permute-done.6), channel_id=1, source_target_pairs={{1,0},{2,1},{5,4},{6,5},{9,8},{10,9},{13,12},{14,13},{17,16},{18,1... | collective-permute-start | bytes 1572872 | tf_op jit(solution)/shard_map/ppermute | solution.py:25
  144.5 15.6 %collective-permute-start.11 = (bf16[64,4096]{1,0:T(8,128)(2,1)S(1)}, bf16[64,4096]{1,0:T(8,128)(2,1)}, u32[]{:S(2)}, u32[]{:S(2)}) collective-permute-start(bf16[64,4096]{1,0:T(8,128)(2,1)S(1)} %collective-permute-done.10), channel_id=1, source_target_pairs={{2,3},{6,7},{10,11},{14,15},{18,19},{22,23},{26,27},{30,31}} | collective-permute-start | bytes 1572872 | tf_op jit(solution)/shard_map/ppermute | solution.py:25
  156.2 11.2 %collective-permute-start.8 = (bf16[64,4096]{1,0:T(8,128)(2,1)S(1)}, bf16[64,4096]{1,0:T(8,128)(2,1)}, u32[]{:S(2)}, u32[]{:S(2)}) collective-permute-start(bf16[64,4096]{1,0:T(8,128)(2,1)S(1)} %collective-permute-done.7), channel_id=1, source_target_pairs={{1,0},{5,4},{9,8},{13,12},{17,16},{21,20},{25,24},{29,28}} | collective-permute-start | bytes 1572872 | tf_op jit(solution)/shard_map/ppermute | solution.py:25
  157.7 2.1 collective-permute-start.12
  170.9 6.0 %copy-start.3 = (bf16[1024,1024]{1,0:T(8,128)(2,1)S(1)}, bf16[1024,1024]{1,0:T(8,128)(2,1)}, u32[]{:S(2)}) copy-start(bf16[1024,1024]{1,0:T(8,128)(2,1)} %wk_ref.1) | copy-start | bytes 6291460
  176.9 1.6 copy-start.4
  187.4 1.7 copy-start.2
  204.8 13.3 %collective-permute-start.13 = (bf16[64,4096]{1,0:T(8,128)(2,1)S(1)}, bf16[64,4096]{1,0:T(8,128)(2,1)S(1)}, u32[]{:S(2)}, u32[]{:S(2)}) collective-permute-start(bf16[64,4096]{1,0:T(8,128)(2,1)S(1)} %get-tuple-element.21), channel_id=1, source_target_pairs={{0,1},{4,5},{8,9},{12,13},{16,17},{20,21},{24,25},{28,29}} | collective-permute-start | bytes 1572872 | tf_op jit(solution)/shard_map/ppermute | solution.py:25
  206.2 16.6 %collective-permute-start.16 = (bf16[64,4096]{1,0:T(8,128)(2,1)S(1)}, bf16[64,4096]{1,0:T(8,128)(2,1)S(1)}, u32[]{:S(2)}, u32[]{:S(2)}) collective-permute-start(bf16[64,4096]{1,0:T(8,128)(2,1)S(1)} %get-tuple-element.22), channel_id=1, source_target_pairs={{3,2},{7,6},{11,10},{15,14},{19,18},{23,22},{27,26},{31,30}} | collective-permute-start | bytes 1572872 | tf_op jit(solution)/shard_map/ppermute | solution.py:25
  218.2 45.5 %copy-start.6 = (f32[64,4096]{1,0:T(8,128)S(1)}, f32[64,4096]{1,0:T(8,128)}, u32[]{:S(2)}) copy-start(f32[64,4096]{1,0:T(8,128)} %copy-done.5) | copy-start | bytes 3145732
  218.2 15.7 %collective-permute-start.14 = (bf16[64,4096]{1,0:T(8,128)(2,1)S(1)}, bf16[64,4096]{1,0:T(8,128)(2,1)S(1)}, u32[]{:S(2)}, u32[]{:S(2)}) collective-permute-start(bf16[64,4096]{1,0:T(8,128)(2,1)S(1)} %fusion.2), channel_id=1, source_target_pairs={{0,1},{1,2},{4,5},{5,6},{8,9},{9,10},{12,13},{13,14},{16,17},{17,1... | collective-permute-start | bytes 1572872 | tf_op jit(solution)/shard_map/ppermute | solution.py:25
  234.2 5.7 %collective-permute-start.17 = (bf16[64,4096]{1,0:T(8,128)(2,1)S(1)}, bf16[64,4096]{1,0:T(8,128)(2,1)S(1)}, u32[]{:S(2)}, u32[]{:S(2)}) collective-permute-start(bf16[64,4096]{1,0:T(8,128)(2,1)S(1)} %get-tuple-element.20), channel_id=1, source_target_pairs={{2,1},{3,2},{6,5},{7,6},{10,9},{11,10},{14,13},{15,14},{18,17},{19... | collective-permute-start | bytes 1572872 | tf_op jit(solution)/shard_map/ppermute | solution.py:25
  234.9 15.3 %collective-permute-start.15 = (bf16[64,4096]{1,0:T(8,128)(2,1)S(1)}, bf16[64,4096]{1,0:T(8,128)(2,1)S(1)}, u32[]{:S(2)}, u32[]{:S(2)}) collective-permute-start(bf16[64,4096]{1,0:T(8,128)(2,1)S(1)} %get-tuple-element.19), channel_id=1, source_target_pairs={{0,1},{1,2},{2,3},{4,5},{5,6},{6,7},{8,9},{9,10},{10,11},{12,13},{... | collective-permute-start | bytes 1572872 | tf_op jit(solution)/shard_map/ppermute | solution.py:25
  239.9 25.0 %copy-start.1 = (bf16[8,128,1024]{2,1,0:T(8,128)(2,1)S(1)}, bf16[8,128,1024]{2,1,0:T(8,128)(2,1)}, u32[]{:S(2)}) copy-start(bf16[8,128,1024]{2,1,0:T(8,128)(2,1)} %param.23) | copy-start | bytes 6291460
  240.1 23.6 %collective-permute-start.18 = (bf16[64,4096]{1,0:T(8,128)(2,1)S(1)}, bf16[64,4096]{1,0:T(8,128)(2,1)S(1)}, u32[]{:S(2)}, u32[]{:S(2)}) collective-permute-start(bf16[64,4096]{1,0:T(8,128)(2,1)S(1)} %fusion.1), channel_id=1, source_target_pairs={{1,0},{2,1},{3,2},{5,4},{6,5},{7,6},{9,8},{10,9},{11,10},{13,12},{... | collective-permute-start | bytes 1572872 | tf_op jit(solution)/shard_map/ppermute | solution.py:25
Sparse Core Ops, SparseCore 0:
  22.8 30.1 all-gather.4
  60.2 54.2 all-gather.6

commit v2 on v1

--- a/solution.py
+++ b/solution.py
@@ -44,20 +44,23 @@
             up_block, down_block = add_rounded(up_block, up), add_rounded(down_block, down)
         up = shift(up_block, "db", 1, range(step + 1))
         down = shift(down_block, "db", -1, range(size - 1 - step, size))
+        up, down = lax.optimization_barrier((up, down))
     total = pick(me).astype(jnp.float32)
     return total + up.astype(jnp.float32) + down.astype(jnp.float32)
 
 
-def line_all_gather(block):
+def line_all_gather(block, beside):
     size = lax.axis_size("db")
     me = lax.axis_index("db")
-    whole = jnp.zeros((size,) + block.shape, block.dtype)
-    whole = lax.dynamic_update_index_in_dim(whole, block, me, 0)
     up = down = block
     pieces = []
     for step in range(size - 1):
         up = shift(up, "db", 1, range(step, size))
         down = shift(down, "db", -1, range(0, size - step))
+        if step == (size - 1) // 2:
+            up, down, beside = lax.optimization_barrier((up, down, beside))
+        else:
+            up, down = lax.optimization_barrier((up, down))
         pieces.append((step + 1, up, down))
     parts = []
     for owner in range(size):
@@ -66,7 +69,7 @@
             chosen = jnp.where(me - owner == distance, from_low, chosen)
             chosen = jnp.where(owner - me == distance, from_high, chosen)
         parts.append(chosen)
-    return jnp.stack(parts)
+    return jnp.stack(parts), beside
 
 
 def self_kernel(qkv_ref, out_ref, *, blocks, rows, scale):
@@ -105,11 +108,41 @@
     )(qkv)
 
 
+def pack_kernel(query_ref, key_ref, value_ref, out_ref, sems, *, heads):
+    copies = []
+    for head in range(heads):
+        for which, ref in enumerate((query_ref, key_ref, value_ref)):
+            copies.append(
+                pltpu.make_async_copy(
+                    ref.at[:, pl.ds(head * HD, HD)], out_ref.at[head, which], sems.at[head, which]
+                )
+            )
+    for copy in copies:
+        copy.start()
+    for copy in copies:
+        copy.wait()
+
+
+def pack_heads(query_rows, key_rows, value_rows):
+    rows, width = query_rows.shape
+    heads = width // HD
+    anywhere = pl.BlockSpec(memory_space=pl.ANY)
+    return pl.pallas_call(
+        functools.partial(pack_kernel, heads=heads),
+        out_shape=jax.ShapeDtypeStruct((heads, 3, rows, HD), jnp.bfloat16),
+        in_specs=[anywhere] * 3,
+        out_specs=anywhere,
+        scratch_shapes=[pltpu.SemaphoreType.DMA((heads, 3))],
+        cost_estimate=pl.CostEstimate(
+            flops=0, bytes_accessed=12 * rows * width, transcendentals=0
+        ),
+        name="pack_heads",
+    )(query_rows, key_rows, value_rows)
+
+
 def self_attention_by_head(query_rows, key_rows, value_rows, scale):
     rows, width = query_rows.shape
-    count = lax.axis_size("seq")
-    packed = jnp.stack((query_rows, key_rows, value_rows)).reshape(3, rows, count, HD)
-    packed = packed.transpose(2, 0, 1, 3)
+    packed = pack_heads(query_rows, key_rows, value_rows)
     held = lax.all_to_all(packed, "seq", 0, 0, tiled=True)
     mixed = self_attend_head(held, scale)
     back = lax.all_to_all(mixed, "seq", 0, 0, tiled=True)
@@ -193,31 +226,41 @@
     )(where, table, table, w_cross_k, w_cross_v)
 
 
+def cross_group(query, keys, values, scale):
+    rows = query.shape[0]
+    first = lax.broadcasted_iota(jnp.int32, (rows, 2 * HD), 1) < HD
+    nothing = jnp.zeros_like(query)
+    apart = jnp.concatenate(
+        (jnp.where(first, query, nothing), jnp.where(first, nothing, query)), axis=0
+    )
+    scores = lax.dot_general(
+        apart, keys, (((1,), (1,)), ((), ())), preferred_element_type=jnp.float32
+    ) * (scale * LOG2E)
+    weights = jnp.exp2(scores - jnp.max(scores, axis=-1, keepdims=True))
+    total = jnp.sum(weights, axis=-1, keepdims=True)
+    mixed = jnp.dot(weights.astype(jnp.bfloat16), values, preferred_element_type=jnp.float32)
+    mixed = mixed / total
+    return jnp.where(first, mixed[:rows], mixed[rows:])
+
+
 def cross_kernel(live_ref, query_ref, keys_ref, values_ref, out_ref, *, spans, heads, scale):
-    row = lax.broadcasted_iota(jnp.int32, (SPAN, 2 * GROUP), 0)
-    column = lax.broadcasted_iota(jnp.int32, (SPAN, 2 * GROUP), 1)
-    allowed = (column >= GROUP) == (row == SPAN - 1)
+    tail = 16
+    row = lax.broadcasted_iota(jnp.int32, (tail, 2 * HD), 0)
     for span in range(spans):
-        for head in range(heads):
-            lanes = slice(head * HD, (head + 1) * HD)
-            query = query_ref[span * SPAN : (span + 1) * SPAN, lanes]
-            keys = keys_ref[span * GROUP : (span + 2) * GROUP, lanes]
-            values = values_ref[span * GROUP : (span + 2) * GROUP, lanes]
-            scores = lax.dot_general(
-                query, keys, (((1,), (1,)), ((), ())), preferred_element_type=jnp.float32
+        top = span * SPAN
+        for pair in range(heads // 2):
+            lanes = slice(2 * pair * HD, 2 * (pair + 1) * HD)
+            here, after = (slice((span + k) * GROUP, (span + k + 1) * GROUP) for k in (0, 1))
+            query = query_ref[top : top + SPAN, lanes]
+            mixed = cross_group(query, keys_ref[here, lanes], values_ref[here, lanes], scale)
+            last = cross_group(
+                query[SPAN - tail :], keys_ref[after, lanes], values_ref[after, lanes], scale
             )
-            scores = jnp.where(allowed, scores * (scale * LOG2E), NEG_BIG)
-            top = jnp.max(scores, axis=-1, keepdims=True)
-            weights = jnp.exp2(scores - top)
-            total = jnp.sum(weights, axis=-1, keepdims=True)
-            mixed = jnp.dot(
-                weights.astype(jnp.bfloat16), values, preferred_element_type=jnp.float32
-            )
-            mixed = mixed / total
             if span == 0:
-                own = lax.broadcasted_iota(jnp.int32, (SPAN, HD), 0) == SPAN - 1
-                mixed = jnp.where(own | (live_ref[0] > 0), mixed, 0.0)
-            out_ref[span * SPAN : (span + 1) * SPAN, lanes] = mixed.astype(jnp.bfloat16)
+                mixed = jnp.where(live_ref[0] > 0, mixed, 0.0)
+            last = jnp.where(row == tail - 1, last, mixed[SPAN - tail :])
+            out_ref[top : top + SPAN - tail, lanes] = mixed[: SPAN - tail].astype(jnp.bfloat16)
+            out_ref[top + SPAN - tail : top + SPAN, lanes] = last.astype(jnp.bfloat16)
 
 
 def cross_attend(live, query, keys, values, scale):
@@ -268,6 +311,9 @@
     part = lax.dynamic_slice_in_dim(
         enc_table.reshape(rows_shard * NLEN, depth), seq_index * piece, piece, 0
     )
+    part, query_rows, key_rows, value_rows = lax.optimization_barrier(
+        (part, query_rows, key_rows, value_rows)
+    )
     along_db = lax.all_gather(part, "db", axis=0)
     wanted = jnp.stack((nb_row, nb_shard), axis=-1).astype(jnp.int32)
     before = shift(wanted[-1], "seq", 1, range(n_seq))
@@ -293,11 +339,12 @@
     normed_share = (
         residual * lax.rsqrt(mean_square + 1e-05) * norm_gain.astype(jnp.float32)
     ).astype(jnp.bfloat16)
-    normed = line_all_gather(normed_share).reshape(rows, features)
+    projected = project_encodings(where, table, w_cross_k, w_cross_v)
+    normed, (keys, values) = line_all_gather(normed_share, projected)
+    normed = normed.reshape(rows, features)
     cross_query = jnp.dot(normed, w_cross_q, preferred_element_type=jnp.float32).astype(
         jnp.bfloat16
     )
-    keys, values = project_encodings(where, table, w_cross_k, w_cross_v)
     live = (seq_index > 0).astype(jnp.int32).reshape(1)
     mixed = cross_attend(live, cross_query, keys, values, scale)
     out_partial = jnp.dot(mixed, w_cross_out, preferred_element_type=jnp.float32).astype(

time: 273 us -> 277 us (1.015)
  Pallas kernels: 24.8 us -> 73.1 us
  waiting for transfers between devices: 130 us -> 91.2 us
  local copies, waits for them, and re-layouts: 12.6 us -> 6.4 us
  starting transfers between devices: 47 us -> 52 us
  matrix products: 17.4 us -> 14 us
    pallas_call x0 -> x1, Pallas kernels: none -> 49 us  [pack_heads(): pl.pallas_call(functools.partial(pack_kernel, heads=heads), out_shape=jax...]
    ppermute x19, waiting for transfers between devices: 110 us -> 70.2 us  [shift(): return lax.ppermute(block, axis, route)]
    ppermute x19, starting transfers between devices: 41.8 us -> 46.8 us  [shift(): return lax.ppermute(block, axis, route)]
    unnamed x25 -> x24, local copies, waits for them, and re-layouts: 8.05 us -> 4.01 us
    dot_general x1, matrix products: 5.73 us -> 2.34 us  [per_device(): jnp.dot(mixed, w_cross_out, preferred_element_type=jnp.float32)]
  transfers between devices with their start and end apart: 22 -> 22, of which waited for: 14 -> 14; matrix products, arithmetic and copies ran while one was open for 9% -> 5% of each run, Pallas kernels for 2% -> 5%
where the time goes in v2:
time: 277 us; the launch traced here: 276 us
  waiting for transfers between devices  91.2 us (33%)
  Pallas kernels  73.1 us (26%)
  starting transfers between devices  52 us (19%)
  matrix products  14 us (5%)
  between operations  13.8 us (5%)
  other arithmetic  13.1 us (5%)
  blocking collectives  12.2 us (4%)
  local copies, waits for them, and re-layouts  6.4 us (2%)
    ppermute x19, waiting for transfers between devices, shift(): return lax.ppermute(block, axis, route)  70.2 us
    pallas_call x1, Pallas kernels, pack_heads(): pl.pallas_call(functools.partial(pack_kernel, heads=heads), out_shape=jax...  49 us
    ppermute x19, starting transfers between devices, shift(): return lax.ppermute(block, axis, route)  46.8 us
    all_to_all x1, waiting for transfers between devices, self_attention_by_head(): held = lax.all_to_all(packed, 'seq', 0, 0, tiled=True)  20.2 us
    all_to_all x1, blocking collectives, self_attention_by_head(): back = lax.all_to_all(mixed, 'seq', 0, 0, tiled=True)  12.2 us
    pallas_call x1, Pallas kernels, cross_attend(): pl.pallas_call(functools.partial(cross_kernel, spans=rows // SPAN, heads=...  10.5 us
    pallas_call x1, Pallas kernels, project_encodings(): pl.pallas_call(project_kernel, out_shape=[jax.ShapeDtypeStruct((groups *...  8.94 us
    dot_general x1, matrix products, per_device(): jnp.dot(normed, w_cross_q, preferred_element_type=jnp.float32)  5.87 us
  transfers between devices with their start and end apart: 22, of which 14 were waited for; matrix products, arithmetic and copies ran while one was open for 5% of the time, Pallas kernels for 5%

profile of v2, /device:TPU:0, one launch (start us, length us, event | category | flops | bytes accessed | tf_op | source)
XLA Modules:
  0.0 275.8 jit_solution(17695371289144791015)
XLA Ops:
  6.5 1.6 copy-done
  8.1 0.7 constant_dynamic-slice_fusion
  8.8 49.0 %pack_heads.1 = bf16[8,3,256,128]{3,2,1,0:T(8,128)(2,1)} custom-call(bf16[256,1024]{1,0:T(8,128)(2,1)} %query_ref, bf16[256,1024]{1,0:T(8,128)(2,1)} %key_ref, bf16[256,1024]{1,0:T(8,128)(2,1)} %value_ref), custom_call_target="tpu_custom_call" | custom-call | bytes 3145728 | tf_op jit(solution)/shard_map/pack_heads/pallas_call | solution.py:130
  57.8 5.2 %all-to-all-start = ((bf16[8,3,256,128]{3,2,1,0:T(8,128)(2,1)}), bf16[8,3,256,128]{3,2,1,0:T(8,128)(2,1)S(1)}, u32[]{:S(2)}, u32[]{:S(2)}) async-start(bf16[8,3,256,128]{3,2,1,0:T(8,128)(2,1)} %pack_heads.1), calls=%async_computation | async-start | bytes 3145728 | tf_op jit(solution)/shard_map/all_to_all | solution.py:146
  63.0 0.7 all-gather.5.cloned.1.call-update
  63.8 20.2 %all-to-all-done.qkv_ref = bf16[8,3,256,128]{3,2,1,0:T(8,128)(2,1)S(1)} async-done(((bf16[8,3,256,128]{3,2,1,0:T(8,128)(2,1)}), bf16[8,3,256,128]{3,2,1,0:T(8,128)(2,1)S(1)}, u32[]{:S(2)}, u32[]{:S(2)}) %all-to-all-start) | async-done | bytes 1572896 | tf_op jit(solution)/shard_map/all_to_all | solution.py:146
  84.0 4.7 %self_attend.1 = bf16[8,256,128]{2,1,0:T(8,128)(2,1)S(1)} custom-call(bf16[8,3,256,128]{3,2,1,0:T(8,128)(2,1)S(1)} %all-to-all-done.qkv_ref), custom_call_target="tpu_custom_call" | custom-call | flops 1073741824 | bytes 2097152 | tf_op jit(solution)/shard_map/self_attend/pallas_call | solution.py:96
  88.7 12.2 %all_to_all.10 = bf16[8,256,128]{2,1,0:T(8,128)(2,1)S(1)} all-to-all(bf16[8,256,128]{2,1,0:T(8,128)(2,1)S(1)} %self_attend.1), channel_id=1, replica_groups=mesh['seq'=8,'db'=4] {'seq'}, dimensions={0} | all-to-all | bytes 1048576 | tf_op jit(solution)/shard_map/all_to_all | solution.py:148
  100.9 0.2 copy.21
  101.1 5.8 %convolution_convert_fusion.1 = bf16[256,4096]{1,0:T(8,128)(2,1)S(1)} fusion(bf16[256,1024]{0,1:T(8,128)(2,1)S(1)} %bitcast.77, bf16[1024,4096]{1,0:T(8,128)(2,1)} %param.17), kind=kOutput, calls=%fused_computation.1 | convolution fusion | flops 2148532224 | bytes 11010048 | tf_op jit(solution)/shard_map/dot_general | solution.py:332
  106.9 1.0 dynamic-slice_bitcast_fusion.2
  107.9 0.7 collective-permute-start.1
  108.6 4.3 %collective-permute-start = (bf16[64,4096]{1,0:T(8,128)(2,1)S(1)}, bf16[64,4096]{1,0:T(8,128)(2,1)}, u32[]{:S(2)}, u32[]{:S(2)}) collective-permute-start(bf16[64,4096]{1,0:T(8,128)(2,1)S(1)} %get-tuple-element.78), channel_id=1, source_target_pairs={{0,1},{4,5},{8,9},{12,13},{16,17},{20,21},{24,25},{28,29}} | collective-permute-start | bytes 1572872 | tf_op jit(solution)/shard_map/ppermute | solution.py:25
  112.9 9.7 %collective-permute-done = bf16[64,4096]{1,0:T(8,128)(2,1)} collective-permute-done((bf16[64,4096]{1,0:T(8,128)(2,1)S(1)}, bf16[64,4096]{1,0:T(8,128)(2,1)}, u32[]{:S(2)}, u32[]{:S(2)}) %collective-permute-start) | collective-permute-done | bytes 524320 | tf_op jit(solution)/shard_map/ppermute | solution.py:25
  122.6 2.1 fusion.7
  124.7 0.8 collective-permute-start.3
  125.5 5.9 %collective-permute-start.2 = (bf16[64,4096]{1,0:T(8,128)(2,1)S(1)}, bf16[64,4096]{1,0:T(8,128)(2,1)}, u32[]{:S(2)}, u32[]{:S(2)}) collective-permute-start(bf16[64,4096]{1,0:T(8,128)(2,1)S(1)} %get-tuple-element.76), channel_id=1, source_target_pairs={{0,1},{1,2},{4,5},{5,6},{8,9},{9,10},{12,13},{13,14},{16,17},{17,1... | collective-permute-start | bytes 1572872 | tf_op jit(solution)/shard_map/ppermute | solution.py:25
  131.4 8.8 %collective-permute-done.2 = bf16[64,4096]{1,0:T(8,128)(2,1)} collective-permute-done((bf16[64,4096]{1,0:T(8,128)(2,1)S(1)}, bf16[64,4096]{1,0:T(8,128)(2,1)}, u32[]{:S(2)}, u32[]{:S(2)}) %collective-permute-start.2) | collective-permute-done | bytes 524320 | tf_op jit(solution)/shard_map/ppermute | solution.py:25
  140.2 2.1 fusion.6
  142.3 1.3 collective-permute-start.5
  143.6 5.9 %collective-permute-start.4 = (bf16[64,4096]{1,0:T(8,128)(2,1)S(1)}, bf16[64,4096]{1,0:T(8,128)(2,1)}, u32[]{:S(2)}, u32[]{:S(2)}) collective-permute-start(bf16[64,4096]{1,0:T(8,128)(2,1)S(1)} %get-tuple-element.74), channel_id=1, source_target_pairs={{0,1},{1,2},{2,3},{4,5},{5,6},{6,7},{8,9},{9,10},{10,11},{12,13},{... | collective-permute-start | bytes 1572872 | tf_op jit(solution)/shard_map/ppermute | solution.py:25
  149.5 6.9 %collective-permute-done.5 = bf16[64,4096]{1,0:T(8,128)(2,1)S(1)} collective-permute-done((bf16[64,4096]{1,0:T(8,128)(2,1)}, bf16[64,4096]{1,0:T(8,128)(2,1)S(1)}, u32[]{:S(2)}, u32[]{:S(2)}) %collective-permute-start.5) | collective-permute-done | bytes 524320 | tf_op jit(solution)/shard_map/ppermute | solution.py:25
  156.4 0.8 copy-done.6
  157.2 0.2 collective-permute-done.4
  157.4 1.9 multiply_reduce_fusion
  159.3 1.0 multiply_convert_fusion
  160.3 1.3 collective-permute-start.7
  161.6 5.9 %collective-permute-start.6 = (bf16[64,4096]{1,0:T(8,128)(2,1)}, bf16[64,4096]{1,0:T(8,128)(2,1)}, u32[]{:S(2)}, u32[]{:S(2)}) collective-permute-start(bf16[64,4096]{1,0:T(8,128)(2,1)} %multiply_convert_fusion), channel_id=1, source_target_pairs={{0,1},{1,2},{2,3},{4,5},{5,6},{6,7},{8,9},{9,10},{10,11},{12,13},{... | collective-permute-start | bytes 1572872 | tf_op jit(solution)/shard_map/ppermute | solution.py:25
  167.6 0.1 copy.22
  167.7 1.3 collective-permute-start.10
  169.0 0.8 collective-permute-done.10
  169.8 0.1 copy.23
  169.9 3.7 %collective-permute-done.7 = bf16[64,4096]{1,0:T(8,128)(2,1)} collective-permute-done((bf16[64,4096]{1,0:T(8,128)(2,1)}, bf16[64,4096]{1,0:T(8,128)(2,1)}, u32[]{:S(2)}, u32[]{:S(2)}) %collective-permute-start.7) | collective-permute-done | bytes 524320 | tf_op jit(solution)/shard_map/ppermute | solution.py:25
  173.6 1.2 collective-permute-done.6
  174.8 1.5 collective-permute-start.8
  176.2 1.3 collective-permute-start.9
  177.6 0.1 copy.24
  177.7 0.1 reshape.60.where_ref
  177.8 1.6 copy-done.4
  179.4 8.9 %project_encodings.1 = (bf16[1280,1024]{1,0:T(8,128)(2,1)}, bf16[1280,1024]{1,0:T(8,128)(2,1)}) custom-call(s32[20]{0:T(128)S(1)} %reshape.60.where_ref, bf16[8,1,4,128,1024]{4,3,2,1,0:T(8,128)(2,1)} %bitcast.67, bf16[8,1,4,128,1024]{4,3,2,1,0:T(8,128)(2,1)} %bitcast.68, bf16[1024,1024]{1,0:T(8,128)(2,1)S(1)} %copy-done.3, bf16[1024,1024]{1,0:T(8,128)(2,1)S(1)} %copy-done.4), custom_call_target="tpu_custom_call" | custom-call | flops 5368709120 | bytes 12058624 | tf_op jit(solution)/shard_map/project_encodings/pallas_call | solution.py:208
  188.4 5.9 %collective-permute-done.9 = bf16[64,4096]{1,0:T(8,128)(2,1)} collective-permute-done((bf16[64,4096]{1,0:T(8,128)(2,1)}, bf16[64,4096]{1,0:T(8,128)(2,1)}, u32[]{:S(2)}, u32[]{:S(2)}) %collective-permute-start.9) | collective-permute-done | bytes 524320 | tf_op jit(solution)/shard_map/ppermute | solution.py:25
  194.2 0.7 collective-permute-start.11
  194.9 1.5 collective-permute-start.12
  196.5 11.8 %collective-permute-done.12 = bf16[64,4096]{1,0:T(8,128)(2,1)S(1)} collective-permute-done((bf16[64,4096]{1,0:T(8,128)(2,1)}, bf16[64,4096]{1,0:T(8,128)(2,1)S(1)}, u32[]{:S(2)}, u32[]{:S(2)}) %collective-permute-start.12) | collective-permute-done | bytes 524320 | tf_op jit(solution)/shard_map/ppermute | solution.py:25
  208.3 1.9 select_bitcast_fusion.2
  210.2 2.0 select_bitcast_fusion.3
  212.2 0.3 pad_maximum_fusion
  212.5 5.9 %convolution_convert_fusion.2.query_ref = bf16[256,1024]{1,0:T(8,128)(2,1)S(1)} fusion(bf16[256,4096]{1,0:T(8,128)(2,1)S(1)} %bitcast.78, bf16[4096,1024]{1,0:T(8,128)(2,1)} %param.19), kind=kOutput, calls=%fused_computation.3 | convolution fusion | flops 2147745792 | bytes 11010048 | tf_op jit(solution)/shard_map/dot_general | solution.py:345
  218.4 10.5 %cross_attend.1 = bf16[256,1024]{1,0:T(8,128)(2,1)S(1)} custom-call(s32[1]{0:T(128)} %bitcast.12.live_ref, bf16[256,1024]{1,0:T(8,128)(2,1)S(1)} %convolution_convert_fusion.2.query_ref, bf16[1280,1024]{1,0:T(8,128)(2,1)S(1)} %copy-done.2, bf16[1280,1024]{1,0:T(8,128)(2,1)} %get-tuple-element.54.values_ref), custom_call_target="tpu_custom_call" | custom-call | flops 536870912 | bytes 6291456 | tf_op jit(solution)/shard_map/cross_attend/pallas_call | solution.py:269
  228.9 2.3 convolution_convert_fusion
  231.3 0.1 dynamic-slice_bitcast_fusion
  231.3 0.7 collective-permute-start.14
  232.0 1.6 collective-permute-start.13
  233.7 7.8 %collective-permute-done.13 = bf16[64,4096]{1,0:T(8,128)(2,1)S(1)} collective-permute-done((bf16[64,4096]{1,0:T(8,128)(2,1)S(1)}, bf16[64,4096]{1,0:T(8,128)(2,1)S(1)}, u32[]{:S(2)}, u32[]{:S(2)}) %collective-permute-start.13) | collective-permute-done | bytes 524320 | tf_op jit(solution)/shard_map/ppermute | solution.py:25
  241.5 0.2 fusion.1
  241.7 0.7 collective-permute-start.16
  242.4 5.0 %collective-permute-start.15 = (bf16[64,4096]{1,0:T(8,128)(2,1)S(1)}, bf16[64,4096]{1,0:T(8,128)(2,1)S(1)}, u32[]{:S(2)}, u32[]{:S(2)}) collective-permute-start(bf16[64,4096]{1,0:T(8,128)(2,1)S(1)} %get-tuple-element.70), channel_id=1, source_target_pairs={{0,1},{1,2},{4,5},{5,6},{8,9},{9,10},{12,13},{13,14},{16,17},{17,1... | collective-permute-start | bytes 1572872 | tf_op jit(solution)/shard_map/ppermute | solution.py:25
  247.4 6.9 %collective-permute-done.15 = bf16[64,4096]{1,0:T(8,128)(2,1)S(1)} collective-permute-done((bf16[64,4096]{1,0:T(8,128)(2,1)S(1)}, bf16[64,4096]{1,0:T(8,128)(2,1)S(1)}, u32[]{:S(2)}, u32[]{:S(2)}) %collective-permute-start.15) | collective-permute-done | bytes 524320 | tf_op jit(solution)/shard_map/ppermute | solution.py:25
  254.3 0.3 fusion
  254.6 1.4 collective-permute-start.18
  256.0 5.0 %collective-permute-start.17 = (bf16[64,4096]{1,0:T(8,128)(2,1)S(1)}, bf16[64,4096]{1,0:T(8,128)(2,1)S(1)}, u32[]{:S(2)}, u32[]{:S(2)}) collective-permute-start(bf16[64,4096]{1,0:T(8,128)(2,1)S(1)} %get-tuple-element.68), channel_id=1, source_target_pairs={{0,1},{1,2},{2,3},{4,5},{5,6},{6,7},{8,9},{9,10},{10,11},{12,13},{... | collective-permute-start | bytes 1572872 | tf_op jit(solution)/shard_map/ppermute | solution.py:25
  261.1 5.2 %collective-permute-done.18 = bf16[64,4096]{1,0:T(8,128)(2,1)S(1)} collective-permute-done((bf16[64,4096]{1,0:T(8,128)(2,1)S(1)}, bf16[64,4096]{1,0:T(8,128)(2,1)S(1)}, u32[]{:S(2)}, u32[]{:S(2)}) %collective-permute-start.18) | collective-permute-done | bytes 524320 | tf_op jit(solution)/shard_map/ppermute | solution.py:25
  266.3 1.5 collective-permute-done.17
  267.7 1.2 fusion.5
  (37 shorter events, 0.4 us)
Async XLA Ops:
  6.5 1.6 copy-start
  57.8 26.2 %all-to-all-start = ((bf16[8,3,256,128]{3,2,1,0:T(8,128)(2,1)}), bf16[8,3,256,128]{3,2,1,0:T(8,128)(2,1)S(1)}, u32[]{:S(2)}, u32[]{:S(2)}) async-start(bf16[8,3,256,128]{3,2,1,0:T(8,128)(2,1)} %pack_heads.1), calls=%async_computation | async-start | bytes 3145728 | tf_op jit(solution)/shard_map/all_to_all | solution.py:146
  63.0 38.1 %all-gather.5.cloned.1.call-start = ((), (), s32[]{:S(2)}) async-start(), calls=%async_computation.2 | async-start | bytes 1310720 | tf_op jit(solution)/shard_map/all_gather | solution.py:317
  63.7 114.1 %all-gather.7.cloned.1.call-start = ((), (), s32[]{:S(2)}) async-start(), calls=%async_computation.3 | async-start | bytes 9437184 | tf_op jit(solution)/shard_map/all_gather | solution.py:328
  106.9 33.3 %copy-start.5 = (bf16[256,4096]{1,0:T(8,128)(2,1)}, bf16[256,4096]{1,0:T(8,128)(2,1)S(1)}, u32[]{:S(2)}) copy-start(bf16[256,4096]{1,0:T(8,128)(2,1)S(1)} %convolution_convert_fusion.1) | copy-start | bytes 6291460
  107.9 5.0 %collective-permute-start.1 = (bf16[64,4096]{1,0:T(8,128)(2,1)}, bf16[64,4096]{1,0:T(8,128)(2,1)S(1)}, u32[]{:S(2)}, u32[]{:S(2)}) collective-permute-start(bf16[64,4096]{1,0:T(8,128)(2,1)} %get-tuple-element.77), channel_id=1, source_target_pairs={{3,2},{7,6},{11,10},{15,14},{19,18},{23,22},{27,26},{31,30}} | collective-permute-start | bytes 1572872 | tf_op jit(solution)/shard_map/ppermute | solution.py:25
  108.6 14.0 %collective-permute-start = (bf16[64,4096]{1,0:T(8,128)(2,1)S(1)}, bf16[64,4096]{1,0:T(8,128)(2,1)}, u32[]{:S(2)}, u32[]{:S(2)}) collective-permute-start(bf16[64,4096]{1,0:T(8,128)(2,1)S(1)} %get-tuple-element.78), channel_id=1, source_target_pairs={{0,1},{4,5},{8,9},{12,13},{16,17},{20,21},{24,25},{28,29}} | collective-permute-start | bytes 1572872 | tf_op jit(solution)/shard_map/ppermute | solution.py:25
  124.7 24.8 %copy-start.7 = (bf16[4096]{0:T(1024)(128)(2,1)S(1)}, bf16[4096]{0:T(1024)(128)(2,1)}, u32[]{:S(2)}) copy-start(bf16[4096]{0:T(1024)(128)(2,1)} %param.18) | copy-start | bytes 24580
  124.7 6.7 %collective-permute-start.3 = (bf16[64,4096]{1,0:T(8,128)(2,1)}, bf16[64,4096]{1,0:T(8,128)(2,1)S(1)}, u32[]{:S(2)}, u32[]{:S(2)}) collective-permute-start(bf16[64,4096]{1,0:T(8,128)(2,1)} %get-tuple-element.75), channel_id=1, source_target_pairs={{2,1},{3,2},{6,5},{7,6},{10,9},{11,10},{14,13},{15,14},{18,17},{19... | collective-permute-start | bytes 1572872 | tf_op jit(solution)/shard_map/ppermute | solution.py:25
  125.5 14.7 %collective-permute-start.2 = (bf16[64,4096]{1,0:T(8,128)(2,1)S(1)}, bf16[64,4096]{1,0:T(8,128)(2,1)}, u32[]{:S(2)}, u32[]{:S(2)}) collective-permute-start(bf16[64,4096]{1,0:T(8,128)(2,1)S(1)} %get-tuple-element.76), channel_id=1, source_target_pairs={{0,1},{1,2},{4,5},{5,6},{8,9},{9,10},{12,13},{13,14},{16,17},{17,1... | collective-permute-start | bytes 1572872 | tf_op jit(solution)/shard_map/ppermute | solution.py:25
  142.3 14.1 %collective-permute-start.5 = (bf16[64,4096]{1,0:T(8,128)(2,1)}, bf16[64,4096]{1,0:T(8,128)(2,1)S(1)}, u32[]{:S(2)}, u32[]{:S(2)}) collective-permute-start(bf16[64,4096]{1,0:T(8,128)(2,1)} %get-tuple-element.73), channel_id=1, source_target_pairs={{1,0},{2,1},{3,2},{5,4},{6,5},{7,6},{9,8},{10,9},{11,10},{13,12},{... | collective-permute-start | bytes 1572872 | tf_op jit(solution)/shard_map/ppermute | solution.py:25
  143.6 13.8 %collective-permute-start.4 = (bf16[64,4096]{1,0:T(8,128)(2,1)S(1)}, bf16[64,4096]{1,0:T(8,128)(2,1)}, u32[]{:S(2)}, u32[]{:S(2)}) collective-permute-start(bf16[64,4096]{1,0:T(8,128)(2,1)S(1)} %get-tuple-element.74), channel_id=1, source_target_pairs={{0,1},{1,2},{2,3},{4,5},{5,6},{6,7},{8,9},{9,10},{10,11},{12,13},{... | collective-permute-start | bytes 1572872 | tf_op jit(solution)/shard_map/ppermute | solution.py:25
  149.5 18.0 %copy-start.8 = (s32[4,2]{0,1:T(2,128)S(1)}, s32[4,2]{0,1:T(2,128)}, u32[]{:S(2)}) copy-start(s32[4,2]{0,1:T(2,128)} %param.24) | copy-start | bytes 100
  149.5 18.0 %copy-start.9 = (s32[4,2]{0,1:T(2,128)S(1)}, s32[4,2]{0,1:T(2,128)}, u32[]{:S(2)}) copy-start(s32[4,2]{0,1:T(2,128)} %param.25) | copy-start | bytes 100
  149.5 28.3 %copy-start.3 = (bf16[1024,1024]{1,0:T(8,128)(2,1)S(1)}, bf16[1024,1024]{1,0:T(8,128)(2,1)}, u32[]{:S(2)}) copy-start(bf16[1024,1024]{1,0:T(8,128)(2,1)} %wk_ref.1) | copy-start | bytes 6291460
  156.4 0.8 copy-start.6
  160.3 13.3 %collective-permute-start.7 = (bf16[64,4096]{1,0:T(8,128)(2,1)}, bf16[64,4096]{1,0:T(8,128)(2,1)}, u32[]{:S(2)}, u32[]{:S(2)}) collective-permute-start(bf16[64,4096]{1,0:T(8,128)(2,1)} %multiply_convert_fusion), channel_id=1, source_target_pairs={{1,0},{2,1},{3,2},{5,4},{6,5},{7,6},{9,8},{10,9},{11,10},{13,12},{... | collective-permute-start | bytes 1572872 | tf_op jit(solution)/shard_map/ppermute | solution.py:25
  161.6 13.2 %collective-permute-start.6 = (bf16[64,4096]{1,0:T(8,128)(2,1)}, bf16[64,4096]{1,0:T(8,128)(2,1)}, u32[]{:S(2)}, u32[]{:S(2)}) collective-permute-start(bf16[64,4096]{1,0:T(8,128)(2,1)} %multiply_convert_fusion), channel_id=1, source_target_pairs={{0,1},{1,2},{2,3},{4,5},{5,6},{6,7},{8,9},{9,10},{10,11},{12,13},{... | collective-permute-start | bytes 1572872 | tf_op jit(solution)/shard_map/ppermute | solution.py:25
  167.7 2.1 collective-permute-start.10
  174.8 13.6 %collective-permute-start.8 = (bf16[64,4096]{1,0:T(8,128)(2,1)}, bf16[64,4096]{1,0:T(8,128)(2,1)}, u32[]{:S(2)}, u32[]{:S(2)}) collective-permute-start(bf16[64,4096]{1,0:T(8,128)(2,1)} %collective-permute-done.6), channel_id=1, source_target_pairs={{1,2},{2,3},{5,6},{6,7},{9,10},{10,11},{13,14},{14,15},{17,18},{18... | collective-permute-start | bytes 1572872 | tf_op jit(solution)/shard_map/ppermute | solution.py:25
  176.2 18.0 %collective-permute-start.9 = (bf16[64,4096]{1,0:T(8,128)(2,1)}, bf16[64,4096]{1,0:T(8,128)(2,1)}, u32[]{:S(2)}, u32[]{:S(2)}) collective-permute-start(bf16[64,4096]{1,0:T(8,128)(2,1)} %collective-permute-done.7), channel_id=1, source_target_pairs={{1,0},{2,1},{5,4},{6,5},{9,8},{10,9},{13,12},{14,13},{17,16},{18,1... | collective-permute-start | bytes 1572872 | tf_op jit(solution)/shard_map/ppermute | solution.py:25
  177.8 1.6 copy-start.4
  194.2 2.2 collective-permute-start.11
  194.9 13.4 %collective-permute-start.12 = (bf16[64,4096]{1,0:T(8,128)(2,1)}, bf16[64,4096]{1,0:T(8,128)(2,1)S(1)}, u32[]{:S(2)}, u32[]{:S(2)}) collective-permute-start(bf16[64,4096]{1,0:T(8,128)(2,1)} %collective-permute-done.9), channel_id=1, source_target_pairs={{1,0},{5,4},{9,8},{13,12},{17,16},{21,20},{25,24},{29,28}} | collective-permute-start | bytes 1572872 | tf_op jit(solution)/shard_map/ppermute | solution.py:25
  212.2 16.7 %slice-start = ((s8[8388608]{0:T(1024)(128)(4,1)}), s8[4194304]{0:T(1024)(128)(4,1)S(1)}, s32[]{:S(2)}) async-start(s8[8388608]{0:T(1024)(128)(4,1)} %bitcast.87), calls=%async_computation.4 | async-start | bytes 8388608
  212.5 5.9 %copy-start.2 = (bf16[1280,1024]{1,0:T(8,128)(2,1)S(1)}, bf16[1280,1024]{1,0:T(8,128)(2,1)}, u32[]{:S(2)}) copy-start(bf16[1280,1024]{1,0:T(8,128)(2,1)} %get-tuple-element.53.keys_ref) | copy-start | bytes 7864324
  212.5 16.4 %slice-start.1 = ((s8[8388608]{0:T(1024)(128)(4,1)}), s8[4194304]{0:T(1024)(128)(4,1)S(1)}, s32[]{:S(2)}) async-start(s8[8388608]{0:T(1024)(128)(4,1)} %bitcast.87), calls=%async_computation.5 | async-start | bytes 8388608
  231.3 2.3 collective-permute-start.14
  232.0 9.4 %collective-permute-start.13 = (bf16[64,4096]{1,0:T(8,128)(2,1)S(1)}, bf16[64,4096]{1,0:T(8,128)(2,1)S(1)}, u32[]{:S(2)}, u32[]{:S(2)}) collective-permute-start(bf16[64,4096]{1,0:T(8,128)(2,1)S(1)} %get-tuple-element.72), channel_id=1, source_target_pairs={{0,1},{4,5},{8,9},{12,13},{16,17},{20,21},{24,25},{28,29}} | collective-permute-start | bytes 1572872 | tf_op jit(solution)/shard_map/ppermute | solution.py:25
  241.7 5.7 %collective-permute-start.16 = (bf16[64,4096]{1,0:T(8,128)(2,1)S(1)}, bf16[64,4096]{1,0:T(8,128)(2,1)S(1)}, u32[]{:S(2)}, u32[]{:S(2)}) collective-permute-start(bf16[64,4096]{1,0:T(8,128)(2,1)S(1)} %get-tuple-element.69), channel_id=1, source_target_pairs={{2,1},{3,2},{6,5},{7,6},{10,9},{11,10},{14,13},{15,14},{18,17},{19... | collective-permute-start | bytes 1572872 | tf_op jit(solution)/shard_map/ppermute | solution.py:25
  242.4 11.9 %collective-permute-start.15 = (bf16[64,4096]{1,0:T(8,128)(2,1)S(1)}, bf16[64,4096]{1,0:T(8,128)(2,1)S(1)}, u32[]{:S(2)}, u32[]{:S(2)}) collective-permute-start(bf16[64,4096]{1,0:T(8,128)(2,1)S(1)} %get-tuple-element.70), channel_id=1, source_target_pairs={{0,1},{1,2},{4,5},{5,6},{8,9},{9,10},{12,13},{13,14},{16,17},{17,1... | collective-permute-start | bytes 1572872 | tf_op jit(solution)/shard_map/ppermute | solution.py:25
  254.3 14.6 %copy-start.1 = (bf16[8,128,1024]{2,1,0:T(8,128)(2,1)S(1)}, bf16[8,128,1024]{2,1,0:T(8,128)(2,1)}, u32[]{:S(2)}) copy-start(bf16[8,128,1024]{2,1,0:T(8,128)(2,1)} %param.23) | copy-start | bytes 6291460
  254.6 11.7 %collective-permute-start.18 = (bf16[64,4096]{1,0:T(8,128)(2,1)S(1)}, bf16[64,4096]{1,0:T(8,128)(2,1)S(1)}, u32[]{:S(2)}, u32[]{:S(2)}) collective-permute-start(bf16[64,4096]{1,0:T(8,128)(2,1)S(1)} %get-tuple-element.67), channel_id=1, source_target_pairs={{1,0},{2,1},{3,2},{5,4},{6,5},{7,6},{9,8},{10,9},{11,10},{13,12},{... | collective-permute-start | bytes 1572872 | tf_op jit(solution)/shard_map/ppermute | solution.py:25
  256.0 11.7 %collective-permute-start.17 = (bf16[64,4096]{1,0:T(8,128)(2,1)S(1)}, bf16[64,4096]{1,0:T(8,128)(2,1)S(1)}, u32[]{:S(2)}, u32[]{:S(2)}) collective-permute-start(bf16[64,4096]{1,0:T(8,128)(2,1)S(1)} %get-tuple-element.68), channel_id=1, source_target_pairs={{0,1},{1,2},{2,3},{4,5},{5,6},{6,7},{8,9},{9,10},{10,11},{12,13},{... | collective-permute-start | bytes 1572872 | tf_op jit(solution)/shard_map/ppermute | solution.py:25
Sparse Core Ops, SparseCore 0:
  65.4 29.6 all-gather.4
  101.2 53.7 all-gather.6

commit v3 on v2

--- a/solution.py
+++ b/solution.py
@@ -16,7 +16,7 @@
 
 NEG_BIG = -1e30
 LOG2E = 1.4426950408889634
-VMEM_BYTES = 48 * 1024 * 1024
+VMEM_BYTES = 16 * 1024 * 1024
 
 
 def shift(block, axis, distance, senders):
@@ -108,31 +108,22 @@
     )(qkv)
 
 
-def pack_kernel(query_ref, key_ref, value_ref, out_ref, sems, *, heads):
-    copies = []
-    for head in range(heads):
-        for which, ref in enumerate((query_ref, key_ref, value_ref)):
-            copies.append(
-                pltpu.make_async_copy(
-                    ref.at[:, pl.ds(head * HD, HD)], out_ref.at[head, which], sems.at[head, which]
-                )
-            )
-    for copy in copies:
-        copy.start()
-    for copy in copies:
-        copy.wait()
+def pack_kernel(query_ref, key_ref, value_ref, out_ref):
+    for which, ref in enumerate((query_ref, key_ref, value_ref)):
+        for head in range(out_ref.shape[0]):
+            out_ref[head, which] = ref[:, head * HD : (head + 1) * HD]
 
 
 def pack_heads(query_rows, key_rows, value_rows):
     rows, width = query_rows.shape
     heads = width // HD
-    anywhere = pl.BlockSpec(memory_space=pl.ANY)
+    step = math.gcd(heads, 2)
     return pl.pallas_call(
-        functools.partial(pack_kernel, heads=heads),
+        pack_kernel,
+        grid=(heads // step,),
         out_shape=jax.ShapeDtypeStruct((heads, 3, rows, HD), jnp.bfloat16),
-        in_specs=[anywhere] * 3,
-        out_specs=anywhere,
-        scratch_shapes=[pltpu.SemaphoreType.DMA((heads, 3))],
+        in_specs=[pl.BlockSpec((rows, step * HD), lambda at: (0, at))] * 3,
+        out_specs=pl.BlockSpec((step, 3, rows, HD), lambda at: (at, 0, 0, 0)),
         cost_estimate=pl.CostEstimate(
             flops=0, bytes_accessed=12 * rows * width, transcendentals=0
         ),
@@ -215,7 +206,7 @@
             out_specs=[made, made],
         ),
         compiler_params=pltpu.CompilerParams(
-            vmem_limit_bytes=VMEM_BYTES, dimension_semantics=("arbitrary",)
+            vmem_limit_bytes=20 * 1024 * 1024, dimension_semantics=("arbitrary",)
         ),
         cost_estimate=pl.CostEstimate(
             flops=4 * groups * GROUP * depth * width,
@@ -226,41 +217,57 @@
     )(where, table, table, w_cross_k, w_cross_v)
 
 
-def cross_group(query, keys, values, scale):
-    rows = query.shape[0]
+def apart_heads(query):
+    first = lax.broadcasted_iota(jnp.int32, query.shape, 1) < HD
+    nothing = jnp.zeros_like(query)
+    return jnp.concatenate(
+        (jnp.where(first, query, nothing), jnp.where(first, nothing, query)), axis=0
+    )
+
+
+def together_heads(mixed):
+    rows = mixed.shape[0] // 2
     first = lax.broadcasted_iota(jnp.int32, (rows, 2 * HD), 1) < HD
-    nothing = jnp.zeros_like(query)
-    apart = jnp.concatenate(
-        (jnp.where(first, query, nothing), jnp.where(first, nothing, query)), axis=0
-    )
-    scores = lax.dot_general(
-        apart, keys, (((1,), (1,)), ((), ())), preferred_element_type=jnp.float32
-    ) * (scale * LOG2E)
-    weights = jnp.exp2(scores - jnp.max(scores, axis=-1, keepdims=True))
-    total = jnp.sum(weights, axis=-1, keepdims=True)
-    mixed = jnp.dot(weights.astype(jnp.bfloat16), values, preferred_element_type=jnp.float32)
-    mixed = mixed / total
     return jnp.where(first, mixed[:rows], mixed[rows:])
 
 
 def cross_kernel(live_ref, query_ref, keys_ref, values_ref, out_ref, *, spans, heads, scale):
     tail = 16
+    pairs = heads // 2
     row = lax.broadcasted_iota(jnp.int32, (tail, 2 * HD), 0)
+    lanes = [slice(2 * pair * HD, 2 * (pair + 1) * HD) for pair in range(pairs)]
     for span in range(spans):
         top = span * SPAN
-        for pair in range(heads // 2):
-            lanes = slice(2 * pair * HD, 2 * (pair + 1) * HD)
-            here, after = (slice((span + k) * GROUP, (span + k + 1) * GROUP) for k in (0, 1))
-            query = query_ref[top : top + SPAN, lanes]
-            mixed = cross_group(query, keys_ref[here, lanes], values_ref[here, lanes], scale)
-            last = cross_group(
-                query[SPAN - tail :], keys_ref[after, lanes], values_ref[after, lanes], scale
+        here, after = (slice((span + k) * GROUP, (span + k + 1) * GROUP) for k in (0, 1))
+        work = [(slice(top, top + SPAN), here, at) for at in lanes]
+        work += [(slice(top + SPAN - tail, top + SPAN), after, at) for at in lanes]
+        scores = [
+            lax.dot_general(
+                apart_heads(query_ref[of, at]),
+                keys_ref[group, at],
+                (((1,), (1,)), ((), ())),
+                preferred_element_type=jnp.float32,
             )
+            * (scale * LOG2E)
+            for of, group, at in work
+        ]
+        tops = [jnp.max(one, axis=-1, keepdims=True) for one in scores]
+        weights = [jnp.exp2(one - top_one) for one, top_one in zip(scores, tops)]
+        totals = [jnp.sum(one, axis=-1, keepdims=True) for one in weights]
+        mixed = [
+            jnp.dot(
+                one.astype(jnp.bfloat16), values_ref[group, at], preferred_element_type=jnp.float32
+            )
+            for one, (_, group, at) in zip(weights, work)
+        ]
+        mixed = [together_heads(one / total) for one, total in zip(mixed, totals)]
+        for pair, at in enumerate(lanes):
+            main, last = mixed[pair], mixed[pairs + pair]
             if span == 0:
-                mixed = jnp.where(live_ref[0] > 0, mixed, 0.0)
-            last = jnp.where(row == tail - 1, last, mixed[SPAN - tail :])
-            out_ref[top : top + SPAN - tail, lanes] = mixed[: SPAN - tail].astype(jnp.bfloat16)
-            out_ref[top + SPAN - tail : top + SPAN, lanes] = last.astype(jnp.bfloat16)
+                main = jnp.where(live_ref[0] > 0, main, 0.0)
+            last = jnp.where(row == tail - 1, last, main[SPAN - tail :])
+            out_ref[top : top + SPAN - tail, at] = main[: SPAN - tail].astype(jnp.bfloat16)
+            out_ref[top + SPAN - tail : top + SPAN, at] = last.astype(jnp.bfloat16)
 
 
 def cross_attend(live, query, keys, values, scale):

time: 277 us -> 232 us (0.84)
  Pallas kernels: 73.1 us -> 17.8 us
  local copies, waits for them, and re-layouts: 6.4 us -> 12 us
  other arithmetic: 13.1 us -> 16.4 us
    pallas_call x1, Pallas kernels: 49 us -> 3.75 us  [pack_heads(): pl.pallas_call(pack_kernel, grid=(heads // step,), out_shape=jax.ShapeDty...]
    pallas_call x1, Pallas kernels: 10.5 us -> 2.46 us  [cross_attend(): pl.pallas_call(functools.partial(cross_kernel, spans=rows // SPAN, heads=...]
    unnamed x24, local copies, waits for them, and re-layouts: 4.01 us -> 9.68 us
  transfers between devices with their start and end apart: 22 -> 22, of which waited for: 14 -> 14; matrix products, arithmetic and copies ran while one was open for 5% -> 7% of each run, Pallas kernels for 5% -> 5%
where the time goes in v3:
time: 232 us; the launch traced here: 230 us
  waiting for transfers between devices  92.3 us (40%)
  starting transfers between devices  51.7 us (22%)
  Pallas kernels  17.8 us (8%)
  other arithmetic  16.4 us (7%)
  matrix products  14.1 us (6%)
  between operations  13.9 us (6%)
  blocking collectives  12.2 us (5%)
  local copies, waits for them, and re-layouts  12 us (5%)
    ppermute x19, waiting for transfers between devices, shift(): return lax.ppermute(block, axis, route)  71.3 us
    ppermute x19, starting transfers between devices, shift(): return lax.ppermute(block, axis, route)  46.5 us
    all_to_all x1, waiting for transfers between devices, self_attention_by_head(): held = lax.all_to_all(packed, 'seq', 0, 0, tiled=True)  20.2 us
    all_to_all x1, blocking collectives, self_attention_by_head(): back = lax.all_to_all(mixed, 'seq', 0, 0, tiled=True)  12.2 us
    unnamed x24, local copies, waits for them, and re-layouts  9.68 us
    pallas_call x1, Pallas kernels, project_encodings(): pl.pallas_call(project_kernel, out_shape=[jax.ShapeDtypeStruct((groups *...  6.92 us
    dot_general x1, matrix products, per_device(): jnp.dot(normed, w_cross_q, preferred_element_type=jnp.float32)  5.94 us
    dot_general x1, matrix products, per_device(): jnp.dot(attended, w_self_out, preferred_element_type=jnp.float32)  5.76 us
  transfers between devices with their start and end apart: 22, of which 14 were waited for; matrix products, arithmetic and copies ran while one was open for 7% of the time, Pallas kernels for 5%

profile of v3, /device:TPU:0, one launch (start us, length us, event | category | flops | bytes accessed | tf_op | source)
XLA Modules:
  0.0 230.3 jit_solution(3499092684729947881)
XLA Ops:
  6.5 1.6 copy-done
  8.1 0.7 constant_dynamic-slice_fusion
  8.8 3.7 %pack_heads.1 = bf16[8,3,256,128]{3,2,1,0:T(8,128)(2,1)} custom-call(bf16[256,1024]{1,0:T(8,128)(2,1)} %query_ref, bf16[256,1024]{1,0:T(8,128)(2,1)} %key_ref, bf16[256,1024]{1,0:T(8,128)(2,1)} %value_ref), custom_call_target="tpu_custom_call" | custom-call | bytes 3145728 | tf_op jit(solution)/shard_map/pack_heads/pallas_call | solution.py:121
  12.6 5.2 %all-to-all-start = ((bf16[8,3,256,128]{3,2,1,0:T(8,128)(2,1)}), bf16[8,3,256,128]{3,2,1,0:T(8,128)(2,1)S(1)}, u32[]{:S(2)}, u32[]{:S(2)}) async-start(bf16[8,3,256,128]{3,2,1,0:T(8,128)(2,1)} %pack_heads.1), calls=%async_computation | async-start | bytes 3145728 | tf_op jit(solution)/shard_map/all_to_all | solution.py:137
  17.8 0.7 all-gather.5.cloned.1.call-update
  18.5 20.2 %all-to-all-done.qkv_ref = bf16[8,3,256,128]{3,2,1,0:T(8,128)(2,1)S(1)} async-done(((bf16[8,3,256,128]{3,2,1,0:T(8,128)(2,1)}), bf16[8,3,256,128]{3,2,1,0:T(8,128)(2,1)S(1)}, u32[]{:S(2)}, u32[]{:S(2)}) %all-to-all-start) | async-done | bytes 1572896 | tf_op jit(solution)/shard_map/all_to_all | solution.py:137
  38.8 4.7 %self_attend.1 = bf16[8,256,128]{2,1,0:T(8,128)(2,1)S(1)} custom-call(bf16[8,3,256,128]{3,2,1,0:T(8,128)(2,1)S(1)} %all-to-all-done.qkv_ref), custom_call_target="tpu_custom_call" | custom-call | flops 1073741824 | bytes 2097152 | tf_op jit(solution)/shard_map/self_attend/pallas_call | solution.py:96
  43.5 12.2 %all_to_all.10 = bf16[8,256,128]{2,1,0:T(8,128)(2,1)S(1)} all-to-all(bf16[8,256,128]{2,1,0:T(8,128)(2,1)S(1)} %self_attend.1), channel_id=1, replica_groups=mesh['seq'=8,'db'=4] {'seq'}, dimensions={0} | all-to-all | bytes 1048576 | tf_op jit(solution)/shard_map/all_to_all | solution.py:139
  55.6 0.2 copy.21
  55.9 5.8 %convolution_convert_fusion.1 = bf16[256,4096]{1,0:T(8,128)(2,1)S(1)} fusion(bf16[256,1024]{0,1:T(8,128)(2,1)S(1)} %bitcast.77, bf16[1024,4096]{1,0:T(8,128)(2,1)} %param.17), kind=kOutput, calls=%fused_computation.1 | convolution fusion | flops 2148532224 | bytes 11010048 | tf_op jit(solution)/shard_map/dot_general | solution.py:339
  61.7 0.9 dynamic-slice_bitcast_fusion.2
  62.6 0.7 collective-permute-start.1
  63.2 4.3 %collective-permute-start = (bf16[64,4096]{1,0:T(8,128)(2,1)S(1)}, bf16[64,4096]{1,0:T(8,128)(2,1)}, u32[]{:S(2)}, u32[]{:S(2)}) collective-permute-start(bf16[64,4096]{1,0:T(8,128)(2,1)S(1)} %get-tuple-element.78), channel_id=1, source_target_pairs={{0,1},{4,5},{8,9},{12,13},{16,17},{20,21},{24,25},{28,29}} | collective-permute-start | bytes 1572872 | tf_op jit(solution)/shard_map/ppermute | solution.py:25
  67.6 9.7 %collective-permute-done = bf16[64,4096]{1,0:T(8,128)(2,1)} collective-permute-done((bf16[64,4096]{1,0:T(8,128)(2,1)S(1)}, bf16[64,4096]{1,0:T(8,128)(2,1)}, u32[]{:S(2)}, u32[]{:S(2)}) %collective-permute-start) | collective-permute-done | bytes 524320 | tf_op jit(solution)/shard_map/ppermute | solution.py:25
  77.2 2.1 fusion.7
  79.3 0.8 collective-permute-start.3
  80.1 5.9 %collective-permute-start.2 = (bf16[64,4096]{1,0:T(8,128)(2,1)S(1)}, bf16[64,4096]{1,0:T(8,128)(2,1)}, u32[]{:S(2)}, u32[]{:S(2)}) collective-permute-start(bf16[64,4096]{1,0:T(8,128)(2,1)S(1)} %get-tuple-element.76), channel_id=1, source_target_pairs={{0,1},{1,2},{4,5},{5,6},{8,9},{9,10},{12,13},{13,14},{16,17},{17,1... | collective-permute-start | bytes 1572872 | tf_op jit(solution)/shard_map/ppermute | solution.py:25
  86.1 8.8 %collective-permute-done.2 = bf16[64,4096]{1,0:T(8,128)(2,1)} collective-permute-done((bf16[64,4096]{1,0:T(8,128)(2,1)S(1)}, bf16[64,4096]{1,0:T(8,128)(2,1)}, u32[]{:S(2)}, u32[]{:S(2)}) %collective-permute-start.2) | collective-permute-done | bytes 524320 | tf_op jit(solution)/shard_map/ppermute | solution.py:25
  94.8 2.3 fusion.6
  97.1 1.3 collective-permute-start.5
  98.4 5.2 %collective-permute-start.4 = (bf16[64,4096]{1,0:T(8,128)(2,1)}, bf16[64,4096]{1,0:T(8,128)(2,1)S(1)}, u32[]{:S(2)}, u32[]{:S(2)}) collective-permute-start(bf16[64,4096]{1,0:T(8,128)(2,1)} %get-tuple-element.74), channel_id=1, source_target_pairs={{0,1},{1,2},{2,3},{4,5},{5,6},{6,7},{8,9},{9,10},{10,11},{12,13},{... | collective-permute-start | bytes 1572872 | tf_op jit(solution)/shard_map/ppermute | solution.py:25
  103.6 7.6 %collective-permute-done.5 = bf16[64,4096]{1,0:T(8,128)(2,1)S(1)} collective-permute-done((bf16[64,4096]{1,0:T(8,128)(2,1)}, bf16[64,4096]{1,0:T(8,128)(2,1)S(1)}, u32[]{:S(2)}, u32[]{:S(2)}) %collective-permute-start.5) | collective-permute-done | bytes 524320 | tf_op jit(solution)/shard_map/ppermute | solution.py:25
  111.2 1.3 collective-permute-done.4
  112.5 2.4 %multiply_reduce_fusion = (f32[64]{0:T(128)S(1)}, f32[64,4096]{1,0:T(8,128)}) fusion(bf16[64,4096]{1,0:T(8,128)(2,1)S(1)} %collective-permute-done.5, bf16[64,4096]{1,0:T(8,128)(2,1)S(1)} %collective-permute-done.4, bf16[4,64,4096]{2,1,0:T(8,128)(2,1)S(1)} %bitcast.72, s32[]{:T(128)S(6)} %min.29, bf16[256,4096]{1,0:T(8,128)(2,1)} %param.13, s32[]{:T(128)S(6)} %select_n.167), kind=kLoop, calls=%fused_computation.27 | loop fusion | flops 2359232 | bytes 3145992 | tf_op jit(solution)/shard_map/reduce_sum | solution.py:345
  114.9 1.4 multiply_convert_fusion
  116.3 1.3 collective-permute-start.7
  117.6 5.7 %collective-permute-start.6 = (bf16[64,4096]{1,0:T(8,128)(2,1)S(1)}, bf16[64,4096]{1,0:T(8,128)(2,1)}, u32[]{:S(2)}, u32[]{:S(2)}) collective-permute-start(bf16[64,4096]{1,0:T(8,128)(2,1)S(1)} %multiply_convert_fusion), channel_id=1, source_target_pairs={{0,1},{1,2},{2,3},{4,5},{5,6},{6,7},{8,9},{9,10},{10,11},{12,13},{... | collective-permute-start | bytes 1572872 | tf_op jit(solution)/shard_map/ppermute | solution.py:25
  123.4 0.1 copy.22
  123.5 1.3 collective-permute-start.10
  124.8 0.8 collective-permute-done.10
  125.6 0.1 copy.23
  125.7 3.4 %collective-permute-done.7 = bf16[64,4096]{1,0:T(8,128)(2,1)S(1)} collective-permute-done((bf16[64,4096]{1,0:T(8,128)(2,1)S(1)}, bf16[64,4096]{1,0:T(8,128)(2,1)S(1)}, u32[]{:S(2)}, u32[]{:S(2)}) %collective-permute-start.7) | collective-permute-done | bytes 524320 | tf_op jit(solution)/shard_map/ppermute | solution.py:25
  129.1 1.2 collective-permute-done.6
  130.3 1.4 collective-permute-start.8
  131.7 1.3 collective-permute-start.9
  133.1 0.1 copy.24
  133.3 3.4 %copy-done.2 = bf16[32,128,1024]{2,1,0:T(8,128)(2,1)S(1)} copy-done((bf16[32,128,1024]{2,1,0:T(8,128)(2,1)S(1)}, bf16[32,128,1024]{2,1,0:T(8,128)(2,1)}, u32[]{:S(2)}) %copy-start.2) | copy-done | bytes 8388632
  136.7 1.6 copy-done.5
  138.3 1.6 copy-done.6
  139.9 6.9 %project_encodings.1 = (bf16[1280,1024]{1,0:T(8,128)(2,1)S(1)}, bf16[1280,1024]{1,0:T(8,128)(2,1)S(1)}) custom-call(s32[20]{0:T(128)S(1)} %reshape.60.where_ref, bf16[8,1,4,128,1024]{4,3,2,1,0:T(8,128)(2,1)S(1)} %bitcast.67, bf16[8,1,4,128,1024]{4,3,2,1,0:T(8,128)(2,1)S(1)} %bitcast.68, bf16[1024,1024]{1,0:T(8,128)(2,1)S(1)} %copy-done.5, ...), custom_call_target="tpu_custom_call" | custom-call | flops 5368709120 | bytes 12058624 | tf_op jit(solution)/shard_map/project_encodings/pallas_call | solution.py:199
  146.8 1.5 copy-done.3
  148.3 0.8 collective-permute-done.9
  149.1 1.5 collective-permute-start.11
  150.6 1.5 collective-permute-start.12
  152.1 15.2 %collective-permute-done.12 = bf16[64,4096]{1,0:T(8,128)(2,1)} collective-permute-done((bf16[64,4096]{1,0:T(8,128)(2,1)}, bf16[64,4096]{1,0:T(8,128)(2,1)}, u32[]{:S(2)}, u32[]{:S(2)}) %collective-permute-start.12) | collective-permute-done | bytes 524320 | tf_op jit(solution)/shard_map/ppermute | solution.py:25
  167.4 2.5 %select_bitcast_fusion.2 = (bf16[1,64,4096]{2,1,0:T(8,128)(2,1)S(1)}, bf16[1,64,4096]{2,1,0:T(8,128)(2,1)S(1)}) fusion(bf16[64,4096]{1,0:T(8,128)(2,1)} %collective-permute-done.12, bf16[64,4096]{1,0:T(8,128)(2,1)} %collective-permute-done.11, bf16[64,4096]{1,0:T(8,128)(2,1)} %collective-permute-done.9, bf16[64,4096]{1,0:T(8,128)(2,1)} %collective-permute-done.8, ...), kind=kLoop, calls=%fused_computation.32 | loop fusion | flops 3932160 | bytes 5259532 | tf_op jit(solution)/shard_map/stack | solution.py:72
  169.8 2.5 %select_bitcast_fusion.3 = (bf16[1,64,4096]{2,1,0:T(8,128)(2,1)S(1)}, bf16[1,64,4096]{2,1,0:T(8,128)(2,1)S(1)}) fusion(bf16[64,4096]{1,0:T(8,128)(2,1)} %collective-permute-done.12, bf16[64,4096]{1,0:T(8,128)(2,1)} %collective-permute-done.11, bf16[64,4096]{1,0:T(8,128)(2,1)} %collective-permute-done.9, bf16[64,4096]{1,0:T(8,128)(2,1)} %collective-permute-done.8, ...), kind=kLoop, calls=%fused_computation.33 | loop fusion | flops 3932160 | bytes 5259532 | tf_op jit(solution)/shard_map/stack | solution.py:72
  172.3 0.3 pad_maximum_fusion
  172.6 5.9 %convolution_convert_fusion.2.query_ref = bf16[256,1024]{1,0:T(8,128)(2,1)S(1)} fusion(bf16[256,4096]{1,0:T(8,128)(2,1)S(1)} %bitcast.78, bf16[4096,1024]{1,0:T(8,128)(2,1)} %param.19), kind=kOutput, calls=%fused_computation.3 | convolution fusion | flops 2147745792 | bytes 11010048 | tf_op jit(solution)/shard_map/dot_general | solution.py:352
  178.6 2.5 %cross_attend.1 = bf16[256,1024]{1,0:T(8,128)(2,1)S(1)} custom-call(s32[1]{0:T(128)} %bitcast.12.live_ref, bf16[256,1024]{1,0:T(8,128)(2,1)S(1)} %convolution_convert_fusion.2.query_ref, bf16[1280,1024]{1,0:T(8,128)(2,1)S(1)} %get-tuple-element.53.keys_ref, bf16[1280,1024]{1,0:T(8,128)(2,1)S(1)} %copy-done.4), custom_call_target="tpu_custom_call" | custom-call | flops 536870912 | bytes 6291456 | tf_op jit(solution)/shard_map/cross_attend/pallas_call | solution.py:276
  181.1 2.4 %convolution_convert_fusion = bf16[256,4096]{1,0:T(8,128)(2,1)S(1)} fusion(bf16[256,1024]{1,0:T(8,128)(2,1)S(1)} %cross_attend.1, bf16[1024,4096]{1,0:T(8,128)(2,1)S(1)} %bitcast.88), kind=kOutput, calls=%fused_computation | convolution fusion | flops 2148532224 | bytes 11010048 | tf_op jit(solution)/shard_map/dot_general | solution.py:357
  183.6 0.7 collective-permute-start.14
  184.3 1.5 collective-permute-start.13
  185.8 8.4 %collective-permute-done.13 = bf16[64,4096]{1,0:T(8,128)(2,1)S(1)} collective-permute-done((bf16[64,4096]{1,0:T(8,128)(2,1)S(1)}, bf16[64,4096]{1,0:T(8,128)(2,1)S(1)}, u32[]{:S(2)}, u32[]{:S(2)}) %collective-permute-start.13) | collective-permute-done | bytes 524320 | tf_op jit(solution)/shard_map/ppermute | solution.py:25
  194.2 0.2 fusion.1
  194.4 0.7 collective-permute-start.16
  195.1 5.0 %collective-permute-start.15 = (bf16[64,4096]{1,0:T(8,128)(2,1)S(1)}, bf16[64,4096]{1,0:T(8,128)(2,1)S(1)}, u32[]{:S(2)}, u32[]{:S(2)}) collective-permute-start(bf16[64,4096]{1,0:T(8,128)(2,1)S(1)} %get-tuple-element.70), channel_id=1, source_target_pairs={{0,1},{1,2},{4,5},{5,6},{8,9},{9,10},{12,13},{13,14},{16,17},{17,1... | collective-permute-start | bytes 1572872 | tf_op jit(solution)/shard_map/ppermute | solution.py:25
  200.2 7.5 %collective-permute-done.15 = bf16[64,4096]{1,0:T(8,128)(2,1)S(1)} collective-permute-done((bf16[64,4096]{1,0:T(8,128)(2,1)S(1)}, bf16[64,4096]{1,0:T(8,128)(2,1)S(1)}, u32[]{:S(2)}, u32[]{:S(2)}) %collective-permute-start.15) | collective-permute-done | bytes 524320 | tf_op jit(solution)/shard_map/ppermute | solution.py:25
  207.7 0.2 fusion
  207.9 1.4 collective-permute-start.18
  209.4 5.0 %collective-permute-start.17 = (bf16[64,4096]{1,0:T(8,128)(2,1)S(1)}, bf16[64,4096]{1,0:T(8,128)(2,1)S(1)}, u32[]{:S(2)}, u32[]{:S(2)}) collective-permute-start(bf16[64,4096]{1,0:T(8,128)(2,1)S(1)} %get-tuple-element.68), channel_id=1, source_target_pairs={{0,1},{1,2},{2,3},{4,5},{5,6},{6,7},{8,9},{9,10},{10,11},{12,13},{... | collective-permute-start | bytes 1572872 | tf_op jit(solution)/shard_map/ppermute | solution.py:25
  214.4 5.4 %collective-permute-done.18 = bf16[64,4096]{1,0:T(8,128)(2,1)S(1)} collective-permute-done((bf16[64,4096]{1,0:T(8,128)(2,1)S(1)}, bf16[64,4096]{1,0:T(8,128)(2,1)S(1)}, u32[]{:S(2)}, u32[]{:S(2)}) %collective-permute-start.18) | collective-permute-done | bytes 524320 | tf_op jit(solution)/shard_map/ppermute | solution.py:25
  219.8 1.3 collective-permute-done.17
  221.1 2.4 %fusion.5 = f32[64,4096]{1,0:T(8,128)} fusion(f32[64,4096]{1,0:T(8,128)} %get-tuple-element.62, bf16[64,4096]{1,0:T(8,128)(2,1)S(1)} %collective-permute-done.18, bf16[64,4096]{1,0:T(8,128)(2,1)S(1)} %collective-permute-done.17, bf16[4,64,4096]{2,1,0:T(8,128)(2,1)S(1)} %bitcast.76, s32[]{:T(128)S(6)} %min.29), kind=kLoop, calls=%fused_computation.14 | loop fusion | flops 1572864 | bytes 3670020 | tf_op jit(solution)/shard_map/add | solution.py:360
  (37 shorter events, 0.5 us)
Async XLA Ops:
  6.5 1.6 copy-start
  12.6 26.2 %all-to-all-start = ((bf16[8,3,256,128]{3,2,1,0:T(8,128)(2,1)}), bf16[8,3,256,128]{3,2,1,0:T(8,128)(2,1)S(1)}, u32[]{:S(2)}, u32[]{:S(2)}) async-start(bf16[8,3,256,128]{3,2,1,0:T(8,128)(2,1)} %pack_heads.1), calls=%async_computation | async-start | bytes 3145728 | tf_op jit(solution)/shard_map/all_to_all | solution.py:137
  17.8 38.1 %all-gather.5.cloned.1.call-start = ((), (), s32[]{:S(2)}) async-start(), calls=%async_computation.2 | async-start | bytes 1310720 | tf_op jit(solution)/shard_map/all_gather | solution.py:324
  18.5 114.8 %all-gather.7.cloned.1.call-start = ((), (), s32[]{:S(2)}) async-start(), calls=%async_computation.3 | async-start | bytes 9437184 | tf_op jit(solution)/shard_map/all_gather | solution.py:335
  62.6 5.0 %collective-permute-start.1 = (bf16[64,4096]{1,0:T(8,128)(2,1)}, bf16[64,4096]{1,0:T(8,128)(2,1)S(1)}, u32[]{:S(2)}, u32[]{:S(2)}) collective-permute-start(bf16[64,4096]{1,0:T(8,128)(2,1)} %get-tuple-element.77), channel_id=1, source_target_pairs={{3,2},{7,6},{11,10},{15,14},{19,18},{23,22},{27,26},{31,30}} | collective-permute-start | bytes 1572872 | tf_op jit(solution)/shard_map/ppermute | solution.py:25
  63.2 14.0 %collective-permute-start = (bf16[64,4096]{1,0:T(8,128)(2,1)S(1)}, bf16[64,4096]{1,0:T(8,128)(2,1)}, u32[]{:S(2)}, u32[]{:S(2)}) collective-permute-start(bf16[64,4096]{1,0:T(8,128)(2,1)S(1)} %get-tuple-element.78), channel_id=1, source_target_pairs={{0,1},{4,5},{8,9},{12,13},{16,17},{20,21},{24,25},{28,29}} | collective-permute-start | bytes 1572872 | tf_op jit(solution)/shard_map/ppermute | solution.py:25
  79.3 24.2 %copy-start.7 = (bf16[4096]{0:T(1024)(128)(2,1)S(1)}, bf16[4096]{0:T(1024)(128)(2,1)}, u32[]{:S(2)}) copy-start(bf16[4096]{0:T(1024)(128)(2,1)} %param.18) | copy-start | bytes 24580
  79.3 6.7 %collective-permute-start.3 = (bf16[64,4096]{1,0:T(8,128)(2,1)}, bf16[64,4096]{1,0:T(8,128)(2,1)S(1)}, u32[]{:S(2)}, u32[]{:S(2)}) collective-permute-start(bf16[64,4096]{1,0:T(8,128)(2,1)} %get-tuple-element.75), channel_id=1, source_target_pairs={{2,1},{3,2},{6,5},{7,6},{10,9},{11,10},{14,13},{15,14},{18,17},{19... | collective-permute-start | bytes 1572872 | tf_op jit(solution)/shard_map/ppermute | solution.py:25
  80.1 14.7 %collective-permute-start.2 = (bf16[64,4096]{1,0:T(8,128)(2,1)S(1)}, bf16[64,4096]{1,0:T(8,128)(2,1)}, u32[]{:S(2)}, u32[]{:S(2)}) collective-permute-start(bf16[64,4096]{1,0:T(8,128)(2,1)S(1)} %get-tuple-element.76), channel_id=1, source_target_pairs={{0,1},{1,2},{4,5},{5,6},{8,9},{9,10},{12,13},{13,14},{16,17},{17,1... | collective-permute-start | bytes 1572872 | tf_op jit(solution)/shard_map/ppermute | solution.py:25
  97.1 14.1 %collective-permute-start.5 = (bf16[64,4096]{1,0:T(8,128)(2,1)}, bf16[64,4096]{1,0:T(8,128)(2,1)S(1)}, u32[]{:S(2)}, u32[]{:S(2)}) collective-permute-start(bf16[64,4096]{1,0:T(8,128)(2,1)} %get-tuple-element.73), channel_id=1, source_target_pairs={{1,0},{2,1},{3,2},{5,4},{6,5},{7,6},{9,8},{10,9},{11,10},{13,12},{... | collective-permute-start | bytes 1572872 | tf_op jit(solution)/shard_map/ppermute | solution.py:25
  98.4 14.1 %collective-permute-start.4 = (bf16[64,4096]{1,0:T(8,128)(2,1)}, bf16[64,4096]{1,0:T(8,128)(2,1)S(1)}, u32[]{:S(2)}, u32[]{:S(2)}) collective-permute-start(bf16[64,4096]{1,0:T(8,128)(2,1)} %get-tuple-element.74), channel_id=1, source_target_pairs={{0,1},{1,2},{2,3},{4,5},{5,6},{6,7},{8,9},{9,10},{10,11},{12,13},{... | collective-permute-start | bytes 1572872 | tf_op jit(solution)/shard_map/ppermute | solution.py:25
  103.6 19.8 %copy-start.8 = (s32[4,2]{0,1:T(2,128)S(1)}, s32[4,2]{0,1:T(2,128)}, u32[]{:S(2)}) copy-start(s32[4,2]{0,1:T(2,128)} %param.24) | copy-start | bytes 100
  103.6 19.8 %copy-start.9 = (s32[4,2]{0,1:T(2,128)S(1)}, s32[4,2]{0,1:T(2,128)}, u32[]{:S(2)}) copy-start(s32[4,2]{0,1:T(2,128)} %param.25) | copy-start | bytes 100
  116.3 12.8 %collective-permute-start.7 = (bf16[64,4096]{1,0:T(8,128)(2,1)S(1)}, bf16[64,4096]{1,0:T(8,128)(2,1)S(1)}, u32[]{:S(2)}, u32[]{:S(2)}) collective-permute-start(bf16[64,4096]{1,0:T(8,128)(2,1)S(1)} %multiply_convert_fusion), channel_id=1, source_target_pairs={{1,0},{2,1},{3,2},{5,4},{6,5},{7,6},{9,8},{10,9},{11,10},{13,12},{... | collective-permute-start | bytes 1572872 | tf_op jit(solution)/shard_map/ppermute | solution.py:25
  117.6 12.7 %collective-permute-start.6 = (bf16[64,4096]{1,0:T(8,128)(2,1)S(1)}, bf16[64,4096]{1,0:T(8,128)(2,1)}, u32[]{:S(2)}, u32[]{:S(2)}) collective-permute-start(bf16[64,4096]{1,0:T(8,128)(2,1)S(1)} %multiply_convert_fusion), channel_id=1, source_target_pairs={{0,1},{1,2},{2,3},{4,5},{5,6},{6,7},{8,9},{9,10},{10,11},{12,13},{... | collective-permute-start | bytes 1572872 | tf_op jit(solution)/shard_map/ppermute | solution.py:25
  123.5 2.1 collective-permute-start.10
  130.3 18.0 %collective-permute-start.8 = (bf16[64,4096]{1,0:T(8,128)(2,1)}, bf16[64,4096]{1,0:T(8,128)(2,1)}, u32[]{:S(2)}, u32[]{:S(2)}) collective-permute-start(bf16[64,4096]{1,0:T(8,128)(2,1)} %collective-permute-done.6), channel_id=1, source_target_pairs={{1,2},{2,3},{5,6},{6,7},{9,10},{10,11},{13,14},{14,15},{17,18},{18... | collective-permute-start | bytes 1572872 | tf_op jit(solution)/shard_map/ppermute | solution.py:25
  131.7 17.4 %collective-permute-start.9 = (bf16[64,4096]{1,0:T(8,128)(2,1)S(1)}, bf16[64,4096]{1,0:T(8,128)(2,1)}, u32[]{:S(2)}, u32[]{:S(2)}) collective-permute-start(bf16[64,4096]{1,0:T(8,128)(2,1)S(1)} %collective-permute-done.7), channel_id=1, source_target_pairs={{1,0},{2,1},{5,4},{6,5},{9,8},{10,9},{13,12},{14,13},{17,16},{18,1... | collective-permute-start | bytes 1572872 | tf_op jit(solution)/shard_map/ppermute | solution.py:25
  133.3 3.4 %copy-start.2 = (bf16[32,128,1024]{2,1,0:T(8,128)(2,1)S(1)}, bf16[32,128,1024]{2,1,0:T(8,128)(2,1)}, u32[]{:S(2)}) copy-start(bf16[32,128,1024]{2,1,0:T(8,128)(2,1)} %all-gather.7.cloned.1.call-done) | copy-start | bytes 25165828
  136.7 1.6 copy-start.5
  138.3 1.6 copy-start.6
  146.8 1.5 copy-start.3
  149.1 3.0 %collective-permute-start.11 = (bf16[64,4096]{1,0:T(8,128)(2,1)}, bf16[64,4096]{1,0:T(8,128)(2,1)}, u32[]{:S(2)}, u32[]{:S(2)}) collective-permute-start(bf16[64,4096]{1,0:T(8,128)(2,1)} %collective-permute-done.8), channel_id=1, source_target_pairs={{2,3},{6,7},{10,11},{14,15},{18,19},{22,23},{26,27},{30,31}} | collective-permute-start | bytes 1572872 | tf_op jit(solution)/shard_map/ppermute | solution.py:25
  150.6 16.8 %collective-permute-start.12 = (bf16[64,4096]{1,0:T(8,128)(2,1)}, bf16[64,4096]{1,0:T(8,128)(2,1)}, u32[]{:S(2)}, u32[]{:S(2)}) collective-permute-start(bf16[64,4096]{1,0:T(8,128)(2,1)} %collective-permute-done.9), channel_id=1, source_target_pairs={{1,0},{5,4},{9,8},{13,12},{17,16},{21,20},{25,24},{29,28}} | collective-permute-start | bytes 1572872 | tf_op jit(solution)/shard_map/ppermute | solution.py:25
  172.3 8.7 %slice-start = ((s8[8388608]{0:T(1024)(128)(4,1)}), s8[4194304]{0:T(1024)(128)(4,1)S(1)}, s32[]{:S(2)}) async-start(s8[8388608]{0:T(1024)(128)(4,1)} %bitcast.87), calls=%async_computation.4 | async-start | bytes 8388608
  172.6 6.0 %copy-start.4 = (bf16[1280,1024]{1,0:T(8,128)(2,1)S(1)}, bf16[1280,1024]{1,0:T(8,128)(2,1)}, u32[]{:S(2)}) copy-start(bf16[1280,1024]{1,0:T(8,128)(2,1)} %copy-done.3) | copy-start | bytes 7864324
  172.6 8.4 %slice-start.1 = ((s8[8388608]{0:T(1024)(128)(4,1)}), s8[4194304]{0:T(1024)(128)(4,1)S(1)}, s32[]{:S(2)}) async-start(s8[8388608]{0:T(1024)(128)(4,1)} %bitcast.87), calls=%async_computation.5 | async-start | bytes 8388608
  183.6 2.2 collective-permute-start.14
  184.3 9.9 %collective-permute-start.13 = (bf16[64,4096]{1,0:T(8,128)(2,1)S(1)}, bf16[64,4096]{1,0:T(8,128)(2,1)S(1)}, u32[]{:S(2)}, u32[]{:S(2)}) collective-permute-start(bf16[64,4096]{1,0:T(8,128)(2,1)S(1)} %get-tuple-element.72), channel_id=1, source_target_pairs={{0,1},{4,5},{8,9},{12,13},{16,17},{20,21},{24,25},{28,29}} | collective-permute-start | bytes 1572872 | tf_op jit(solution)/shard_map/ppermute | solution.py:25
  194.4 5.7 %collective-permute-start.16 = (bf16[64,4096]{1,0:T(8,128)(2,1)S(1)}, bf16[64,4096]{1,0:T(8,128)(2,1)S(1)}, u32[]{:S(2)}, u32[]{:S(2)}) collective-permute-start(bf16[64,4096]{1,0:T(8,128)(2,1)S(1)} %get-tuple-element.69), channel_id=1, source_target_pairs={{2,1},{3,2},{6,5},{7,6},{10,9},{11,10},{14,13},{15,14},{18,17},{19... | collective-permute-start | bytes 1572872 | tf_op jit(solution)/shard_map/ppermute | solution.py:25
  195.1 12.5 %collective-permute-start.15 = (bf16[64,4096]{1,0:T(8,128)(2,1)S(1)}, bf16[64,4096]{1,0:T(8,128)(2,1)S(1)}, u32[]{:S(2)}, u32[]{:S(2)}) collective-permute-start(bf16[64,4096]{1,0:T(8,128)(2,1)S(1)} %get-tuple-element.70), channel_id=1, source_target_pairs={{0,1},{1,2},{4,5},{5,6},{8,9},{9,10},{12,13},{13,14},{16,17},{17,1... | collective-permute-start | bytes 1572872 | tf_op jit(solution)/shard_map/ppermute | solution.py:25
  207.7 15.8 %copy-start.1 = (bf16[8,128,1024]{2,1,0:T(8,128)(2,1)S(1)}, bf16[8,128,1024]{2,1,0:T(8,128)(2,1)}, u32[]{:S(2)}) copy-start(bf16[8,128,1024]{2,1,0:T(8,128)(2,1)} %param.23) | copy-start | bytes 6291460
  207.9 11.9 %collective-permute-start.18 = (bf16[64,4096]{1,0:T(8,128)(2,1)S(1)}, bf16[64,4096]{1,0:T(8,128)(2,1)S(1)}, u32[]{:S(2)}, u32[]{:S(2)}) collective-permute-start(bf16[64,4096]{1,0:T(8,128)(2,1)S(1)} %get-tuple-element.67), channel_id=1, source_target_pairs={{1,0},{2,1},{3,2},{5,4},{6,5},{7,6},{9,8},{10,9},{11,10},{13,12},{... | collective-permute-start | bytes 1572872 | tf_op jit(solution)/shard_map/ppermute | solution.py:25
  209.4 11.7 %collective-permute-start.17 = (bf16[64,4096]{1,0:T(8,128)(2,1)S(1)}, bf16[64,4096]{1,0:T(8,128)(2,1)S(1)}, u32[]{:S(2)}, u32[]{:S(2)}) collective-permute-start(bf16[64,4096]{1,0:T(8,128)(2,1)S(1)} %get-tuple-element.68), channel_id=1, source_target_pairs={{0,1},{1,2},{2,3},{4,5},{5,6},{6,7},{8,9},{9,10},{10,11},{12,13},{... | collective-permute-start | bytes 1572872 | tf_op jit(solution)/shard_map/ppermute | solution.py:25
Sparse Core Ops, SparseCore 0:
  20.2 29.6 all-gather.4
  56.0 53.7 all-gather.6

commit v4 on v3

--- a/solution.py
+++ b/solution.py
@@ -29,47 +29,63 @@
     return (first.astype(jnp.float32) + second.astype(jnp.float32)).astype(jnp.bfloat16)
 
 
-def line_reduce_scatter(blocks):
+def pick(blocks, index):
+    return lax.dynamic_index_in_dim(
+        blocks, jnp.clip(index, 0, blocks.shape[0] - 1), 0, keepdims=False
+    )
+
+
+def reduce_step(blocks, carried, step):
     size = lax.axis_size("db")
     me = lax.axis_index("db")
-
-    def pick(d):
-        return lax.dynamic_index_in_dim(blocks, jnp.clip(d, 0, size - 1), 0, keepdims=False)
-
-    up = down = None
-    for step in range(size - 1):
-        far = size - 1 - step
-        up_block, down_block = pick(me + far), pick(me - far)
+    far = size - 1 - step
+    up_block, down_block = pick(blocks, me + far), pick(blocks, me - far)
+    if carried is not None:
+        up_block = add_rounded(up_block, carried[0])
+        down_block = add_rounded(down_block, carried[1])
+    return (
+        shift(up_block, "db", 1, range(step + 1)),
+        shift(down_block, "db", -1, range(size - 1 - step, size)),
+    )
+
+
+def reduced(blocks, carried):
+    total = pick(blocks, lax.axis_index("db")).astype(jnp.float32)
+    return total + carried[0].astype(jnp.float32) + carried[1].astype(jnp.float32)
+
+
+def gather_step(carried, step):
+    size = lax.axis_size("db")
+    return (
+        shift(carried[0], "db", 1, range(step, size)),
+        shift(carried[1], "db", -1, range(0, size - step)),
+    )
+
+
+def gather_reduce(normed, blocks, beside, at):
+    size = lax.axis_size("db")
+    carried_gather, carried_reduce, pieces = (normed, normed), None, []
+    for step in range(size):
+        if step < size - 1:
+            carried_gather = gather_step(carried_gather, step)
         if step:
-            up_block, down_block = add_rounded(up_block, up), add_rounded(down_block, down)
-        up = shift(up_block, "db", 1, range(step + 1))
-        down = shift(down_block, "db", -1, range(size - 1 - step, size))
-        up, down = lax.optimization_barrier((up, down))
-    total = pick(me).astype(jnp.float32)
-    return total + up.astype(jnp.float32) + down.astype(jnp.float32)
-
-
-def line_all_gather(block, beside):
-    size = lax.axis_size("db")
-    me = lax.axis_index("db")
-    up = down = block
-    pieces = []
-    for step in range(size - 1):
-        up = shift(up, "db", 1, range(step, size))
-        down = shift(down, "db", -1, range(0, size - step))
-        if step == (size - 1) // 2:
-            up, down, beside = lax.optimization_barrier((up, down, beside))
-        else:
-            up, down = lax.optimization_barrier((up, down))
-        pieces.append((step + 1, up, down))
-    parts = []
-    for owner in range(size):
-        chosen = block
-        for distance, from_low, from_high in pieces:
-            chosen = jnp.where(me - owner == distance, from_low, chosen)
-            chosen = jnp.where(owner - me == distance, from_high, chosen)
-        parts.append(chosen)
-    return jnp.stack(parts), beside
+            carried_reduce = reduce_step(blocks, carried_reduce, step - 1)
+        held = (
+            carried_gather if step < size - 1 else None,
+            carried_reduce,
+            blocks if step == 0 else None,
+            beside if step == at else None,
+        )
+        held = lax.optimization_barrier(held)
+        if step < size - 1:
+            carried_gather = held[0]
+            pieces.append(held[0])
+        carried_reduce = held[1]
+        if step == 0:
+            blocks = held[2]
+        if step == at:
+            beside = held[3]
+    return pieces, blocks, carried_reduce, beside
 
 
 def self_kernel(qkv_ref, out_ref, *, blocks, rows, scale):
@@ -132,12 +148,10 @@
 
 
 def self_attention_by_head(query_rows, key_rows, value_rows, scale):
-    rows, width = query_rows.shape
     packed = pack_heads(query_rows, key_rows, value_rows)
     held = lax.all_to_all(packed, "seq", 0, 0, tiled=True)
     mixed = self_attend_head(held, scale)
-    back = lax.all_to_all(mixed, "seq", 0, 0, tiled=True)
-    return back.transpose(1, 0, 2).reshape(rows, width)
+    return lax.all_to_all(mixed, "seq", 0, 0, tiled=True)
 
 
 def self_attention_gathered(query_rows, key_rows, value_rows, scale):
@@ -166,7 +180,53 @@
         values.reshape(count, heads, HD),
         preferred_element_type=jnp.float32,
     )
-    return (mixed / total[..., None]).transpose(1, 0, 2).reshape(rows, width).astype(jnp.bfloat16)
+    return (mixed / total[..., None]).astype(jnp.bfloat16)
+
+
+def self_out_kernel(attended_ref, weight_ref, first_ref, second_ref, rows_ref):
+    heads, rows, _ = attended_ref.shape
+    n_db, half, features = first_ref.shape
+    for chunk in range(2):
+        for owner in range(n_db):
+            source = (2 * owner + chunk) * half
+            target = (chunk * n_db + owner) * half
+            for head in range(heads):
+                rows_ref[target : target + half, head * HD : (head + 1) * HD] = attended_ref[
+                    head, source : source + half, :
+                ]
+    step = math.gcd(features, 512)
+
+    def columns(at, carried):
+        here = pl.ds(pl.multiple_of(at * step, step), step)
+        product = jnp.dot(rows_ref[...], weight_ref[:, here], preferred_element_type=jnp.float32)
+        product = product.astype(jnp.bfloat16)
+        for owner in range(n_db):
+            first_ref[owner, :, here] = product[owner * half : (owner + 1) * half]
+            second_ref[owner, :, here] = product[(n_db + owner) * half : (n_db + owner + 1) * half]
+        return carried
+
+    lax.fori_loop(0, features // step, columns, 0)
+
+
+def self_out(attended, weight, n_db):
+    heads, rows, _ = attended.shape
+    width, features = weight.shape
+    half = rows // n_db // 2
+    vmem = pl.BlockSpec(memory_space=pltpu.VMEM)
+    return pl.pallas_call(
+        self_out_kernel,
+        out_shape=[jax.ShapeDtypeStruct((n_db, half, features), jnp.bfloat16)] * 2,
+        in_specs=[vmem, vmem],
+        out_specs=[vmem, vmem],
+        scratch_shapes=[pltpu.VMEM((rows, width), jnp.bfloat16)],
+        compiler_params=pltpu.CompilerParams(vmem_limit_bytes=VMEM_BYTES),
+        cost_estimate=pl.CostEstimate(
+            flops=2 * rows * width * features,
+            bytes_accessed=2 * (rows * width + width * features + rows * features),
+            transcendentals=0,
+        ),
+        name="self_out",
+    )(attended, weight)
 
 
 def project_kernel(where_ref, first_ref, second_ref, wk_ref, wv_ref, keys_ref, values_ref):
@@ -184,15 +244,20 @@
 
 def project_encodings(where, table, w_cross_k, w_cross_v):
     groups = where.shape[0] // (2 * NEIGH)
-    _, cuts, _, piece, depth = table.shape
+    _, _, _, piece, depth = table.shape
+    cuts = NLEN // piece
+    assert cuts in (1, 2)
     width = w_cross_k.shape[1]
 
     def entry(neighbour):
         def index(group, where_ref):
             at = 2 * (NEIGH * group + neighbour)
-            return (where_ref[at], 0, where_ref[at + 1], 0, 0)
-
-        return pl.BlockSpec((1, cuts, 1, piece, depth), index)
+            row, shard = where_ref[at], where_ref[at + 1]
+            if cuts == 2:
+                return (0, row, shard, 0, 0)
+            return (lax.rem(row, 2), lax.div(row, 2), shard, 0, 0)
+
+        return pl.BlockSpec((cuts, 1, 1, piece, depth), index)
 
     fixed = pl.BlockSpec((depth, width), lambda group, where_ref: (0, 0))
     made = pl.BlockSpec((GROUP, width), lambda group, where_ref: (group, 0))
@@ -231,63 +296,117 @@
     return jnp.where(first, mixed[:rows], mixed[rows:])
 
 
-def cross_kernel(live_ref, query_ref, keys_ref, values_ref, out_ref, *, spans, heads, scale):
+def cross_kernel(place_ref, *refs, chunk, scale):
+    out_ref, rows_ref, mixed_ref = refs[-3:]
+    wq_ref, keys_ref, values_ref, wo_ref = refs[-7:-3]
+    own_ref, pieces = refs[0], refs[1:-7]
+    n_db, half, features = out_ref.shape
+    heads = wq_ref.shape[1] // HD
+    pairs = heads // 2
     tail = 16
-    pairs = heads // 2
+    for me in range(n_db):
+
+        @pl.when(place_ref[0] == me)
+        def _(me=me):
+            for owner in range(n_db):
+                if owner == me:
+                    source = own_ref
+                elif owner < me:
+                    source = pieces[2 * (me - owner - 1)]
+                else:
+                    source = pieces[2 * (owner - me - 1) + 1]
+                rows_ref[owner * half : (owner + 1) * half, :] = source[...]
+
     row = lax.broadcasted_iota(jnp.int32, (tail, 2 * HD), 0)
     lanes = [slice(2 * pair * HD, 2 * (pair + 1) * HD) for pair in range(pairs)]
-    for span in range(spans):
-        top = span * SPAN
-        here, after = (slice((span + k) * GROUP, (span + k + 1) * GROUP) for k in (0, 1))
-        work = [(slice(top, top + SPAN), here, at) for at in lanes]
-        work += [(slice(top + SPAN - tail, top + SPAN), after, at) for at in lanes]
+    queries = [
+        jnp.dot(rows_ref[...], wq_ref[:, at], preferred_element_type=jnp.float32).astype(
+            jnp.bfloat16
+        )
+        for at in lanes
+    ]
+    for owner in range(n_db):
+        top = owner * half
+        place = (2 * owner + chunk) * half
+        group = place // SPAN
+        ends = (place + half) % SPAN == 0
+        here, after = (slice((group + k) * GROUP, (group + k + 1) * GROUP) for k in (0, 1))
+        work = [(query[top : top + half], here, at) for query, at in zip(queries, lanes)]
+        if ends:
+            work += [
+                (query[top + half - tail : top + half], after, at)
+                for query, at in zip(queries, lanes)
+            ]
         scores = [
             lax.dot_general(
-                apart_heads(query_ref[of, at]),
-                keys_ref[group, at],
+                apart_heads(query),
+                keys_ref[which, at],
                 (((1,), (1,)), ((), ())),
                 preferred_element_type=jnp.float32,
             )
             * (scale * LOG2E)
-            for of, group, at in work
+            for query, which, at in work
         ]
         tops = [jnp.max(one, axis=-1, keepdims=True) for one in scores]
         weights = [jnp.exp2(one - top_one) for one, top_one in zip(scores, tops)]
         totals = [jnp.sum(one, axis=-1, keepdims=True) for one in weights]
         mixed = [
             jnp.dot(
-                one.astype(jnp.bfloat16), values_ref[group, at], preferred_element_type=jnp.float32
+                one.astype(jnp.bfloat16), values_ref[which, at], preferred_element_type=jnp.float32
             )
-            for one, (_, group, at) in zip(weights, work)
+            for one, (_, which, at) in zip(weights, work)
         ]
         mixed = [together_heads(one / total) for one, total in zip(mixed, totals)]
         for pair, at in enumerate(lanes):
-            main, last = mixed[pair], mixed[pairs + pair]
-            if span == 0:
-                main = jnp.where(live_ref[0] > 0, main, 0.0)
-            last = jnp.where(row == tail - 1, last, main[SPAN - tail :])
-            out_ref[top : top + SPAN - tail, at] = main[: SPAN - tail].astype(jnp.bfloat16)
-            out_ref[top + SPAN - tail : top + SPAN, at] = last.astype(jnp.bfloat16)
-
-
-def cross_attend(live, query, keys, values, scale):
-    rows, width = query.shape
+            main = mixed[pair]
+            if group == 0:
+                main = jnp.where(place_ref[1] > 0, main, 0.0)
+            if ends:
+                last = jnp.where(row == tail - 1, mixed[pairs + pair], main[half - tail :])
+                if half > tail:
+                    mixed_ref[top : top + half - tail, at] = main[: half - tail].astype(
+                        jnp.bfloat16
+                    )
+                mixed_ref[top + half - tail : top + half, at] = last.astype(jnp.bfloat16)
+            else:
+                mixed_ref[top : top + half, at] = main.astype(jnp.bfloat16)
+
+    step = math.gcd(features, 512)
+
+    def columns(at, carried):
+        here = pl.ds(pl.multiple_of(at * step, step), step)
+        product = jnp.dot(mixed_ref[...], wo_ref[:, here], preferred_element_type=jnp.float32)
+        product = product.astype(jnp.bfloat16)
+        for owner in range(n_db):
+            out_ref[owner, :, here] = product[owner * half : (owner + 1) * half]
+        return carried
+
+    lax.fori_loop(0, features // step, columns, 0)
+
+
+def cross_chunk(chunk, place, normed, pieces, w_cross_q, keys, values, w_cross_out, n_db, scale):
+    half, features = normed.shape
+    width = w_cross_q.shape[1]
+    rows = n_db * half
     vmem = pl.BlockSpec(memory_space=pltpu.VMEM)
+    flat = [one for pair in pieces for one in pair]
     return pl.pallas_call(
-        functools.partial(
-            cross_kernel, spans=rows // SPAN, heads=width // HD, scale=scale
-        ),
-        out_shape=jax.ShapeDtypeStruct((rows, width), jnp.bfloat16),
-        in_specs=[pl.BlockSpec(memory_space=pltpu.SMEM), vmem, vmem, vmem],
+        functools.partial(cross_kernel, chunk=chunk, scale=scale),
+        out_shape=jax.ShapeDtypeStruct((n_db, half, features), jnp.bfloat16),
+        in_specs=[pl.BlockSpec(memory_space=pltpu.SMEM)] + [vmem] * (5 + len(flat)),
         out_specs=vmem,
+        scratch_shapes=[
+            pltpu.VMEM((rows, features), jnp.bfloat16),
+            pltpu.VMEM((rows, width), jnp.bfloat16),
+        ],
         compiler_params=pltpu.CompilerParams(vmem_limit_bytes=VMEM_BYTES),
         cost_estimate=pl.CostEstimate(
-            flops=8 * rows * GROUP * width,
-            bytes_accessed=2 * (2 * rows + 2 * keys.shape[0]) * width,
-            transcendentals=2 * rows * GROUP * width // HD,
-        ),
-        name="cross_attend",
-    )(live, query, keys, values)
+            flops=4 * rows * width * (features + GROUP),
+            bytes_accessed=4 * width * (features + keys.shape[0]) + 4 * rows * features,
+            transcendentals=rows * GROUP * width // HD,
+        ),
+        name="cross_chunk",
+    )(place, normed, *flat, w_cross_q, keys, values, w_cross_out)
 
 
 def per_device(
@@ -305,13 +424,12 @@
     nb_shard,
     nb_row,
 ):
-    rows, features = hidden_in.shape
-    width = query_rows.shape[1]
-    heads = width // HD
+    rows = hidden_in.shape[0]
+    heads = query_rows.shape[1] // HD
     n_seq, n_db = lax.axis_size("seq"), lax.axis_size("db")
     seq_index, db_index = lax.axis_index("seq"), lax.axis_index("db")
     scale = 1.0 / math.sqrt(HD)
-    share = rows // n_db
+    half = rows // n_db // 2
 
     rows_shard, _, depth = enc_table.shape
     piece = rows_shard * NLEN // n_seq
@@ -322,42 +440,56 @@
         (part, query_rows, key_rows, value_rows)
     )
     along_db = lax.all_gather(part, "db", axis=0)
+    cores = [list(range(core, n_seq, 2)) for core in range(2)]
+    chips = [[chip, chip + 1] for chip in range(0, n_seq, 2)]
+    of_core = lax.all_gather(along_db, "seq", axis=0, axis_index_groups=cores)
+    table = lax.all_gather(of_core, "seq", axis=0, axis_index_groups=chips)
     wanted = jnp.stack((nb_row, nb_shard), axis=-1).astype(jnp.int32)
     before = shift(wanted[-1], "seq", 1, range(n_seq))
     where = jnp.concatenate((before[None], wanted), axis=0).reshape(-1)
+    place = jnp.stack((db_index, (seq_index > 0).astype(jnp.int32))).astype(jnp.int32)
 
     if heads == n_seq:
         attended = self_attention_by_head(query_rows, key_rows, value_rows, scale)
     else:
         attended = self_attention_gathered(query_rows, key_rows, value_rows, scale)
-
-    along_db, attended = lax.optimization_barrier((along_db, attended))
-    table = lax.all_gather(along_db, "seq", axis=0).reshape(
-        rows_shard, NLEN // piece, n_db, piece, depth
-    )
-
-    partial = jnp.dot(attended, w_self_out, preferred_element_type=jnp.float32).astype(jnp.bfloat16)
-    attn_share = line_reduce_scatter(partial.reshape(n_db, share, features))
-    residual = (
-        lax.dynamic_slice_in_dim(hidden_in, db_index * share, share, 0).astype(jnp.float32)
-        + attn_share
-    )
-    mean_square = jnp.mean(residual * residual, axis=-1, keepdims=True)
-    normed_share = (
-        residual * lax.rsqrt(mean_square + 1e-05) * norm_gain.astype(jnp.float32)
-    ).astype(jnp.bfloat16)
+    attended, where = lax.optimization_barrier((attended, where))
+
+    gain = norm_gain.astype(jnp.float32)
+
+    def finish_norm(chunk, blocks, carried):
+        own = lax.dynamic_slice_in_dim(hidden_in, (2 * db_index + chunk) * half, half, 0)
+        residual = own.astype(jnp.float32) + reduced(blocks, carried)
+        mean_square = jnp.mean(residual * residual, axis=-1, keepdims=True)
+        return residual, (residual * lax.rsqrt(mean_square + 1e-05) * gain).astype(jnp.bfloat16)
+
+    def cross(chunk, normed, pieces, keys, values):
+        return cross_chunk(
+            chunk, place, normed, pieces, w_cross_q, keys, values, w_cross_out, n_db, scale
+        )
+
+    first, second = self_out(attended, w_self_out, n_db)
+    carried = None
+    for step in range(n_db - 1):
+        carried = lax.optimization_barrier(reduce_step(first, carried, step))
+    residual_first, normed_first = finish_norm(0, first, carried)
+
     projected = project_encodings(where, table, w_cross_k, w_cross_v)
-    normed, (keys, values) = line_all_gather(normed_share, projected)
-    normed = normed.reshape(rows, features)
-    cross_query = jnp.dot(normed, w_cross_q, preferred_element_type=jnp.float32).astype(
-        jnp.bfloat16
-    )
-    live = (seq_index > 0).astype(jnp.int32).reshape(1)
-    mixed = cross_attend(live, cross_query, keys, values, scale)
-    out_partial = jnp.dot(mixed, w_cross_out, preferred_element_type=jnp.float32).astype(
-        jnp.bfloat16
-    )
-    return residual + line_reduce_scatter(out_partial.reshape(n_db, share, features))
+    pieces, second, carried, (keys, values) = gather_reduce(
+        normed_first, second, projected, n_db - 2
+    )
+    out_first = cross(0, normed_first, pieces, keys, values)
+    residual_second, normed_second = finish_norm(1, second, carried)
+
+    pieces, out_first, carried, _ = gather_reduce(normed_second, out_first, None, 0)
+    out_second = cross(1, normed_second, pieces, keys, values)
+    block_first = residual_first + reduced(out_first, carried)
+
+    carried = None
+    for step in range(n_db - 1):
+        carried = lax.optimization_barrier(reduce_step(out_second, carried, step))
+    block_second = residual_second + reduced(out_second, carried)
+    return jnp.concatenate((block_first, block_second), axis=0)
 
 
 def solution(mesh):

time: 232 us -> 335 us (1.44)
  starting transfers between devices: 51.7 us -> 105 us
  waiting for transfers between devices: 92.3 us -> 142 us
  local copies, waits for them, and re-layouts: 12 us -> 29.6 us
  Pallas kernels: 17.8 us -> 33.3 us
  matrix products: 14.1 us -> 0 us
  blocking collectives: 12.2 us -> 0 us
  other arithmetic: 16.4 us -> 8.09 us
    all_gather x1 -> x2, waiting for transfers between devices: 0.01 us -> 60.3 us  [the longest x1 60.3 us: per_device(): of_core = lax.all_gather(along_db, 'seq', axis=0, axis_index_groups=cores)]
    ppermute x19 -> x37, starting transfers between devices: 46.5 us -> 97.9 us  [shift(): return lax.ppermute(block, axis, route)]
    all_gather x1, waiting for transfers between devices: 0.02 us -> 30.7 us  [per_device(): along_db = lax.all_gather(part, 'db', axis=0)]
    ppermute x19 -> x37, waiting for transfers between devices: 71.3 us -> 45 us  [shift(): return lax.ppermute(block, axis, route)]
    all_to_all x1, waiting for transfers between devices: 20.2 us -> 0.01 us  [self_attention_by_head(): held = lax.all_to_all(packed, 'seq', 0, 0, tiled=True)]
    unnamed x24 -> x38, local copies, waits for them, and re-layouts: 9.68 us -> 28.3 us
    pallas_call x1 -> x3, Pallas kernels: 2.46 us -> 17.2 us  [the longest x2 13.6 us: cross_chunk(): pl.pallas_call(functools.partial(cross_kernel, chunk=chunk, scale=scale),...]
    dot_general x3 -> x0, matrix products: 14.1 us -> none  [the longest x1 5.94 us: per_device(): jnp.dot(normed, w_cross_q, preferred_element_type=jnp.float32)]
  transfers between devices with their start and end apart: 22 -> 42, of which waited for: 14 -> 21; matrix products, arithmetic and copies ran while one was open for 7% -> 1% of each run, Pallas kernels for 5% -> 8%
where the time goes in v4:
time: 335 us; the launch traced here: 332 us
  waiting for transfers between devices  142 us (42%)
  starting transfers between devices  105 us (31%)
  Pallas kernels  33.3 us (10%)
  local copies, waits for them, and re-layouts  29.6 us (9%)
  between operations  13.8 us (4%)
  other arithmetic  8.09 us (2%)
    ppermute x37, starting transfers between devices, shift(): return lax.ppermute(block, axis, route)  97.9 us
    all_gather x1, waiting for transfers between devices, per_device(): of_core = lax.all_gather(along_db, 'seq', axis=0, axis_index_groups=cores)  60.3 us
    ppermute x37, waiting for transfers between devices, shift(): return lax.ppermute(block, axis, route)  45 us
    all_gather x1, waiting for transfers between devices, per_device(): along_db = lax.all_gather(part, 'db', axis=0)  30.7 us
    unnamed x38, local copies, waits for them, and re-layouts  28.3 us
    pallas_call x2, Pallas kernels, cross_chunk(): pl.pallas_call(functools.partial(cross_kernel, chunk=chunk, scale=scale),...  13.6 us
    pallas_call x1, Pallas kernels, project_encodings(): pl.pallas_call(project_kernel, out_shape=[jax.ShapeDtypeStruct((groups *...  6.92 us
  transfers between devices with their start and end apart: 42, of which 21 were waited for; matrix products, arithmetic and copies ran while one was open for 1% of the time, Pallas kernels for 8%

profile of v4, /device:TPU:0, one launch (start us, length us, event | category | flops | bytes accessed | tf_op | source)
XLA Modules:
  0.0 332.1 jit_solution(348768035308814246)
XLA Ops:
  6.5 1.6 copy-done
  8.9 30.7 %all-gather.7.cloned.1.call-done = bf16[512,1024]{1,0:T(8,128)(2,1)} async-done(((bf16[128,1024]{1,0:T(8,128)(2,1)}), bf16[512,1024]{1,0:T(8,128)(2,1)}) %all-gather.7.cloned.1.call-update) | async-done | bytes 1048592 | tf_op jit(solution)/shard_map/all_gather | solution.py:442
  39.7 3.7 %pack_heads.1 = bf16[8,3,256,128]{3,2,1,0:T(8,128)(2,1)} custom-call(bf16[256,1024]{1,0:T(8,128)(2,1)} %query_ref, bf16[256,1024]{1,0:T(8,128)(2,1)} %key_ref, bf16[256,1024]{1,0:T(8,128)(2,1)} %value_ref), custom_call_target="tpu_custom_call" | custom-call | bytes 3145728 | tf_op jit(solution)/shard_map/pack_heads/pallas_call | solution.py:137
  43.4 3.7 %all-to-all-start = ((bf16[8,3,256,128]{3,2,1,0:T(8,128)(2,1)}), bf16[8,3,256,128]{3,2,1,0:T(8,128)(2,1)S(1)}, u32[]{:S(2)}, u32[]{:S(2)}) async-start(bf16[8,3,256,128]{3,2,1,0:T(8,128)(2,1)} %pack_heads.1), calls=%async_computation | async-start | bytes 3145728 | tf_op jit(solution)/shard_map/all_to_all | solution.py:152
  47.1 60.3 %all-gather.9.cloned.1.call-done = bf16[16,128,1024]{2,1,0:T(8,128)(2,1)} async-done(((bf16[4,128,1024]{2,1,0:T(8,128)(2,1)}), bf16[16,128,1024]{2,1,0:T(8,128)(2,1)}) %all-gather.9.cloned.1.call-update) | async-done | bytes 4194320 | tf_op jit(solution)/shard_map/all_gather | solution.py:445
  107.5 5.5 %self_attend.1 = bf16[8,256,128]{2,1,0:T(8,128)(2,1)} custom-call(bf16[8,3,256,128]{3,2,1,0:T(8,128)(2,1)S(1)} %all-to-all-done.qkv_ref), custom_call_target="tpu_custom_call" | custom-call | flops 1073741824 | bytes 2097152 | tf_op jit(solution)/shard_map/self_attend/pallas_call | solution.py:112
  113.0 3.5 %all-to-all-start.1 = ((bf16[8,256,128]{2,1,0:T(8,128)(2,1)}), bf16[8,256,128]{2,1,0:T(8,128)(2,1)S(1)}, u32[]{:S(2)}, u32[]{:S(2)}) async-start(bf16[8,256,128]{2,1,0:T(8,128)(2,1)} %self_attend.1), calls=%async_computation.1 | async-start | bytes 1048576 | tf_op jit(solution)/shard_map/all_to_all | solution.py:154
  116.7 2.3 collective-permute-start
  120.1 6.0 %all-to-all-done.1.attended_ref = bf16[8,256,128]{2,1,0:T(8,128)(2,1)S(1)} async-done(((bf16[8,256,128]{2,1,0:T(8,128)(2,1)}), bf16[8,256,128]{2,1,0:T(8,128)(2,1)S(1)}, u32[]{:S(2)}, u32[]{:S(2)}) %all-to-all-start.1) | async-done | bytes 524320 | tf_op jit(solution)/shard_map/all_to_all | solution.py:154
  126.1 3.4 %copy-done.9 = bf16[1024,4096]{1,0:T(8,128)(2,1)S(1)} copy-done((bf16[1024,4096]{1,0:T(8,128)(2,1)S(1)}, bf16[1024,4096]{1,0:T(8,128)(2,1)}, u32[]{:S(2)}) %copy-start.9) | copy-done | bytes 8388632
  129.5 3.6 %self_out.1 = (bf16[4,32,4096]{2,1,0:T(8,128)(2,1)S(1)}, bf16[4,32,4096]{2,1,0:T(8,128)(2,1)S(1)}) custom-call(bf16[8,256,128]{2,1,0:T(8,128)(2,1)S(1)} %all-to-all-done.1.attended_ref, bf16[1024,4096]{1,0:T(8,128)(2,1)S(1)} %copy-done.9), custom_call_target="tpu_custom_call" | custom-call | flops 2147483648 | bytes 11010048 | tf_op jit(solution)/shard_map/self_out/pallas_call | solution.py:216
  133.9 3.4 %collective-permute-start.1 = (bf16[32,4096]{1,0:T(8,128)(2,1)S(1)}, bf16[32,4096]{1,0:T(8,128)(2,1)S(1)}, u32[]{:S(2)}, u32[]{:S(2)}) collective-permute-start(bf16[32,4096]{1,0:T(8,128)(2,1)S(1)} %get-tuple-element.132), channel_id=1, source_target_pairs={{0,1},{4,5},{8,9},{12,13},{16,17},{20,21},{24,25},{28,29}} | collective-permute-start | bytes 786440 | tf_op jit(solution)/shard_map/ppermute | solution.py:25
  137.4 3.8 %collective-permute-done.1 = bf16[32,4096]{1,0:T(8,128)(2,1)S(1)} collective-permute-done((bf16[32,4096]{1,0:T(8,128)(2,1)S(1)}, bf16[32,4096]{1,0:T(8,128)(2,1)S(1)}, u32[]{:S(2)}, u32[]{:S(2)}) %collective-permute-start.1) | collective-permute-done | bytes 262176 | tf_op jit(solution)/shard_map/ppermute | solution.py:25
  142.0 5.0 %collective-permute-start.3 = (bf16[32,4096]{1,0:T(8,128)(2,1)S(1)}, bf16[32,4096]{1,0:T(8,128)(2,1)S(1)}, u32[]{:S(2)}, u32[]{:S(2)}) collective-permute-start(bf16[32,4096]{1,0:T(8,128)(2,1)S(1)} %get-tuple-element.130), channel_id=1, source_target_pairs={{0,1},{1,2},{4,5},{5,6},{8,9},{9,10},{12,13},{13,14},{16,17},{17,1... | collective-permute-start | bytes 786440 | tf_op jit(solution)/shard_map/ppermute | solution.py:25
  147.1 3.8 %collective-permute-done.3 = bf16[32,4096]{1,0:T(8,128)(2,1)S(1)} collective-permute-done((bf16[32,4096]{1,0:T(8,128)(2,1)S(1)}, bf16[32,4096]{1,0:T(8,128)(2,1)S(1)}, u32[]{:S(2)}, u32[]{:S(2)}) %collective-permute-start.3) | collective-permute-done | bytes 262176 | tf_op jit(solution)/shard_map/ppermute | solution.py:25
  151.0 1.3 collective-permute-start.6
  152.3 5.2 %collective-permute-start.5 = (bf16[32,4096]{1,0:T(8,128)(2,1)S(1)}, bf16[32,4096]{1,0:T(8,128)(2,1)S(1)}, u32[]{:S(2)}, u32[]{:S(2)}) collective-permute-start(bf16[32,4096]{1,0:T(8,128)(2,1)S(1)} %get-tuple-element.128), channel_id=1, source_target_pairs={{0,1},{1,2},{2,3},{4,5},{5,6},{6,7},{8,9},{9,10},{10,11},{12,13},{... | collective-permute-start | bytes 786440 | tf_op jit(solution)/shard_map/ppermute | solution.py:25
  157.5 2.4 collective-permute-done.6
  159.9 1.5 collective-permute-done.5
  162.7 1.3 collective-permute-start.8
  164.0 5.0 %collective-permute-start.7 = (bf16[32,4096]{1,0:T(8,128)(2,1)S(1)}, bf16[32,4096]{1,0:T(8,128)(2,1)S(1)}, u32[]{:S(2)}, u32[]{:S(2)}) collective-permute-start(bf16[32,4096]{1,0:T(8,128)(2,1)S(1)} %multiply_convert_fusion.1.refs_0_), channel_id=1, source_target_pairs={{0,1},{1,2},{2,3},{4,5},{5,6},{6,7},{8,9},{9,10},{10,11},{12,13},{... | collective-permute-start | bytes 786440 | tf_op jit(solution)/shard_map/ppermute | solution.py:25
  169.1 2.4 collective-permute-done.8.refs_2_
  171.5 1.5 collective-permute-done.7.refs_1_
  172.9 1.4 collective-permute-start.9
  176.3 10.8 %collective-permute-start.11 = (bf16[32,4096]{1,0:T(8,128)(2,1)S(1)}, bf16[32,4096]{1,0:T(8,128)(2,1)S(1)}, u32[]{:S(2)}, u32[]{:S(2)}) collective-permute-start(bf16[32,4096]{1,0:T(8,128)(2,1)S(1)} %get-tuple-element.126), channel_id=1, source_target_pairs={{0,1},{4,5},{8,9},{12,13},{16,17},{20,21},{24,25},{28,29}} | collective-permute-start | bytes 786440 | tf_op jit(solution)/shard_map/ppermute | solution.py:25
  187.1 1.8 collective-permute-done.10.refs_4_
  188.9 4.7 %collective-permute-done.11 = bf16[32,4096]{1,0:T(8,128)(2,1)S(1)} collective-permute-done((bf16[32,4096]{1,0:T(8,128)(2,1)S(1)}, bf16[32,4096]{1,0:T(8,128)(2,1)S(1)}, u32[]{:S(2)}, u32[]{:S(2)}) %collective-permute-start.11) | collective-permute-done | bytes 262176 | tf_op jit(solution)/shard_map/ppermute | solution.py:25
  194.5 1.4 collective-permute-start.16
  195.9 5.0 %collective-permute-start.15 = (bf16[32,4096]{1,0:T(8,128)(2,1)}, bf16[32,4096]{1,0:T(8,128)(2,1)}, u32[]{:S(2)}, u32[]{:S(2)}) collective-permute-start(bf16[32,4096]{1,0:T(8,128)(2,1)} %get-tuple-element.124), channel_id=1, source_target_pairs={{0,1},{1,2},{4,5},{5,6},{8,9},{9,10},{12,13},{13,14},{16,17},{17,1... | collective-permute-start | bytes 786440 | tf_op jit(solution)/shard_map/ppermute | solution.py:25
  200.9 1.4 collective-permute-start.13
  203.7 3.4 %copy-done.6 = bf16[8,4,128,1024]{3,2,1,0:T(8,128)(2,1)S(1)} copy-done((bf16[8,4,128,1024]{3,2,1,0:T(8,128)(2,1)S(1)}, bf16[8,4,128,1024]{3,2,1,0:T(8,128)(2,1)}, u32[]{:S(2)}) %copy-start.6) | copy-done | bytes 8388632
  207.0 1.6 copy-done.12
  208.6 1.6 copy-done.13
  210.2 6.9 %project_encodings.1 = (bf16[1280,1024]{1,0:T(8,128)(2,1)S(1)}, bf16[1280,1024]{1,0:T(8,128)(2,1)S(1)}) custom-call(s32[20]{0:T(128)S(1)} %reshape.64.where_ref, bf16[2,4,4,128,1024]{4,3,2,1,0:T(8,128)(2,1)S(1)} %bitcast.89, bf16[2,4,4,128,1024]{4,3,2,1,0:T(8,128)(2,1)S(1)} %bitcast.90, bf16[1024,1024]{1,0:T(8,128)(2,1)S(1)} %copy-done.12, ...), custom_call_target="tpu_custom_call" | custom-call | flops 5368709120 | bytes 12058624 | tf_op jit(solution)/shard_map/project_encodings/pallas_call | solution.py:264
  217.2 1.5 copy-done.7
  218.7 2.0 fusion.12
  221.9 6.6 %collective-permute-start.17 = (bf16[32,4096]{1,0:T(8,128)(2,1)}, bf16[32,4096]{1,0:T(8,128)(2,1)}, u32[]{:S(2)}, u32[]{:S(2)}) collective-permute-start(bf16[32,4096]{1,0:T(8,128)(2,1)} %get-tuple-element.122), channel_id=1, source_target_pairs={{0,1},{1,2},{2,3},{4,5},{5,6},{6,7},{8,9},{9,10},{10,11},{12,13},{... | collective-permute-start | bytes 786440 | tf_op jit(solution)/shard_map/ppermute | solution.py:25
  228.5 2.0 collective-permute-done.18
  230.5 1.5 collective-permute-done.17
  231.9 1.4 multiply_reduce_fusion
  233.5 1.3 collective-permute-start.20
  234.8 5.0 %collective-permute-start.19 = (bf16[32,4096]{1,0:T(8,128)(2,1)S(1)}, bf16[32,4096]{1,0:T(8,128)(2,1)S(1)}, u32[]{:S(2)}, u32[]{:S(2)}) collective-permute-start(bf16[32,4096]{1,0:T(8,128)(2,1)S(1)} %multiply_convert_fusion.refs_0_), channel_id=1, source_target_pairs={{0,1},{1,2},{2,3},{4,5},{5,6},{6,7},{8,9},{9,10},{10,11},{12,13},{... | collective-permute-start | bytes 786440 | tf_op jit(solution)/shard_map/ppermute | solution.py:25
  240.0 3.4 %copy-done.2 = bf16[4096,1024]{1,0:T(8,128)(2,1)S(1)} copy-done((bf16[4096,1024]{1,0:T(8,128)(2,1)S(1)}, bf16[4096,1024]{1,0:T(8,128)(2,1)}, u32[]{:S(2)}) %copy-start.2) | copy-done | bytes 8388632
  243.3 3.4 %copy-done.4 = bf16[1024,4096]{1,0:T(8,128)(2,1)S(1)} copy-done((bf16[1024,4096]{1,0:T(8,128)(2,1)S(1)}, bf16[1024,4096]{1,0:T(8,128)(2,1)}, u32[]{:S(2)}) %copy-start.4) | copy-done | bytes 8388632
  246.7 1.7 copy-done.8
  248.5 6.9 %cross_chunk.2 = bf16[4,32,4096]{2,1,0:T(8,128)(2,1)S(1)} custom-call(s32[2]{0:T(128)S(1)} %pad_add_fusion.1.place_ref, bf16[32,4096]{1,0:T(8,128)(2,1)S(1)} %multiply_convert_fusion.1.refs_0_, bf16[32,4096]{1,0:T(8,128)(2,1)S(1)} %collective-permute-done.7.refs_1_, bf16[32,4096]{1,0:T(8,128)(2,1)S(1)} %collective-permute-done.8.refs_2_, ...), custom_call_target="tpu_custom_call" | custom-call | flops 2281701376 | bytes 24117248 | tf_op jit(solution)/shard_map/cross_chunk/pallas_call | solution.py:393
  256.0 1.3 collective-permute-start.22
  258.1 7.8 %collective-permute-start.23 = (bf16[32,4096]{1,0:T(8,128)(2,1)S(1)}, bf16[32,4096]{1,0:T(8,128)(2,1)S(1)}, u32[]{:S(2)}, u32[]{:S(2)}) collective-permute-start(bf16[32,4096]{1,0:T(8,128)(2,1)S(1)} %get-tuple-element.120), channel_id=1, source_target_pairs={{0,1},{4,5},{8,9},{12,13},{16,17},{20,21},{24,25},{28,29}} | collective-permute-start | bytes 786440 | tf_op jit(solution)/shard_map/ppermute | solution.py:25
  265.9 4.4 %collective-permute-done.22.refs_4_ = bf16[32,4096]{1,0:T(8,128)(2,1)S(1)} collective-permute-done((bf16[32,4096]{1,0:T(8,128)(2,1)S(1)}, bf16[32,4096]{1,0:T(8,128)(2,1)S(1)}, u32[]{:S(2)}, u32[]{:S(2)}) %collective-permute-start.22) | collective-permute-done | bytes 262176 | tf_op jit(solution)/shard_map/ppermute | solution.py:25
  271.1 4.5 %collective-permute-start.27 = (bf16[32,4096]{1,0:T(8,128)(2,1)S(1)}, bf16[32,4096]{1,0:T(8,128)(2,1)S(1)}, u32[]{:S(2)}, u32[]{:S(2)}) collective-permute-start(bf16[32,4096]{1,0:T(8,128)(2,1)S(1)} %get-tuple-element.118), channel_id=1, source_target_pairs={{0,1},{1,2},{4,5},{5,6},{8,9},{9,10},{12,13},{13,14},{16,17},{17,1... | collective-permute-start | bytes 786440 | tf_op jit(solution)/shard_map/ppermute | solution.py:25
  276.3 1.3 collective-permute-start.26
  277.6 1.9 collective-permute-done.27
  279.5 5.1 %collective-permute-done.26.refs_6_ = bf16[32,4096]{1,0:T(8,128)(2,1)S(1)} collective-permute-done((bf16[32,4096]{1,0:T(8,128)(2,1)S(1)}, bf16[32,4096]{1,0:T(8,128)(2,1)S(1)}, u32[]{:S(2)}, u32[]{:S(2)}) %collective-permute-start.26) | collective-permute-done | bytes 262176 | tf_op jit(solution)/shard_map/ppermute | solution.py:25
  284.5 3.4 %copy-done.3 = bf16[4096,1024]{1,0:T(8,128)(2,1)S(1)} copy-done((bf16[4096,1024]{1,0:T(8,128)(2,1)S(1)}, bf16[4096,1024]{1,0:T(8,128)(2,1)}, u32[]{:S(2)}) %copy-start.3) | copy-done | bytes 8388632
  287.9 3.4 %copy-done.5 = bf16[1024,4096]{1,0:T(8,128)(2,1)S(1)} copy-done((bf16[1024,4096]{1,0:T(8,128)(2,1)S(1)}, bf16[1024,4096]{1,0:T(8,128)(2,1)}, u32[]{:S(2)}) %copy-start.5) | copy-done | bytes 8388632
  291.3 6.7 %cross_chunk.3 = bf16[4,32,4096]{2,1,0:T(8,128)(2,1)S(1)} custom-call(s32[2]{0:T(128)S(1)} %pad_add_fusion.1.place_ref, bf16[32,4096]{1,0:T(8,128)(2,1)S(1)} %multiply_convert_fusion.refs_0_, bf16[32,4096]{1,0:T(8,128)(2,1)S(1)} %collective-permute-done.19.refs_1_, bf16[32,4096]{1,0:T(8,128)(2,1)S(1)} %collective-permute-done.20.refs_2_, ...), custom_call_target="tpu_custom_call" | custom-call | flops 2281701376 | bytes 24117248 | tf_op jit(solution)/shard_map/cross_chunk/pallas_call | solution.py:393
  298.8 1.6 collective-permute-start.31
  300.5 1.3 collective-permute-start.30
  301.8 4.6 %collective-permute-start.29 = (bf16[32,4096]{1,0:T(8,128)(2,1)S(1)}, bf16[32,4096]{1,0:T(8,128)(2,1)S(1)}, u32[]{:S(2)}, u32[]{:S(2)}) collective-permute-start(bf16[32,4096]{1,0:T(8,128)(2,1)S(1)} %get-tuple-element.110), channel_id=1, source_target_pairs={{0,1},{1,2},{2,3},{4,5},{5,6},{6,7},{8,9},{9,10},{10,11},{12,13},{... | collective-permute-start | bytes 786440 | tf_op jit(solution)/shard_map/ppermute | solution.py:25
  307.2 2.8 collective-permute-start.33
  310.2 3.7 %collective-permute-done.33 = bf16[32,4096]{1,0:T(8,128)(2,1)S(1)} collective-permute-done((bf16[32,4096]{1,0:T(8,128)(2,1)S(1)}, bf16[32,4096]{1,0:T(8,128)(2,1)S(1)}, u32[]{:S(2)}, u32[]{:S(2)}) %collective-permute-start.33) | collective-permute-done | bytes 262176 | tf_op jit(solution)/shard_map/ppermute | solution.py:25
  315.3 5.2 %collective-permute-start.35 = (bf16[32,4096]{1,0:T(8,128)(2,1)S(1)}, bf16[32,4096]{1,0:T(8,128)(2,1)S(1)}, u32[]{:S(2)}, u32[]{:S(2)}) collective-permute-start(bf16[32,4096]{1,0:T(8,128)(2,1)S(1)} %get-tuple-element.112), channel_id=1, source_target_pairs={{0,1},{1,2},{2,3},{4,5},{5,6},{6,7},{8,9},{9,10},{10,11},{12,13},{... | collective-permute-start | bytes 786440 | tf_op jit(solution)/shard_map/ppermute | solution.py:25
  320.7 2.3 collective-permute-done.36
  322.9 1.5 collective-permute-done.35
  (97 shorter events, 18.4 us)
Async XLA Ops:
  6.5 1.6 copy-start
  6.5 33.1 %all-gather.7.cloned.1.call-start = ((), (), s32[]{:S(2)}) async-start(), calls=%async_computation.2 | async-start | bytes 1310720 | tf_op jit(solution)/shard_map/all_gather | solution.py:442
  8.9 98.5 %all-gather.9.cloned.1.call-start = ((), (), s32[]{:S(2)}) async-start(), calls=%async_computation.3 | async-start | bytes 5242880 | tf_op jit(solution)/shard_map/all_gather | solution.py:445
  43.4 64.0 %all-to-all-start = ((bf16[8,3,256,128]{3,2,1,0:T(8,128)(2,1)}), bf16[8,3,256,128]{3,2,1,0:T(8,128)(2,1)S(1)}, u32[]{:S(2)}, u32[]{:S(2)}) async-start(bf16[8,3,256,128]{3,2,1,0:T(8,128)(2,1)} %pack_heads.1), calls=%async_computation | async-start | bytes 3145728 | tf_op jit(solution)/shard_map/all_to_all | solution.py:152
  47.1 156.5 %all-gather.11.cloned.1.call-start = ((), (), s32[]{:S(2)}) async-start(), calls=%async_computation.4 | async-start | bytes 12582912 | tf_op jit(solution)/shard_map/all_gather | solution.py:446
  107.4 9.0 %copy-start.17 = (s32[4,2]{0,1:T(2,128)S(1)}, s32[4,2]{0,1:T(2,128)}, u32[]{:S(2)}) copy-start(s32[4,2]{0,1:T(2,128)} %param.24) | copy-start | bytes 100
  107.5 9.0 %copy-start.18 = (s32[4,2]{0,1:T(2,128)S(1)}, s32[4,2]{0,1:T(2,128)}, u32[]{:S(2)}) copy-start(s32[4,2]{0,1:T(2,128)} %param.25) | copy-start | bytes 100
  113.0 13.2 %all-to-all-start.1 = ((bf16[8,256,128]{2,1,0:T(8,128)(2,1)}), bf16[8,256,128]{2,1,0:T(8,128)(2,1)S(1)}, u32[]{:S(2)}, u32[]{:S(2)}) async-start(bf16[8,256,128]{2,1,0:T(8,128)(2,1)} %self_attend.1), calls=%async_computation.1 | async-start | bytes 1048576 | tf_op jit(solution)/shard_map/all_to_all | solution.py:154
  116.7 3.1 collective-permute-start
  126.1 3.4 %copy-start.9 = (bf16[1024,4096]{1,0:T(8,128)(2,1)S(1)}, bf16[1024,4096]{1,0:T(8,128)(2,1)}, u32[]{:S(2)}) copy-start(bf16[1024,4096]{1,0:T(8,128)(2,1)} %weight_ref.1) | copy-start | bytes 25165828
  133.2 70.5 %copy-start.10 = (bf16[4,32,4096]{2,1,0:T(8,128)(2,1)}, bf16[4,32,4096]{2,1,0:T(8,128)(2,1)S(1)}, u32[]{:S(2)}) copy-start(bf16[4,32,4096]{2,1,0:T(8,128)(2,1)S(1)} %get-tuple-element.67) | copy-start | bytes 3145732
  133.2 24.3 %copy-start.16 = (bf16[4096]{0:T(1024)(128)(2,1)S(1)}, bf16[4096]{0:T(1024)(128)(2,1)}, u32[]{:S(2)}) copy-start(bf16[4096]{0:T(1024)(128)(2,1)} %param.18) | copy-start | bytes 24580
  133.2 4.1 %collective-permute-start.2 = (bf16[32,4096]{1,0:T(8,128)(2,1)S(1)}, bf16[32,4096]{1,0:T(8,128)(2,1)S(1)}, u32[]{:S(2)}, u32[]{:S(2)}) collective-permute-start(bf16[32,4096]{1,0:T(8,128)(2,1)S(1)} %get-tuple-element.131), channel_id=1, source_target_pairs={{3,2},{7,6},{11,10},{15,14},{19,18},{23,22},{27,26},{31,30}} | collective-permute-start | bytes 786440 | tf_op jit(solution)/shard_map/ppermute | solution.py:25
  133.9 7.3 %collective-permute-start.1 = (bf16[32,4096]{1,0:T(8,128)(2,1)S(1)}, bf16[32,4096]{1,0:T(8,128)(2,1)S(1)}, u32[]{:S(2)}, u32[]{:S(2)}) collective-permute-start(bf16[32,4096]{1,0:T(8,128)(2,1)S(1)} %get-tuple-element.132), channel_id=1, source_target_pairs={{0,1},{4,5},{8,9},{12,13},{16,17},{20,21},{24,25},{28,29}} | collective-permute-start | bytes 786440 | tf_op jit(solution)/shard_map/ppermute | solution.py:25
  141.3 5.7 %collective-permute-start.4 = (bf16[32,4096]{1,0:T(8,128)(2,1)S(1)}, bf16[32,4096]{1,0:T(8,128)(2,1)S(1)}, u32[]{:S(2)}, u32[]{:S(2)}) collective-permute-start(bf16[32,4096]{1,0:T(8,128)(2,1)S(1)} %get-tuple-element.129), channel_id=1, source_target_pairs={{2,1},{3,2},{6,5},{7,6},{10,9},{11,10},{14,13},{15,14},{18,17},{19... | collective-permute-start | bytes 786440 | tf_op jit(solution)/shard_map/ppermute | solution.py:25
  142.0 8.9 %collective-permute-start.3 = (bf16[32,4096]{1,0:T(8,128)(2,1)S(1)}, bf16[32,4096]{1,0:T(8,128)(2,1)S(1)}, u32[]{:S(2)}, u32[]{:S(2)}) collective-permute-start(bf16[32,4096]{1,0:T(8,128)(2,1)S(1)} %get-tuple-element.130), channel_id=1, source_target_pairs={{0,1},{1,2},{4,5},{5,6},{8,9},{9,10},{12,13},{13,14},{16,17},{17,1... | collective-permute-start | bytes 786440 | tf_op jit(solution)/shard_map/ppermute | solution.py:25
  151.0 8.9 %collective-permute-start.6 = (bf16[32,4096]{1,0:T(8,128)(2,1)S(1)}, bf16[32,4096]{1,0:T(8,128)(2,1)S(1)}, u32[]{:S(2)}, u32[]{:S(2)}) collective-permute-start(bf16[32,4096]{1,0:T(8,128)(2,1)S(1)} %get-tuple-element.127), channel_id=1, source_target_pairs={{1,0},{2,1},{3,2},{5,4},{6,5},{7,6},{9,8},{10,9},{11,10},{13,12},{... | collective-permute-start | bytes 786440 | tf_op jit(solution)/shard_map/ppermute | solution.py:25
  152.3 9.1 %collective-permute-start.5 = (bf16[32,4096]{1,0:T(8,128)(2,1)S(1)}, bf16[32,4096]{1,0:T(8,128)(2,1)S(1)}, u32[]{:S(2)}, u32[]{:S(2)}) collective-permute-start(bf16[32,4096]{1,0:T(8,128)(2,1)S(1)} %get-tuple-element.128), channel_id=1, source_target_pairs={{0,1},{1,2},{2,3},{4,5},{5,6},{6,7},{8,9},{9,10},{10,11},{12,13},{... | collective-permute-start | bytes 786440 | tf_op jit(solution)/shard_map/ppermute | solution.py:25
  162.6 41.0 %copy-start.14 = (f32[32,4096]{1,0:T(8,128)}, f32[32,4096]{1,0:T(8,128)S(1)}, u32[]{:S(2)}) copy-start(f32[32,4096]{1,0:T(8,128)S(1)} %get-tuple-element.108) | copy-start | bytes 1572868
  162.7 8.7 %collective-permute-start.8 = (bf16[32,4096]{1,0:T(8,128)(2,1)S(1)}, bf16[32,4096]{1,0:T(8,128)(2,1)S(1)}, u32[]{:S(2)}, u32[]{:S(2)}) collective-permute-start(bf16[32,4096]{1,0:T(8,128)(2,1)S(1)} %multiply_convert_fusion.1.refs_0_), channel_id=1, source_target_pairs={{1,0},{2,1},{3,2},{5,4},{6,5},{7,6},{9,8},{10,9},{11,10},{13,12},{... | collective-permute-start | bytes 786440 | tf_op jit(solution)/shard_map/ppermute | solution.py:25
  164.0 8.9 %collective-permute-start.7 = (bf16[32,4096]{1,0:T(8,128)(2,1)S(1)}, bf16[32,4096]{1,0:T(8,128)(2,1)S(1)}, u32[]{:S(2)}, u32[]{:S(2)}) collective-permute-start(bf16[32,4096]{1,0:T(8,128)(2,1)S(1)} %multiply_convert_fusion.1.refs_0_), channel_id=1, source_target_pairs={{0,1},{1,2},{2,3},{4,5},{5,6},{6,7},{8,9},{9,10},{10,11},{12,13},{... | collective-permute-start | bytes 786440 | tf_op jit(solution)/shard_map/ppermute | solution.py:25
  172.9 14.2 %collective-permute-start.9 = (bf16[32,4096]{1,0:T(8,128)(2,1)S(1)}, bf16[32,4096]{1,0:T(8,128)(2,1)}, u32[]{:S(2)}, u32[]{:S(2)}) collective-permute-start(bf16[32,4096]{1,0:T(8,128)(2,1)S(1)} %collective-permute-done.7.refs_1_), channel_id=1, source_target_pairs={{1,2},{2,3},{5,6},{6,7},{9,10},{10,11},{13,14},{14,15},{17,18},{18... | collective-permute-start | bytes 786440 | tf_op jit(solution)/shard_map/ppermute | solution.py:25
  174.3 14.6 %collective-permute-start.10 = (bf16[32,4096]{1,0:T(8,128)(2,1)S(1)}, bf16[32,4096]{1,0:T(8,128)(2,1)}, u32[]{:S(2)}, u32[]{:S(2)}) collective-permute-start(bf16[32,4096]{1,0:T(8,128)(2,1)S(1)} %collective-permute-done.8.refs_2_), channel_id=1, source_target_pairs={{1,0},{2,1},{5,4},{6,5},{9,8},{10,9},{13,12},{14,13},{17,16},{18,1... | collective-permute-start | bytes 786440 | tf_op jit(solution)/shard_map/ppermute | solution.py:25
  175.6 13.2 %collective-permute-start.12 = (bf16[32,4096]{1,0:T(8,128)(2,1)S(1)}, bf16[32,4096]{1,0:T(8,128)(2,1)S(1)}, u32[]{:S(2)}, u32[]{:S(2)}) collective-permute-start(bf16[32,4096]{1,0:T(8,128)(2,1)S(1)} %get-tuple-element.125), channel_id=1, source_target_pairs={{3,2},{7,6},{11,10},{15,14},{19,18},{23,22},{27,26},{31,30}} | collective-permute-start | bytes 786440 | tf_op jit(solution)/shard_map/ppermute | solution.py:25
  176.3 17.3 %collective-permute-start.11 = (bf16[32,4096]{1,0:T(8,128)(2,1)S(1)}, bf16[32,4096]{1,0:T(8,128)(2,1)S(1)}, u32[]{:S(2)}, u32[]{:S(2)}) collective-permute-start(bf16[32,4096]{1,0:T(8,128)(2,1)S(1)} %get-tuple-element.126), channel_id=1, source_target_pairs={{0,1},{4,5},{8,9},{12,13},{16,17},{20,21},{24,25},{28,29}} | collective-permute-start | bytes 786440 | tf_op jit(solution)/shard_map/ppermute | solution.py:25
  194.5 24.1 %collective-permute-start.16 = (bf16[32,4096]{1,0:T(8,128)(2,1)}, bf16[32,4096]{1,0:T(8,128)(2,1)}, u32[]{:S(2)}, u32[]{:S(2)}) collective-permute-start(bf16[32,4096]{1,0:T(8,128)(2,1)} %get-tuple-element.123), channel_id=1, source_target_pairs={{2,1},{3,2},{6,5},{7,6},{10,9},{11,10},{14,13},{15,14},{18,17},{19... | collective-permute-start | bytes 786440 | tf_op jit(solution)/shard_map/ppermute | solution.py:25
  195.9 22.7 %collective-permute-start.15 = (bf16[32,4096]{1,0:T(8,128)(2,1)}, bf16[32,4096]{1,0:T(8,128)(2,1)}, u32[]{:S(2)}, u32[]{:S(2)}) collective-permute-start(bf16[32,4096]{1,0:T(8,128)(2,1)} %get-tuple-element.124), channel_id=1, source_target_pairs={{0,1},{1,2},{4,5},{5,6},{8,9},{9,10},{12,13},{13,14},{16,17},{17,1... | collective-permute-start | bytes 786440 | tf_op jit(solution)/shard_map/ppermute | solution.py:25
  200.9 17.7 %collective-permute-start.13 = (bf16[32,4096]{1,0:T(8,128)(2,1)}, bf16[32,4096]{1,0:T(8,128)(2,1)}, u32[]{:S(2)}, u32[]{:S(2)}) collective-permute-start(bf16[32,4096]{1,0:T(8,128)(2,1)} %collective-permute-done.9.refs_3_), channel_id=1, source_target_pairs={{2,3},{6,7},{10,11},{14,15},{18,19},{22,23},{26,27},{30,31}} | collective-permute-start | bytes 786440 | tf_op jit(solution)/shard_map/ppermute | solution.py:25
  202.3 16.3 %collective-permute-start.14 = (bf16[32,4096]{1,0:T(8,128)(2,1)}, bf16[32,4096]{1,0:T(8,128)(2,1)}, u32[]{:S(2)}, u32[]{:S(2)}) collective-permute-start(bf16[32,4096]{1,0:T(8,128)(2,1)} %collective-permute-done.10.refs_4_), channel_id=1, source_target_pairs={{1,0},{5,4},{9,8},{13,12},{17,16},{21,20},{25,24},{29,28}} | collective-permute-start | bytes 786440 | tf_op jit(solution)/shard_map/ppermute | solution.py:25
  203.6 3.4 %copy-start.6 = (bf16[8,4,128,1024]{3,2,1,0:T(8,128)(2,1)S(1)}, bf16[8,4,128,1024]{3,2,1,0:T(8,128)(2,1)}, u32[]{:S(2)}) copy-start(bf16[8,4,128,1024]{3,2,1,0:T(8,128)(2,1)} %all-gather.11.cloned.1.call-done) | copy-start | bytes 25165828
  207.0 1.6 copy-start.12
  208.6 1.6 copy-start.13
  210.2 8.4 %copy-start.11 = (bf16[4,32,4096]{2,1,0:T(8,128)(2,1)S(1)}, bf16[4,32,4096]{2,1,0:T(8,128)(2,1)}, u32[]{:S(2)}) copy-start(bf16[4,32,4096]{2,1,0:T(8,128)(2,1)} %copy-done.10) | copy-start | bytes 3145732
  217.1 1.5 copy-start.7
  220.6 9.9 %collective-permute-start.18 = (bf16[32,4096]{1,0:T(8,128)(2,1)}, bf16[32,4096]{1,0:T(8,128)(2,1)}, u32[]{:S(2)}, u32[]{:S(2)}) collective-permute-start(bf16[32,4096]{1,0:T(8,128)(2,1)} %get-tuple-element.121), channel_id=1, source_target_pairs={{1,0},{2,1},{3,2},{5,4},{6,5},{7,6},{9,8},{10,9},{11,10},{13,12},{... | collective-permute-start | bytes 786440 | tf_op jit(solution)/shard_map/ppermute | solution.py:25
  221.9 10.0 %collective-permute-start.17 = (bf16[32,4096]{1,0:T(8,128)(2,1)}, bf16[32,4096]{1,0:T(8,128)(2,1)}, u32[]{:S(2)}, u32[]{:S(2)}) collective-permute-start(bf16[32,4096]{1,0:T(8,128)(2,1)} %get-tuple-element.122), channel_id=1, source_target_pairs={{0,1},{1,2},{2,3},{4,5},{5,6},{6,7},{8,9},{9,10},{10,11},{12,13},{... | collective-permute-start | bytes 786440 | tf_op jit(solution)/shard_map/ppermute | solution.py:25
  233.5 21.8 %collective-permute-start.20 = (bf16[32,4096]{1,0:T(8,128)(2,1)S(1)}, bf16[32,4096]{1,0:T(8,128)(2,1)S(1)}, u32[]{:S(2)}, u32[]{:S(2)}) collective-permute-start(bf16[32,4096]{1,0:T(8,128)(2,1)S(1)} %multiply_convert_fusion.refs_0_), channel_id=1, source_target_pairs={{1,0},{2,1},{3,2},{5,4},{6,5},{7,6},{9,8},{10,9},{11,10},{13,12},{... | collective-permute-start | bytes 786440 | tf_op jit(solution)/shard_map/ppermute | solution.py:25
  234.8 20.5 %collective-permute-start.19 = (bf16[32,4096]{1,0:T(8,128)(2,1)S(1)}, bf16[32,4096]{1,0:T(8,128)(2,1)S(1)}, u32[]{:S(2)}, u32[]{:S(2)}) collective-permute-start(bf16[32,4096]{1,0:T(8,128)(2,1)S(1)} %multiply_convert_fusion.refs_0_), channel_id=1, source_target_pairs={{0,1},{1,2},{2,3},{4,5},{5,6},{6,7},{8,9},{9,10},{10,11},{12,13},{... | collective-permute-start | bytes 786440 | tf_op jit(solution)/shard_map/ppermute | solution.py:25
  240.0 3.4 %copy-start.2 = (bf16[4096,1024]{1,0:T(8,128)(2,1)S(1)}, bf16[4096,1024]{1,0:T(8,128)(2,1)}, u32[]{:S(2)}) copy-start(bf16[4096,1024]{1,0:T(8,128)(2,1)} %refs_7_.3) | copy-start | bytes 25165828
  243.3 3.4 %copy-start.4 = (bf16[1024,4096]{1,0:T(8,128)(2,1)S(1)}, bf16[1024,4096]{1,0:T(8,128)(2,1)}, u32[]{:S(2)}) copy-start(bf16[1024,4096]{1,0:T(8,128)(2,1)} %refs_10_.3) | copy-start | bytes 25165828
  246.7 1.7 copy-start.8
  255.4 10.5 %collective-permute-start.21 = (bf16[32,4096]{1,0:T(8,128)(2,1)S(1)}, bf16[32,4096]{1,0:T(8,128)(2,1)S(1)}, u32[]{:S(2)}, u32[]{:S(2)}) collective-permute-start(bf16[32,4096]{1,0:T(8,128)(2,1)S(1)} %collective-permute-done.19.refs_1_), channel_id=1, source_target_pairs={{1,2},{2,3},{5,6},{6,7},{9,10},{10,11},{13,14},{14,15},{17,18},{18... | collective-permute-start | bytes 786440 | tf_op jit(solution)/shard_map/ppermute | solution.py:25
  256.0 14.2 %collective-permute-start.22 = (bf16[32,4096]{1,0:T(8,128)(2,1)S(1)}, bf16[32,4096]{1,0:T(8,128)(2,1)S(1)}, u32[]{:S(2)}, u32[]{:S(2)}) collective-permute-start(bf16[32,4096]{1,0:T(8,128)(2,1)S(1)} %collective-permute-done.20.refs_2_), channel_id=1, source_target_pairs={{1,0},{2,1},{5,4},{6,5},{9,8},{10,9},{13,12},{14,13},{17,16},{18,1... | collective-permute-start | bytes 786440 | tf_op jit(solution)/shard_map/ppermute | solution.py:25
  257.4 12.9 %collective-permute-start.24 = (bf16[32,4096]{1,0:T(8,128)(2,1)S(1)}, bf16[32,4096]{1,0:T(8,128)(2,1)S(1)}, u32[]{:S(2)}, u32[]{:S(2)}) collective-permute-start(bf16[32,4096]{1,0:T(8,128)(2,1)S(1)} %get-tuple-element.119), channel_id=1, source_target_pairs={{3,2},{7,6},{11,10},{15,14},{19,18},{23,22},{27,26},{31,30}} | collective-permute-start | bytes 786440 | tf_op jit(solution)/shard_map/ppermute | solution.py:25
  258.1 12.2 %collective-permute-start.23 = (bf16[32,4096]{1,0:T(8,128)(2,1)S(1)}, bf16[32,4096]{1,0:T(8,128)(2,1)S(1)}, u32[]{:S(2)}, u32[]{:S(2)}) collective-permute-start(bf16[32,4096]{1,0:T(8,128)(2,1)S(1)} %get-tuple-element.120), channel_id=1, source_target_pairs={{0,1},{4,5},{8,9},{12,13},{16,17},{20,21},{24,25},{28,29}} | collective-permute-start | bytes 786440 | tf_op jit(solution)/shard_map/ppermute | solution.py:25
  270.4 7.2 %collective-permute-start.28 = (bf16[32,4096]{1,0:T(8,128)(2,1)S(1)}, bf16[32,4096]{1,0:T(8,128)(2,1)S(1)}, u32[]{:S(2)}, u32[]{:S(2)}) collective-permute-start(bf16[32,4096]{1,0:T(8,128)(2,1)S(1)} %get-tuple-element.117), channel_id=1, source_target_pairs={{2,1},{3,2},{6,5},{7,6},{10,9},{11,10},{14,13},{15,14},{18,17},{19... | collective-permute-start | bytes 786440 | tf_op jit(solution)/shard_map/ppermute | solution.py:25
  271.1 8.4 %collective-permute-start.27 = (bf16[32,4096]{1,0:T(8,128)(2,1)S(1)}, bf16[32,4096]{1,0:T(8,128)(2,1)S(1)}, u32[]{:S(2)}, u32[]{:S(2)}) collective-permute-start(bf16[32,4096]{1,0:T(8,128)(2,1)S(1)} %get-tuple-element.118), channel_id=1, source_target_pairs={{0,1},{1,2},{4,5},{5,6},{8,9},{9,10},{12,13},{13,14},{16,17},{17,1... | collective-permute-start | bytes 786440 | tf_op jit(solution)/shard_map/ppermute | solution.py:25
  275.6 3.9 %collective-permute-start.25 = (bf16[32,4096]{1,0:T(8,128)(2,1)S(1)}, bf16[32,4096]{1,0:T(8,128)(2,1)S(1)}, u32[]{:S(2)}, u32[]{:S(2)}) collective-permute-start(bf16[32,4096]{1,0:T(8,128)(2,1)S(1)} %collective-permute-done.21.refs_3_), channel_id=1, source_target_pairs={{2,3},{6,7},{10,11},{14,15},{18,19},{22,23},{26,27},{30,31}} | collective-permute-start | bytes 786440 | tf_op jit(solution)/shard_map/ppermute | solution.py:25
  276.3 8.3 %collective-permute-start.26 = (bf16[32,4096]{1,0:T(8,128)(2,1)S(1)}, bf16[32,4096]{1,0:T(8,128)(2,1)S(1)}, u32[]{:S(2)}, u32[]{:S(2)}) collective-permute-start(bf16[32,4096]{1,0:T(8,128)(2,1)S(1)} %collective-permute-done.22.refs_4_), channel_id=1, source_target_pairs={{1,0},{5,4},{9,8},{13,12},{17,16},{21,20},{25,24},{29,28}} | collective-permute-start | bytes 786440 | tf_op jit(solution)/shard_map/ppermute | solution.py:25
  284.5 3.4 %copy-start.3 = (bf16[4096,1024]{1,0:T(8,128)(2,1)S(1)}, bf16[4096,1024]{1,0:T(8,128)(2,1)}, u32[]{:S(2)}) copy-start(bf16[4096,1024]{1,0:T(8,128)(2,1)} %refs_7_.3) | copy-start | bytes 25165828
  287.9 3.4 %copy-start.5 = (bf16[1024,4096]{1,0:T(8,128)(2,1)S(1)}, bf16[1024,4096]{1,0:T(8,128)(2,1)}, u32[]{:S(2)}) copy-start(bf16[1024,4096]{1,0:T(8,128)(2,1)} %refs_10_.3) | copy-start | bytes 25165828
  298.1 8.3 %collective-permute-start.32 = (bf16[32,4096]{1,0:T(8,128)(2,1)S(1)}, bf16[32,4096]{1,0:T(8,128)(2,1)S(1)}, u32[]{:S(2)}, u32[]{:S(2)}) collective-permute-start(bf16[32,4096]{1,0:T(8,128)(2,1)S(1)} %get-tuple-element.115), channel_id=1, source_target_pairs={{3,2},{7,6},{11,10},{15,14},{19,18},{23,22},{27,26},{31,30}} | collective-permute-start | bytes 786440 | tf_op jit(solution)/shard_map/ppermute | solution.py:25
  298.7 21.8 %copy-start.15 = (f32[32,4096]{1,0:T(8,128)S(1)}, f32[32,4096]{1,0:T(8,128)}, u32[]{:S(2)}) copy-start(f32[32,4096]{1,0:T(8,128)} %copy-done.14) | copy-start | bytes 1572868
  298.8 7.6 %collective-permute-start.31 = (bf16[32,4096]{1,0:T(8,128)(2,1)S(1)}, bf16[32,4096]{1,0:T(8,128)(2,1)S(1)}, u32[]{:S(2)}, u32[]{:S(2)}) collective-permute-start(bf16[32,4096]{1,0:T(8,128)(2,1)S(1)} %get-tuple-element.116), channel_id=1, source_target_pairs={{0,1},{4,5},{8,9},{12,13},{16,17},{20,21},{24,25},{28,29}} | collective-permute-start | bytes 786440 | tf_op jit(solution)/shard_map/ppermute | solution.py:25
  300.5 9.6 %collective-permute-start.30 = (bf16[32,4096]{1,0:T(8,128)(2,1)S(1)}, bf16[32,4096]{1,0:T(8,128)(2,1)S(1)}, u32[]{:S(2)}, u32[]{:S(2)}) collective-permute-start(bf16[32,4096]{1,0:T(8,128)(2,1)S(1)} %get-tuple-element.109), channel_id=1, source_target_pairs={{1,0},{2,1},{3,2},{5,4},{6,5},{7,6},{9,8},{10,9},{11,10},{13,12},{... | collective-permute-start | bytes 786440 | tf_op jit(solution)/shard_map/ppermute | solution.py:25
  301.8 8.4 %collective-permute-start.29 = (bf16[32,4096]{1,0:T(8,128)(2,1)S(1)}, bf16[32,4096]{1,0:T(8,128)(2,1)S(1)}, u32[]{:S(2)}, u32[]{:S(2)}) collective-permute-start(bf16[32,4096]{1,0:T(8,128)(2,1)S(1)} %get-tuple-element.110), channel_id=1, source_target_pairs={{0,1},{1,2},{2,3},{4,5},{5,6},{6,7},{8,9},{9,10},{10,11},{12,13},{... | collective-permute-start | bytes 786440 | tf_op jit(solution)/shard_map/ppermute | solution.py:25
  306.5 3.7 %collective-permute-start.34 = (bf16[32,4096]{1,0:T(8,128)(2,1)S(1)}, bf16[32,4096]{1,0:T(8,128)(2,1)S(1)}, u32[]{:S(2)}, u32[]{:S(2)}) collective-permute-start(bf16[32,4096]{1,0:T(8,128)(2,1)S(1)} %get-tuple-element.113), channel_id=1, source_target_pairs={{2,1},{3,2},{6,5},{7,6},{10,9},{11,10},{14,13},{15,14},{18,17},{19... | collective-permute-start | bytes 786440 | tf_op jit(solution)/shard_map/ppermute | solution.py:25
  307.2 6.7 %collective-permute-start.33 = (bf16[32,4096]{1,0:T(8,128)(2,1)S(1)}, bf16[32,4096]{1,0:T(8,128)(2,1)S(1)}, u32[]{:S(2)}, u32[]{:S(2)}) collective-permute-start(bf16[32,4096]{1,0:T(8,128)(2,1)S(1)} %get-tuple-element.114), channel_id=1, source_target_pairs={{0,1},{1,2},{4,5},{5,6},{8,9},{9,10},{12,13},{13,14},{16,17},{17,1... | collective-permute-start | bytes 786440 | tf_op jit(solution)/shard_map/ppermute | solution.py:25
  314.0 8.9 %collective-permute-start.36 = (bf16[32,4096]{1,0:T(8,128)(2,1)S(1)}, bf16[32,4096]{1,0:T(8,128)(2,1)S(1)}, u32[]{:S(2)}, u32[]{:S(2)}) collective-permute-start(bf16[32,4096]{1,0:T(8,128)(2,1)S(1)} %get-tuple-element.111), channel_id=1, source_target_pairs={{1,0},{2,1},{3,2},{5,4},{6,5},{7,6},{9,8},{10,9},{11,10},{13,12},{... | collective-permute-start | bytes 786440 | tf_op jit(solution)/shard_map/ppermute | solution.py:25
  315.3 9.1 %collective-permute-start.35 = (bf16[32,4096]{1,0:T(8,128)(2,1)S(1)}, bf16[32,4096]{1,0:T(8,128)(2,1)S(1)}, u32[]{:S(2)}, u32[]{:S(2)}) collective-permute-start(bf16[32,4096]{1,0:T(8,128)(2,1)S(1)} %get-tuple-element.112), channel_id=1, source_target_pairs={{0,1},{1,2},{2,3},{4,5},{5,6},{6,7},{8,9},{9,10},{10,11},{12,13},{... | collective-permute-start | bytes 786440 | tf_op jit(solution)/shard_map/ppermute | solution.py:25
  320.5 5.0 %copy-start.1 = (bf16[8,128,1024]{2,1,0:T(8,128)(2,1)S(1)}, bf16[8,128,1024]{2,1,0:T(8,128)(2,1)}, u32[]{:S(2)}) copy-start(bf16[8,128,1024]{2,1,0:T(8,128)(2,1)} %param.23) | copy-start | bytes 6291460
Sparse Core Ops, SparseCore 0:
  9.0 30.6 all-gather.6
  41.5 65.8 all-gather.8
  109.0 19.8 all-gather.10

commit v5 on v3

--- a/solution.py
+++ b/solution.py
@@ -16,7 +16,7 @@
 
 NEG_BIG = -1e30
 LOG2E = 1.4426950408889634
-VMEM_BYTES = 16 * 1024 * 1024
+VMEM_BYTES = 48 * 1024 * 1024
 
 
 def shift(block, axis, distance, senders):
@@ -29,47 +29,57 @@
     return (first.astype(jnp.float32) + second.astype(jnp.float32)).astype(jnp.bfloat16)
 
 
-def line_reduce_scatter(blocks):
+def pick(blocks, index):
+    return lax.dynamic_index_in_dim(
+        blocks, jnp.clip(index, 0, blocks.shape[0] - 1), 0, keepdims=False
+    )
+
+
+def reduce_step(blocks, carried, step):
     size = lax.axis_size("db")
     me = lax.axis_index("db")
-
-    def pick(d):
-        return lax.dynamic_index_in_dim(blocks, jnp.clip(d, 0, size - 1), 0, keepdims=False)
-
-    up = down = None
+    far = size - 1 - step
+    up_block, down_block = pick(blocks, me + far), pick(blocks, me - far)
+    if carried is not None:
+        up_block = add_rounded(up_block, carried[0])
+        down_block = add_rounded(down_block, carried[1])
+    return (
+        shift(up_block, "db", 1, range(step + 1)),
+        shift(down_block, "db", -1, range(size - 1 - step, size)),
+    )
+
+
+def reduced(blocks, carried):
+    total = pick(blocks, lax.axis_index("db")).astype(jnp.float32)
+    return total + carried[0].astype(jnp.float32) + carried[1].astype(jnp.float32)
+
+
+def gather_step(carried, step):
+    size = lax.axis_size("db")
+    return (
+        shift(carried[0], "db", 1, range(step, size)),
+        shift(carried[1], "db", -1, range(0, size - step)),
+    )
+
+
+def reduce_scatter(blocks):
+    carried = None
+    for step in range(lax.axis_size("db") - 1):
+        carried = lax.optimization_barrier(reduce_step(blocks, carried, step))
+    return reduced(blocks, carried)
+
+
+def gather(block, beside):
+    size = lax.axis_size("db")
+    carried, pieces = (block, block), []
     for step in range(size - 1):
-        far = size - 1 - step
-        up_block, down_block = pick(me + far), pick(me - far)
-        if step:
-            up_block, down_block = add_rounded(up_block, up), add_rounded(down_block, down)
-        up = shift(up_block, "db", 1, range(step + 1))
-        down = shift(down_block, "db", -1, range(size - 1 - step, size))
-        up, down = lax.optimization_barrier((up, down))
-    total = pick(me).astype(jnp.float32)
-    return total + up.astype(jnp.float32) + down.astype(jnp.float32)
-
-
-def line_all_gather(block, beside):
-    size = lax.axis_size("db")
-    me = lax.axis_index("db")
-    up = down = block
-    pieces = []
-    for step in range(size - 1):
-        up = shift(up, "db", 1, range(step, size))
-        down = shift(down, "db", -1, range(0, size - step))
+        carried = gather_step(carried, step)
         if step == (size - 1) // 2:
-            up, down, beside = lax.optimization_barrier((up, down, beside))
+            carried, beside = lax.optimization_barrier((carried, beside))
         else:
-            up, down = lax.optimization_barrier((up, down))
-        pieces.append((step + 1, up, down))
-    parts = []
-    for owner in range(size):
-        chosen = block
-        for distance, from_low, from_high in pieces:
-            chosen = jnp.where(me - owner == distance, from_low, chosen)
-            chosen = jnp.where(owner - me == distance, from_high, chosen)
-        parts.append(chosen)
-    return jnp.stack(parts), beside
+            carried = lax.optimization_barrier(carried)
+        pieces.append(carried)
+    return pieces, beside
 
 
 def self_kernel(qkv_ref, out_ref, *, blocks, rows, scale):
@@ -108,6 +118,10 @@
     )(qkv)
 
 
+def span_before(wanted):
+    return shift(wanted[-1], "seq", 1, range(lax.axis_size("seq")))
+
+
 def pack_kernel(query_ref, key_ref, value_ref, out_ref):
     for which, ref in enumerate((query_ref, key_ref, value_ref)):
         for head in range(out_ref.shape[0]):
@@ -131,13 +145,13 @@
     )(query_rows, key_rows, value_rows)
 
 
-def self_attention_by_head(query_rows, key_rows, value_rows, scale):
-    rows, width = query_rows.shape
-    packed = pack_heads(query_rows, key_rows, value_rows)
-    held = lax.all_to_all(packed, "seq", 0, 0, tiled=True)
+def self_attention_by_head(query_rows, key_rows, value_rows, wanted, scale):
+    packed, wanted = lax.optimization_barrier((pack_heads(query_rows, key_rows, value_rows), wanted))
+    held, before = lax.optimization_barrier(
+        (lax.all_to_all(packed, "seq", 0, 0, tiled=True), span_before(wanted))
+    )
     mixed = self_attend_head(held, scale)
-    back = lax.all_to_all(mixed, "seq", 0, 0, tiled=True)
-    return back.transpose(1, 0, 2).reshape(rows, width)
+    return lax.all_to_all(mixed, "seq", 0, 0, tiled=True), before
 
 
 def self_attention_gathered(query_rows, key_rows, value_rows, scale):
@@ -166,7 +180,41 @@
         values.reshape(count, heads, HD),
         preferred_element_type=jnp.float32,
     )
-    return (mixed / total[..., None]).transpose(1, 0, 2).reshape(rows, width).astype(jnp.bfloat16)
+    return (mixed / total[..., None]).astype(jnp.bfloat16)
+
+
+def self_out_kernel(attended_ref, weight_ref, out_ref, rows_ref):
+    @pl.when(pl.program_id(0) == 0)
+    def _():
+        for head in range(attended_ref.shape[0]):
+            rows_ref[:, head * HD : (head + 1) * HD] = attended_ref[head]
+
+    product = jnp.dot(rows_ref[...], weight_ref[...], preferred_element_type=jnp.float32)
+    out_ref[...] = product.astype(jnp.bfloat16)
+
+
+def self_out(attended, weight):
+    heads, rows, _ = attended.shape
+    width, features = weight.shape
+    step = math.gcd(features, 512)
+    return pl.pallas_call(
+        self_out_kernel,
+        grid=(features // step,),
+        out_shape=jax.ShapeDtypeStruct((rows, features), jnp.bfloat16),
+        in_specs=[
+            pl.BlockSpec((heads, rows, HD), lambda at: (0, 0, 0)),
+            pl.BlockSpec((width, step), lambda at: (0, at)),
+        ],
+        out_specs=pl.BlockSpec((rows, step), lambda at: (0, at)),
+        scratch_shapes=[pltpu.VMEM((rows, width), jnp.bfloat16)],
+        compiler_params=pltpu.CompilerParams(vmem_limit_bytes=VMEM_BYTES),
+        cost_estimate=pl.CostEstimate(
+            flops=2 * rows * width * features,
+            bytes_accessed=2 * (rows * width + width * features + rows * features),
+            transcendentals=0,
+        ),
+        name="self_out",
+    )(attended, weight)
 
 
 def project_kernel(where_ref, first_ref, second_ref, wk_ref, wv_ref, keys_ref, values_ref):
@@ -206,7 +254,7 @@
             out_specs=[made, made],
         ),
         compiler_params=pltpu.CompilerParams(
-            vmem_limit_bytes=20 * 1024 * 1024, dimension_semantics=("arbitrary",)
+            vmem_limit_bytes=VMEM_BYTES, dimension_semantics=("arbitrary",)
         ),
         cost_estimate=pl.CostEstimate(
             flops=4 * groups * GROUP * depth * width,
@@ -231,11 +279,60 @@
     return jnp.where(first, mixed[:rows], mixed[rows:])
 
 
-def cross_kernel(live_ref, query_ref, keys_ref, values_ref, out_ref, *, spans, heads, scale):
+def cross_kernel(place_ref, own_ref, *refs, scale):
+    wq_hbm, keys_hbm, values_hbm, wo_hbm, out_ref = refs[-13:-8]
+    wq_ref, keys_ref, values_ref, wo_ref, rows_ref, query_ref, mixed_ref, sems = refs[-8:]
+    pieces = refs[:-13]
+    share, features = own_ref.shape
+    width = wq_ref.shape[1]
+    n_db = out_ref.shape[0]
+    pairs = width // HD // 2
     tail = 16
-    pairs = heads // 2
+    cut = features // 4
+    low = width // 4
+    wq_copies = [
+        pltpu.make_async_copy(
+            wq_hbm.at[pl.ds(k * cut, cut)], wq_ref.at[pl.ds(k * cut, cut)], sems.at[k]
+        )
+        for k in range(4)
+    ]
+    other_copies = [
+        pltpu.make_async_copy(keys_hbm, keys_ref, sems.at[4]),
+        pltpu.make_async_copy(values_hbm, values_ref, sems.at[5]),
+    ] + [
+        pltpu.make_async_copy(
+            wo_hbm.at[pl.ds(k * low, low)], wo_ref.at[pl.ds(k * low, low)], sems.at[6 + k]
+        )
+        for k in range(4)
+    ]
+    for copy in wq_copies + other_copies:
+        copy.start()
+    for me in range(n_db):
+
+        @pl.when(place_ref[0] == me)
+        def _(me=me):
+            for owner in range(n_db):
+                if owner == me:
+                    source = own_ref
+                elif owner < me:
+                    source = pieces[2 * (me - owner - 1)]
+                else:
+                    source = pieces[2 * (owner - me - 1) + 1]
+                rows_ref[owner * share : (owner + 1) * share, :] = source[...]
+
+    lanes = [slice(2 * pair * HD, 2 * (pair + 1) * HD) for pair in range(pairs)]
+    for k, copy in enumerate(wq_copies):
+        copy.wait()
+        inner = slice(k * cut, (k + 1) * cut)
+        for at in lanes:
+            part = jnp.dot(
+                rows_ref[:, inner], wq_ref[inner, at], preferred_element_type=jnp.float32
+            )
+            query_ref[:, at] = part if k == 0 else query_ref[:, at] + part
+    for copy in other_copies[:2]:
+        copy.wait()
     row = lax.broadcasted_iota(jnp.int32, (tail, 2 * HD), 0)
-    lanes = [slice(2 * pair * HD, 2 * (pair + 1) * HD) for pair in range(pairs)]
+    spans = n_db * share // SPAN
     for span in range(spans):
         top = span * SPAN
         here, after = (slice((span + k) * GROUP, (span + k + 1) * GROUP) for k in (0, 1))
@@ -243,51 +340,78 @@
         work += [(slice(top + SPAN - tail, top + SPAN), after, at) for at in lanes]
         scores = [
             lax.dot_general(
-                apart_heads(query_ref[of, at]),
-                keys_ref[group, at],
+                apart_heads(query_ref[of, at].astype(jnp.bfloat16)),
+                keys_ref[which, at],
                 (((1,), (1,)), ((), ())),
                 preferred_element_type=jnp.float32,
             )
             * (scale * LOG2E)
-            for of, group, at in work
+            for of, which, at in work
         ]
         tops = [jnp.max(one, axis=-1, keepdims=True) for one in scores]
         weights = [jnp.exp2(one - top_one) for one, top_one in zip(scores, tops)]
         totals = [jnp.sum(one, axis=-1, keepdims=True) for one in weights]
         mixed = [
             jnp.dot(
-                one.astype(jnp.bfloat16), values_ref[group, at], preferred_element_type=jnp.float32
+                one.astype(jnp.bfloat16), values_ref[which, at], preferred_element_type=jnp.float32
             )
-            for one, (_, group, at) in zip(weights, work)
+            for one, (_, which, at) in zip(weights, work)
         ]
         mixed = [together_heads(one / total) for one, total in zip(mixed, totals)]
         for pair, at in enumerate(lanes):
             main, last = mixed[pair], mixed[pairs + pair]
             if span == 0:
-                main = jnp.where(live_ref[0] > 0, main, 0.0)
+                main = jnp.where(place_ref[1] > 0, main, 0.0)
             last = jnp.where(row == tail - 1, last, main[SPAN - tail :])
-            out_ref[top : top + SPAN - tail, at] = main[: SPAN - tail].astype(jnp.bfloat16)
-            out_ref[top + SPAN - tail : top + SPAN, at] = last.astype(jnp.bfloat16)
-
-
-def cross_attend(live, query, keys, values, scale):
-    rows, width = query.shape
+            mixed_ref[top : top + SPAN - tail, at] = main[: SPAN - tail].astype(jnp.bfloat16)
+            mixed_ref[top + SPAN - tail : top + SPAN, at] = last.astype(jnp.bfloat16)
+    for copy in other_copies[2:]:
+        copy.wait()
+    step = math.gcd(features, 512)
+
+    def columns(at, carried):
+        here = pl.ds(pl.multiple_of(at * step, step), step)
+        product = jnp.dot(mixed_ref[...], wo_ref[:, here], preferred_element_type=jnp.float32)
+        product = product.astype(jnp.bfloat16)
+        for owner in range(n_db):
+            out_ref[owner, :, here] = product[owner * share : (owner + 1) * share]
+        return carried
+
+    lax.fori_loop(0, features // step, columns, 0)
+
+
+def cross_block(place, normed, pieces, w_cross_q, keys, values, w_cross_out, n_db, scale):
+    share, features = normed.shape
+    width = w_cross_q.shape[1]
+    rows = n_db * share
     vmem = pl.BlockSpec(memory_space=pltpu.VMEM)
+    anywhere = pl.BlockSpec(memory_space=pl.ANY)
+    flat = [one for pair in pieces for one in pair]
     return pl.pallas_call(
-        functools.partial(
-            cross_kernel, spans=rows // SPAN, heads=width // HD, scale=scale
-        ),
-        out_shape=jax.ShapeDtypeStruct((rows, width), jnp.bfloat16),
-        in_specs=[pl.BlockSpec(memory_space=pltpu.SMEM), vmem, vmem, vmem],
+        functools.partial(cross_kernel, scale=scale),
+        out_shape=jax.ShapeDtypeStruct((n_db, share, features), jnp.bfloat16),
+        in_specs=[pl.BlockSpec(memory_space=pltpu.SMEM)]
+        + [vmem] * (1 + len(flat))
+        + [anywhere] * 4,
         out_specs=vmem,
+        scratch_shapes=[
+            pltpu.VMEM((features, width), jnp.bfloat16),
+            pltpu.VMEM(keys.shape, jnp.bfloat16),
+            pltpu.VMEM(values.shape, jnp.bfloat16),
+            pltpu.VMEM((width, features), jnp.bfloat16),
+            pltpu.VMEM((rows, features), jnp.bfloat16),
+            pltpu.VMEM((rows, width), jnp.float32),
+            pltpu.VMEM((rows, width), jnp.bfloat16),
+            pltpu.SemaphoreType.DMA((10,)),
+        ],
         compiler_params=pltpu.CompilerParams(vmem_limit_bytes=VMEM_BYTES),
         cost_estimate=pl.CostEstimate(
-            flops=8 * rows * GROUP * width,
-            bytes_accessed=2 * (2 * rows + 2 * keys.shape[0]) * width,
-            transcendentals=2 * rows * GROUP * width // HD,
-        ),
-        name="cross_attend",
-    )(live, query, keys, values)
+            flops=4 * rows * width * (features + GROUP),
+            bytes_accessed=4 * width * (features + keys.shape[0]) + 4 * rows * features,
+            transcendentals=rows * GROUP * width // HD,
+        ),
+        name="cross_block",
+    )(place, normed, *flat, w_cross_q, keys, values, w_cross_out)
 
 
 def per_device(
@@ -306,8 +430,7 @@
     nb_row,
 ):
     rows, features = hidden_in.shape
-    width = query_rows.shape[1]
-    heads = width // HD
+    heads = query_rows.shape[1] // HD
     n_seq, n_db = lax.axis_size("seq"), lax.axis_size("db")
     seq_index, db_index = lax.axis_index("seq"), lax.axis_index("db")
     scale = 1.0 / math.sqrt(HD)
@@ -323,41 +446,33 @@
     )
     along_db = lax.all_gather(part, "db", axis=0)
     wanted = jnp.stack((nb_row, nb_shard), axis=-1).astype(jnp.int32)
-    before = shift(wanted[-1], "seq", 1, range(n_seq))
-    where = jnp.concatenate((before[None], wanted), axis=0).reshape(-1)
+    place = jnp.stack((db_index, (seq_index > 0).astype(jnp.int32))).astype(jnp.int32)
 
     if heads == n_seq:
-        attended = self_attention_by_head(query_rows, key_rows, value_rows, scale)
+        attended, before = self_attention_by_head(query_rows, key_rows, value_rows, wanted, scale)
     else:
         attended = self_attention_gathered(query_rows, key_rows, value_rows, scale)
+        before = span_before(wanted)
+    where = jnp.concatenate((before[None], wanted), axis=0).reshape(-1)
 
     along_db, attended = lax.optimization_barrier((along_db, attended))
     table = lax.all_gather(along_db, "seq", axis=0).reshape(
         rows_shard, NLEN // piece, n_db, piece, depth
     )
 
-    partial = jnp.dot(attended, w_self_out, preferred_element_type=jnp.float32).astype(jnp.bfloat16)
-    attn_share = line_reduce_scatter(partial.reshape(n_db, share, features))
-    residual = (
-        lax.dynamic_slice_in_dim(hidden_in, db_index * share, share, 0).astype(jnp.float32)
-        + attn_share
-    )
+    partial = self_out(attended, w_self_out).reshape(n_db, share, features)
+    own = lax.dynamic_slice_in_dim(hidden_in, db_index * share, share, 0)
+    residual = own.astype(jnp.float32) + reduce_scatter(partial)
     mean_square = jnp.mean(residual * residual, axis=-1, keepdims=True)
-    normed_share = (
+    normed = (
         residual * lax.rsqrt(mean_square + 1e-05) * norm_gain.astype(jnp.float32)
     ).astype(jnp.bfloat16)
     projected = project_encodings(where, table, w_cross_k, w_cross_v)
-    normed, (keys, values) = line_all_gather(normed_share, projected)
-    normed = normed.reshape(rows, features)
-    cross_query = jnp.dot(normed, w_cross_q, preferred_element_type=jnp.float32).astype(
-        jnp.bfloat16
-    )
-    live = (seq_index > 0).astype(jnp.int32).reshape(1)
-    mixed = cross_attend(live, cross_query, keys, values, scale)
-    out_partial = jnp.dot(mixed, w_cross_out, preferred_element_type=jnp.float32).astype(
-        jnp.bfloat16
-    )
-    return residual + line_reduce_scatter(out_partial.reshape(n_db, share, features))
+    pieces, (keys, values) = gather(normed, projected)
+    out_partial = cross_block(
+        place, normed, pieces, w_cross_q, keys, values, w_cross_out, n_db, scale
+    )
+    return residual + reduce_scatter(out_partial)
 
 
 def solution(mesh):

time: 232 us -> 226 us (0.974)
  Pallas kernels: 17.8 us -> 37.8 us
  matrix products: 14.1 us -> 0 us
  blocking collectives: 12.2 us -> 0 us
  other arithmetic: 16.4 us -> 8.52 us
  waiting for transfers between devices: 92.3 us -> 99.7 us
  starting transfers between devices: 51.7 us -> 56.1 us
  local copies, waits for them, and re-layouts: 12 us -> 7.74 us
    pallas_call x1 -> x2, Pallas kernels: 2.46 us -> 19.7 us  [the longest x1 12 us: cross_block(): pl.pallas_call(functools.partial(cross_kernel, scale=scale), out_shape=ja...]
    dot_general x3 -> x0, matrix products: 14.1 us -> none  [the longest x1 5.94 us: per_device(): jnp.dot(normed, w_cross_q, preferred_element_type=jnp.float32)]
    all_to_all x1 -> x0, blocking collectives: 12.2 us -> none  [self_attention_by_head(): back = lax.all_to_all(mixed, 'seq', 0, 0, tiled=True)]
    another operation x3 -> x1, other arithmetic: 5.2 us -> 0.08 us  [per_device(): jnp.stack((db_index, (seq_index > 0).astype(jnp.int32))).astype(jnp.int32)]
    all_to_all x1 -> x2, waiting for transfers between devices: 20.2 us -> 24.5 us  [the longest x1 16.9 us: self_attention_by_head(): lax.all_to_all(packed, 'seq', 0, 0, tiled=True)]
    unnamed x24 -> x18, local copies, waits for them, and re-layouts: 9.68 us -> 5.57 us
    all_to_all x1 -> x2, starting transfers between devices: 5.17 us -> 8.66 us  [the longest x1 5.17 us: self_attention_by_head(): lax.all_to_all(packed, 'seq', 0, 0, tiled=True)]
  transfers between devices with their start and end apart: 22 -> 23, of which waited for: 14 -> 16; matrix products, arithmetic and copies ran while one was open for 7% -> 3% of each run, Pallas kernels for 5% -> 10%
where the time goes in v5:
time: 226 us; the launch traced here: 224 us
  waiting for transfers between devices  99.7 us (44%)
  starting transfers between devices  56.1 us (25%)
  Pallas kernels  37.8 us (17%)
  between operations  13.7 us (6%)
  other arithmetic  8.52 us (4%)
  local copies, waits for them, and re-layouts  7.74 us (3%)
    ppermute x19, waiting for transfers between devices, shift(): return lax.ppermute(block, axis, route)  72.5 us
    ppermute x19, starting transfers between devices, shift(): return lax.ppermute(block, axis, route)  47.4 us
    all_to_all x1, waiting for transfers between devices, self_attention_by_head(): lax.all_to_all(packed, 'seq', 0, 0, tiled=True)  16.9 us
    pallas_call x1, Pallas kernels, cross_block(): pl.pallas_call(functools.partial(cross_kernel, scale=scale), out_shape=ja...  12 us
    pallas_call x1, Pallas kernels, project_encodings(): pl.pallas_call(project_kernel, out_shape=[jax.ShapeDtypeStruct((groups *...  8.87 us
    pallas_call x1, Pallas kernels, self_out(): pl.pallas_call(self_out_kernel, grid=(features // step,), out_shape=jax.S...  7.67 us
    all_to_all x1, waiting for transfers between devices, self_attention_by_head(): return (lax.all_to_all(mixed, 'seq', 0, 0, tiled=True), before)  7.59 us
    unnamed x18, local copies, waits for them, and re-layouts  5.57 us
  transfers between devices with their start and end apart: 23, of which 16 were waited for; matrix products, arithmetic and copies ran while one was open for 3% of the time, Pallas kernels for 10%

profile of v5, /device:TPU:0, one launch (start us, length us, event | category | flops | bytes accessed | tf_op | source)
XLA Modules:
  0.0 223.6 jit_solution(14097717319100778052)
XLA Ops:
  6.5 1.6 copy-done
  8.1 0.7 constant_dynamic-slice_fusion
  8.8 0.7 pad_add_fusion
  9.5 3.7 %pack_heads.1 = bf16[8,3,256,128]{3,2,1,0:T(8,128)(2,1)} custom-call(bf16[256,1024]{1,0:T(8,128)(2,1)} %query_ref, bf16[256,1024]{1,0:T(8,128)(2,1)} %key_ref, bf16[256,1024]{1,0:T(8,128)(2,1)} %value_ref), custom_call_target="tpu_custom_call" | custom-call | bytes 3145728 | tf_op jit(solution)/shard_map/pack_heads/pallas_call | solution.py:135
  13.3 5.2 %all-to-all-start = ((bf16[8,3,256,128]{3,2,1,0:T(8,128)(2,1)}), bf16[8,3,256,128]{3,2,1,0:T(8,128)(2,1)S(1)}, u32[]{:S(2)}, u32[]{:S(2)}) async-start(bf16[8,3,256,128]{3,2,1,0:T(8,128)(2,1)} %pack_heads.1), calls=%async_computation | async-start | bytes 3145728 | tf_op jit(solution)/shard_map/all_to_all | solution.py:151
  18.5 0.7 all-gather.5.cloned.1.call-update
  19.2 0.1 copy.20
  19.3 2.4 %collective-permute-start = (s32[2,2]{1,0:T(2,128)S(1)}, s32[2,2]{1,0:T(2,128)S(1)}, u32[]{:S(2)}, u32[]{:S(2)}) collective-permute-start(s32[2,2]{1,0:T(2,128)S(1)} %bitcast.62), channel_id=1, source_target_pairs={{0,4},{4,8},{8,12},{12,16},{16,20},{20,24},{24,28},{1,5},{5,9},{9,... | collective-permute-start | bytes 56 | tf_op jit(solution)/shard_map/ppermute | solution.py:25
  21.7 0.8 collective-permute-done
  22.5 16.9 %all-to-all-done.qkv_ref = bf16[8,3,256,128]{3,2,1,0:T(8,128)(2,1)S(1)} async-done(((bf16[8,3,256,128]{3,2,1,0:T(8,128)(2,1)}), bf16[8,3,256,128]{3,2,1,0:T(8,128)(2,1)S(1)}, u32[]{:S(2)}, u32[]{:S(2)}) %all-to-all-start) | async-done | bytes 1572896 | tf_op jit(solution)/shard_map/all_to_all | solution.py:151
  39.5 5.5 %self_attend.1 = bf16[8,256,128]{2,1,0:T(8,128)(2,1)} custom-call(bf16[8,3,256,128]{3,2,1,0:T(8,128)(2,1)S(1)} %all-to-all-done.qkv_ref), custom_call_target="tpu_custom_call" | custom-call | flops 1073741824 | bytes 2097152 | tf_op jit(solution)/shard_map/self_attend/pallas_call | solution.py:106
  44.9 3.5 %all-to-all-start.1 = ((bf16[8,256,128]{2,1,0:T(8,128)(2,1)}), bf16[8,256,128]{2,1,0:T(8,128)(2,1)S(1)}, u32[]{:S(2)}, u32[]{:S(2)}) async-start(bf16[8,256,128]{2,1,0:T(8,128)(2,1)} %self_attend.1), calls=%async_computation.1 | async-start | bytes 1048576 | tf_op jit(solution)/shard_map/all_to_all | solution.py:154
  48.5 2.0 all-gather.5.cloned.1.call-done
  50.5 7.6 %all-to-all-done.1.attended_ref = bf16[8,256,128]{2,1,0:T(8,128)(2,1)S(1)} async-done(((bf16[8,256,128]{2,1,0:T(8,128)(2,1)}), bf16[8,256,128]{2,1,0:T(8,128)(2,1)S(1)}, u32[]{:S(2)}, u32[]{:S(2)}) %all-to-all-start.1) | async-done | bytes 524320 | tf_op jit(solution)/shard_map/all_to_all | solution.py:154
  58.1 7.7 %self_out.1 = bf16[256,4096]{1,0:T(8,128)(2,1)S(1)} custom-call(bf16[8,256,128]{2,1,0:T(8,128)(2,1)S(1)} %all-to-all-done.1.attended_ref, bf16[1024,4096]{1,0:T(8,128)(2,1)} %weight_ref.1), custom_call_target="tpu_custom_call" | custom-call | flops 2147483648 | bytes 11010048 | tf_op jit(solution)/shard_map/self_out/pallas_call | solution.py:200
  65.8 0.9 dynamic-slice_bitcast_fusion.2
  66.7 0.7 collective-permute-start.2
  67.4 4.3 %collective-permute-start.1 = (bf16[64,4096]{1,0:T(8,128)(2,1)S(1)}, bf16[64,4096]{1,0:T(8,128)(2,1)}, u32[]{:S(2)}, u32[]{:S(2)}) collective-permute-start(bf16[64,4096]{1,0:T(8,128)(2,1)S(1)} %get-tuple-element.82), channel_id=1, source_target_pairs={{0,1},{4,5},{8,9},{12,13},{16,17},{20,21},{24,25},{28,29}} | collective-permute-start | bytes 1572872 | tf_op jit(solution)/shard_map/ppermute | solution.py:25
  71.7 7.9 %collective-permute-done.1 = bf16[64,4096]{1,0:T(8,128)(2,1)} collective-permute-done((bf16[64,4096]{1,0:T(8,128)(2,1)S(1)}, bf16[64,4096]{1,0:T(8,128)(2,1)}, u32[]{:S(2)}, u32[]{:S(2)}) %collective-permute-start.1) | collective-permute-done | bytes 524320 | tf_op jit(solution)/shard_map/ppermute | solution.py:25
  79.6 2.1 fusion.7
  81.7 0.8 collective-permute-start.4
  82.5 5.9 %collective-permute-start.3 = (bf16[64,4096]{1,0:T(8,128)(2,1)S(1)}, bf16[64,4096]{1,0:T(8,128)(2,1)}, u32[]{:S(2)}, u32[]{:S(2)}) collective-permute-start(bf16[64,4096]{1,0:T(8,128)(2,1)S(1)} %get-tuple-element.80), channel_id=1, source_target_pairs={{0,1},{1,2},{4,5},{5,6},{8,9},{9,10},{12,13},{13,14},{16,17},{17,1... | collective-permute-start | bytes 1572872 | tf_op jit(solution)/shard_map/ppermute | solution.py:25
  88.4 7.0 %collective-permute-done.3 = bf16[64,4096]{1,0:T(8,128)(2,1)} collective-permute-done((bf16[64,4096]{1,0:T(8,128)(2,1)S(1)}, bf16[64,4096]{1,0:T(8,128)(2,1)}, u32[]{:S(2)}, u32[]{:S(2)}) %collective-permute-start.3) | collective-permute-done | bytes 524320 | tf_op jit(solution)/shard_map/ppermute | solution.py:25
  95.4 2.3 %fusion.6 = (bf16[64,4096]{1,0:T(8,128)(2,1)}, bf16[64,4096]{1,0:T(8,128)(2,1)}) fusion(bf16[64,4096]{1,0:T(8,128)(2,1)S(1)} %collective-permute-done.4, bf16[4,64,4096]{2,1,0:T(8,128)(2,1)S(1)} %bitcast.52, s32[]{:T(128)S(6)} %min.35, bf16[64,4096]{1,0:T(8,128)(2,1)} %collective-permute-done.3, s32[]{:T(128)S(6)} %min.30), kind=kLoop, calls=%fused_computation.12 | loop fusion | flops 2097152 | bytes 3145736 | tf_op jit(solution)/shard_map/convert_element_type | solution.py:29
  97.6 1.3 collective-permute-start.6
  98.9 5.2 %collective-permute-start.5 = (bf16[64,4096]{1,0:T(8,128)(2,1)}, bf16[64,4096]{1,0:T(8,128)(2,1)S(1)}, u32[]{:S(2)}, u32[]{:S(2)}) collective-permute-start(bf16[64,4096]{1,0:T(8,128)(2,1)} %get-tuple-element.78), channel_id=1, source_target_pairs={{0,1},{1,2},{2,3},{4,5},{5,6},{6,7},{8,9},{9,10},{10,11},{12,13},{... | collective-permute-start | bytes 1572872 | tf_op jit(solution)/shard_map/ppermute | solution.py:25
  104.1 5.8 %collective-permute-done.6 = bf16[64,4096]{1,0:T(8,128)(2,1)S(1)} collective-permute-done((bf16[64,4096]{1,0:T(8,128)(2,1)}, bf16[64,4096]{1,0:T(8,128)(2,1)S(1)}, u32[]{:S(2)}, u32[]{:S(2)}) %collective-permute-start.6) | collective-permute-done | bytes 524320 | tf_op jit(solution)/shard_map/ppermute | solution.py:25
  109.9 1.3 collective-permute-done.5
  111.2 1.4 multiply_reduce_fusion
  112.7 0.2 multiply_convert_fusion.own_ref
  112.9 0.8 copy-done.4
  113.6 1.3 collective-permute-start.8
  114.9 4.9 %collective-permute-start.7 = (bf16[64,4096]{1,0:T(8,128)(2,1)S(1)}, bf16[64,4096]{1,0:T(8,128)(2,1)S(1)}, u32[]{:S(2)}, u32[]{:S(2)}) collective-permute-start(bf16[64,4096]{1,0:T(8,128)(2,1)S(1)} %multiply_convert_fusion.own_ref), channel_id=1, source_target_pairs={{0,1},{1,2},{2,3},{4,5},{5,6},{6,7},{8,9},{9,10},{10,11},{12,13},{... | collective-permute-start | bytes 1572872 | tf_op jit(solution)/shard_map/ppermute | solution.py:25
  119.9 0.1 copy.21
  120.0 5.1 %collective-permute-done.8.refs_1_ = bf16[64,4096]{1,0:T(8,128)(2,1)S(1)} collective-permute-done((bf16[64,4096]{1,0:T(8,128)(2,1)S(1)}, bf16[64,4096]{1,0:T(8,128)(2,1)S(1)}, u32[]{:S(2)}, u32[]{:S(2)}) %collective-permute-start.8) | collective-permute-done | bytes 524320 | tf_op jit(solution)/shard_map/ppermute | solution.py:25
  125.1 1.5 collective-permute-done.7.refs_0_
  126.5 0.7 collective-permute-start.9
  127.2 1.3 collective-permute-start.10
  128.5 0.1 add_add_fusion
  128.6 0.1 copy.22
  128.7 0.1 reshape.43.where_ref
  128.8 1.6 copy-done.2
  130.4 1.6 copy-done.3
  132.0 8.9 %project_encodings.1 = (bf16[1280,1024]{1,0:T(8,128)(2,1)}, bf16[1280,1024]{1,0:T(8,128)(2,1)}) custom-call(s32[20]{0:T(128)S(1)} %reshape.43.where_ref, bf16[8,1,4,128,1024]{4,3,2,1,0:T(8,128)(2,1)} %bitcast.54, bf16[8,1,4,128,1024]{4,3,2,1,0:T(8,128)(2,1)} %bitcast.55, bf16[1024,1024]{1,0:T(8,128)(2,1)S(1)} %copy-done.2, bf16[1024,1024]{1,0:T(8,128)(2,1)S(1)} %copy-done.3), custom_call_target="tpu_custom_call" | custom-call | flops 5368709120 | bytes 12058624 | tf_op jit(solution)/shard_map/project_encodings/pallas_call | solution.py:247
  140.9 3.7 %collective-permute-done.10.refs_3_ = bf16[64,4096]{1,0:T(8,128)(2,1)S(1)} collective-permute-done((bf16[64,4096]{1,0:T(8,128)(2,1)S(1)}, bf16[64,4096]{1,0:T(8,128)(2,1)S(1)}, u32[]{:S(2)}, u32[]{:S(2)}) %collective-permute-start.10) | collective-permute-done | bytes 524320 | tf_op jit(solution)/shard_map/ppermute | solution.py:25
  144.6 0.7 collective-permute-start.11
  145.3 1.3 collective-permute-start.12
  146.6 0.1 pad_add_fusion.1.place_ref
  146.7 12.0 %collective-permute-done.12.refs_5_ = bf16[64,4096]{1,0:T(8,128)(2,1)} collective-permute-done((bf16[64,4096]{1,0:T(8,128)(2,1)S(1)}, bf16[64,4096]{1,0:T(8,128)(2,1)}, u32[]{:S(2)}, u32[]{:S(2)}) %collective-permute-start.12) | collective-permute-done | bytes 524320 | tf_op jit(solution)/shard_map/ppermute | solution.py:25
  158.6 12.0 %cross_block.1 = bf16[4,64,4096]{2,1,0:T(8,128)(2,1)S(1)} custom-call(s32[2]{0:T(128)S(1)} %pad_add_fusion.1.place_ref, bf16[64,4096]{1,0:T(8,128)(2,1)S(1)} %multiply_convert_fusion.own_ref, bf16[64,4096]{1,0:T(8,128)(2,1)S(1)} %collective-permute-done.7.refs_0_, bf16[64,4096]{1,0:T(8,128)(2,1)S(1)} %collective-permute-done.8.refs_1_, ...), custom_call_target="tpu_custom_call" | custom-call | flops 4563402752 | bytes 26214400 | tf_op jit(solution)/shard_map/cross_block/pallas_call | solution.py:390
  170.7 0.1 dynamic-slice_bitcast_fusion
  170.8 0.7 collective-permute-start.14
  171.5 1.4 collective-permute-start.13
  172.9 10.2 %collective-permute-done.13 = bf16[64,4096]{1,0:T(8,128)(2,1)S(1)} collective-permute-done((bf16[64,4096]{1,0:T(8,128)(2,1)S(1)}, bf16[64,4096]{1,0:T(8,128)(2,1)S(1)}, u32[]{:S(2)}, u32[]{:S(2)}) %collective-permute-start.13) | collective-permute-done | bytes 524320 | tf_op jit(solution)/shard_map/ppermute | solution.py:25
  183.1 0.2 fusion.1
  183.3 0.8 collective-permute-start.16
  184.2 5.0 %collective-permute-start.15 = (bf16[64,4096]{1,0:T(8,128)(2,1)S(1)}, bf16[64,4096]{1,0:T(8,128)(2,1)S(1)}, u32[]{:S(2)}, u32[]{:S(2)}) collective-permute-start(bf16[64,4096]{1,0:T(8,128)(2,1)S(1)} %get-tuple-element.74), channel_id=1, source_target_pairs={{0,1},{1,2},{4,5},{5,6},{8,9},{9,10},{12,13},{13,14},{16,17},{17,1... | collective-permute-start | bytes 1572872 | tf_op jit(solution)/shard_map/ppermute | solution.py:25
  189.2 10.6 %collective-permute-done.15 = bf16[64,4096]{1,0:T(8,128)(2,1)S(1)} collective-permute-done((bf16[64,4096]{1,0:T(8,128)(2,1)S(1)}, bf16[64,4096]{1,0:T(8,128)(2,1)S(1)}, u32[]{:S(2)}, u32[]{:S(2)}) %collective-permute-start.15) | collective-permute-done | bytes 524320 | tf_op jit(solution)/shard_map/ppermute | solution.py:25
  199.8 0.3 fusion
  200.1 1.4 collective-permute-start.18
  201.5 7.4 %collective-permute-start.17 = (bf16[64,4096]{1,0:T(8,128)(2,1)S(1)}, bf16[64,4096]{1,0:T(8,128)(2,1)S(1)}, u32[]{:S(2)}, u32[]{:S(2)}) collective-permute-start(bf16[64,4096]{1,0:T(8,128)(2,1)S(1)} %get-tuple-element.72), channel_id=1, source_target_pairs={{0,1},{1,2},{2,3},{4,5},{5,6},{6,7},{8,9},{9,10},{10,11},{12,13},{... | collective-permute-start | bytes 1572872 | tf_op jit(solution)/shard_map/ppermute | solution.py:25
  208.9 5.2 %collective-permute-done.18 = bf16[64,4096]{1,0:T(8,128)(2,1)S(1)} collective-permute-done((bf16[64,4096]{1,0:T(8,128)(2,1)S(1)}, bf16[64,4096]{1,0:T(8,128)(2,1)S(1)}, u32[]{:S(2)}, u32[]{:S(2)}) %collective-permute-start.18) | collective-permute-done | bytes 524320 | tf_op jit(solution)/shard_map/ppermute | solution.py:25
  214.1 1.5 collective-permute-done.17
  215.6 1.2 fusion.5
  (27 shorter events, 0.2 us)
Async XLA Ops:
  6.5 1.6 copy-start
  13.3 26.2 %all-to-all-start = ((bf16[8,3,256,128]{3,2,1,0:T(8,128)(2,1)}), bf16[8,3,256,128]{3,2,1,0:T(8,128)(2,1)S(1)}, u32[]{:S(2)}, u32[]{:S(2)}) async-start(bf16[8,3,256,128]{3,2,1,0:T(8,128)(2,1)} %pack_heads.1), calls=%async_computation | async-start | bytes 3145728 | tf_op jit(solution)/shard_map/all_to_all | solution.py:151
  18.4 32.1 %all-gather.5.cloned.1.call-start = ((), (), s32[]{:S(2)}) async-start(), calls=%async_computation.2 | async-start | bytes 1310720 | tf_op jit(solution)/shard_map/all_gather | solution.py:447
  19.3 3.2 %collective-permute-start = (s32[2,2]{1,0:T(2,128)S(1)}, s32[2,2]{1,0:T(2,128)S(1)}, u32[]{:S(2)}, u32[]{:S(2)}) collective-permute-start(s32[2,2]{1,0:T(2,128)S(1)} %bitcast.62), channel_id=1, source_target_pairs={{0,4},{4,8},{8,12},{12,16},{16,20},{20,24},{24,28},{1,5},{5,9},{9,... | collective-permute-start | bytes 56 | tf_op jit(solution)/shard_map/ppermute | solution.py:25
  44.9 13.2 %all-to-all-start.1 = ((bf16[8,256,128]{2,1,0:T(8,128)(2,1)}), bf16[8,256,128]{2,1,0:T(8,128)(2,1)S(1)}, u32[]{:S(2)}, u32[]{:S(2)}) async-start(bf16[8,256,128]{2,1,0:T(8,128)(2,1)} %self_attend.1), calls=%async_computation.1 | async-start | bytes 1048576 | tf_op jit(solution)/shard_map/all_to_all | solution.py:154
  48.4 80.4 %all-gather.7.cloned.1.call-start = ((), (), s32[]{:S(2)}) async-start(), calls=%async_computation.3 | async-start | bytes 9437184 | tf_op jit(solution)/shard_map/all_gather | solution.py:459
  66.7 5.0 %collective-permute-start.2 = (bf16[64,4096]{1,0:T(8,128)(2,1)}, bf16[64,4096]{1,0:T(8,128)(2,1)S(1)}, u32[]{:S(2)}, u32[]{:S(2)}) collective-permute-start(bf16[64,4096]{1,0:T(8,128)(2,1)} %get-tuple-element.81), channel_id=1, source_target_pairs={{3,2},{7,6},{11,10},{15,14},{19,18},{23,22},{27,26},{31,30}} | collective-permute-start | bytes 1572872 | tf_op jit(solution)/shard_map/ppermute | solution.py:25
  67.4 12.2 %collective-permute-start.1 = (bf16[64,4096]{1,0:T(8,128)(2,1)S(1)}, bf16[64,4096]{1,0:T(8,128)(2,1)}, u32[]{:S(2)}, u32[]{:S(2)}) collective-permute-start(bf16[64,4096]{1,0:T(8,128)(2,1)S(1)} %get-tuple-element.82), channel_id=1, source_target_pairs={{0,1},{4,5},{8,9},{12,13},{16,17},{20,21},{24,25},{28,29}} | collective-permute-start | bytes 1572872 | tf_op jit(solution)/shard_map/ppermute | solution.py:25
  81.7 22.4 %copy-start.6 = (bf16[4096]{0:T(1024)(128)(2,1)S(1)}, bf16[4096]{0:T(1024)(128)(2,1)}, u32[]{:S(2)}) copy-start(bf16[4096]{0:T(1024)(128)(2,1)} %param.18) | copy-start | bytes 24580
  81.7 6.7 %collective-permute-start.4 = (bf16[64,4096]{1,0:T(8,128)(2,1)}, bf16[64,4096]{1,0:T(8,128)(2,1)S(1)}, u32[]{:S(2)}, u32[]{:S(2)}) collective-permute-start(bf16[64,4096]{1,0:T(8,128)(2,1)} %get-tuple-element.79), channel_id=1, source_target_pairs={{2,1},{3,2},{6,5},{7,6},{10,9},{11,10},{14,13},{15,14},{18,17},{19... | collective-permute-start | bytes 1572872 | tf_op jit(solution)/shard_map/ppermute | solution.py:25
  82.5 12.9 %collective-permute-start.3 = (bf16[64,4096]{1,0:T(8,128)(2,1)S(1)}, bf16[64,4096]{1,0:T(8,128)(2,1)}, u32[]{:S(2)}, u32[]{:S(2)}) collective-permute-start(bf16[64,4096]{1,0:T(8,128)(2,1)S(1)} %get-tuple-element.80), channel_id=1, source_target_pairs={{0,1},{1,2},{4,5},{5,6},{8,9},{9,10},{12,13},{13,14},{16,17},{17,1... | collective-permute-start | bytes 1572872 | tf_op jit(solution)/shard_map/ppermute | solution.py:25
  97.6 12.3 %collective-permute-start.6 = (bf16[64,4096]{1,0:T(8,128)(2,1)}, bf16[64,4096]{1,0:T(8,128)(2,1)S(1)}, u32[]{:S(2)}, u32[]{:S(2)}) collective-permute-start(bf16[64,4096]{1,0:T(8,128)(2,1)} %get-tuple-element.77), channel_id=1, source_target_pairs={{1,0},{2,1},{3,2},{5,4},{6,5},{7,6},{9,8},{10,9},{11,10},{13,12},{... | collective-permute-start | bytes 1572872 | tf_op jit(solution)/shard_map/ppermute | solution.py:25
  98.9 12.3 %collective-permute-start.5 = (bf16[64,4096]{1,0:T(8,128)(2,1)}, bf16[64,4096]{1,0:T(8,128)(2,1)S(1)}, u32[]{:S(2)}, u32[]{:S(2)}) collective-permute-start(bf16[64,4096]{1,0:T(8,128)(2,1)} %get-tuple-element.78), channel_id=1, source_target_pairs={{0,1},{1,2},{2,3},{4,5},{5,6},{6,7},{8,9},{9,10},{10,11},{12,13},{... | collective-permute-start | bytes 1572872 | tf_op jit(solution)/shard_map/ppermute | solution.py:25
  104.1 24.4 %copy-start.7 = (s32[4,2]{0,1:T(2,128)S(1)}, s32[4,2]{0,1:T(2,128)}, u32[]{:S(2)}) copy-start(s32[4,2]{0,1:T(2,128)} %param.24) | copy-start | bytes 100
  104.1 24.4 %copy-start.8 = (s32[4,2]{0,1:T(2,128)S(1)}, s32[4,2]{0,1:T(2,128)}, u32[]{:S(2)}) copy-start(s32[4,2]{0,1:T(2,128)} %param.25) | copy-start | bytes 100
  112.7 1.0 copy-start.4
  113.6 11.4 %collective-permute-start.8 = (bf16[64,4096]{1,0:T(8,128)(2,1)S(1)}, bf16[64,4096]{1,0:T(8,128)(2,1)S(1)}, u32[]{:S(2)}, u32[]{:S(2)}) collective-permute-start(bf16[64,4096]{1,0:T(8,128)(2,1)S(1)} %multiply_convert_fusion.own_ref), channel_id=1, source_target_pairs={{1,0},{2,1},{3,2},{5,4},{6,5},{7,6},{9,8},{10,9},{11,10},{13,12},{... | collective-permute-start | bytes 1572872 | tf_op jit(solution)/shard_map/ppermute | solution.py:25
  114.9 11.6 %collective-permute-start.7 = (bf16[64,4096]{1,0:T(8,128)(2,1)S(1)}, bf16[64,4096]{1,0:T(8,128)(2,1)S(1)}, u32[]{:S(2)}, u32[]{:S(2)}) collective-permute-start(bf16[64,4096]{1,0:T(8,128)(2,1)S(1)} %multiply_convert_fusion.own_ref), channel_id=1, source_target_pairs={{0,1},{1,2},{2,3},{4,5},{5,6},{6,7},{8,9},{9,10},{10,11},{12,13},{... | collective-permute-start | bytes 1572872 | tf_op jit(solution)/shard_map/ppermute | solution.py:25
  126.5 14.4 %collective-permute-start.9 = (bf16[64,4096]{1,0:T(8,128)(2,1)S(1)}, bf16[64,4096]{1,0:T(8,128)(2,1)S(1)}, u32[]{:S(2)}, u32[]{:S(2)}) collective-permute-start(bf16[64,4096]{1,0:T(8,128)(2,1)S(1)} %collective-permute-done.7.refs_0_), channel_id=1, source_target_pairs={{1,2},{2,3},{5,6},{6,7},{9,10},{10,11},{13,14},{14,15},{17,18},{18... | collective-permute-start | bytes 1572872 | tf_op jit(solution)/shard_map/ppermute | solution.py:25
  127.2 17.4 %collective-permute-start.10 = (bf16[64,4096]{1,0:T(8,128)(2,1)S(1)}, bf16[64,4096]{1,0:T(8,128)(2,1)S(1)}, u32[]{:S(2)}, u32[]{:S(2)}) collective-permute-start(bf16[64,4096]{1,0:T(8,128)(2,1)S(1)} %collective-permute-done.8.refs_1_), channel_id=1, source_target_pairs={{1,0},{2,1},{5,4},{6,5},{9,8},{10,9},{13,12},{14,13},{17,16},{18,1... | collective-permute-start | bytes 1572872 | tf_op jit(solution)/shard_map/ppermute | solution.py:25
  128.8 1.6 copy-start.2
  130.4 1.6 copy-start.3
  144.6 2.1 collective-permute-start.11
  145.3 13.3 %collective-permute-start.12 = (bf16[64,4096]{1,0:T(8,128)(2,1)S(1)}, bf16[64,4096]{1,0:T(8,128)(2,1)}, u32[]{:S(2)}, u32[]{:S(2)}) collective-permute-start(bf16[64,4096]{1,0:T(8,128)(2,1)S(1)} %collective-permute-done.10.refs_3_), channel_id=1, source_target_pairs={{1,0},{5,4},{9,8},{13,12},{17,16},{21,20},{25,24},{29,28}} | collective-permute-start | bytes 1572872 | tf_op jit(solution)/shard_map/ppermute | solution.py:25
  170.8 2.1 collective-permute-start.14
  171.5 11.6 %collective-permute-start.13 = (bf16[64,4096]{1,0:T(8,128)(2,1)S(1)}, bf16[64,4096]{1,0:T(8,128)(2,1)S(1)}, u32[]{:S(2)}, u32[]{:S(2)}) collective-permute-start(bf16[64,4096]{1,0:T(8,128)(2,1)S(1)} %get-tuple-element.76), channel_id=1, source_target_pairs={{0,1},{4,5},{8,9},{12,13},{16,17},{20,21},{24,25},{28,29}} | collective-permute-start | bytes 1572872 | tf_op jit(solution)/shard_map/ppermute | solution.py:25
  183.3 32.3 %copy-start.5 = (f32[64,4096]{1,0:T(8,128)S(1)}, f32[64,4096]{1,0:T(8,128)}, u32[]{:S(2)}) copy-start(f32[64,4096]{1,0:T(8,128)} %copy-done.4) | copy-start | bytes 3145732
  183.3 5.9 %collective-permute-start.16 = (bf16[64,4096]{1,0:T(8,128)(2,1)S(1)}, bf16[64,4096]{1,0:T(8,128)(2,1)S(1)}, u32[]{:S(2)}, u32[]{:S(2)}) collective-permute-start(bf16[64,4096]{1,0:T(8,128)(2,1)S(1)} %get-tuple-element.73), channel_id=1, source_target_pairs={{2,1},{3,2},{6,5},{7,6},{10,9},{11,10},{14,13},{15,14},{18,17},{19... | collective-permute-start | bytes 1572872 | tf_op jit(solution)/shard_map/ppermute | solution.py:25
  184.2 15.7 %collective-permute-start.15 = (bf16[64,4096]{1,0:T(8,128)(2,1)S(1)}, bf16[64,4096]{1,0:T(8,128)(2,1)S(1)}, u32[]{:S(2)}, u32[]{:S(2)}) collective-permute-start(bf16[64,4096]{1,0:T(8,128)(2,1)S(1)} %get-tuple-element.74), channel_id=1, source_target_pairs={{0,1},{1,2},{4,5},{5,6},{8,9},{9,10},{12,13},{13,14},{16,17},{17,1... | collective-permute-start | bytes 1572872 | tf_op jit(solution)/shard_map/ppermute | solution.py:25
  199.8 17.0 %copy-start.1 = (bf16[8,128,1024]{2,1,0:T(8,128)(2,1)S(1)}, bf16[8,128,1024]{2,1,0:T(8,128)(2,1)}, u32[]{:S(2)}) copy-start(bf16[8,128,1024]{2,1,0:T(8,128)(2,1)} %param.23) | copy-start | bytes 6291460
  200.1 14.0 %collective-permute-start.18 = (bf16[64,4096]{1,0:T(8,128)(2,1)S(1)}, bf16[64,4096]{1,0:T(8,128)(2,1)S(1)}, u32[]{:S(2)}, u32[]{:S(2)}) collective-permute-start(bf16[64,4096]{1,0:T(8,128)(2,1)S(1)} %get-tuple-element.71), channel_id=1, source_target_pairs={{1,0},{2,1},{3,2},{5,4},{6,5},{7,6},{9,8},{10,9},{11,10},{13,12},{... | collective-permute-start | bytes 1572872 | tf_op jit(solution)/shard_map/ppermute | solution.py:25
  201.5 14.1 %collective-permute-start.17 = (bf16[64,4096]{1,0:T(8,128)(2,1)S(1)}, bf16[64,4096]{1,0:T(8,128)(2,1)S(1)}, u32[]{:S(2)}, u32[]{:S(2)}) collective-permute-start(bf16[64,4096]{1,0:T(8,128)(2,1)S(1)} %get-tuple-element.72), channel_id=1, source_target_pairs={{0,1},{1,2},{2,3},{4,5},{5,6},{6,7},{8,9},{9,10},{10,11},{12,13},{... | collective-permute-start | bytes 1572872 | tf_op jit(solution)/shard_map/ppermute | solution.py:25
Sparse Core Ops, SparseCore 0:
  20.8 29.6 all-gather.4
  58.2 53.7 all-gather.6

commit v6 on v5

v6 whole, which is shorter than its diff:
```python
import functools
import math

import jax
import jax.numpy as jnp
from jax import lax
from jax.experimental import pallas as pl
from jax.experimental.pallas import tpu as pltpu
from jax.sharding import PartitionSpec as P

HD = 128
SPAN = 64
NEIGH = 2
NLEN = 128
GROUP = NEIGH * NLEN

NEG_BIG = -1e30
LOG2E = 1.4426950408889634
VMEM_BYTES = 14 * 1024 * 1024


def shift(block, axis, distance, senders):
    size = lax.axis_size(axis)
    route = [(k, k + distance) for k in senders if 0 <= k + distance < size]
    return lax.ppermute(block, axis, route)


def add_rounded(first, second):
    return (first.astype(jnp.float32) + second.astype(jnp.float32)).astype(jnp.bfloat16)


def pick(blocks, index):
    return lax.dynamic_index_in_dim(
        blocks, jnp.clip(index, 0, blocks.shape[0] - 1), 0, keepdims=False
    )


def reduce_step(blocks, carried, step):
    size = lax.axis_size("db")
    me = lax.axis_index("db")
    far = size - 1 - step
    up_block, down_block = pick(blocks, me + far), pick(blocks, me - far)
    if carried is not None:
        up_block = add_rounded(up_block, carried[0])
        down_block = add_rounded(down_block, carried[1])
    return (
        shift(up_block, "db", 1, range(step + 1)),
        shift(down_block, "db", -1, range(size - 1 - step, size)),
    )


def reduced(blocks, carried):
    total = pick(blocks, lax.axis_index("db")).astype(jnp.float32)
    return total + carried[0].astype(jnp.float32) + carried[1].astype(jnp.float32)


def reduce_scatter(blocks):
    carried = None
    for step in range(lax.axis_size("db") - 1):
        carried = lax.optimization_barrier(reduce_step(blocks, carried, step))
    return reduced(blocks, carried)


def plane_swap(block, masks):
    return lax.ppermute(block, "seq", [(i, i ^ masks[i & 1]) for i in range(8)])


def plane_pieces(mine, near):
    swap = plane_swap
    four = (mine, near, swap(mine, (4, 2)), swap(near, (4, 2)))
    four = lax.optimization_barrier(four)
    return four + tuple(swap(one, (1, 1)) for one in four)


def plane_slot(owner, me):
    apart = owner ^ me
    core, x, y = apart & 1, (apart >> 1) & 1, apart >> 2
    return 4 * core + jnp.where((owner & 1) == 0, x + 2 * y, y + 2 * x)


def self_kernel(qkv_ref, weight_hbm, out_ref, weight_ref, sem, *, blocks, rows, scale):
    bring = pltpu.make_async_copy(weight_hbm, weight_ref, sem)
    bring.start()
    for block in range(blocks):
        query = qkv_ref[block, 0]
        live = (block + 1) * rows
        keys = qkv_ref[0 : block + 1, 1].reshape(live, HD)
        values = qkv_ref[0 : block + 1, 2].reshape(live, HD)
        scores = lax.dot_general(
            query, keys, (((1,), (1,)), ((), ())), preferred_element_type=jnp.float32
        )
        query_pos = block * rows + lax.broadcasted_iota(jnp.int32, (rows, live), 0)
        key_pos = lax.broadcasted_iota(jnp.int32, (rows, live), 1)
        scores = jnp.where(key_pos <= query_pos, scores * (scale * LOG2E), NEG_BIG)
        top = jnp.max(scores, axis=-1, keepdims=True)
        weights = jnp.exp2(scores - top)
        total = jnp.sum(weights, axis=-1, keepdims=True)
        mixed = jnp.dot(weights.astype(jnp.bfloat16), values, preferred_element_type=jnp.float32)
        out_ref[block] = (mixed / total).astype(jnp.bfloat16)
    bring.wait()


def self_attend_head(qkv, weight, scale):
    blocks, _, rows, _ = qkv.shape
    vmem = pl.BlockSpec(memory_space=pltpu.VMEM)
    return pl.pallas_call(
        functools.partial(self_kernel, blocks=blocks, rows=rows, scale=scale),
        out_shape=[
            jax.ShapeDtypeStruct((blocks, rows, HD), jnp.bfloat16),
            jax.ShapeDtypeStruct(weight.shape, weight.dtype),
        ],
        in_specs=[vmem, pl.BlockSpec(memory_space=pl.ANY)],
        out_specs=[vmem, vmem],
        scratch_shapes=[pltpu.SemaphoreType.DMA],
        compiler_params=pltpu.CompilerParams(vmem_limit_bytes=VMEM_BYTES),
        cost_estimate=pl.CostEstimate(
            flops=2 * blocks * blocks * rows * rows * HD,
            bytes_accessed=8 * blocks * rows * HD + 2 * weight.size,
            transcendentals=blocks * blocks * rows * rows // 2,
        ),
        name="self_attend",
    )(qkv, weight)


def span_before(wanted):
    return shift(wanted[-1], "seq", 1, range(lax.axis_size("seq")))


def pack_kernel(query_ref, key_ref, value_ref, out_ref):
    for which, ref in enumerate((query_ref, key_ref, value_ref)):
        for head in range(out_ref.shape[0]):
            out_ref[head, which] = ref[:, head * HD : (head + 1) * HD]


def pack_heads(query_rows, key_rows, value_rows):
    rows, width = query_rows.shape
    heads = width // HD
    step = math.gcd(heads, 2)
    return pl.pallas_call(
        pack_kernel,
        grid=(heads // step,),
        out_shape=jax.ShapeDtypeStruct((heads, 3, rows, HD), jnp.bfloat16),
        in_specs=[pl.BlockSpec((rows, step * HD), lambda at: (0, at))] * 3,
        out_specs=pl.BlockSpec((step, 3, rows, HD), lambda at: (at, 0, 0, 0)),
        cost_estimate=pl.CostEstimate(
            flops=0, bytes_accessed=12 * rows * width, transcendentals=0
        ),
        name="pack_heads",
    )(query_rows, key_rows, value_rows)


def self_attention_by_head(query_rows, key_rows, value_rows, wanted, weight, scale):
    packed, wanted = lax.optimization_barrier((pack_heads(query_rows, key_rows, value_rows), wanted))
    held, before = lax.optimization_barrier(
        (lax.all_to_all(packed, "seq", 0, 0, tiled=True), span_before(wanted))
    )
    mixed, weight = self_attend_head(held, weight, scale)
    return lax.all_to_all(mixed, "seq", 0, 0, tiled=True), before, weight


def self_attention_gathered(query_rows, key_rows, value_rows, scale):
    rows, width = query_rows.shape
    heads = width // HD
    keys = lax.all_gather(key_rows, "seq", axis=0, tiled=True)
    values = lax.all_gather(value_rows, "seq", axis=0, tiled=True)
    count = keys.shape[0]
    query_pos = lax.axis_index("seq") * rows + jnp.arange(rows, dtype=jnp.int32)
    allowed = jnp.arange(count, dtype=jnp.int32)[None, :] <= query_pos[:, None]
    scores = (
        jnp.einsum(
            "qhd,khd->hqk",
            query_rows.reshape(rows, heads, HD),
            keys.reshape(count, heads, HD),
            preferred_element_type=jnp.float32,
        )
        * scale
    )
    scores = jnp.where(allowed[None], scores, NEG_BIG)
    weights = jnp.exp(scores - jnp.max(scores, axis=-1, keepdims=True))
    total = jnp.sum(weights, axis=-1)
    mixed = jnp.einsum(
        "hqk,khd->hqd",
        weights.astype(jnp.bfloat16),
        values.reshape(count, heads, HD),
        preferred_element_type=jnp.float32,
    )
    return (mixed / total[..., None]).astype(jnp.bfloat16)


def self_out_kernel(attended_ref, weight_ref, out_ref, rows_ref):
    for head in range(attended_ref.shape[0]):
        rows_ref[:, head * HD : (head + 1) * HD] = attended_ref[head]
    features = out_ref.shape[1]
    step = math.gcd(features, 512)

    def columns(at, carried):
        here = pl.ds(pl.multiple_of(at * step, step), step)
        product = jnp.dot(rows_ref[...], weight_ref[:, here], preferred_element_type=jnp.float32)
        out_ref[:, here] = product.astype(jnp.bfloat16)
        return carried

    lax.fori_loop(0, features // step, columns, 0)


def self_out(attended, weight):
    heads, rows, _ = attended.shape
    width, features = weight.shape
    vmem = pl.BlockSpec(memory_space=pltpu.VMEM)
    return pl.pallas_call(
        self_out_kernel,
        out_shape=jax.ShapeDtypeStruct((rows, features), jnp.bfloat16),
        in_specs=[vmem, vmem],
        out_specs=vmem,
        scratch_shapes=[pltpu.VMEM((rows, width), jnp.bfloat16)],
        compiler_params=pltpu.CompilerParams(vmem_limit_bytes=VMEM_BYTES),
        cost_estimate=pl.CostEstimate(
            flops=2 * rows * width * features,
            bytes_accessed=2 * (rows * width + width * features + rows * features),
            transcendentals=0,
        ),
        name="self_out",
    )(attended, weight)


def project_kernel(where_ref, *refs, cuts):
    wk_hbm, wv_hbm, wq_hbm, wo_hbm, keys_ref, values_ref, wq_ref, wo_ref = refs[-12:-4]
    rows_ref, wk_ref, wv_ref, sems = refs[-4:]
    tables = refs[:-12]
    entries = keys_ref.shape[0] // NLEN
    piece = NLEN // cuts
    bring = [
        pltpu.make_async_copy(source, target, sems.at[entries * cuts + at])
        for at, (source, target) in enumerate(
            ((wk_hbm, wk_ref), (wv_hbm, wv_ref), (wq_hbm, wq_ref), (wo_hbm, wo_ref))
        )
    ]
    for copy in bring[:2]:
        copy.start()

    def entry_copy(entry, cut, table, first, shard):
        return pltpu.make_async_copy(
            table.at[first + cut, shard],
            rows_ref.at[pl.ds(entry * NLEN + cut * piece, piece)],
            sems.at[entry * cuts + cut],
        )

    for entry in range(entries):
        for slot, table in enumerate(tables):

            @pl.when(where_ref[3 * entry] == slot)
            def _(entry=entry, table=table):
                for cut in range(cuts):
                    entry_copy(
                        entry, cut, table, where_ref[3 * entry + 1], where_ref[3 * entry + 2]
                    ).start()

    for copy in bring[2:]:
        copy.start()
    for copy in bring[:2]:
        copy.wait()
    width = keys_ref.shape[1]
    step = math.gcd(width, 512)
    for group in range(entries // NEIGH):
        for entry in range(NEIGH * group, NEIGH * (group + 1)):
            for cut in range(cuts):
                entry_copy(entry, cut, tables[0], 0, 0).wait()
        here = slice(group * GROUP, (group + 1) * GROUP)
        for at in range(0, width, step):
            lanes = slice(at, at + step)
            for weight, made in ((wk_ref, keys_ref), (wv_ref, values_ref)):
                made[here, lanes] = jnp.dot(
                    rows_ref[here, :], weight[:, lanes], preferred_element_type=jnp.float32
                ).astype(jnp.bfloat16)
    for copy in bring[2:]:
        copy.wait()


def project_encodings(where, tables, w_cross_k, w_cross_v, w_cross_q, w_cross_out):
    entries = where.shape[0] // 3
    piece, depth = tables[0].shape[2:]
    cuts = NLEN // piece
    width = w_cross_k.shape[1]
    vmem = pl.BlockSpec(memory_space=pltpu.VMEM)
    anywhere = pl.BlockSpec(memory_space=pl.ANY)
    made = jax.ShapeDtypeStruct((entries * NLEN, width), jnp.bfloat16)
    return pl.pallas_call(
        functools.partial(project_kernel, cuts=cuts),
        out_shape=[made, made]
        + [jax.ShapeDtypeStruct(one.shape, one.dtype) for one in (w_cross_q, w_cross_out)],
        in_specs=[pl.BlockSpec(memory_space=pltpu.SMEM)] + [anywhere] * (len(tables) + 4),
        out_specs=[vmem] * 4,
        scratch_shapes=[
            pltpu.VMEM((entries * NLEN, depth), jnp.bfloat16),
            pltpu.VMEM(w_cross_k.shape, jnp.bfloat16),
            pltpu.VMEM(w_cross_v.shape, jnp.bfloat16),
            pltpu.SemaphoreType.DMA((entries * cuts + 4,)),
        ],
        compiler_params=pltpu.CompilerParams(vmem_limit_bytes=VMEM_BYTES),
        cost_estimate=pl.CostEstimate(
            flops=entries * NLEN * depth,
            bytes_accessed=2 * entries * NLEN * depth,
            transcendentals=0,
        ),
        name="project_encodings",
    )(where, *tables, w_cross_k, w_cross_v, w_cross_q, w_cross_out)


def apart_heads(query):
    first = lax.broadcasted_iota(jnp.int32, query.shape, 1) < HD
    nothing = jnp.zeros_like(query)
    return jnp.concatenate(
        (jnp.where(first, query, nothing), jnp.where(first, nothing, query)), axis=0
    )


def together_heads(mixed):
    rows = mixed.shape[0] // 2
    first = lax.broadcasted_iota(jnp.int32, (rows, 2 * HD), 1) < HD
    return jnp.where(first, mixed[:rows], mixed[rows:])


def cross_kernel(
    place_ref,
    hidden_ref,
    total_ref,
    gain_ref,
    wq_ref,
    keys_ref,
    values_ref,
    wo_ref,
    out_ref,
    residual_ref,
    rows_ref,
    query_ref,
    mixed_ref,
    *,
    scale,
):
    rows, features = hidden_ref.shape
    n_db, share, _ = out_ref.shape
    pairs = wq_ref.shape[1] // HD // 2
    tail = 16
    block = math.gcd(rows, 32)

    def norm(at, carried):
        here = pl.ds(pl.multiple_of(at * block, block), block)
        residual = hidden_ref[here, :].astype(jnp.float32) + total_ref[here, :].astype(jnp.float32)
        mean_square = jnp.mean(residual * residual, axis=-1, keepdims=True)
        rows_ref[here, :] = (
            residual * lax.rsqrt(mean_square + 1e-05) * gain_ref[...].astype(jnp.float32)
        ).astype(jnp.bfloat16)
        return carried

    lax.fori_loop(0, rows // block, norm, 0)
    own = pl.ds(pl.multiple_of(place_ref[0] * share, share), share)
    residual_ref[...] = hidden_ref[own, :].astype(jnp.float32) + total_ref[own, :].astype(
        jnp.float32
    )
    lanes = [slice(2 * pair * HD, 2 * (pair + 1) * HD) for pair in range(pairs)]
    for at in lanes:
        query_ref[:, at] = jnp.dot(
            rows_ref[...], wq_ref[:, at], preferred_element_type=jnp.float32
        ).astype(jnp.bfloat16)
    row = lax.broadcasted_iota(jnp.int32, (tail, 2 * HD), 0)
    spans = rows // SPAN
    for span in range(spans):
        top = span * SPAN
        here, after = (slice((span + k) * GROUP, (span + k + 1) * GROUP) for k in (0, 1))
        work = [(slice(top, top + SPAN), here, at) for at in lanes]
        work += [(slice(top + SPAN - tail, top + SPAN), after, at) for at in lanes]
        scores = [
            lax.dot_general(
                apart_heads(query_ref[of, at]),
                keys_ref[which, at],
                (((1,), (1,)), ((), ())),
                preferred_element_type=jnp.float32,
            )
            * (scale * LOG2E)
            for of, which, at in work
        ]
        tops = [jnp.max(one, axis=-1, keepdims=True) for one in scores]
        weights = [jnp.exp2(one - top_one) for one, top_one in zip(scores, tops)]
        totals = [jnp.sum(one, axis=-1, keepdims=True) for one in weights]
        mixed = [
            jnp.dot(
                one.astype(jnp.bfloat16), values_ref[which, at], preferred_element_type=jnp.float32
            )
            for one, (_, which, at) in zip(weights, work)
        ]
        mixed = [together_heads(one / total) for one, total in zip(mixed, totals)]
        for pair, at in enumerate(lanes):
            main, last = mixed[pair], mixed[pairs + pair]
            if span == 0:
                main = jnp.where(place_ref[1] > 0, main, 0.0)
            last = jnp.where(row == tail - 1, last, main[SPAN - tail :])
            mixed_ref[top : top + SPAN - tail, at] = main[: SPAN - tail].astype(jnp.bfloat16)
            mixed_ref[top + SPAN - tail : top + SPAN, at] = last.astype(jnp.bfloat16)
    step = math.gcd(features, 512)

    def columns(at, carried):
        here = pl.ds(pl.multiple_of(at * step, step), step)
        product = jnp.dot(mixed_ref[...], wo_ref[:, here], preferred_element_type=jnp.float32)
        product = product.astype(jnp.bfloat16)
        for owner in range(n_db):
            out_ref[owner, :, here] = product[owner * share : (owner + 1) * share]
        return carried

    lax.fori_loop(0, features // step, columns, 0)


def cross_block(place, hidden, total, gain, w_cross_q, keys, values, w_cross_out, n_db, scale):
    rows, features = hidden.shape
    share = rows // n_db
    width = w_cross_q.shape[1]
    vmem = pl.BlockSpec(memory_space=pltpu.VMEM)
    return pl.pallas_call(
        functools.partial(cross_kernel, scale=scale),
        out_shape=[
            jax.ShapeDtypeStruct((n_db, share, features), jnp.bfloat16),
            jax.ShapeDtypeStruct((share, features), jnp.float32),
        ],
        in_specs=[pl.BlockSpec(memory_space=pltpu.SMEM)] + [vmem] * 7,
        out_specs=[vmem, vmem],
        scratch_shapes=[
            pltpu.VMEM((rows, features), jnp.bfloat16),
            pltpu.VMEM((rows, width), jnp.bfloat16),
            pltpu.VMEM((rows, width), jnp.bfloat16),
        ],
        compiler_params=pltpu.CompilerParams(vmem_limit_bytes=VMEM_BYTES),
        cost_estimate=pl.CostEstimate(
            flops=4 * rows * width * (features + GROUP),
            bytes_accessed=4 * width * (features + keys.shape[0]) + 8 * rows * features,
            transcendentals=rows * GROUP * width // HD,
        ),
        name="cross_block",
    )(place, hidden, total, gain, w_cross_q, keys, values, w_cross_out)


def per_device(
    hidden_in,
    query_rows,
    key_rows,
    value_rows,
    w_self_out,
    norm_gain,
    w_cross_q,
    w_cross_k,
    w_cross_v,
    w_cross_out,
    enc_table,
    nb_shard,
    nb_row,
):
    rows, features = hidden_in.shape
    heads = query_rows.shape[1] // HD
    n_seq, n_db = lax.axis_size("seq"), lax.axis_size("db")
    seq_index, db_index = lax.axis_index("seq"), lax.axis_index("db")
    scale = 1.0 / math.sqrt(HD)

    rows_shard, _, depth = enc_table.shape
    piece = rows_shard * NLEN // n_seq
    part = lax.dynamic_slice_in_dim(
        enc_table.reshape(rows_shard * NLEN, depth), seq_index * piece, piece, 0
    )
    part, query_rows, key_rows, value_rows = lax.optimization_barrier(
        (part, query_rows, key_rows, value_rows)
    )
    along_db = lax.all_gather(part, "db", axis=0)
    wanted = jnp.stack((nb_row, nb_shard), axis=-1).astype(jnp.int32)
    place = jnp.stack((db_index, (seq_index > 0).astype(jnp.int32))).astype(jnp.int32)

    by_head = heads == n_seq
    if by_head:
        attended, before, w_self_out = self_attention_by_head(
            query_rows, key_rows, value_rows, wanted, w_self_out, scale
        )
    else:
        attended = self_attention_gathered(query_rows, key_rows, value_rows, scale)
        before = span_before(wanted)

    in_plane = n_seq == 8 and piece == NLEN
    along_db, attended = lax.optimization_barrier((along_db, attended))
    partial = self_out(attended, w_self_out)
    if in_plane:
        along_db = (along_db, plane_swap(along_db, (2, 4)))
    along_db, partial = lax.optimization_barrier((along_db, partial))
    total = lax.psum(partial, "db")

    nearest = jnp.concatenate((before[None], wanted), axis=0)
    row, shard = nearest[..., 0], nearest[..., 1]
    if in_plane:
        tables = tuple(one[None] for one in plane_pieces(*along_db))
        where = jnp.stack((plane_slot(row, seq_index), jnp.zeros_like(row), shard), axis=-1)
    else:
        tables = (lax.all_gather(along_db, "seq", axis=0),)
        where = jnp.stack((jnp.zeros_like(row), row * (NLEN // piece), shard), axis=-1)
    projected = project_encodings(
        where.astype(jnp.int32).reshape(-1), tables, w_cross_k, w_cross_v, w_cross_q, w_cross_out
    )
    total, (keys, values, w_cross_q, w_cross_out) = lax.optimization_barrier((total, projected))
    out_partial, residual = cross_block(
        place,
        hidden_in,
        total,
        norm_gain.reshape(1, features),
        w_cross_q,
        keys,
        values,
        w_cross_out,
        n_db,
        scale,
    )
    return residual + reduce_scatter(out_partial)


def solution(mesh):
    placed = (
        P("seq", None),
        P("seq", "db"),
        P("seq", "db"),
        P("seq", "db"),
        P("db", None),
        P(),
        P(None, "db"),
        P(None, "db"),
        P(None, "db"),
        P("db", None),
        P("db", None, None),
        P("seq", None),
        P("seq", None),
    )
    return jax.shard_map(
        per_device, mesh=mesh, in_specs=placed, out_specs=P(("seq", "db"), None), check_vma=False
    )
```

time: 226 us -> 260 us (1.15)
  local copies, waits for them, and re-layouts: 7.74 us -> 39.9 us
  waiting for transfers between devices: 99.7 us -> 130 us
  starting transfers between devices: 56.1 us -> 35.1 us
  Pallas kernels: 37.8 us -> 33 us
    ppermute x19 -> x7, waiting for transfers between devices: 72.5 us -> 31.3 us  [shift(): return lax.ppermute(block, axis, route)]
    ppermute x0 -> x7, waiting for transfers between devices: none -> 36.1 us  [plane_swap(): return lax.ppermute(block, 'seq', [(i, i ^ masks[i & 1]) for i in range(8)])]
    psum x0 -> x1, waiting for transfers between devices: none -> 35.7 us  [per_device(): total = lax.psum(partial, 'db')]
    unnamed x18 -> x44, local copies, waits for them, and re-layouts: 5.57 us -> 37.6 us
    ppermute x19 -> x7, starting transfers between devices: 47.4 us -> 22.7 us  [shift(): return lax.ppermute(block, axis, route)]
    pallas_call x3, Pallas kernels: 28.6 us -> 23.2 us  [the longest x1 10.5 us: cross_block(): pl.pallas_call(functools.partial(cross_kernel, scale=scale), out_shape=[j...]
    ppermute x0 -> x7, starting transfers between devices: none -> 3.6 us  [plane_swap(): return lax.ppermute(block, 'seq', [(i, i ^ masks[i & 1]) for i in range(8)])]
  transfers between devices with their start and end apart: 23 -> 18, of which waited for: 16 -> 15; matrix products, arithmetic and copies ran while one was open for 3% -> 0% of each run, Pallas kernels for 10% -> 7%
where the time goes in v6:
time: 260 us
  waiting for transfers between devices  130 us (50%)
  local copies, waits for them, and re-layouts  39.9 us (15%)
  starting transfers between devices  35.1 us (14%)
  Pallas kernels  33 us (13%)
  between operations  13.6 us (5%)
  other arithmetic  7.74 us (3%)
    unnamed x44, local copies, waits for them, and re-layouts  37.6 us
    ppermute x7, waiting for transfers between devices, plane_swap(): return lax.ppermute(block, 'seq', [(i, i ^ masks[i & 1]) for i in range(8)])  36.1 us
    psum x1, waiting for transfers between devices, per_device(): total = lax.psum(partial, 'db')  35.7 us
    ppermute x7, waiting for transfers between devices, shift(): return lax.ppermute(block, axis, route)  31.3 us
    ppermute x7, starting transfers between devices, shift(): return lax.ppermute(block, axis, route)  22.7 us
    all_to_all x1, waiting for transfers between devices, self_attention_by_head(): lax.all_to_all(packed, 'seq', 0, 0, tiled=True)  16.9 us
    pallas_call x1, Pallas kernels, cross_block(): pl.pallas_call(functools.partial(cross_kernel, scale=scale), out_shape=[j...  10.5 us
    all_to_all x1, waiting for transfers between devices, self_attention_by_head(): return (lax.all_to_all(mixed, 'seq', 0, 0, tiled=True), before, weight)  9.6 us
  transfers between devices with their start and end apart: 18, of which 15 were waited for; matrix products, arithmetic and copies ran while one was open for 0% of the time, Pallas kernels for 7%

profile of v6, /device:TPU:0, one launch (start us, length us, event | category | flops | bytes accessed | tf_op | source)
XLA Modules:
  0.0 259.6 jit_solution(15008932262872551291)
XLA Ops:
  6.5 1.6 copy-done
  8.1 0.7 constant_dynamic-slice_fusion
  8.9 0.7 pad_add_fusion.1
  9.6 3.7 %pack_heads.1 = bf16[8,3,256,128]{3,2,1,0:T(8,128)(2,1)} custom-call(bf16[256,1024]{1,0:T(8,128)(2,1)} %query_ref, bf16[256,1024]{1,0:T(8,128)(2,1)} %key_ref, bf16[256,1024]{1,0:T(8,128)(2,1)} %value_ref), custom_call_target="tpu_custom_call" | custom-call | bytes 3145728 | tf_op jit(solution)/shard_map/pack_heads/pallas_call | solution.py:139
  13.3 5.2 %all-to-all-start = ((bf16[8,3,256,128]{3,2,1,0:T(8,128)(2,1)}), bf16[8,3,256,128]{3,2,1,0:T(8,128)(2,1)S(1)}, u32[]{:S(2)}, u32[]{:S(2)}) async-start(bf16[8,3,256,128]{3,2,1,0:T(8,128)(2,1)} %pack_heads.1), calls=%async_computation | async-start | bytes 3145728 | tf_op jit(solution)/shard_map/all_to_all | solution.py:155
  18.5 0.7 all-gather.3.cloned.1.call-update
  19.2 0.1 slice.9
  19.3 0.1 copy.17
  19.4 2.4 collective-permute-start
  21.8 0.8 collective-permute-done
  22.6 16.9 %all-to-all-done.qkv_ref = bf16[8,3,256,128]{3,2,1,0:T(8,128)(2,1)S(1)} async-done(((bf16[8,3,256,128]{3,2,1,0:T(8,128)(2,1)}), bf16[8,3,256,128]{3,2,1,0:T(8,128)(2,1)S(1)}, u32[]{:S(2)}, u32[]{:S(2)}) %all-to-all-start) | async-done | bytes 1572896 | tf_op jit(solution)/shard_map/all_to_all | solution.py:155
  39.5 3.4 %copy-done.6 = bf16[1024,4096]{1,0:T(8,128)(2,1)S(1)} copy-done((bf16[1024,4096]{1,0:T(8,128)(2,1)S(1)}, bf16[1024,4096]{1,0:T(8,128)(2,1)}, u32[]{:S(2)}) %copy-start.6) | copy-done | bytes 8388632
  42.9 6.0 %self_attend.1 = (bf16[8,256,128]{2,1,0:T(8,128)(2,1)}, bf16[1024,4096]{1,0:T(8,128)(2,1)S(1)}) custom-call(bf16[8,3,256,128]{3,2,1,0:T(8,128)(2,1)S(1)} %all-to-all-done.qkv_ref, bf16[1024,4096]{1,0:T(8,128)(2,1)S(1)} %copy-done.6), custom_call_target="tpu_custom_call" | custom-call | flops 1073741824 | bytes 10485760 | tf_op jit(solution)/shard_map/self_attend/pallas_call | solution.py:106
  49.0 3.3 %copy-done.7 = bf16[1024,4096]{1,0:T(8,128)(2,1)} copy-done((bf16[1024,4096]{1,0:T(8,128)(2,1)}, bf16[1024,4096]{1,0:T(8,128)(2,1)S(1)}, u32[]{:S(2)}) %copy-start.7) | copy-done | bytes 8388632
  52.3 3.5 %all-to-all-start.1 = ((bf16[8,256,128]{2,1,0:T(8,128)(2,1)}), bf16[8,256,128]{2,1,0:T(8,128)(2,1)S(1)}, u32[]{:S(2)}, u32[]{:S(2)}) async-start(bf16[8,256,128]{2,1,0:T(8,128)(2,1)} %get-tuple-element.48), calls=%async_computation.1 | async-start | bytes 1048576 | tf_op jit(solution)/shard_map/all_to_all | solution.py:158
  55.9 9.6 %all-to-all-done.1.attended_ref = bf16[8,256,128]{2,1,0:T(8,128)(2,1)S(1)} async-done(((bf16[8,256,128]{2,1,0:T(8,128)(2,1)}), bf16[8,256,128]{2,1,0:T(8,128)(2,1)S(1)}, u32[]{:S(2)}, u32[]{:S(2)}) %all-to-all-start.1) | async-done | bytes 524320 | tf_op jit(solution)/shard_map/all_to_all | solution.py:158
  65.5 0.6 collective-permute-start.1
  66.0 3.4 %copy-done.8 = bf16[1024,4096]{1,0:T(8,128)(2,1)S(1)} copy-done((bf16[1024,4096]{1,0:T(8,128)(2,1)S(1)}, bf16[1024,4096]{1,0:T(8,128)(2,1)}, u32[]{:S(2)}) %copy-start.8) | copy-done | bytes 8388632
  69.4 5.1 %self_out.1 = bf16[256,4096]{1,0:T(8,128)(2,1)} custom-call(bf16[8,256,128]{2,1,0:T(8,128)(2,1)S(1)} %all-to-all-done.1.attended_ref, bf16[1024,4096]{1,0:T(8,128)(2,1)S(1)} %copy-done.8), custom_call_target="tpu_custom_call" | custom-call | flops 2147483648 | bytes 11010048 | tf_op jit(solution)/shard_map/self_out/pallas_call | solution.py:209
  74.5 6.1 %collective-permute-done.1 = bf16[4,128,1024]{2,1,0:T(8,128)(2,1)} collective-permute-done((bf16[4,128,1024]{2,1,0:T(8,128)(2,1)}, bf16[4,128,1024]{2,1,0:T(8,128)(2,1)}, u32[]{:S(2)}, u32[]{:S(2)}) %collective-permute-start.1) | collective-permute-done | bytes 1048608 | tf_op jit(solution)/shard_map/ppermute | solution.py:65
  80.6 0.5 collective-permute-start.2
  81.1 1.5 collective-permute-start.3
  82.6 12.9 %collective-permute-done.2 = bf16[4,128,1024]{2,1,0:T(8,128)(2,1)} collective-permute-done((bf16[4,128,1024]{2,1,0:T(8,128)(2,1)S(1)}, bf16[4,128,1024]{2,1,0:T(8,128)(2,1)}, u32[]{:S(2)}, u32[]{:S(2)}) %collective-permute-start.2) | collective-permute-done | bytes 1048608 | tf_op jit(solution)/shard_map/ppermute | solution.py:65
  95.5 11.2 %collective-permute-done.3 = bf16[4,128,1024]{2,1,0:T(8,128)(2,1)} collective-permute-done((bf16[4,128,1024]{2,1,0:T(8,128)(2,1)}, bf16[4,128,1024]{2,1,0:T(8,128)(2,1)}, u32[]{:S(2)}, u32[]{:S(2)}) %collective-permute-start.3) | collective-permute-done | bytes 1048608 | tf_op jit(solution)/shard_map/ppermute | solution.py:65
  106.7 0.5 collective-permute-start.5
  107.2 0.5 collective-permute-start.7
  107.8 0.1 pad_add_fusion.2.place_ref
  107.8 0.1 copy.18
  107.9 0.1 add_add_fusion
  108.0 0.1 copy.19
  108.1 0.1 reshape.20.where_ref
  108.2 2.7 %collective-permute-done.4 = bf16[4,128,1024]{2,1,0:T(8,128)(2,1)} collective-permute-done((bf16[4,128,1024]{2,1,0:T(8,128)(2,1)S(1)}, bf16[4,128,1024]{2,1,0:T(8,128)(2,1)}, u32[]{:S(2)}, u32[]{:S(2)}) %collective-permute-start.4) | collective-permute-done | bytes 1048608 | tf_op jit(solution)/shard_map/ppermute | solution.py:65
  111.0 0.2 collective-permute-done.5
  111.2 1.5 collective-permute-done.6
  112.7 1.5 collective-permute-done.7
  114.2 1.6 copy-done.17
  115.8 7.6 %project_encodings.1 = (bf16[1280,1024]{1,0:T(8,128)(2,1)S(1)}, bf16[1280,1024]{1,0:T(8,128)(2,1)S(1)}, bf16[4096,1024]{1,0:T(8,128)(2,1)S(1)}, bf16[1024,4096]{1,0:T(8,128)(2,1)S(1)}) custom-call(s32[30]{0:T(128)S(1)} %reshape.20.where_ref, bf16[1,4,128,1024]{3,2,1,0:T(8,128)(2,1)S(1)} %bitcast.39, bf16[1,4,128,1024]{3,2,1,0:T(8,128)(2,1)} %bitcast.9.refs_1_, ...), custom_call_target="tpu_custom_call" | custom-call | flops 1310720 | bytes 2621440 | tf_op jit(solution)/shard_map/project_encodings/pallas_call | solution.py:286
  123.4 3.3 %copy-done.2 = bf16[4096,1024]{1,0:T(8,128)(2,1)} copy-done((bf16[4096,1024]{1,0:T(8,128)(2,1)}, bf16[4096,1024]{1,0:T(8,128)(2,1)S(1)}, u32[]{:S(2)}) %copy-start.2) | copy-done | bytes 8388632
  126.7 3.2 %copy-done.4 = bf16[1024,4096]{1,0:T(8,128)(2,1)} copy-done((bf16[1024,4096]{1,0:T(8,128)(2,1)}, bf16[1024,4096]{1,0:T(8,128)(2,1)S(1)}, u32[]{:S(2)}) %copy-start.4) | copy-done | bytes 8388632
  130.0 1.5 copy-done.10
  131.5 1.5 copy-done.12
  133.0 35.7 %all-reduce.2.cloned.1.call-done.total_ref = bf16[256,4096]{1,0:T(8,128)(2,1)} async-done(((bf16[256,4096]{1,0:T(8,128)(2,1)}), bf16[256,4096]{1,0:T(8,128)(2,1)}) %all-reduce.2.cloned.1.call-update) | async-done | bytes 2097168 | tf_op jit(solution)/shard_map/psum | solution.py:487
  168.7 3.4 %copy-done.3 = bf16[4096,1024]{1,0:T(8,128)(2,1)S(1)} copy-done((bf16[4096,1024]{1,0:T(8,128)(2,1)S(1)}, bf16[4096,1024]{1,0:T(8,128)(2,1)}, u32[]{:S(2)}) %copy-start.3) | copy-done | bytes 8388632
  172.0 3.4 %copy-done.5 = bf16[1024,4096]{1,0:T(8,128)(2,1)S(1)} copy-done((bf16[1024,4096]{1,0:T(8,128)(2,1)S(1)}, bf16[1024,4096]{1,0:T(8,128)(2,1)}, u32[]{:S(2)}) %copy-start.5) | copy-done | bytes 8388632
  175.4 1.7 copy-done.11
  177.2 1.7 copy-done.13
  178.9 1.6 copy-done.14
  180.5 1.6 copy-done.15
  182.1 10.5 %cross_block.1 = (bf16[4,64,4096]{2,1,0:T(8,128)(2,1)S(1)}, f32[64,4096]{1,0:T(8,128)S(1)}) custom-call(s32[2]{0:T(128)S(1)} %pad_add_fusion.2.place_ref, bf16[256,4096]{1,0:T(8,128)(2,1)S(1)} %copy-done.14, bf16[256,4096]{1,0:T(8,128)(2,1)S(1)} %copy-done.15, bf16[1,4096]{1,0:T(2,128)(2,1)S(1)} %reshape.21.gain_ref, bf16[4096,1024]{1,0:T(8,128)(2,1)S(1)} %copy-done.3, ...), custom_call_target="tpu_custom_call" | custom-call | flops 4563402752 | bytes 30408704 | tf_op jit(solution)/shard_map/cross_block/pallas_call | solution.py:416
  192.6 1.3 copy-done.9
  193.9 1.1 dynamic-slice_bitcast_fusion
  195.0 2.0 collective-permute-start.8
  197.0 0.7 collective-permute-start.9
  197.7 10.5 %collective-permute-done.8 = bf16[64,4096]{1,0:T(8,128)(2,1)S(1)} collective-permute-done((bf16[64,4096]{1,0:T(8,128)(2,1)}, bf16[64,4096]{1,0:T(8,128)(2,1)S(1)}, u32[]{:S(2)}, u32[]{:S(2)}) %collective-permute-start.8) | collective-permute-done | bytes 524320 | tf_op jit(solution)/shard_map/ppermute | solution.py:25
  208.2 1.4 fusion.1
  209.7 5.1 %collective-permute-start.10 = (bf16[64,4096]{1,0:T(8,128)(2,1)S(1)}, bf16[64,4096]{1,0:T(8,128)(2,1)}, u32[]{:S(2)}, u32[]{:S(2)}) collective-permute-start(bf16[64,4096]{1,0:T(8,128)(2,1)S(1)} %get-tuple-element.80), channel_id=1, source_target_pairs={{0,1},{1,2},{4,5},{5,6},{8,9},{9,10},{12,13},{13,14},{16,17},{17,1... | collective-permute-start | bytes 1572872 | tf_op jit(solution)/shard_map/ppermute | solution.py:25
  214.8 1.5 collective-permute-start.11
  216.2 7.8 %collective-permute-done.10 = bf16[64,4096]{1,0:T(8,128)(2,1)} collective-permute-done((bf16[64,4096]{1,0:T(8,128)(2,1)S(1)}, bf16[64,4096]{1,0:T(8,128)(2,1)}, u32[]{:S(2)}, u32[]{:S(2)}) %collective-permute-start.10) | collective-permute-done | bytes 524320 | tf_op jit(solution)/shard_map/ppermute | solution.py:25
  224.0 2.9 %fusion = (bf16[64,4096]{1,0:T(8,128)(2,1)}, bf16[64,4096]{1,0:T(8,128)(2,1)}) fusion(bf16[64,4096]{1,0:T(8,128)(2,1)} %collective-permute-done.11, bf16[4,64,4096]{2,1,0:T(8,128)(2,1)} %copy-done.9, s32[]{:T(128)S(6)} %min.28, bf16[64,4096]{1,0:T(8,128)(2,1)} %collective-permute-done.10, s32[]{:T(128)S(6)} %min.23), kind=kLoop, calls=%fused_computation.1 | loop fusion | flops 2097152 | bytes 3145736 | tf_op jit(solution)/shard_map/convert_element_type | solution.py:29
  226.9 9.8 %collective-permute-start.12 = (bf16[64,4096]{1,0:T(8,128)(2,1)}, bf16[64,4096]{1,0:T(8,128)(2,1)}, u32[]{:S(2)}, u32[]{:S(2)}) collective-permute-start(bf16[64,4096]{1,0:T(8,128)(2,1)} %get-tuple-element.78), channel_id=1, source_target_pairs={{0,1},{1,2},{2,3},{4,5},{5,6},{6,7},{8,9},{9,10},{10,11},{12,13},{... | collective-permute-start | bytes 1572872 | tf_op jit(solution)/shard_map/ppermute | solution.py:25
  236.7 1.3 collective-permute-start.13
  238.0 7.3 %collective-permute-done.12 = bf16[64,4096]{1,0:T(8,128)(2,1)} collective-permute-done((bf16[64,4096]{1,0:T(8,128)(2,1)}, bf16[64,4096]{1,0:T(8,128)(2,1)}, u32[]{:S(2)}, u32[]{:S(2)}) %collective-permute-start.12) | collective-permute-done | bytes 524320 | tf_op jit(solution)/shard_map/ppermute | solution.py:25
  245.3 4.9 %collective-permute-done.13 = bf16[64,4096]{1,0:T(8,128)(2,1)} collective-permute-done((bf16[64,4096]{1,0:T(8,128)(2,1)}, bf16[64,4096]{1,0:T(8,128)(2,1)}, u32[]{:S(2)}, u32[]{:S(2)}) %collective-permute-start.13) | collective-permute-done | bytes 524320 | tf_op jit(solution)/shard_map/ppermute | solution.py:25
  250.2 2.5 fusion.5
  (40 shorter events, 0.2 us)
Async XLA Ops:
  6.5 1.6 copy-start
  13.3 26.2 %all-to-all-start = ((bf16[8,3,256,128]{3,2,1,0:T(8,128)(2,1)}), bf16[8,3,256,128]{3,2,1,0:T(8,128)(2,1)S(1)}, u32[]{:S(2)}, u32[]{:S(2)}) async-start(bf16[8,3,256,128]{3,2,1,0:T(8,128)(2,1)} %pack_heads.1), calls=%async_computation | async-start | bytes 3145728 | tf_op jit(solution)/shard_map/all_to_all | solution.py:155
  18.5 37.4 %all-gather.3.cloned.1.call-start = ((), (), s32[]{:S(2)}) async-start(), calls=%async_computation.3 | async-start | bytes 1310720 | tf_op jit(solution)/shard_map/all_gather | solution.py:468
  19.4 3.2 %collective-permute-start = (s32[2,2]{1,0:T(2,128)S(1)}, s32[2,2]{1,0:T(2,128)S(1)}, u32[]{:S(2)}, u32[]{:S(2)}) collective-permute-start(s32[2,2]{1,0:T(2,128)S(1)} %bitcast.45), channel_id=1, source_target_pairs={{0,4},{4,8},{8,12},{12,16},{16,20},{20,24},{24,28},{1,5},{5,9},{9,... | collective-permute-start | bytes 56 | tf_op jit(solution)/shard_map/ppermute | solution.py:25
  39.5 3.4 %copy-start.6 = (bf16[1024,4096]{1,0:T(8,128)(2,1)S(1)}, bf16[1024,4096]{1,0:T(8,128)(2,1)}, u32[]{:S(2)}) copy-start(bf16[1024,4096]{1,0:T(8,128)(2,1)} %weight_hbm.1) | copy-start | bytes 25165828
  49.0 3.3 %copy-start.7 = (bf16[1024,4096]{1,0:T(8,128)(2,1)}, bf16[1024,4096]{1,0:T(8,128)(2,1)S(1)}, u32[]{:S(2)}) copy-start(bf16[1024,4096]{1,0:T(8,128)(2,1)S(1)} %get-tuple-element.51.weight_ref) | copy-start | bytes 25165828
  52.3 13.2 %all-to-all-start.1 = ((bf16[8,256,128]{2,1,0:T(8,128)(2,1)}), bf16[8,256,128]{2,1,0:T(8,128)(2,1)S(1)}, u32[]{:S(2)}, u32[]{:S(2)}) async-start(bf16[8,256,128]{2,1,0:T(8,128)(2,1)} %get-tuple-element.48), calls=%async_computation.1 | async-start | bytes 1048576 | tf_op jit(solution)/shard_map/all_to_all | solution.py:158
  55.8 112.9 %all-reduce.2.cloned.1.call-start = ((), (), s32[]{:S(2)}) async-start(), calls=%async_computation.2 | async-start | bytes 4194304 | tf_op jit(solution)/shard_map/psum | solution.py:487
  65.5 15.1 %collective-permute-start.1 = (bf16[4,128,1024]{2,1,0:T(8,128)(2,1)}, bf16[4,128,1024]{2,1,0:T(8,128)(2,1)}, u32[]{:S(2)}, u32[]{:S(2)}) collective-permute-start(bf16[4,128,1024]{2,1,0:T(8,128)(2,1)} %bitcast.36), channel_id=1, source_target_pairs={{0,8},{4,20},{8,0},{12,28},{16,24},{20,4},{24,16},{28,12},{1,9},{5... | collective-permute-start | bytes 3145736 | tf_op jit(solution)/shard_map/ppermute | solution.py:65
  66.0 3.4 %copy-start.8 = (bf16[1024,4096]{1,0:T(8,128)(2,1)S(1)}, bf16[1024,4096]{1,0:T(8,128)(2,1)}, u32[]{:S(2)}) copy-start(bf16[1024,4096]{1,0:T(8,128)(2,1)} %copy-done.7) | copy-start | bytes 25165828
  69.4 11.2 %copy-start.18 = (bf16[512,1024]{1,0:T(8,128)(2,1)S(1)}, bf16[512,1024]{1,0:T(8,128)(2,1)}, u32[]{:S(2)}) copy-start(bf16[512,1024]{1,0:T(8,128)(2,1)} %all-gather.3.cloned.1.call-done) | copy-start | bytes 3145732
  74.5 33.3 %copy-start.19 = (bf16[4096]{0:T(1024)(128)(2,1)S(1)}, bf16[4096]{0:T(1024)(128)(2,1)}, u32[]{:S(2)}) copy-start(bf16[4096]{0:T(1024)(128)(2,1)} %param.18) | copy-start | bytes 24580
  74.5 33.5 %copy-start.20 = (s32[4,2]{0,1:T(2,128)S(1)}, s32[4,2]{0,1:T(2,128)}, u32[]{:S(2)}) copy-start(s32[4,2]{0,1:T(2,128)} %param.24) | copy-start | bytes 100
  74.5 33.5 %copy-start.21 = (s32[4,2]{0,1:T(2,128)S(1)}, s32[4,2]{0,1:T(2,128)}, u32[]{:S(2)}) copy-start(s32[4,2]{0,1:T(2,128)} %param.25) | copy-start | bytes 100
  74.5 39.7 %copy-start.16 = (bf16[1024,1024]{1,0:T(8,128)(2,1)S(1)}, bf16[1024,1024]{1,0:T(8,128)(2,1)}, u32[]{:S(2)}) copy-start(bf16[1024,1024]{1,0:T(8,128)(2,1)} %refs_8_.1) | copy-start | bytes 6291460
  80.6 14.9 %collective-permute-start.2 = (bf16[4,128,1024]{2,1,0:T(8,128)(2,1)S(1)}, bf16[4,128,1024]{2,1,0:T(8,128)(2,1)}, u32[]{:S(2)}, u32[]{:S(2)}) collective-permute-start(bf16[4,128,1024]{2,1,0:T(8,128)(2,1)S(1)} %bitcast.37), channel_id=1, source_target_pairs={{0,16},{4,12},{8,24},{12,4},{16,0},{20,28},{24,8},{28,20},{1,17},{... | collective-permute-start | bytes 3145736 | tf_op jit(solution)/shard_map/ppermute | solution.py:65
  81.1 25.6 %collective-permute-start.3 = (bf16[4,128,1024]{2,1,0:T(8,128)(2,1)}, bf16[4,128,1024]{2,1,0:T(8,128)(2,1)}, u32[]{:S(2)}, u32[]{:S(2)}) collective-permute-start(bf16[4,128,1024]{2,1,0:T(8,128)(2,1)} %collective-permute-done.1), channel_id=1, source_target_pairs={{0,16},{4,12},{8,24},{12,4},{16,0},{20,28},{24,8},{28,20},{1,17},{... | collective-permute-start | bytes 3145736 | tf_op jit(solution)/shard_map/ppermute | solution.py:65
  106.7 4.3 %collective-permute-start.4 = (bf16[4,128,1024]{2,1,0:T(8,128)(2,1)S(1)}, bf16[4,128,1024]{2,1,0:T(8,128)(2,1)}, u32[]{:S(2)}, u32[]{:S(2)}) collective-permute-start(bf16[4,128,1024]{2,1,0:T(8,128)(2,1)S(1)} %bitcast.38), channel_id=1, source_target_pairs={{0,4},{4,0},{8,12},{12,8},{16,20},{20,16},{24,28},{28,24},{1,5},{5... | collective-permute-start | bytes 3145736 | tf_op jit(solution)/shard_map/ppermute | solution.py:65
  106.7 4.5 %collective-permute-start.5 = (bf16[4,128,1024]{2,1,0:T(8,128)(2,1)}, bf16[4,128,1024]{2,1,0:T(8,128)(2,1)}, u32[]{:S(2)}, u32[]{:S(2)}) collective-permute-start(bf16[4,128,1024]{2,1,0:T(8,128)(2,1)} %collective-permute-done.1), channel_id=1, source_target_pairs={{0,4},{4,0},{8,12},{12,8},{16,20},{20,16},{24,28},{28,24},{1,5},{5... | collective-permute-start | bytes 3145736 | tf_op jit(solution)/shard_map/ppermute | solution.py:65
  107.2 5.5 %collective-permute-start.6 = (bf16[4,128,1024]{2,1,0:T(8,128)(2,1)}, bf16[4,128,1024]{2,1,0:T(8,128)(2,1)}, u32[]{:S(2)}, u32[]{:S(2)}) collective-permute-start(bf16[4,128,1024]{2,1,0:T(8,128)(2,1)} %collective-permute-done.2), channel_id=1, source_target_pairs={{0,4},{4,0},{8,12},{12,8},{16,20},{20,16},{24,28},{28,24},{1,5},{5... | collective-permute-start | bytes 3145736 | tf_op jit(solution)/shard_map/ppermute | solution.py:65
  107.2 7.0 %collective-permute-start.7 = (bf16[4,128,1024]{2,1,0:T(8,128)(2,1)}, bf16[4,128,1024]{2,1,0:T(8,128)(2,1)}, u32[]{:S(2)}, u32[]{:S(2)}) collective-permute-start(bf16[4,128,1024]{2,1,0:T(8,128)(2,1)} %collective-permute-done.3), channel_id=1, source_target_pairs={{0,4},{4,0},{8,12},{12,8},{16,20},{20,16},{24,28},{28,24},{1,5},{5... | collective-permute-start | bytes 3145736 | tf_op jit(solution)/shard_map/ppermute | solution.py:65
  114.2 1.6 copy-start.17
  123.4 3.3 %copy-start.2 = (bf16[4096,1024]{1,0:T(8,128)(2,1)}, bf16[4096,1024]{1,0:T(8,128)(2,1)S(1)}, u32[]{:S(2)}) copy-start(bf16[4096,1024]{1,0:T(8,128)(2,1)S(1)} %get-tuple-element.65.wq_ref) | copy-start | bytes 25165828
  126.7 3.2 %copy-start.4 = (bf16[1024,4096]{1,0:T(8,128)(2,1)}, bf16[1024,4096]{1,0:T(8,128)(2,1)S(1)}, u32[]{:S(2)}) copy-start(bf16[1024,4096]{1,0:T(8,128)(2,1)S(1)} %get-tuple-element.68.wo_ref) | copy-start | bytes 25165828
  130.0 1.5 copy-start.10
  131.5 1.5 copy-start.12
  168.7 3.4 %copy-start.3 = (bf16[4096,1024]{1,0:T(8,128)(2,1)S(1)}, bf16[4096,1024]{1,0:T(8,128)(2,1)}, u32[]{:S(2)}) copy-start(bf16[4096,1024]{1,0:T(8,128)(2,1)} %copy-done.2) | copy-start | bytes 25165828
  172.0 3.4 %copy-start.5 = (bf16[1024,4096]{1,0:T(8,128)(2,1)S(1)}, bf16[1024,4096]{1,0:T(8,128)(2,1)}, u32[]{:S(2)}) copy-start(bf16[1024,4096]{1,0:T(8,128)(2,1)} %copy-done.4) | copy-start | bytes 25165828
  175.4 1.7 copy-start.11
  177.2 1.7 copy-start.13
  178.9 1.6 copy-start.14
  180.5 1.6 copy-start.15
  192.6 1.3 copy-start.9
  195.0 13.2 %collective-permute-start.8 = (bf16[64,4096]{1,0:T(8,128)(2,1)}, bf16[64,4096]{1,0:T(8,128)(2,1)S(1)}, u32[]{:S(2)}, u32[]{:S(2)}) collective-permute-start(bf16[64,4096]{1,0:T(8,128)(2,1)} %get-tuple-element.82), channel_id=1, source_target_pairs={{0,1},{4,5},{8,9},{12,13},{16,17},{20,21},{24,25},{28,29}} | collective-permute-start | bytes 1572872 | tf_op jit(solution)/shard_map/ppermute | solution.py:25
  197.0 11.2 %collective-permute-start.9 = (bf16[64,4096]{1,0:T(8,128)(2,1)}, bf16[64,4096]{1,0:T(8,128)(2,1)S(1)}, u32[]{:S(2)}, u32[]{:S(2)}) collective-permute-start(bf16[64,4096]{1,0:T(8,128)(2,1)} %get-tuple-element.81), channel_id=1, source_target_pairs={{3,2},{7,6},{11,10},{15,14},{19,18},{23,22},{27,26},{31,30}} | collective-permute-start | bytes 1572872 | tf_op jit(solution)/shard_map/ppermute | solution.py:25
  209.7 14.3 %collective-permute-start.10 = (bf16[64,4096]{1,0:T(8,128)(2,1)S(1)}, bf16[64,4096]{1,0:T(8,128)(2,1)}, u32[]{:S(2)}, u32[]{:S(2)}) collective-permute-start(bf16[64,4096]{1,0:T(8,128)(2,1)S(1)} %get-tuple-element.80), channel_id=1, source_target_pairs={{0,1},{1,2},{4,5},{5,6},{8,9},{9,10},{12,13},{13,14},{16,17},{17,1... | collective-permute-start | bytes 1572872 | tf_op jit(solution)/shard_map/ppermute | solution.py:25
  214.8 9.2 %collective-permute-start.11 = (bf16[64,4096]{1,0:T(8,128)(2,1)S(1)}, bf16[64,4096]{1,0:T(8,128)(2,1)}, u32[]{:S(2)}, u32[]{:S(2)}) collective-permute-start(bf16[64,4096]{1,0:T(8,128)(2,1)S(1)} %get-tuple-element.79), channel_id=1, source_target_pairs={{2,1},{3,2},{6,5},{7,6},{10,9},{11,10},{14,13},{15,14},{18,17},{19... | collective-permute-start | bytes 1572872 | tf_op jit(solution)/shard_map/ppermute | solution.py:25
  224.0 28.8 %copy-start.1 = (bf16[8,128,1024]{2,1,0:T(8,128)(2,1)S(1)}, bf16[8,128,1024]{2,1,0:T(8,128)(2,1)}, u32[]{:S(2)}) copy-start(bf16[8,128,1024]{2,1,0:T(8,128)(2,1)} %param.23) | copy-start | bytes 6291460
  226.9 18.4 %collective-permute-start.12 = (bf16[64,4096]{1,0:T(8,128)(2,1)}, bf16[64,4096]{1,0:T(8,128)(2,1)}, u32[]{:S(2)}, u32[]{:S(2)}) collective-permute-start(bf16[64,4096]{1,0:T(8,128)(2,1)} %get-tuple-element.78), channel_id=1, source_target_pairs={{0,1},{1,2},{2,3},{4,5},{5,6},{6,7},{8,9},{9,10},{10,11},{12,13},{... | collective-permute-start | bytes 1572872 | tf_op jit(solution)/shard_map/ppermute | solution.py:25
  236.7 13.5 %collective-permute-start.13 = (bf16[64,4096]{1,0:T(8,128)(2,1)}, bf16[64,4096]{1,0:T(8,128)(2,1)}, u32[]{:S(2)}, u32[]{:S(2)}) collective-permute-start(bf16[64,4096]{1,0:T(8,128)(2,1)} %get-tuple-element.77), channel_id=1, source_target_pairs={{1,0},{2,1},{3,2},{5,4},{6,5},{7,6},{9,8},{10,9},{11,10},{13,12},{... | collective-permute-start | bytes 1572872 | tf_op jit(solution)/shard_map/ppermute | solution.py:25
Sparse Core Ops, SparseCore 0:
  20.9 29.6 all-gather.2
  82.7 85.8 all-reduce.1

commit v7 on v5

v7 whole, which is shorter than its diff:
```python
import functools
import math

import jax
import jax.numpy as jnp
from jax import lax
from jax.experimental import pallas as pl
from jax.experimental.pallas import tpu as pltpu
from jax.sharding import PartitionSpec as P

HD = 128
SPAN = 64
NEIGH = 2
NLEN = 128
GROUP = NEIGH * NLEN

NEG_BIG = -1e30
LOG2E = 1.4426950408889634
VMEM_BYTES = 48 * 1024 * 1024
MIDDLE_BYTES = 36 * 1024 * 1024
BLOCK_BYTES = 14 * 1024 * 1024
SMALL_BYTES = 4 * 1024 * 1024


def shift(block, axis, distance, senders):
    size = lax.axis_size(axis)
    route = [(k, k + distance) for k in senders if 0 <= k + distance < size]
    return lax.ppermute(block, axis, route)


def far_blocks(blocks_ref, me, far):
    last = blocks_ref.shape[0] - 1
    return jnp.minimum(me + far, last), jnp.maximum(me - far, 0)


def add_kernel(info_ref, blocks_ref, up_ref, down_ref, up_out_ref, down_out_ref, *, far):
    above, below = far_blocks(blocks_ref, info_ref[0], far)
    rows = 16

    def add(at, carried):
        here = pl.ds(pl.multiple_of(at * rows, rows), rows)
        for index, ref, out_ref in ((above, up_ref, up_out_ref), (below, down_ref, down_out_ref)):
            out_ref[here, :] = (
                blocks_ref[index, here, :].astype(jnp.float32) + ref[here, :].astype(jnp.float32)
            ).astype(jnp.bfloat16)
        return carried

    lax.fori_loop(0, up_ref.shape[0] // rows, add, 0)


def add_step(info, blocks, up, down, far):
    vmem = pl.BlockSpec(memory_space=pltpu.VMEM)
    one = jax.ShapeDtypeStruct(up.shape, up.dtype)
    return pl.pallas_call(
        functools.partial(add_kernel, far=far),
        out_shape=[one, one],
        in_specs=[pl.BlockSpec(memory_space=pltpu.SMEM), vmem, vmem, vmem],
        out_specs=[vmem, vmem],
        compiler_params=pltpu.CompilerParams(vmem_limit_bytes=SMALL_BYTES),
        cost_estimate=pl.CostEstimate(
            flops=2 * up.size, bytes_accessed=12 * up.size, transcendentals=0
        ),
        name="add_step",
    )(info, blocks, up, down)


def reduce_scatter(info, blocks, up, down):
    size = lax.axis_size("db")
    for step in range(size - 1):
        if step:
            up, down = add_step(info, blocks, up, down, size - 1 - step)
        up = shift(up, "db", 1, range(step + 1))
        down = shift(down, "db", -1, range(size - 1 - step, size))
        up, down = lax.optimization_barrier((up, down))
    return up, down


def gather_step(carried, step):
    size = lax.axis_size("db")
    return (
        shift(carried[0], "db", 1, range(step, size)),
        shift(carried[1], "db", -1, range(0, size - step)),
    )


def gather(block, beside):
    size = lax.axis_size("db")
    carried, pieces = (block, block), []
    for step in range(size - 1):
        carried = gather_step(carried, step)
        if step == (size - 1) // 2:
            carried, beside = lax.optimization_barrier((carried, beside))
        else:
            carried = lax.optimization_barrier(carried)
        pieces.append(carried)
    return pieces, beside


def self_kernel(qkv_ref, out_ref, *, blocks, rows, scale):
    for block in range(blocks):
        query = qkv_ref[block, 0]
        live = (block + 1) * rows
        keys = qkv_ref[0 : block + 1, 1].reshape(live, HD)
        values = qkv_ref[0 : block + 1, 2].reshape(live, HD)
        scores = lax.dot_general(
            query, keys, (((1,), (1,)), ((), ())), preferred_element_type=jnp.float32
        )
        query_pos = block * rows + lax.broadcasted_iota(jnp.int32, (rows, live), 0)
        key_pos = lax.broadcasted_iota(jnp.int32, (rows, live), 1)
        scores = jnp.where(key_pos <= query_pos, scores * (scale * LOG2E), NEG_BIG)
        top = jnp.max(scores, axis=-1, keepdims=True)
        weights = jnp.exp2(scores - top)
        total = jnp.sum(weights, axis=-1, keepdims=True)
        mixed = jnp.dot(weights.astype(jnp.bfloat16), values, preferred_element_type=jnp.float32)
        out_ref[block] = (mixed / total).astype(jnp.bfloat16)


def self_attend_head(qkv, scale):
    blocks, _, rows, _ = qkv.shape
    return pl.pallas_call(
        functools.partial(self_kernel, blocks=blocks, rows=rows, scale=scale),
        out_shape=jax.ShapeDtypeStruct((blocks, rows, HD), jnp.bfloat16),
        in_specs=[pl.BlockSpec(memory_space=pltpu.VMEM)],
        out_specs=pl.BlockSpec(memory_space=pltpu.VMEM),
        compiler_params=pltpu.CompilerParams(vmem_limit_bytes=VMEM_BYTES),
        cost_estimate=pl.CostEstimate(
            flops=2 * blocks * blocks * rows * rows * HD,
            bytes_accessed=8 * blocks * rows * HD,
            transcendentals=blocks * blocks * rows * rows // 2,
        ),
        name="self_attend",
    )(qkv)


def span_before(wanted):
    return shift(wanted[-1], "seq", 1, range(lax.axis_size("seq")))


def pack_kernel(index_ref, query_ref, key_ref, value_ref, part_ref, out_ref, part_out_ref):
    for which, ref in enumerate((query_ref, key_ref, value_ref)):
        for head in range(out_ref.shape[0]):
            out_ref[head, which] = ref[:, head * HD : (head + 1) * HD]
    part_out_ref[...] = part_ref[...]


def pack_heads(index, query_rows, key_rows, value_rows, encodings, piece):
    rows, width = query_rows.shape
    heads = width // HD
    depth = encodings.shape[1]
    steps = 4
    block, part = rows // steps, piece // steps
    row_block = pl.BlockSpec((block, width), lambda at, index_ref: (at, 0))
    return pl.pallas_call(
        pack_kernel,
        out_shape=[
            jax.ShapeDtypeStruct((heads, 3, rows, HD), jnp.bfloat16),
            jax.ShapeDtypeStruct((piece, depth), jnp.bfloat16),
        ],
        grid_spec=pltpu.PrefetchScalarGridSpec(
            num_scalar_prefetch=1,
            grid=(steps,),
            in_specs=[row_block] * 3
            + [pl.BlockSpec((part, depth), lambda at, index_ref: (index_ref[0] * steps + at, 0))],
            out_specs=[
                pl.BlockSpec((heads, 3, block, HD), lambda at, index_ref: (0, 0, at, 0)),
                pl.BlockSpec((part, depth), lambda at, index_ref: (at, 0)),
            ],
        ),
        compiler_params=pltpu.CompilerParams(
            vmem_limit_bytes=VMEM_BYTES, dimension_semantics=("arbitrary",)
        ),
        cost_estimate=pl.CostEstimate(
            flops=0, bytes_accessed=12 * rows * width, transcendentals=0
        ),
        name="pack_heads",
    )(index, query_rows, key_rows, value_rows, encodings)


def self_attention_gathered(query_rows, key_rows, value_rows, scale):
    rows, width = query_rows.shape
    heads = width // HD
    keys = lax.all_gather(key_rows, "seq", axis=0, tiled=True)
    values = lax.all_gather(value_rows, "seq", axis=0, tiled=True)
    count = keys.shape[0]
    query_pos = lax.axis_index("seq") * rows + jnp.arange(rows, dtype=jnp.int32)
    allowed = jnp.arange(count, dtype=jnp.int32)[None, :] <= query_pos[:, None]
    scores = (
        jnp.einsum(
            "qhd,khd->hqk",
            query_rows.reshape(rows, heads, HD),
            keys.reshape(count, heads, HD),
            preferred_element_type=jnp.float32,
        )
        * scale
    )
    scores = jnp.where(allowed[None], scores, NEG_BIG)
    weights = jnp.exp(scores - jnp.max(scores, axis=-1, keepdims=True))
    total = jnp.sum(weights, axis=-1)
    mixed = jnp.einsum(
        "hqk,khd->hqd",
        weights.astype(jnp.bfloat16),
        values.reshape(count, heads, HD),
        preferred_element_type=jnp.float32,
    )
    return (mixed / total[..., None]).astype(jnp.bfloat16)


def self_out_kernel(
    info_ref, attended_ref, weight_hbm, out_ref, up_ref, down_ref, rows_ref, weight_ref, sum_ref, sems
):
    heads, rows, _ = attended_ref.shape
    n_db, share, features = out_ref.shape
    width = weight_hbm.shape[0]
    cuts = 4
    depth = width // cuts
    copies = [
        pltpu.make_async_copy(
            weight_hbm.at[pl.ds(k * depth, depth)], weight_ref.at[pl.ds(k * depth, depth)], sems.at[k]
        )
        for k in range(cuts)
    ]
    for copy in copies:
        copy.start()
    for head in range(heads):
        rows_ref[:, head * HD : (head + 1) * HD] = attended_ref[head]
    step = math.gcd(features, 512)

    def columns(at, carried, begin, end):
        here = pl.ds(pl.multiple_of(at * step, step), step)
        inner = slice(begin * depth, end * depth)
        product = jnp.dot(
            rows_ref[:, inner], weight_ref[inner, here], preferred_element_type=jnp.float32
        )
        if begin == 0:
            sum_ref[:, here] = product
            return carried
        product = (product + sum_ref[:, here]).astype(jnp.bfloat16)
        for owner in range(n_db):
            out_ref[owner, :, here] = product[owner * share : (owner + 1) * share]
        return carried

    for begin, end in ((0, cuts // 2), (cuts // 2, cuts)):
        for copy in copies[begin:end]:
            copy.wait()
        lax.fori_loop(
            0, features // step, functools.partial(columns, begin=begin, end=end), 0
        )
    above, below = far_blocks(out_ref, info_ref[0], n_db - 1)
    up_ref[...] = out_ref[above]
    down_ref[...] = out_ref[below]


def self_out(info, attended, weight, n_db):
    heads, rows, _ = attended.shape
    width, features = weight.shape
    share = rows // n_db
    vmem = pl.BlockSpec(memory_space=pltpu.VMEM)
    one = jax.ShapeDtypeStruct((share, features), jnp.bfloat16)
    return pl.pallas_call(
        self_out_kernel,
        out_shape=[jax.ShapeDtypeStruct((n_db, share, features), jnp.bfloat16), one, one],
        in_specs=[
            pl.BlockSpec(memory_space=pltpu.SMEM), vmem, pl.BlockSpec(memory_space=pl.ANY)
        ],
        out_specs=[vmem] * 3,
        scratch_shapes=[
            pltpu.VMEM((rows, width), jnp.bfloat16),
            pltpu.VMEM((width, features), jnp.bfloat16),
            pltpu.VMEM((rows, features), jnp.float32),
            pltpu.SemaphoreType.DMA((4,)),
        ],
        compiler_params=pltpu.CompilerParams(vmem_limit_bytes=VMEM_BYTES),
        cost_estimate=pl.CostEstimate(
            flops=2 * rows * width * features,
            bytes_accessed=2 * (rows * width + width * features + rows * features),
            transcendentals=0,
        ),
        name="self_out",
    )(info, attended, weight)


def norm_kernel(
    info_ref, blocks_ref, up_ref, down_ref, gain_ref, hidden_hbm, residual_ref, normed_ref, own_ref, sem
):
    me = info_ref[0]
    share = up_ref.shape[0]
    bring = pltpu.make_async_copy(
        hidden_hbm.at[pl.ds(pl.multiple_of(me * share, share), share)], own_ref, sem
    )
    bring.start()
    bring.wait()
    rows = 16

    def norm(at, carried):
        here = pl.ds(pl.multiple_of(at * rows, rows), rows)
        residual = own_ref[here, :].astype(jnp.float32) + blocks_ref[me, here, :].astype(jnp.float32)
        residual = residual + up_ref[here, :].astype(jnp.float32)
        residual = residual + down_ref[here, :].astype(jnp.float32)
        residual_ref[here, :] = residual
        mean_square = jnp.mean(residual * residual, axis=-1, keepdims=True)
        normed_ref[here, :] = (
            residual * lax.rsqrt(mean_square + 1e-05) * gain_ref[...].astype(jnp.float32)
        ).astype(jnp.bfloat16)
        return carried

    lax.fori_loop(0, share // rows, norm, 0)


def norm_share(info, blocks, up, down, gain, hidden):
    share, features = up.shape
    vmem = pl.BlockSpec(memory_space=pltpu.VMEM)
    return pl.pallas_call(
        norm_kernel,
        out_shape=[
            jax.ShapeDtypeStruct((share, features), jnp.float32),
            jax.ShapeDtypeStruct((share, features), jnp.bfloat16),
        ],
        in_specs=[pl.BlockSpec(memory_space=pltpu.SMEM)]
        + [vmem] * 4
        + [pl.BlockSpec(memory_space=pl.ANY)],
        out_specs=[vmem, vmem],
        scratch_shapes=[pltpu.VMEM((share, features), jnp.bfloat16), pltpu.SemaphoreType.DMA],
        compiler_params=pltpu.CompilerParams(vmem_limit_bytes=SMALL_BYTES),
        cost_estimate=pl.CostEstimate(
            flops=8 * up.size, bytes_accessed=16 * up.size, transcendentals=0
        ),
        name="norm_share",
    )(info, blocks, up, down, gain, hidden)


def project_kernel(where_ref, *refs, cuts):
    wk_hbm, wv_hbm, wq_hbm, wo_hbm, keys_ref, values_ref, wq_ref, wo_ref = refs[-12:-4]
    rows_ref, wk_ref, wv_ref, sems = refs[-4:]
    (table,) = refs[:-12]
    entries = keys_ref.shape[0] // NLEN
    piece = NLEN // cuts
    bring = [
        pltpu.make_async_copy(source, target, sems.at[entries * cuts + at])
        for at, (source, target) in enumerate(
            ((wk_hbm, wk_ref), (wv_hbm, wv_ref), (wq_hbm, wq_ref), (wo_hbm, wo_ref))
        )
    ]
    for copy in bring[:2]:
        copy.start()

    def entry_copy(entry, cut):
        row, shard = where_ref[2 + 2 * entry], where_ref[3 + 2 * entry]
        return pltpu.make_async_copy(
            table.at[row * cuts + cut, shard],
            rows_ref.at[pl.ds(entry * NLEN + cut * piece, piece)],
            sems.at[entry * cuts + cut],
        )

    for entry in range(entries):
        for cut in range(cuts):
            entry_copy(entry, cut).start()

    for copy in bring[2:]:
        copy.start()
    for copy in bring[:2]:
        copy.wait()
    width = keys_ref.shape[1]
    step = math.gcd(width, 512)
    for group in range(entries // NEIGH):
        for entry in range(NEIGH * group, NEIGH * (group + 1)):
            for cut in range(cuts):
                entry_copy(entry, cut).wait()
        here = slice(group * GROUP, (group + 1) * GROUP)
        for at in range(0, width, step):
            lanes = slice(at, at + step)
            for weight, made in ((wk_ref, keys_ref), (wv_ref, values_ref)):
                made[here, lanes] = jnp.dot(
                    rows_ref[here, :], weight[:, lanes], preferred_element_type=jnp.float32
                ).astype(jnp.bfloat16)
    for copy in bring[2:]:
        copy.wait()


def project_encodings(info, table, w_cross_k, w_cross_v, w_cross_q, w_cross_out):
    entries = (info.shape[0] - 2) // 2
    piece, depth = table.shape[2:]
    cuts = NLEN // piece
    width = w_cross_k.shape[1]
    vmem = pl.BlockSpec(memory_space=pltpu.VMEM)
    anywhere = pl.BlockSpec(memory_space=pl.ANY)
    made = jax.ShapeDtypeStruct((entries * NLEN, width), jnp.bfloat16)
    return pl.pallas_call(
        functools.partial(project_kernel, cuts=cuts),
        out_shape=[made, made]
        + [jax.ShapeDtypeStruct(one.shape, one.dtype) for one in (w_cross_q, w_cross_out)],
        in_specs=[pl.BlockSpec(memory_space=pltpu.SMEM)] + [anywhere] * 5,
        out_specs=[vmem] * 4,
        scratch_shapes=[
            pltpu.VMEM((entries * NLEN, depth), jnp.bfloat16),
            pltpu.VMEM(w_cross_k.shape, jnp.bfloat16),
            pltpu.VMEM(w_cross_v.shape, jnp.bfloat16),
            pltpu.SemaphoreType.DMA((entries * cuts + 4,)),
        ],
        compiler_params=pltpu.CompilerParams(vmem_limit_bytes=MIDDLE_BYTES),
        cost_estimate=pl.CostEstimate(
            flops=4 * entries * NLEN * depth * width,
            bytes_accessed=2 * (entries * NLEN * depth + 2 * depth * width + 2 * w_cross_q.size),
            transcendentals=0,
        ),
        name="project_encodings",
    )(info, table, w_cross_k, w_cross_v, w_cross_q, w_cross_out)


def apart_heads(query):
    first = lax.broadcasted_iota(jnp.int32, query.shape, 1) < HD
    nothing = jnp.zeros_like(query)
    return jnp.concatenate(
        (jnp.where(first, query, nothing), jnp.where(first, nothing, query)), axis=0
    )


def together_heads(mixed):
    rows = mixed.shape[0] // 2
    first = lax.broadcasted_iota(jnp.int32, (rows, 2 * HD), 1) < HD
    return jnp.where(first, mixed[:rows], mixed[rows:])


def cross_kernel(info_ref, own_ref, *refs, scale):
    wq_ref, keys_ref, values_ref, wo_ref, out_ref, up_ref, down_ref = refs[-10:-3]
    rows_ref, query_ref, mixed_ref = refs[-3:]
    pieces = refs[:-10]
    share, features = own_ref.shape
    width = wq_ref.shape[1]
    n_db = out_ref.shape[0]
    pairs = width // HD // 2
    tail = 16
    for me in range(n_db):

        @pl.when(info_ref[0] == me)
        def _(me=me):
            for owner in range(n_db):
                if owner == me:
                    source = own_ref
                elif owner < me:
                    source = pieces[2 * (me - owner - 1)]
                else:
                    source = pieces[2 * (owner - me - 1) + 1]
                rows_ref[owner * share : (owner + 1) * share, :] = source[...]

    lanes = [slice(2 * pair * HD, 2 * (pair + 1) * HD) for pair in range(pairs)]
    for at in lanes:
        query_ref[:, at] = jnp.dot(
            rows_ref[...], wq_ref[:, at], preferred_element_type=jnp.float32
        ).astype(jnp.bfloat16)
    row = lax.broadcasted_iota(jnp.int32, (tail, 2 * HD), 0)
    spans = n_db * share // SPAN
    for span in range(spans):
        top = span * SPAN
        here, after = (slice((span + k) * GROUP, (span + k + 1) * GROUP) for k in (0, 1))
        work = [(slice(top, top + SPAN), here, at) for at in lanes]
        work += [(slice(top + SPAN - tail, top + SPAN), after, at) for at in lanes]
        scores = [
            lax.dot_general(
                apart_heads(query_ref[of, at]),
                keys_ref[which, at],
                (((1,), (1,)), ((), ())),
                preferred_element_type=jnp.float32,
            )
            * (scale * LOG2E)
            for of, which, at in work
        ]
        tops = [jnp.max(one, axis=-1, keepdims=True) for one in scores]
        weights = [jnp.exp2(one - top_one) for one, top_one in zip(scores, tops)]
        totals = [jnp.sum(one, axis=-1, keepdims=True) for one in weights]
        mixed = [
            jnp.dot(
                one.astype(jnp.bfloat16), values_ref[which, at], preferred_element_type=jnp.float32
            )
            for one, (_, which, at) in zip(weights, work)
        ]
        mixed = [together_heads(one / total) for one, total in zip(mixed, totals)]
        for pair, at in enumerate(lanes):
            main, last = mixed[pair], mixed[pairs + pair]
            if span == 0:
                main = jnp.where(info_ref[1] > 0, main, 0.0)
            last = jnp.where(row == tail - 1, last, main[SPAN - tail :])
            mixed_ref[top : top + SPAN - tail, at] = main[: SPAN - tail].astype(jnp.bfloat16)
            mixed_ref[top + SPAN - tail : top + SPAN, at] = last.astype(jnp.bfloat16)
    step = math.gcd(features, 512)

    def columns(at, carried):
        here = pl.ds(pl.multiple_of(at * step, step), step)
        product = jnp.dot(mixed_ref[...], wo_ref[:, here], preferred_element_type=jnp.float32)
        product = product.astype(jnp.bfloat16)
        for owner in range(n_db):
            out_ref[owner, :, here] = product[owner * share : (owner + 1) * share]
        return carried

    lax.fori_loop(0, features // step, columns, 0)
    above, below = far_blocks(out_ref, info_ref[0], n_db - 1)
    up_ref[...] = out_ref[above]
    down_ref[...] = out_ref[below]


def cross_block(info, normed, pieces, w_cross_q, keys, values, w_cross_out, n_db, scale):
    share, features = normed.shape
    width = w_cross_q.shape[1]
    rows = n_db * share
    vmem = pl.BlockSpec(memory_space=pltpu.VMEM)
    one = jax.ShapeDtypeStruct((share, features), jnp.bfloat16)
    flat = [one for pair in pieces for one in pair]
    return pl.pallas_call(
        functools.partial(cross_kernel, scale=scale),
        out_shape=[jax.ShapeDtypeStruct((n_db, share, features), jnp.bfloat16), one, one],
        in_specs=[pl.BlockSpec(memory_space=pltpu.SMEM)] + [vmem] * (5 + len(flat)),
        out_specs=[vmem] * 3,
        scratch_shapes=[
            pltpu.VMEM((rows, features), jnp.bfloat16),
            pltpu.VMEM((rows, width), jnp.bfloat16),
            pltpu.VMEM((rows, width), jnp.bfloat16),
        ],
        compiler_params=pltpu.CompilerParams(vmem_limit_bytes=BLOCK_BYTES),
        cost_estimate=pl.CostEstimate(
            flops=4 * rows * width * (features + GROUP),
            bytes_accessed=4 * width * (features + keys.shape[0]) + 4 * rows * features,
            transcendentals=rows * GROUP * width // HD,
        ),
        name="cross_block",
    )(info, normed, *flat, w_cross_q, keys, values, w_cross_out)


def per_device(
    hidden_in,
    query_rows,
    key_rows,
    value_rows,
    w_self_out,
    norm_gain,
    w_cross_q,
    w_cross_k,
    w_cross_v,
    w_cross_out,
    enc_table,
    nb_shard,
    nb_row,
):
    features = hidden_in.shape[1]
    heads = query_rows.shape[1] // HD
    n_seq, n_db = lax.axis_size("seq"), lax.axis_size("db")
    seq_index, db_index = lax.axis_index("seq"), lax.axis_index("db")
    scale = 1.0 / math.sqrt(HD)

    rows_shard, _, depth = enc_table.shape
    encodings = enc_table.reshape(rows_shard * NLEN, depth)
    piece = rows_shard * NLEN // n_seq
    packed, part = pack_heads(
        seq_index.reshape(1).astype(jnp.int32), query_rows, key_rows, value_rows, encodings, piece
    )
    along_db = lax.all_gather(part, "db", axis=0)

    packed, nb_row, nb_shard = lax.optimization_barrier((packed, nb_row, nb_shard))
    wanted = jnp.stack((nb_row, nb_shard), axis=-1).astype(jnp.int32)
    place = jnp.stack((db_index, (seq_index > 0).astype(jnp.int32))).astype(jnp.int32)
    info = jnp.concatenate((place, span_before(wanted).reshape(-1), wanted.reshape(-1)))
    if heads == n_seq:
        held = lax.all_to_all(packed, "seq", 0, 0, tiled=True)
        held, info = lax.optimization_barrier((held, info))
        attended = lax.all_to_all(self_attend_head(held, scale), "seq", 0, 0, tiled=True)
    else:
        attended = self_attention_gathered(query_rows, key_rows, value_rows, scale)

    along_db, attended = lax.optimization_barrier((along_db, attended))
    table = lax.all_gather(along_db, "seq", axis=0)

    partial, up, down = self_out(info, attended, w_self_out, n_db)
    up, down = reduce_scatter(info, partial, up, down)
    residual, normed = norm_share(
        info, partial, up, down, norm_gain.reshape(1, features), hidden_in
    )
    projected = project_encodings(info, table, w_cross_k, w_cross_v, w_cross_q, w_cross_out)
    pieces, (keys, values, w_cross_q, w_cross_out) = gather(normed, projected)
    partial, up, down = cross_block(
        info, normed, pieces, w_cross_q, keys, values, w_cross_out, n_db, scale
    )
    up, down = reduce_scatter(info, partial, up, down)
    own = lax.dynamic_index_in_dim(partial, db_index, 0, keepdims=False).astype(jnp.float32)
    return residual + own + up.astype(jnp.float32) + down.astype(jnp.float32)


def solution(mesh):
    placed = (
        P("seq", None),
        P("seq", "db"),
        P("seq", "db"),
        P("seq", "db"),
        P("db", None),
        P(),
        P(None, "db"),
        P(None, "db"),
        P(None, "db"),
        P("db", None),
        P("db", None, None),
        P("seq", None),
        P("seq", None),
    )
    return jax.shard_map(
        per_device, mesh=mesh, in_specs=placed, out_specs=P(("seq", "db"), None), check_vma=False
    )
```

time: 226 us -> 232 us (1.027)
  other arithmetic: 8.52 us -> 2.54 us
  Pallas kernels: 37.8 us -> 42.5 us
  waiting for transfers between devices: 99.7 us -> 103 us
  local copies, waits for them, and re-layouts: 7.74 us -> 10.9 us
    convert_element_type x6 -> x0, other arithmetic: 5.03 us -> none  [the longest x4 4.85 us: add_rounded(): (first.astype(jnp.float32) + second.astype(jnp.float32)).astype(jnp.bfloa...]
    unnamed x18 -> x26, local copies, waits for them, and re-layouts: 5.57 us -> 10.5 us
    pallas_call x4 -> x9, Pallas kernels: 32.3 us -> 37 us  [the longest x1 11.7 us: project_encodings(): pl.pallas_call(functools.partial(project_kernel, cuts=cuts), out_shape=[m...]
    ppermute x19, waiting for transfers between devices: 72.5 us -> 75.7 us  [shift(): return lax.ppermute(block, axis, route)]
  transfers between devices with their start and end apart: 23 -> 23, of which waited for: 16 -> 16; matrix products, arithmetic and copies ran while one was open for 3% -> 0% of each run, Pallas kernels for 10% -> 12%
where the time goes in v7:
time: 232 us; the launch traced here: 231 us
  waiting for transfers between devices  103 us (44%)
  starting transfers between devices  58.4 us (25%)
  Pallas kernels  42.5 us (18%)
  between operations  13.7 us (6%)
  local copies, waits for them, and re-layouts  10.9 us (5%)
  other arithmetic  2.54 us (1%)
    ppermute x19, waiting for transfers between devices, shift(): return lax.ppermute(block, axis, route)  75.7 us
    ppermute x19, starting transfers between devices, shift(): return lax.ppermute(block, axis, route)  49.5 us
    all_to_all x1, waiting for transfers between devices, per_device(): held = lax.all_to_all(packed, 'seq', 0, 0, tiled=True)  16.7 us
    pallas_call x1, Pallas kernels, project_encodings(): pl.pallas_call(functools.partial(project_kernel, cuts=cuts), out_shape=[m...  11.7 us
    unnamed x26, local copies, waits for them, and re-layouts  10.5 us
    pallas_call x1, Pallas kernels, cross_block(): pl.pallas_call(functools.partial(cross_kernel, scale=scale), out_shape=[j...  9.97 us
    pallas_call x1, Pallas kernels, self_out(): pl.pallas_call(self_out_kernel, out_shape=[jax.ShapeDtypeStruct((n_db, sh...  7.8 us
    all_to_all x1, waiting for transfers between devices, per_device(): lax.all_to_all(self_attend_head(held, scale), 'seq', 0, 0, tiled=True)  7.58 us
  transfers between devices with their start and end apart: 23, of which 16 were waited for; matrix products, arithmetic and copies ran while one was open for 0% of the time, Pallas kernels for 12%

profile of v7, /device:TPU:0, one launch (start us, length us, event | category | flops | bytes accessed | tf_op | source)
XLA Modules:
  0.0 230.8 jit_solution(7068051594525046300)
XLA Ops:
  6.5 1.6 copy-done.1
  8.1 1.0 copy-done.7
  9.2 1.0 copy-done.8
  10.2 1.0 copy-done.9
  11.3 1.9 pack_heads.1
  13.2 5.3 %all-to-all-start = ((bf16[8,3,256,128]{3,2,1,0:T(8,128)(2,1)}), bf16[8,3,256,128]{3,2,1,0:T(8,128)(2,1)S(1)}, u32[]{:S(2)}, u32[]{:S(2)}) async-start(bf16[8,3,256,128]{3,2,1,0:T(8,128)(2,1)} %get-tuple-element.57), calls=%async_computation | async-start | bytes 3145728 | tf_op jit(solution)/shard_map/all_to_all | solution.py:561
  18.5 0.0 all-gather.5.cloned.1.call-start
  18.5 0.7 all-gather.5.cloned.1.call-update
  19.2 0.1 fusion.2
  19.3 0.1 copy.18
  19.4 2.4 %collective-permute-start = (s32[2,2]{1,0:T(2,128)S(1)}, s32[2,2]{1,0:T(2,128)S(1)}, u32[]{:S(2)}, u32[]{:S(2)}) collective-permute-start(s32[2,2]{1,0:T(2,128)S(1)} %bitcast.19), channel_id=1, source_target_pairs={{0,4},{4,8},{8,12},{12,16},{16,20},{20,24},{24,28},{1,5},{5,9},{9,... | collective-permute-start | bytes 56 | tf_op jit(solution)/shard_map/ppermute | solution.py:28
  21.8 0.1 copy.19
  21.9 0.1 reshape.20
  22.0 0.6 collective-permute-done
  22.6 0.1 reshape.19
  22.7 0.1 pad_add_fusion.1.info_ref.where_ref
  22.8 16.7 %all-to-all-done.qkv_ref = bf16[8,3,256,128]{3,2,1,0:T(8,128)(2,1)S(1)} async-done(((bf16[8,3,256,128]{3,2,1,0:T(8,128)(2,1)}), bf16[8,3,256,128]{3,2,1,0:T(8,128)(2,1)S(1)}, u32[]{:S(2)}, u32[]{:S(2)}) %all-to-all-start) | async-done | bytes 1572896 | tf_op jit(solution)/shard_map/all_to_all | solution.py:561
  39.5 5.5 %self_attend.1 = bf16[8,256,128]{2,1,0:T(8,128)(2,1)} custom-call(bf16[8,3,256,128]{3,2,1,0:T(8,128)(2,1)S(1)} %all-to-all-done.qkv_ref), custom_call_target="tpu_custom_call" | custom-call | flops 1073741824 | bytes 2097152 | tf_op jit(solution)/shard_map/self_attend/pallas_call | solution.py:120
  45.0 3.5 %all-to-all-start.1 = ((bf16[8,256,128]{2,1,0:T(8,128)(2,1)}), bf16[8,256,128]{2,1,0:T(8,128)(2,1)S(1)}, u32[]{:S(2)}, u32[]{:S(2)}) async-start(bf16[8,256,128]{2,1,0:T(8,128)(2,1)} %self_attend.1), calls=%async_computation.1 | async-start | bytes 1048576 | tf_op jit(solution)/shard_map/all_to_all | solution.py:563
  48.5 0.0 all-gather.7.cloned.1.call-start
  48.5 2.0 all-gather.5.cloned.1.call-done
  50.6 7.6 %all-to-all-done.1.attended_ref = bf16[8,256,128]{2,1,0:T(8,128)(2,1)S(1)} async-done(((bf16[8,256,128]{2,1,0:T(8,128)(2,1)}), bf16[8,256,128]{2,1,0:T(8,128)(2,1)S(1)}, u32[]{:S(2)}, u32[]{:S(2)}) %all-to-all-start.1) | async-done | bytes 524320 | tf_op jit(solution)/shard_map/all_to_all | solution.py:563
  58.2 7.8 %self_out.1 = (bf16[4,64,4096]{2,1,0:T(8,128)(2,1)S(1)}, bf16[64,4096]{1,0:T(8,128)(2,1)S(1)}, bf16[64,4096]{1,0:T(8,128)(2,1)S(1)}) custom-call(s32[22]{0:T(128)S(1)} %pad_add_fusion.1.info_ref.where_ref, bf16[8,256,128]{2,1,0:T(8,128)(2,1)S(1)} %all-to-all-done.1.attended_ref, bf16[1024,4096]{1,0:T(8,128)(2,1)} %weight_hbm.1), custom_call_target="tpu_custom_call" | custom-call | flops 2147483648 | bytes 11010048 | tf_op jit(solution)/shard_map/self_out/pallas_call | solution.py:259
  66.0 3.5 %collective-permute-start.1 = (bf16[64,4096]{1,0:T(8,128)(2,1)S(1)}, bf16[64,4096]{1,0:T(8,128)(2,1)S(1)}, u32[]{:S(2)}, u32[]{:S(2)}) collective-permute-start(bf16[64,4096]{1,0:T(8,128)(2,1)S(1)} %get-tuple-element.65), channel_id=1, source_target_pairs={{0,1},{4,5},{8,9},{12,13},{16,17},{20,21},{24,25},{28,29}} | collective-permute-start | bytes 1572872 | tf_op jit(solution)/shard_map/ppermute | solution.py:28
  69.5 0.7 collective-permute-start.2
  70.2 8.1 %collective-permute-done.1.up_ref = bf16[64,4096]{1,0:T(8,128)(2,1)S(1)} collective-permute-done((bf16[64,4096]{1,0:T(8,128)(2,1)S(1)}, bf16[64,4096]{1,0:T(8,128)(2,1)S(1)}, u32[]{:S(2)}, u32[]{:S(2)}) %collective-permute-start.1) | collective-permute-done | bytes 524320 | tf_op jit(solution)/shard_map/ppermute | solution.py:28
  78.3 0.8 add_step.4
  79.1 4.5 %collective-permute-start.3 = (bf16[64,4096]{1,0:T(8,128)(2,1)S(1)}, bf16[64,4096]{1,0:T(8,128)(2,1)S(1)}, u32[]{:S(2)}, u32[]{:S(2)}) collective-permute-start(bf16[64,4096]{1,0:T(8,128)(2,1)S(1)} %get-tuple-element.69), channel_id=1, source_target_pairs={{0,1},{1,2},{4,5},{5,6},{8,9},{9,10},{12,13},{13,14},{16,17},{17,1... | collective-permute-start | bytes 1572872 | tf_op jit(solution)/shard_map/ppermute | solution.py:28
  83.7 0.7 collective-permute-start.4
  84.4 7.3 %collective-permute-done.3.up_ref = bf16[64,4096]{1,0:T(8,128)(2,1)S(1)} collective-permute-done((bf16[64,4096]{1,0:T(8,128)(2,1)S(1)}, bf16[64,4096]{1,0:T(8,128)(2,1)S(1)}, u32[]{:S(2)}, u32[]{:S(2)}) %collective-permute-start.3) | collective-permute-done | bytes 524320 | tf_op jit(solution)/shard_map/ppermute | solution.py:28
  91.7 0.8 add_step.5
  92.5 8.3 %collective-permute-start.5 = (bf16[64,4096]{1,0:T(8,128)(2,1)S(1)}, bf16[64,4096]{1,0:T(8,128)(2,1)S(1)}, u32[]{:S(2)}, u32[]{:S(2)}) collective-permute-start(bf16[64,4096]{1,0:T(8,128)(2,1)S(1)} %get-tuple-element.73), channel_id=1, source_target_pairs={{0,1},{1,2},{2,3},{4,5},{5,6},{6,7},{8,9},{9,10},{10,11},{12,13},{... | collective-permute-start | bytes 1572872 | tf_op jit(solution)/shard_map/ppermute | solution.py:28
  100.8 1.3 collective-permute-start.6
  102.1 5.5 %collective-permute-done.5.up_ref = bf16[64,4096]{1,0:T(8,128)(2,1)S(1)} collective-permute-done((bf16[64,4096]{1,0:T(8,128)(2,1)S(1)}, bf16[64,4096]{1,0:T(8,128)(2,1)S(1)}, u32[]{:S(2)}, u32[]{:S(2)}) %collective-permute-start.5) | collective-permute-done | bytes 524320 | tf_op jit(solution)/shard_map/ppermute | solution.py:28
  107.7 4.2 %collective-permute-done.6.down_ref = bf16[64,4096]{1,0:T(8,128)(2,1)S(1)} collective-permute-done((bf16[64,4096]{1,0:T(8,128)(2,1)S(1)}, bf16[64,4096]{1,0:T(8,128)(2,1)S(1)}, u32[]{:S(2)}, u32[]{:S(2)}) %collective-permute-start.6) | collective-permute-done | bytes 524320 | tf_op jit(solution)/shard_map/ppermute | solution.py:28
  111.9 1.4 norm_share.1
  113.3 1.3 collective-permute-start.8
  114.6 5.4 %collective-permute-start.7 = (bf16[64,4096]{1,0:T(8,128)(2,1)S(1)}, bf16[64,4096]{1,0:T(8,128)(2,1)}, u32[]{:S(2)}, u32[]{:S(2)}) collective-permute-start(bf16[64,4096]{1,0:T(8,128)(2,1)S(1)} %get-tuple-element.78.own_ref), channel_id=1, source_target_pairs={{0,1},{1,2},{2,3},{4,5},{5,6},{6,7},{8,9},{9,10},{10,11},{12,13},{... | collective-permute-start | bytes 1572872 | tf_op jit(solution)/shard_map/ppermute | solution.py:28
  120.0 0.8 copy-done.5
  120.8 3.7 %collective-permute-done.8.refs_1_ = bf16[64,4096]{1,0:T(8,128)(2,1)} collective-permute-done((bf16[64,4096]{1,0:T(8,128)(2,1)S(1)}, bf16[64,4096]{1,0:T(8,128)(2,1)}, u32[]{:S(2)}, u32[]{:S(2)}) %collective-permute-start.8) | collective-permute-done | bytes 524320 | tf_op jit(solution)/shard_map/ppermute | solution.py:28
  124.5 1.4 collective-permute-done.7.refs_0_
  125.9 1.5 collective-permute-start.9
  127.3 1.3 collective-permute-start.10
  128.7 1.6 copy-done.4
  130.2 11.7 %project_encodings.1 = (bf16[1280,1024]{1,0:T(8,128)(2,1)S(1)}, bf16[1280,1024]{1,0:T(8,128)(2,1)S(1)}, bf16[4096,1024]{1,0:T(8,128)(2,1)S(1)}, bf16[1024,4096]{1,0:T(8,128)(2,1)}) custom-call(s32[22]{0:T(128)S(1)} %pad_add_fusion.1.info_ref.where_ref, bf16[8,4,128,1024]{3,2,1,0:T(8,128)(2,1)} %bitcast.13, bf16[1024,1024]{1,0:T(8,128)(2,1)S(1)} %copy-done.3, ...), custom_call_target="tpu_custom_call" | custom-call | flops 5368709120 | bytes 23592960 | tf_op jit(solution)/shard_map/project_encodings/pallas_call | solution.py:387
  141.9 0.3 collective-permute-done.10.refs_3_
  142.2 0.7 collective-permute-start.11
  142.9 1.5 collective-permute-start.12
  144.4 13.0 %collective-permute-done.12.refs_5_ = bf16[64,4096]{1,0:T(8,128)(2,1)S(1)} collective-permute-done((bf16[64,4096]{1,0:T(8,128)(2,1)}, bf16[64,4096]{1,0:T(8,128)(2,1)S(1)}, u32[]{:S(2)}, u32[]{:S(2)}) %collective-permute-start.12) | collective-permute-done | bytes 524320 | tf_op jit(solution)/shard_map/ppermute | solution.py:28
  157.5 3.4 %copy-done = bf16[1024,4096]{1,0:T(8,128)(2,1)S(1)} copy-done((bf16[1024,4096]{1,0:T(8,128)(2,1)S(1)}, bf16[1024,4096]{1,0:T(8,128)(2,1)}, u32[]{:S(2)}) %copy-start) | copy-done | bytes 8388632
  160.9 10.0 %cross_block.1 = (bf16[4,64,4096]{2,1,0:T(8,128)(2,1)S(1)}, bf16[64,4096]{1,0:T(8,128)(2,1)S(1)}, bf16[64,4096]{1,0:T(8,128)(2,1)S(1)}) custom-call(s32[22]{0:T(128)S(1)} %pad_add_fusion.1.info_ref.where_ref, bf16[64,4096]{1,0:T(8,128)(2,1)S(1)} %copy-done.6, bf16[64,4096]{1,0:T(8,128)(2,1)} %collective-permute-done.7.refs_0_, ...), custom_call_target="tpu_custom_call" | custom-call | flops 4563402752 | bytes 26214400 | tf_op jit(solution)/shard_map/cross_block/pallas_call | solution.py:507
  170.8 1.6 collective-permute-start.13
  172.4 0.7 collective-permute-start.14
  173.1 10.7 %collective-permute-done.13.up_ref = bf16[64,4096]{1,0:T(8,128)(2,1)S(1)} collective-permute-done((bf16[64,4096]{1,0:T(8,128)(2,1)S(1)}, bf16[64,4096]{1,0:T(8,128)(2,1)S(1)}, u32[]{:S(2)}, u32[]{:S(2)}) %collective-permute-start.13) | collective-permute-done | bytes 524320 | tf_op jit(solution)/shard_map/ppermute | solution.py:28
  183.8 0.8 add_step.6
  184.7 4.4 %collective-permute-start.15 = (bf16[64,4096]{1,0:T(8,128)(2,1)S(1)}, bf16[64,4096]{1,0:T(8,128)(2,1)S(1)}, u32[]{:S(2)}, u32[]{:S(2)}) collective-permute-start(bf16[64,4096]{1,0:T(8,128)(2,1)S(1)} %get-tuple-element.99), channel_id=1, source_target_pairs={{0,1},{1,2},{4,5},{5,6},{8,9},{9,10},{12,13},{13,14},{16,17},{17,1... | collective-permute-start | bytes 1572872 | tf_op jit(solution)/shard_map/ppermute | solution.py:28
  189.1 0.7 collective-permute-start.16
  189.8 10.7 %collective-permute-done.15.up_ref = bf16[64,4096]{1,0:T(8,128)(2,1)S(1)} collective-permute-done((bf16[64,4096]{1,0:T(8,128)(2,1)S(1)}, bf16[64,4096]{1,0:T(8,128)(2,1)S(1)}, u32[]{:S(2)}, u32[]{:S(2)}) %collective-permute-start.15) | collective-permute-done | bytes 524320 | tf_op jit(solution)/shard_map/ppermute | solution.py:28
  200.5 1.8 add_step.7
  202.3 7.9 %collective-permute-start.17 = (bf16[64,4096]{1,0:T(8,128)(2,1)}, bf16[64,4096]{1,0:T(8,128)(2,1)}, u32[]{:S(2)}, u32[]{:S(2)}) collective-permute-start(bf16[64,4096]{1,0:T(8,128)(2,1)} %get-tuple-element.103), channel_id=1, source_target_pairs={{0,1},{1,2},{2,3},{4,5},{5,6},{6,7},{8,9},{9,10},{10,11},{12,13},{... | collective-permute-start | bytes 1572872 | tf_op jit(solution)/shard_map/ppermute | solution.py:28
  210.2 1.3 collective-permute-start.18
  211.5 4.9 %collective-permute-done.17 = bf16[64,4096]{1,0:T(8,128)(2,1)} collective-permute-done((bf16[64,4096]{1,0:T(8,128)(2,1)}, bf16[64,4096]{1,0:T(8,128)(2,1)}, u32[]{:S(2)}, u32[]{:S(2)}) %collective-permute-start.17) | collective-permute-done | bytes 524320 | tf_op jit(solution)/shard_map/ppermute | solution.py:28
  216.3 5.2 %collective-permute-done.18 = bf16[64,4096]{1,0:T(8,128)(2,1)} collective-permute-done((bf16[64,4096]{1,0:T(8,128)(2,1)}, bf16[64,4096]{1,0:T(8,128)(2,1)}, u32[]{:S(2)}, u32[]{:S(2)}) %collective-permute-start.18) | collective-permute-done | bytes 524320 | tf_op jit(solution)/shard_map/ppermute | solution.py:28
  221.5 2.4 %fusion.1 = f32[64,4096]{1,0:T(8,128)} fusion(f32[64,4096]{1,0:T(8,128)S(1)} %get-tuple-element.77, bf16[64,4096]{1,0:T(8,128)(2,1)} %collective-permute-done.18, bf16[64,4096]{1,0:T(8,128)(2,1)} %collective-permute-done.17, bf16[4,64,4096]{2,1,0:T(8,128)(2,1)S(1)} %get-tuple-element.94.blocks_ref, s32[]{:T(128)S(6)} %select_n.4), kind=kLoop, calls=%fused_computation.2 | loop fusion | flops 1572864 | bytes 3670020 | tf_op jit(solution)/shard_map/add | solution.py:582
  (29 shorter events, 0.1 us)
Async XLA Ops:
  6.5 1.6 copy-start.1
  8.1 1.0 copy-start.7
  9.2 1.0 copy-start.8
  10.2 1.0 copy-start.9
  13.2 6.0 %copy-start.11 = (s32[4,2]{0,1:T(2,128)S(1)}, s32[4,2]{0,1:T(2,128)}, u32[]{:S(2)}) copy-start(s32[4,2]{0,1:T(2,128)} %param.24) | copy-start | bytes 100
  13.2 6.0 %copy-start.12 = (s32[4,2]{0,1:T(2,128)S(1)}, s32[4,2]{0,1:T(2,128)}, u32[]{:S(2)}) copy-start(s32[4,2]{0,1:T(2,128)} %param.25) | copy-start | bytes 100
  13.2 26.3 %all-to-all-start = ((bf16[8,3,256,128]{3,2,1,0:T(8,128)(2,1)}), bf16[8,3,256,128]{3,2,1,0:T(8,128)(2,1)S(1)}, u32[]{:S(2)}, u32[]{:S(2)}) async-start(bf16[8,3,256,128]{3,2,1,0:T(8,128)(2,1)} %get-tuple-element.57), calls=%async_computation | async-start | bytes 3145728 | tf_op jit(solution)/shard_map/all_to_all | solution.py:561
  18.5 32.1 %all-gather.5.cloned.1.call-start = ((), (), s32[]{:S(2)}) async-start(), calls=%async_computation.2 | async-start | bytes 1310720 | tf_op jit(solution)/shard_map/all_gather | solution.py:554
  19.4 3.2 %collective-permute-start = (s32[2,2]{1,0:T(2,128)S(1)}, s32[2,2]{1,0:T(2,128)S(1)}, u32[]{:S(2)}, u32[]{:S(2)}) collective-permute-start(s32[2,2]{1,0:T(2,128)S(1)} %bitcast.19), channel_id=1, source_target_pairs={{0,4},{4,8},{8,12},{12,16},{16,20},{20,24},{24,28},{1,5},{5,9},{9,... | collective-permute-start | bytes 56 | tf_op jit(solution)/shard_map/ppermute | solution.py:28
  45.0 13.2 %all-to-all-start.1 = ((bf16[8,256,128]{2,1,0:T(8,128)(2,1)}), bf16[8,256,128]{2,1,0:T(8,128)(2,1)S(1)}, u32[]{:S(2)}, u32[]{:S(2)}) async-start(bf16[8,256,128]{2,1,0:T(8,128)(2,1)} %self_attend.1), calls=%async_computation.1 | async-start | bytes 1048576 | tf_op jit(solution)/shard_map/all_to_all | solution.py:563
  48.5 80.2 %all-gather.7.cloned.1.call-start = ((), (), s32[]{:S(2)}) async-start(), calls=%async_computation.3 | async-start | bytes 9437184 | tf_op jit(solution)/shard_map/all_gather | solution.py:568
  66.0 12.3 %collective-permute-start.1 = (bf16[64,4096]{1,0:T(8,128)(2,1)S(1)}, bf16[64,4096]{1,0:T(8,128)(2,1)S(1)}, u32[]{:S(2)}, u32[]{:S(2)}) collective-permute-start(bf16[64,4096]{1,0:T(8,128)(2,1)S(1)} %get-tuple-element.65), channel_id=1, source_target_pairs={{0,1},{4,5},{8,9},{12,13},{16,17},{20,21},{24,25},{28,29}} | collective-permute-start | bytes 1572872 | tf_op jit(solution)/shard_map/ppermute | solution.py:28
  69.5 8.8 %collective-permute-start.2 = (bf16[64,4096]{1,0:T(8,128)(2,1)S(1)}, bf16[64,4096]{1,0:T(8,128)(2,1)S(1)}, u32[]{:S(2)}, u32[]{:S(2)}) collective-permute-start(bf16[64,4096]{1,0:T(8,128)(2,1)S(1)} %get-tuple-element.66), channel_id=1, source_target_pairs={{3,2},{7,6},{11,10},{15,14},{19,18},{23,22},{27,26},{31,30}} | collective-permute-start | bytes 1572872 | tf_op jit(solution)/shard_map/ppermute | solution.py:28
  79.1 23.0 %copy-start.10 = (bf16[4096]{0:T(1024)(128)(2,1)S(1)}, bf16[4096]{0:T(1024)(128)(2,1)}, u32[]{:S(2)}) copy-start(bf16[4096]{0:T(1024)(128)(2,1)} %param.18) | copy-start | bytes 24580
  79.1 32.8 %copy-start.2 = (bf16[256,4096]{1,0:T(8,128)(2,1)S(1)}, bf16[256,4096]{1,0:T(8,128)(2,1)}, u32[]{:S(2)}) copy-start(bf16[256,4096]{1,0:T(8,128)(2,1)} %hidden_hbm.1) | copy-start | bytes 6291460
  79.1 12.5 %collective-permute-start.3 = (bf16[64,4096]{1,0:T(8,128)(2,1)S(1)}, bf16[64,4096]{1,0:T(8,128)(2,1)S(1)}, u32[]{:S(2)}, u32[]{:S(2)}) collective-permute-start(bf16[64,4096]{1,0:T(8,128)(2,1)S(1)} %get-tuple-element.69), channel_id=1, source_target_pairs={{0,1},{1,2},{4,5},{5,6},{8,9},{9,10},{12,13},{13,14},{16,17},{17,1... | collective-permute-start | bytes 1572872 | tf_op jit(solution)/shard_map/ppermute | solution.py:28
  83.7 8.0 %collective-permute-start.4 = (bf16[64,4096]{1,0:T(8,128)(2,1)S(1)}, bf16[64,4096]{1,0:T(8,128)(2,1)S(1)}, u32[]{:S(2)}, u32[]{:S(2)}) collective-permute-start(bf16[64,4096]{1,0:T(8,128)(2,1)S(1)} %get-tuple-element.70), channel_id=1, source_target_pairs={{2,1},{3,2},{6,5},{7,6},{10,9},{11,10},{14,13},{15,14},{18,17},{19... | collective-permute-start | bytes 1572872 | tf_op jit(solution)/shard_map/ppermute | solution.py:28
  92.5 15.2 %collective-permute-start.5 = (bf16[64,4096]{1,0:T(8,128)(2,1)S(1)}, bf16[64,4096]{1,0:T(8,128)(2,1)S(1)}, u32[]{:S(2)}, u32[]{:S(2)}) collective-permute-start(bf16[64,4096]{1,0:T(8,128)(2,1)S(1)} %get-tuple-element.73), channel_id=1, source_target_pairs={{0,1},{1,2},{2,3},{4,5},{5,6},{6,7},{8,9},{9,10},{10,11},{12,13},{... | collective-permute-start | bytes 1572872 | tf_op jit(solution)/shard_map/ppermute | solution.py:28
  100.8 11.1 %collective-permute-start.6 = (bf16[64,4096]{1,0:T(8,128)(2,1)S(1)}, bf16[64,4096]{1,0:T(8,128)(2,1)S(1)}, u32[]{:S(2)}, u32[]{:S(2)}) collective-permute-start(bf16[64,4096]{1,0:T(8,128)(2,1)S(1)} %get-tuple-element.74), channel_id=1, source_target_pairs={{1,0},{2,1},{3,2},{5,4},{6,5},{7,6},{9,8},{10,9},{11,10},{13,12},{... | collective-permute-start | bytes 1572872 | tf_op jit(solution)/shard_map/ppermute | solution.py:28
  102.1 26.5 %copy-start.3 = (bf16[1024,1024]{1,0:T(8,128)(2,1)S(1)}, bf16[1024,1024]{1,0:T(8,128)(2,1)}, u32[]{:S(2)}) copy-start(bf16[1024,1024]{1,0:T(8,128)(2,1)} %refs_1_.1) | copy-start | bytes 6291460
  113.3 11.2 %collective-permute-start.8 = (bf16[64,4096]{1,0:T(8,128)(2,1)S(1)}, bf16[64,4096]{1,0:T(8,128)(2,1)}, u32[]{:S(2)}, u32[]{:S(2)}) collective-permute-start(bf16[64,4096]{1,0:T(8,128)(2,1)S(1)} %get-tuple-element.78.own_ref), channel_id=1, source_target_pairs={{1,0},{2,1},{3,2},{5,4},{6,5},{7,6},{9,8},{10,9},{11,10},{13,12},{... | collective-permute-start | bytes 1572872 | tf_op jit(solution)/shard_map/ppermute | solution.py:28
  114.6 11.2 %collective-permute-start.7 = (bf16[64,4096]{1,0:T(8,128)(2,1)S(1)}, bf16[64,4096]{1,0:T(8,128)(2,1)}, u32[]{:S(2)}, u32[]{:S(2)}) collective-permute-start(bf16[64,4096]{1,0:T(8,128)(2,1)S(1)} %get-tuple-element.78.own_ref), channel_id=1, source_target_pairs={{0,1},{1,2},{2,3},{4,5},{5,6},{6,7},{8,9},{9,10},{10,11},{12,13},{... | collective-permute-start | bytes 1572872 | tf_op jit(solution)/shard_map/ppermute | solution.py:28
  120.0 0.8 copy-start.5
  125.9 16.1 %collective-permute-start.9 = (bf16[64,4096]{1,0:T(8,128)(2,1)}, bf16[64,4096]{1,0:T(8,128)(2,1)}, u32[]{:S(2)}, u32[]{:S(2)}) collective-permute-start(bf16[64,4096]{1,0:T(8,128)(2,1)} %collective-permute-done.7.refs_0_), channel_id=1, source_target_pairs={{1,2},{2,3},{5,6},{6,7},{9,10},{10,11},{13,14},{14,15},{17,18},{18... | collective-permute-start | bytes 1572872 | tf_op jit(solution)/shard_map/ppermute | solution.py:28
  127.3 14.9 %collective-permute-start.10 = (bf16[64,4096]{1,0:T(8,128)(2,1)}, bf16[64,4096]{1,0:T(8,128)(2,1)}, u32[]{:S(2)}, u32[]{:S(2)}) collective-permute-start(bf16[64,4096]{1,0:T(8,128)(2,1)} %collective-permute-done.8.refs_1_), channel_id=1, source_target_pairs={{1,0},{2,1},{5,4},{6,5},{9,8},{10,9},{13,12},{14,13},{17,16},{18,1... | collective-permute-start | bytes 1572872 | tf_op jit(solution)/shard_map/ppermute | solution.py:28
  128.7 1.6 copy-start.4
  130.2 27.2 %copy-start.6 = (bf16[64,4096]{1,0:T(8,128)(2,1)S(1)}, bf16[64,4096]{1,0:T(8,128)(2,1)}, u32[]{:S(2)}) copy-start(bf16[64,4096]{1,0:T(8,128)(2,1)} %copy-done.5) | copy-start | bytes 1572868
  142.2 2.2 collective-permute-start.11
  142.9 14.5 %collective-permute-start.12 = (bf16[64,4096]{1,0:T(8,128)(2,1)}, bf16[64,4096]{1,0:T(8,128)(2,1)S(1)}, u32[]{:S(2)}, u32[]{:S(2)}) collective-permute-start(bf16[64,4096]{1,0:T(8,128)(2,1)} %collective-permute-done.10.refs_3_), channel_id=1, source_target_pairs={{1,0},{5,4},{9,8},{13,12},{17,16},{21,20},{25,24},{29,28}} | collective-permute-start | bytes 1572872 | tf_op jit(solution)/shard_map/ppermute | solution.py:28
  157.5 3.4 %copy-start = (bf16[1024,4096]{1,0:T(8,128)(2,1)S(1)}, bf16[1024,4096]{1,0:T(8,128)(2,1)}, u32[]{:S(2)}) copy-start(bf16[1024,4096]{1,0:T(8,128)(2,1)} %get-tuple-element.93.refs_9_) | copy-start | bytes 25165828
  170.8 13.0 %collective-permute-start.13 = (bf16[64,4096]{1,0:T(8,128)(2,1)S(1)}, bf16[64,4096]{1,0:T(8,128)(2,1)S(1)}, u32[]{:S(2)}, u32[]{:S(2)}) collective-permute-start(bf16[64,4096]{1,0:T(8,128)(2,1)S(1)} %get-tuple-element.95), channel_id=1, source_target_pairs={{0,1},{4,5},{8,9},{12,13},{16,17},{20,21},{24,25},{28,29}} | collective-permute-start | bytes 1572872 | tf_op jit(solution)/shard_map/ppermute | solution.py:28
  172.4 11.4 %collective-permute-start.14 = (bf16[64,4096]{1,0:T(8,128)(2,1)S(1)}, bf16[64,4096]{1,0:T(8,128)(2,1)S(1)}, u32[]{:S(2)}, u32[]{:S(2)}) collective-permute-start(bf16[64,4096]{1,0:T(8,128)(2,1)S(1)} %get-tuple-element.96), channel_id=1, source_target_pairs={{3,2},{7,6},{11,10},{15,14},{19,18},{23,22},{27,26},{31,30}} | collective-permute-start | bytes 1572872 | tf_op jit(solution)/shard_map/ppermute | solution.py:28
  184.7 15.8 %collective-permute-start.15 = (bf16[64,4096]{1,0:T(8,128)(2,1)S(1)}, bf16[64,4096]{1,0:T(8,128)(2,1)S(1)}, u32[]{:S(2)}, u32[]{:S(2)}) collective-permute-start(bf16[64,4096]{1,0:T(8,128)(2,1)S(1)} %get-tuple-element.99), channel_id=1, source_target_pairs={{0,1},{1,2},{4,5},{5,6},{8,9},{9,10},{12,13},{13,14},{16,17},{17,1... | collective-permute-start | bytes 1572872 | tf_op jit(solution)/shard_map/ppermute | solution.py:28
  189.1 11.4 %collective-permute-start.16 = (bf16[64,4096]{1,0:T(8,128)(2,1)S(1)}, bf16[64,4096]{1,0:T(8,128)(2,1)S(1)}, u32[]{:S(2)}, u32[]{:S(2)}) collective-permute-start(bf16[64,4096]{1,0:T(8,128)(2,1)S(1)} %get-tuple-element.100), channel_id=1, source_target_pairs={{2,1},{3,2},{6,5},{7,6},{10,9},{11,10},{14,13},{15,14},{18,17},{19... | collective-permute-start | bytes 1572872 | tf_op jit(solution)/shard_map/ppermute | solution.py:28
  202.3 14.0 %collective-permute-start.17 = (bf16[64,4096]{1,0:T(8,128)(2,1)}, bf16[64,4096]{1,0:T(8,128)(2,1)}, u32[]{:S(2)}, u32[]{:S(2)}) collective-permute-start(bf16[64,4096]{1,0:T(8,128)(2,1)} %get-tuple-element.103), channel_id=1, source_target_pairs={{0,1},{1,2},{2,3},{4,5},{5,6},{6,7},{8,9},{9,10},{10,11},{12,13},{... | collective-permute-start | bytes 1572872 | tf_op jit(solution)/shard_map/ppermute | solution.py:28
  210.2 11.4 %collective-permute-start.18 = (bf16[64,4096]{1,0:T(8,128)(2,1)}, bf16[64,4096]{1,0:T(8,128)(2,1)}, u32[]{:S(2)}, u32[]{:S(2)}) collective-permute-start(bf16[64,4096]{1,0:T(8,128)(2,1)} %get-tuple-element.104), channel_id=1, source_target_pairs={{1,0},{2,1},{3,2},{5,4},{6,5},{7,6},{9,8},{10,9},{11,10},{13,12},{... | collective-permute-start | bytes 1572872 | tf_op jit(solution)/shard_map/ppermute | solution.py:28
Sparse Core Ops, SparseCore 0:
  20.9 29.6 all-gather.4
  58.3 53.7 all-gather.6

commit v8 on v7

--- a/solution.py
+++ b/solution.py
@@ -17,8 +17,7 @@
 NEG_BIG = -1e30
 LOG2E = 1.4426950408889634
 VMEM_BYTES = 48 * 1024 * 1024
-MIDDLE_BYTES = 36 * 1024 * 1024
-BLOCK_BYTES = 14 * 1024 * 1024
+LARGE_BYTES = 58 * 1024 * 1024
 SMALL_BYTES = 4 * 1024 * 1024
 
 
@@ -28,71 +27,84 @@
     return lax.ppermute(block, axis, route)
 
 
-def far_blocks(blocks_ref, me, far):
-    last = blocks_ref.shape[0] - 1
-    return jnp.minimum(me + far, last), jnp.maximum(me - far, 0)
-
-
-def add_kernel(info_ref, blocks_ref, up_ref, down_ref, up_out_ref, down_out_ref, *, far):
-    above, below = far_blocks(blocks_ref, info_ref[0], far)
+def line_shift(block, lead, up_from, down_from):
+    n_seq, size = lax.axis_size("seq"), lax.axis_size("db")
+    route = []
+    for row in range(n_seq):
+        up = row % 2 == lead
+        for k in up_from if up else down_from:
+            other = k + 1 if up else k - 1
+            if 0 <= other < size:
+                route.append((row * size + k, row * size + other))
+    return lax.ppermute(block, ("seq", "db"), route)
+
+
+def far_block(blocks_ref, info_ref, lead, far):
+    way = 1 - 2 * (info_ref[2] ^ lead)
+    return jnp.clip(info_ref[0] + way * far, 0, blocks_ref.shape[0] - 1)
+
+
+def add_kernel(info_ref, blocks_ref, sum_ref, out_ref, *, lead, far):
+    index = far_block(blocks_ref, info_ref, lead, far)
     rows = 16
 
     def add(at, carried):
         here = pl.ds(pl.multiple_of(at * rows, rows), rows)
-        for index, ref, out_ref in ((above, up_ref, up_out_ref), (below, down_ref, down_out_ref)):
-            out_ref[here, :] = (
-                blocks_ref[index, here, :].astype(jnp.float32) + ref[here, :].astype(jnp.float32)
-            ).astype(jnp.bfloat16)
+        out_ref[here, :] = (
+            blocks_ref[index, here, :].astype(jnp.float32) + sum_ref[here, :].astype(jnp.float32)
+        ).astype(jnp.bfloat16)
         return carried
 
-    lax.fori_loop(0, up_ref.shape[0] // rows, add, 0)
-
-
-def add_step(info, blocks, up, down, far):
+    lax.fori_loop(0, sum_ref.shape[0] // rows, add, 0)
+
+
+def add_step(info, blocks, arrived, lead, far):
     vmem = pl.BlockSpec(memory_space=pltpu.VMEM)
-    one = jax.ShapeDtypeStruct(up.shape, up.dtype)
     return pl.pallas_call(
-        functools.partial(add_kernel, far=far),
-        out_shape=[one, one],
-        in_specs=[pl.BlockSpec(memory_space=pltpu.SMEM), vmem, vmem, vmem],
-        out_specs=[vmem, vmem],
+        functools.partial(add_kernel, lead=lead, far=far),
+        out_shape=jax.ShapeDtypeStruct(arrived.shape, arrived.dtype),
+        in_specs=[pl.BlockSpec(memory_space=pltpu.SMEM), vmem, vmem],
+        out_specs=vmem,
         compiler_params=pltpu.CompilerParams(vmem_limit_bytes=SMALL_BYTES),
         cost_estimate=pl.CostEstimate(
-            flops=2 * up.size, bytes_accessed=12 * up.size, transcendentals=0
+            flops=arrived.size, bytes_accessed=6 * arrived.size, transcendentals=0
         ),
         name="add_step",
-    )(info, blocks, up, down)
-
-
-def reduce_scatter(info, blocks, up, down):
+    )(info, blocks, arrived)
+
+
+def reduce_scatter(info, blocks, first, second):
     size = lax.axis_size("db")
     for step in range(size - 1):
+        senders = (range(step + 1), range(size - 1 - step, size))
         if step:
-            up, down = add_step(info, blocks, up, down, size - 1 - step)
-        up = shift(up, "db", 1, range(step + 1))
-        down = shift(down, "db", -1, range(size - 1 - step, size))
-        up, down = lax.optimization_barrier((up, down))
-    return up, down
-
-
-def gather_step(carried, step):
-    size = lax.axis_size("db")
-    return (
-        shift(carried[0], "db", 1, range(step, size)),
-        shift(carried[1], "db", -1, range(0, size - step)),
-    )
+            first = add_step(info, blocks, first, 0, size - 1 - step)
+            first, held = lax.optimization_barrier((first, held))
+        first_sent = first
+        first = line_shift(first, 0, *senders)
+        if step:
+            second = add_step(info, blocks, second, 1, size - 1 - step)
+        second, first_sent = lax.optimization_barrier((second, first_sent))
+        held = second
+        second = line_shift(second, 1, *senders)
+    return first, second
 
 
 def gather(block, beside):
     size = lax.axis_size("db")
-    carried, pieces = (block, block), []
+    first, second, pieces = block, block, []
     for step in range(size - 1):
-        carried = gather_step(carried, step)
-        if step == (size - 1) // 2:
-            carried, beside = lax.optimization_barrier((carried, beside))
-        else:
-            carried = lax.optimization_barrier(carried)
-        pieces.append(carried)
+        senders = (range(step, size), range(0, size - step))
+        if step == size // 2:
+            first, held, beside = lax.optimization_barrier((first, held, beside))
+        elif step:
+            first, held = lax.optimization_barrier((first, held))
+        first_sent = first
+        first = line_shift(first, 0, *senders)
+        second, first_sent = lax.optimization_barrier((second, first_sent))
+        held = second
+        second = line_shift(second, 1, *senders)
+        pieces.append((first, second))
     return pieces, beside
 
 
@@ -167,7 +179,7 @@
             ],
         ),
         compiler_params=pltpu.CompilerParams(
-            vmem_limit_bytes=VMEM_BYTES, dimension_semantics=("arbitrary",)
+            vmem_limit_bytes=LARGE_BYTES, dimension_semantics=("arbitrary",)
         ),
         cost_estimate=pl.CostEstimate(
             flops=0, bytes_accessed=12 * rows * width, transcendentals=0
@@ -206,7 +218,7 @@
 
 
 def self_out_kernel(
-    info_ref, attended_ref, weight_hbm, out_ref, up_ref, down_ref, rows_ref, weight_ref, sum_ref, sems
+    info_ref, attended_ref, weight_hbm, out_ref, first_ref, second_ref, rows_ref, weight_ref, sum_ref, sems
 ):
     heads, rows, _ = attended_ref.shape
     n_db, share, features = out_ref.shape
@@ -243,11 +255,10 @@
         for copy in copies[begin:end]:
             copy.wait()
         lax.fori_loop(
-            0, features // step, functools.partial(columns, begin=begin, end=end), 0
+            0, features // step, functools.partial(columns, begin=begin, end=end), 0, unroll=4
         )
-    above, below = far_blocks(out_ref, info_ref[0], n_db - 1)
-    up_ref[...] = out_ref[above]
-    down_ref[...] = out_ref[below]
+    first_ref[...] = out_ref[far_block(out_ref, info_ref, 0, n_db - 1)]
+    second_ref[...] = out_ref[far_block(out_ref, info_ref, 1, n_db - 1)]
 
 
 def self_out(info, attended, weight, n_db):
@@ -328,82 +339,52 @@
     )(info, blocks, up, down, gain, hidden)
 
 
-def project_kernel(where_ref, *refs, cuts):
-    wk_hbm, wv_hbm, wq_hbm, wo_hbm, keys_ref, values_ref, wq_ref, wo_ref = refs[-12:-4]
-    rows_ref, wk_ref, wv_ref, sems = refs[-4:]
-    (table,) = refs[:-12]
-    entries = keys_ref.shape[0] // NLEN
-    piece = NLEN // cuts
-    bring = [
-        pltpu.make_async_copy(source, target, sems.at[entries * cuts + at])
-        for at, (source, target) in enumerate(
-            ((wk_hbm, wk_ref), (wv_hbm, wv_ref), (wq_hbm, wq_ref), (wo_hbm, wo_ref))
-        )
-    ]
-    for copy in bring[:2]:
-        copy.start()
-
-    def entry_copy(entry, cut):
-        row, shard = where_ref[2 + 2 * entry], where_ref[3 + 2 * entry]
-        return pltpu.make_async_copy(
-            table.at[row * cuts + cut, shard],
-            rows_ref.at[pl.ds(entry * NLEN + cut * piece, piece)],
-            sems.at[entry * cuts + cut],
-        )
-
-    for entry in range(entries):
-        for cut in range(cuts):
-            entry_copy(entry, cut).start()
-
-    for copy in bring[2:]:
-        copy.start()
-    for copy in bring[:2]:
-        copy.wait()
-    width = keys_ref.shape[1]
-    step = math.gcd(width, 512)
-    for group in range(entries // NEIGH):
-        for entry in range(NEIGH * group, NEIGH * (group + 1)):
-            for cut in range(cuts):
-                entry_copy(entry, cut).wait()
-        here = slice(group * GROUP, (group + 1) * GROUP)
-        for at in range(0, width, step):
-            lanes = slice(at, at + step)
-            for weight, made in ((wk_ref, keys_ref), (wv_ref, values_ref)):
-                made[here, lanes] = jnp.dot(
-                    rows_ref[here, :], weight[:, lanes], preferred_element_type=jnp.float32
-                ).astype(jnp.bfloat16)
-    for copy in bring[2:]:
-        copy.wait()
-
-
-def project_encodings(info, table, w_cross_k, w_cross_v, w_cross_q, w_cross_out):
-    entries = (info.shape[0] - 2) // 2
-    piece, depth = table.shape[2:]
-    cuts = NLEN // piece
+def project_kernel(where_ref, first_ref, second_ref, wk_ref, wv_ref, keys_ref, values_ref):
+    depth = first_ref.shape[-1]
+    rows = jnp.concatenate(
+        (first_ref[...].reshape(NLEN, depth), second_ref[...].reshape(NLEN, depth)), axis=0
+    )
+    keys_ref[...] = jnp.dot(rows, wk_ref[...], preferred_element_type=jnp.float32).astype(
+        jnp.bfloat16
+    )
+    values_ref[...] = jnp.dot(rows, wv_ref[...], preferred_element_type=jnp.float32).astype(
+        jnp.bfloat16
+    )
+
+
+def project_encodings(where, table, w_cross_k, w_cross_v):
+    groups = (where.shape[0] - 3) // (2 * NEIGH)
+    _, cuts, _, piece, depth = table.shape
     width = w_cross_k.shape[1]
-    vmem = pl.BlockSpec(memory_space=pltpu.VMEM)
-    anywhere = pl.BlockSpec(memory_space=pl.ANY)
-    made = jax.ShapeDtypeStruct((entries * NLEN, width), jnp.bfloat16)
+
+    def entry(neighbour):
+        def index(group, where_ref):
+            at = 3 + 2 * (NEIGH * group + neighbour)
+            return (where_ref[at], 0, where_ref[at + 1], 0, 0)
+
+        return pl.BlockSpec((1, cuts, 1, piece, depth), index)
+
+    fixed = pl.BlockSpec((depth, width), lambda group, where_ref: (0, 0))
+    made = pl.BlockSpec((GROUP, width), lambda group, where_ref: (group, 0))
     return pl.pallas_call(
-        functools.partial(project_kernel, cuts=cuts),
-        out_shape=[made, made]
-        + [jax.ShapeDtypeStruct(one.shape, one.dtype) for one in (w_cross_q, w_cross_out)],
-        in_specs=[pl.BlockSpec(memory_space=pltpu.SMEM)] + [anywhere] * 5,
-        out_specs=[vmem] * 4,
-        scratch_shapes=[
-            pltpu.VMEM((entries * NLEN, depth), jnp.bfloat16),
-            pltpu.VMEM(w_cross_k.shape, jnp.bfloat16),
-            pltpu.VMEM(w_cross_v.shape, jnp.bfloat16),
-            pltpu.SemaphoreType.DMA((entries * cuts + 4,)),
-        ],
-        compiler_params=pltpu.CompilerParams(vmem_limit_bytes=MIDDLE_BYTES),
+        project_kernel,
+        out_shape=[jax.ShapeDtypeStruct((groups * GROUP, width), jnp.bfloat16)] * 2,
+        grid_spec=pltpu.PrefetchScalarGridSpec(
+            num_scalar_prefetch=1,
+            grid=(groups,),
+            in_specs=[entry(0), entry(1), fixed, fixed],
+            out_specs=[made, made],
+        ),
+        compiler_params=pltpu.CompilerParams(
+            vmem_limit_bytes=LARGE_BYTES, dimension_semantics=("arbitrary",)
+        ),
         cost_estimate=pl.CostEstimate(
-            flops=4 * entries * NLEN * depth * width,
-            bytes_accessed=2 * (entries * NLEN * depth + 2 * depth * width + 2 * w_cross_q.size),
+            flops=4 * groups * GROUP * depth * width,
+            bytes_accessed=2 * (groups * GROUP * (depth + 2 * width) + 2 * depth * width),
             transcendentals=0,
         ),
         name="project_encodings",
-    )(info, table, w_cross_k, w_cross_v, w_cross_q, w_cross_out)
+    )(where, table, table, w_cross_k, w_cross_v)
 
 
 def apart_heads(query):
@@ -421,32 +402,56 @@
 
 
 def cross_kernel(info_ref, own_ref, *refs, scale):
-    wq_ref, keys_ref, values_ref, wo_ref, out_ref, up_ref, down_ref = refs[-10:-3]
-    rows_ref, query_ref, mixed_ref = refs[-3:]
-    pieces = refs[:-10]
+    wq_hbm, keys_hbm, values_hbm, wo_hbm, out_ref, first_ref, second_ref = refs[-15:-8]
+    wq_ref, keys_ref, values_ref, wo_ref, rows_ref, query_ref, mixed_ref, sems = refs[-8:]
+    pieces = refs[:-15]
     share, features = own_ref.shape
     width = wq_ref.shape[1]
     n_db = out_ref.shape[0]
     pairs = width // HD // 2
     tail = 16
-    for me in range(n_db):
-
-        @pl.when(info_ref[0] == me)
-        def _(me=me):
-            for owner in range(n_db):
-                if owner == me:
-                    source = own_ref
-                elif owner < me:
-                    source = pieces[2 * (me - owner - 1)]
-                else:
-                    source = pieces[2 * (owner - me - 1) + 1]
-                rows_ref[owner * share : (owner + 1) * share, :] = source[...]
-
+    cut = features // 4
+    low = width // 4
+    wq_copies = [
+        pltpu.make_async_copy(
+            wq_hbm.at[pl.ds(k * cut, cut)], wq_ref.at[pl.ds(k * cut, cut)], sems.at[k]
+        )
+        for k in range(4)
+    ]
+    other_copies = [
+        pltpu.make_async_copy(keys_hbm, keys_ref, sems.at[4]),
+        pltpu.make_async_copy(values_hbm, values_ref, sems.at[5]),
+    ] + [
+        pltpu.make_async_copy(
+            wo_hbm.at[pl.ds(k * low, low)], wo_ref.at[pl.ds(k * low, low)], sems.at[6 + k]
+        )
+        for k in range(4)
+    ]
+    for copy in wq_copies + other_copies:
+        copy.start()
+    me = info_ref[0]
+
+    def place(source, owner):
+        @pl.when((owner >= 0) & (owner < n_db))
+        def _():
+            at = pl.multiple_of(jnp.clip(owner, 0, n_db - 1) * share, share)
+            rows_ref[pl.ds(at, share), :] = source[...]
+
+    place(own_ref, me)
+    for at, source in enumerate(pieces):
+        way = 1 - 2 * (info_ref[2] ^ (at % 2))
+        place(source, me - way * (at // 2 + 1))
     lanes = [slice(2 * pair * HD, 2 * (pair + 1) * HD) for pair in range(pairs)]
-    for at in lanes:
-        query_ref[:, at] = jnp.dot(
-            rows_ref[...], wq_ref[:, at], preferred_element_type=jnp.float32
-        ).astype(jnp.bfloat16)
+    for k, copy in enumerate(wq_copies):
+        copy.wait()
+        inner = slice(k * cut, (k + 1) * cut)
+        for at in lanes:
+            part = jnp.dot(
+                rows_ref[:, inner], wq_ref[inner, at], preferred_element_type=jnp.float32
+            )
+            query_ref[:, at] = part if k == 0 else query_ref[:, at] + part
+    for copy in other_copies[:2]:
+        copy.wait()
     row = lax.broadcasted_iota(jnp.int32, (tail, 2 * HD), 0)
     spans = n_db * share // SPAN
     for span in range(spans):
@@ -456,7 +461,7 @@
         work += [(slice(top + SPAN - tail, top + SPAN), after, at) for at in lanes]
         scores = [
             lax.dot_general(
-                apart_heads(query_ref[of, at]),
+                apart_heads(query_ref[of, at].astype(jnp.bfloat16)),
                 keys_ref[which, at],
                 (((1,), (1,)), ((), ())),
                 preferred_element_type=jnp.float32,
@@ -481,6 +486,8 @@
             last = jnp.where(row == tail - 1, last, main[SPAN - tail :])
             mixed_ref[top : top + SPAN - tail, at] = main[: SPAN - tail].astype(jnp.bfloat16)
             mixed_ref[top + SPAN - tail : top + SPAN, at] = last.astype(jnp.bfloat16)
+    for copy in other_copies[2:]:
+        copy.wait()
     step = math.gcd(features, 512)
 
     def columns(at, carried):
@@ -491,10 +498,9 @@
             out_ref[owner, :, here] = product[owner * share : (owner + 1) * share]
         return carried
 
-    lax.fori_loop(0, features // step, columns, 0)
-    above, below = far_blocks(out_ref, info_ref[0], n_db - 1)
-    up_ref[...] = out_ref[above]
-    down_ref[...] = out_ref[below]
+    lax.fori_loop(0, features // step, columns, 0, unroll=4)
+    first_ref[...] = out_ref[far_block(out_ref, info_ref, 0, n_db - 1)]
+    second_ref[...] = out_ref[far_block(out_ref, info_ref, 1, n_db - 1)]
 
 
 def cross_block(info, normed, pieces, w_cross_q, keys, values, w_cross_out, n_db, scale):
@@ -502,19 +508,27 @@
     width = w_cross_q.shape[1]
     rows = n_db * share
     vmem = pl.BlockSpec(memory_space=pltpu.VMEM)
+    anywhere = pl.BlockSpec(memory_space=pl.ANY)
     one = jax.ShapeDtypeStruct((share, features), jnp.bfloat16)
     flat = [one for pair in pieces for one in pair]
     return pl.pallas_call(
         functools.partial(cross_kernel, scale=scale),
         out_shape=[jax.ShapeDtypeStruct((n_db, share, features), jnp.bfloat16), one, one],
-        in_specs=[pl.BlockSpec(memory_space=pltpu.SMEM)] + [vmem] * (5 + len(flat)),
+        in_specs=[pl.BlockSpec(memory_space=pltpu.SMEM)]
+        + [vmem] * (1 + len(flat))
+        + [anywhere] * 4,
         out_specs=[vmem] * 3,
         scratch_shapes=[
+            pltpu.VMEM((features, width), jnp.bfloat16),
+            pltpu.VMEM(keys.shape, jnp.bfloat16),
+            pltpu.VMEM(values.shape, jnp.bfloat16),
+            pltpu.VMEM((width, features), jnp.bfloat16),
             pltpu.VMEM((rows, features), jnp.bfloat16),
+            pltpu.VMEM((rows, width), jnp.float32),
             pltpu.VMEM((rows, width), jnp.bfloat16),
-            pltpu.VMEM((rows, width), jnp.bfloat16),
+            pltpu.SemaphoreType.DMA((10,)),
         ],
-        compiler_params=pltpu.CompilerParams(vmem_limit_bytes=BLOCK_BYTES),
+        compiler_params=pltpu.CompilerParams(vmem_limit_bytes=VMEM_BYTES),
         cost_estimate=pl.CostEstimate(
             flops=4 * rows * width * (features + GROUP),
             bytes_accessed=4 * width * (features + keys.shape[0]) + 4 * rows * features,
@@ -555,7 +569,7 @@
 
     packed, nb_row, nb_shard = lax.optimization_barrier((packed, nb_row, nb_shard))
     wanted = jnp.stack((nb_row, nb_shard), axis=-1).astype(jnp.int32)
-    place = jnp.stack((db_index, (seq_index > 0).astype(jnp.int32))).astype(jnp.int32)
+    place = jnp.stack((db_index, (seq_index > 0).astype(jnp.int32), seq_index % 2)).astype(jnp.int32)
     info = jnp.concatenate((place, span_before(wanted).reshape(-1), wanted.reshape(-1)))
     if heads == n_seq:
         held = lax.all_to_all(packed, "seq", 0, 0, tiled=True)
@@ -565,15 +579,17 @@
         attended = self_attention_gathered(query_rows, key_rows, value_rows, scale)
 
     along_db, attended = lax.optimization_barrier((along_db, attended))
-    table = lax.all_gather(along_db, "seq", axis=0)
+    table = lax.all_gather(along_db, "seq", axis=0).reshape(
+        rows_shard, NLEN // piece, n_db, piece, depth
+    )
 
     partial, up, down = self_out(info, attended, w_self_out, n_db)
     up, down = reduce_scatter(info, partial, up, down)
     residual, normed = norm_share(
         info, partial, up, down, norm_gain.reshape(1, features), hidden_in
     )
-    projected = project_encodings(info, table, w_cross_k, w_cross_v, w_cross_q, w_cross_out)
-    pieces, (keys, values, w_cross_q, w_cross_out) = gather(normed, projected)
+    projected = project_encodings(info, table, w_cross_k, w_cross_v)
+    pieces, (keys, values) = gather(normed, projected)
     partial, up, down = cross_block(
         info, normed, pieces, w_cross_q, keys, values, w_cross_out, n_db, scale
     )

time: 232 us -> 230 us (level)
  the two profiles are of different devices: /device:TPU:0 before, /device:TPU:18 now
where the time goes in v8:
time: 230 us; the launch traced here: 229 us
  waiting for transfers between devices  113 us (49%)
  starting transfers between devices  53.8 us (23%)
  Pallas kernels  44.9 us (20%)
  between operations  13.8 us (6%)
    ppermute x18, waiting for transfers between devices, line_shift(): return lax.ppermute(block, ('seq', 'db'), route)  87.4 us
    ppermute x18, starting transfers between devices, line_shift(): return lax.ppermute(block, ('seq', 'db'), route)  42.4 us
    ppermute x1, waiting for transfers between devices, shift(): return lax.ppermute(block, axis, route)  15.2 us
    pallas_call x1, Pallas kernels, cross_block(): pl.pallas_call(functools.partial(cross_kernel, scale=scale), out_shape=[j...  12.4 us
    pallas_call x1, Pallas kernels, project_encodings(): pl.pallas_call(project_kernel, out_shape=[jax.ShapeDtypeStruct((groups *...  10.5 us
    all_to_all x1, waiting for transfers between devices, per_device(): lax.all_to_all(self_attend_head(held, scale), 'seq', 0, 0, tiled=True)  7.35 us
    pallas_call x1, Pallas kernels, self_out(): pl.pallas_call(self_out_kernel, out_shape=[jax.ShapeDtypeStruct((n_db, sh...  5.77 us
    pallas_call x8, Pallas kernels, add_step(): pl.pallas_call(functools.partial(add_kernel, lead=lead, far=far), out_sha...  5.49 us
  transfers between devices with their start and end apart: 23, of which 12 were waited for; matrix products, arithmetic and copies ran while one was open for 0% of the time, Pallas kernels for 12%

profile of v8, /device:TPU:18, one launch (start us, length us, event | category | flops | bytes accessed | tf_op | source)
XLA Modules:
  0.0 229.5 jit_solution(8365326044899549179)
XLA Ops:
  6.5 3.8 %pack_heads.1 = (bf16[8,3,256,128]{3,2,1,0:T(8,128)(2,1)}, bf16[128,1024]{1,0:T(8,128)(2,1)}) custom-call(s32[1]{0:T(128)} %bitcast.index_ref, bf16[256,1024]{1,0:T(8,128)(2,1)} %query_ref.1, bf16[256,1024]{1,0:T(8,128)(2,1)} %key_ref.1, bf16[256,1024]{1,0:T(8,128)(2,1)} %value_ref.1, bf16[1024,1024]{1,0:T(8,128)(2,1)} %bitcast.15), custom_call_target="tpu_custom_call" | custom-call | bytes 3145728 | tf_op jit(solution)/shard_map/pack_heads/pallas_call | solution.py:165
  10.4 4.4 %all-to-all-start = ((bf16[8,3,256,128]{3,2,1,0:T(8,128)(2,1)}), bf16[8,3,256,128]{3,2,1,0:T(8,128)(2,1)S(1)}, u32[]{:S(2)}, u32[]{:S(2)}) async-start(bf16[8,3,256,128]{3,2,1,0:T(8,128)(2,1)} %get-tuple-element.42), calls=%async_computation | async-start | bytes 3145728 | tf_op jit(solution)/shard_map/all_to_all | solution.py:575
  14.8 0.7 all-gather.5.cloned.1.call-update
  15.5 0.1 fusion.2
  15.6 0.1 copy.18
  15.7 2.0 collective-permute-start
  17.8 0.1 copy.19
  17.9 0.1 reshape.23
  17.9 15.2 %collective-permute-done = s32[2,2]{1,0:T(2,128)S(1)} collective-permute-done((s32[2,2]{1,0:T(2,128)S(1)}, s32[2,2]{1,0:T(2,128)S(1)}, u32[]{:S(2)}, u32[]{:S(2)}) %collective-permute-start) | collective-permute-done | bytes 48 | tf_op jit(solution)/shard_map/ppermute | solution.py:27
  33.1 0.1 reshape.22
  33.2 0.1 concatenate.3.info_ref.where_ref
  33.3 1.0 all-to-all-done.qkv_ref
  34.3 5.5 %self_attend.1 = bf16[8,256,128]{2,1,0:T(8,128)(2,1)} custom-call(bf16[8,3,256,128]{3,2,1,0:T(8,128)(2,1)S(1)} %all-to-all-done.qkv_ref), custom_call_target="tpu_custom_call" | custom-call | flops 1073741824 | bytes 2097152 | tf_op jit(solution)/shard_map/self_attend/pallas_call | solution.py:132
  39.7 4.9 %all-to-all-start.1 = ((bf16[8,256,128]{2,1,0:T(8,128)(2,1)}), bf16[8,256,128]{2,1,0:T(8,128)(2,1)S(1)}, u32[]{:S(2)}, u32[]{:S(2)}) async-start(bf16[8,256,128]{2,1,0:T(8,128)(2,1)} %self_attend.1), calls=%async_computation.1 | async-start | bytes 1048576 | tf_op jit(solution)/shard_map/all_to_all | solution.py:577
  44.7 0.9 all-gather.5.cloned.1.call-done
  45.6 7.4 %all-to-all-done.1.attended_ref = bf16[8,256,128]{2,1,0:T(8,128)(2,1)S(1)} async-done(((bf16[8,256,128]{2,1,0:T(8,128)(2,1)}), bf16[8,256,128]{2,1,0:T(8,128)(2,1)S(1)}, u32[]{:S(2)}, u32[]{:S(2)}) %all-to-all-start.1) | async-done | bytes 524320 | tf_op jit(solution)/shard_map/all_to_all | solution.py:577
  53.0 0.0 all-gather.7.cloned.1.call-update
  53.0 5.8 %self_out.1 = (bf16[4,64,4096]{2,1,0:T(8,128)(2,1)S(1)}, bf16[64,4096]{1,0:T(8,128)(2,1)S(1)}, bf16[64,4096]{1,0:T(8,128)(2,1)S(1)}) custom-call(s32[23]{0:T(128)S(1)} %concatenate.3.info_ref.where_ref, bf16[8,256,128]{2,1,0:T(8,128)(2,1)S(1)} %all-to-all-done.1.attended_ref, bf16[1024,4096]{1,0:T(8,128)(2,1)} %weight_hbm.1), custom_call_target="tpu_custom_call" | custom-call | flops 2147483648 | bytes 11010048 | tf_op jit(solution)/shard_map/self_out/pallas_call | solution.py:270
  58.8 1.3 collective-permute-start.3
  60.1 0.7 collective-permute-start.1
  60.8 14.5 %collective-permute-done.3.sum_ref = bf16[64,4096]{1,0:T(8,128)(2,1)S(1)} collective-permute-done((bf16[64,4096]{1,0:T(8,128)(2,1)S(1)}, bf16[64,4096]{1,0:T(8,128)(2,1)S(1)}, u32[]{:S(2)}, u32[]{:S(2)}) %collective-permute-start.3) | collective-permute-done | bytes 524320 | tf_op jit(solution)/shard_map/ppermute | solution.py:39
  75.3 0.7 add_step.10
  76.0 0.7 add_step.8
  76.7 1.9 collective-permute-start.5
  78.6 1.3 collective-permute-start.2
  79.9 13.1 %collective-permute-done.5.sum_ref = bf16[64,4096]{1,0:T(8,128)(2,1)S(1)} collective-permute-done((bf16[64,4096]{1,0:T(8,128)(2,1)S(1)}, bf16[64,4096]{1,0:T(8,128)(2,1)S(1)}, u32[]{:S(2)}, u32[]{:S(2)}) %collective-permute-start.5) | collective-permute-done | bytes 524320 | tf_op jit(solution)/shard_map/ppermute | solution.py:39
  93.0 0.7 add_step.11
  93.7 0.0 copy-start.4
  93.7 0.0 copy-start.1
  93.7 0.0 collective-permute-done.2.sum_ref
  93.7 0.7 add_step.9
  94.4 1.9 collective-permute-start.6
  96.3 4.0 %collective-permute-start.4 = (bf16[64,4096]{1,0:T(8,128)(2,1)S(1)}, bf16[64,4096]{1,0:T(8,128)(2,1)S(1)}, u32[]{:S(2)}, u32[]{:S(2)}) collective-permute-start(bf16[64,4096]{1,0:T(8,128)(2,1)S(1)} %add_step.9), channel_id=1, source_target_pairs={{0,1},{1,2},{2,3},{5,4},{6,5},{7,6},{8,9},{9,10},{10,11},{13,12},{... | collective-permute-start | bytes 1572872 | tf_op jit(solution)/shard_map/ppermute | solution.py:39
  100.3 10.6 %collective-permute-done.6.down_ref = bf16[64,4096]{1,0:T(8,128)(2,1)S(1)} collective-permute-done((bf16[64,4096]{1,0:T(8,128)(2,1)S(1)}, bf16[64,4096]{1,0:T(8,128)(2,1)S(1)}, u32[]{:S(2)}, u32[]{:S(2)}) %collective-permute-start.6) | collective-permute-done | bytes 524320 | tf_op jit(solution)/shard_map/ppermute | solution.py:39
  110.9 0.0 collective-permute-done.4.up_ref
  110.9 1.4 norm_share.1
  112.4 1.9 collective-permute-start.7
  114.3 3.9 %collective-permute-start.8 = (bf16[64,4096]{1,0:T(8,128)(2,1)S(1)}, bf16[64,4096]{1,0:T(8,128)(2,1)S(1)}, u32[]{:S(2)}, u32[]{:S(2)}) collective-permute-start(bf16[64,4096]{1,0:T(8,128)(2,1)S(1)} %get-tuple-element.59.own_ref), channel_id=1, source_target_pairs={{1,0},{2,1},{3,2},{4,5},{5,6},{6,7},{9,8},{10,9},{11,10},{12,13},{... | collective-permute-start | bytes 1572872 | tf_op jit(solution)/shard_map/ppermute | solution.py:39
  118.2 9.8 %collective-permute-done.7.refs_0_ = bf16[64,4096]{1,0:T(8,128)(2,1)S(1)} collective-permute-done((bf16[64,4096]{1,0:T(8,128)(2,1)S(1)}, bf16[64,4096]{1,0:T(8,128)(2,1)S(1)}, u32[]{:S(2)}, u32[]{:S(2)}) %collective-permute-start.7) | collective-permute-done | bytes 524320 | tf_op jit(solution)/shard_map/ppermute | solution.py:39
  128.0 1.9 collective-permute-start.9
  129.9 0.0 collective-permute-done.8.refs_1_
  129.9 4.7 %collective-permute-start.10 = (bf16[64,4096]{1,0:T(8,128)(2,1)S(1)}, bf16[64,4096]{1,0:T(8,128)(2,1)}, u32[]{:S(2)}, u32[]{:S(2)}) collective-permute-start(bf16[64,4096]{1,0:T(8,128)(2,1)S(1)} %collective-permute-done.8.refs_1_), channel_id=1, source_target_pairs={{1,0},{2,1},{5,6},{6,7},{9,8},{10,9},{13,14},{14,15},{17,16},{18,1... | collective-permute-start | bytes 1572872 | tf_op jit(solution)/shard_map/ppermute | solution.py:39
  134.7 10.5 %project_encodings.1 = (bf16[1280,1024]{1,0:T(8,128)(2,1)}, bf16[1280,1024]{1,0:T(8,128)(2,1)}) custom-call(s32[23]{0:T(128)} %copy-done.2, bf16[8,1,4,128,1024]{4,3,2,1,0:T(8,128)(2,1)} %bitcast.13, bf16[8,1,4,128,1024]{4,3,2,1,0:T(8,128)(2,1)} %bitcast.14, bf16[1024,1024]{1,0:T(8,128)(2,1)} %wk_ref.1, bf16[1024,1024]{1,0:T(8,128)(2,1)} %wv_ref.1), custom_call_target="tpu_custom_call" | custom-call | flops 5368709120 | bytes 12058624 | tf_op jit(solution)/shard_map/project_encodings/pallas_call | solution.py:369
  145.2 0.0 collective-permute-done.9.refs_2_
  145.2 0.0 collective-permute-done.10.refs_3_
  145.2 0.7 collective-permute-start.12
  145.9 1.3 collective-permute-start.11
  147.2 10.8 %collective-permute-done.11.refs_4_ = bf16[64,4096]{1,0:T(8,128)(2,1)S(1)} collective-permute-done((bf16[64,4096]{1,0:T(8,128)(2,1)S(1)}, bf16[64,4096]{1,0:T(8,128)(2,1)S(1)}, u32[]{:S(2)}, u32[]{:S(2)}) %collective-permute-start.11) | collective-permute-done | bytes 524320 | tf_op jit(solution)/shard_map/ppermute | solution.py:39
  158.1 12.4 %cross_block.1 = (bf16[4,64,4096]{2,1,0:T(8,128)(2,1)}, bf16[64,4096]{1,0:T(8,128)(2,1)S(1)}, bf16[64,4096]{1,0:T(8,128)(2,1)S(1)}) custom-call(s32[23]{0:T(128)S(1)} %copy-done.3, bf16[64,4096]{1,0:T(8,128)(2,1)S(1)} %get-tuple-element.59.own_ref, bf16[64,4096]{1,0:T(8,128)(2,1)S(1)} %collective-permute-done.7.refs_0_, ...), custom_call_target="tpu_custom_call" | custom-call | flops 4563402752 | bytes 26214400 | tf_op jit(solution)/shard_map/cross_block/pallas_call | solution.py:514
  170.5 0.7 collective-permute-start.13
  171.2 1.3 collective-permute-start.15
  172.5 1.6 copy-done
  174.1 0.7 add_step.12
  174.8 1.3 collective-permute-start.14
  176.1 8.9 %collective-permute-done.15.sum_ref = bf16[64,4096]{1,0:T(8,128)(2,1)S(1)} collective-permute-done((bf16[64,4096]{1,0:T(8,128)(2,1)S(1)}, bf16[64,4096]{1,0:T(8,128)(2,1)S(1)}, u32[]{:S(2)}, u32[]{:S(2)}) %collective-permute-start.15) | collective-permute-done | bytes 524320 | tf_op jit(solution)/shard_map/ppermute | solution.py:39
  184.9 0.7 add_step.14
  185.6 7.7 %collective-permute-start.17 = (bf16[64,4096]{1,0:T(8,128)(2,1)S(1)}, bf16[64,4096]{1,0:T(8,128)(2,1)S(1)}, u32[]{:S(2)}, u32[]{:S(2)}) collective-permute-start(bf16[64,4096]{1,0:T(8,128)(2,1)S(1)} %add_step.14), channel_id=1, source_target_pairs={{2,1},{3,2},{4,5},{5,6},{10,9},{11,10},{12,13},{13,14},{18,17},{19... | collective-permute-start | bytes 1572872 | tf_op jit(solution)/shard_map/ppermute | solution.py:39
  193.4 9.3 %collective-permute-done.14.sum_ref = bf16[64,4096]{1,0:T(8,128)(2,1)S(1)} collective-permute-done((bf16[64,4096]{1,0:T(8,128)(2,1)S(1)}, bf16[64,4096]{1,0:T(8,128)(2,1)S(1)}, u32[]{:S(2)}, u32[]{:S(2)}) %collective-permute-start.14) | collective-permute-done | bytes 524320 | tf_op jit(solution)/shard_map/ppermute | solution.py:39
  202.7 0.7 add_step.13
  203.4 0.7 add_step.15
  204.1 1.9 collective-permute-start.18
  206.0 4.0 %collective-permute-start.16 = (bf16[64,4096]{1,0:T(8,128)(2,1)S(1)}, bf16[64,4096]{1,0:T(8,128)(2,1)S(1)}, u32[]{:S(2)}, u32[]{:S(2)}) collective-permute-start(bf16[64,4096]{1,0:T(8,128)(2,1)S(1)} %add_step.13), channel_id=1, source_target_pairs={{0,1},{1,2},{2,3},{5,4},{6,5},{7,6},{8,9},{9,10},{10,11},{13,12},{... | collective-permute-start | bytes 1572872 | tf_op jit(solution)/shard_map/ppermute | solution.py:39
  210.0 10.4 %collective-permute-done.18 = bf16[64,4096]{1,0:T(8,128)(2,1)S(1)} collective-permute-done((bf16[64,4096]{1,0:T(8,128)(2,1)S(1)}, bf16[64,4096]{1,0:T(8,128)(2,1)S(1)}, u32[]{:S(2)}, u32[]{:S(2)}) %collective-permute-start.18) | collective-permute-done | bytes 524320 | tf_op jit(solution)/shard_map/ppermute | solution.py:39
  220.4 2.2 fusion.1
  (21 shorter events, 0.1 us)
Async XLA Ops:
  10.4 5.1 %copy-start.5 = (s32[4,2]{0,1:T(2,128)S(1)}, s32[4,2]{0,1:T(2,128)}, u32[]{:S(2)}) copy-start(s32[4,2]{0,1:T(2,128)} %param.25) | copy-start | bytes 100
  10.4 5.1 %copy-start.6 = (s32[4,2]{0,1:T(2,128)S(1)}, s32[4,2]{0,1:T(2,128)}, u32[]{:S(2)}) copy-start(s32[4,2]{0,1:T(2,128)} %param.24) | copy-start | bytes 100
  10.4 23.9 %all-to-all-start = ((bf16[8,3,256,128]{3,2,1,0:T(8,128)(2,1)}), bf16[8,3,256,128]{3,2,1,0:T(8,128)(2,1)S(1)}, u32[]{:S(2)}, u32[]{:S(2)}) async-start(bf16[8,3,256,128]{3,2,1,0:T(8,128)(2,1)} %get-tuple-element.42), calls=%async_computation | async-start | bytes 3145728 | tf_op jit(solution)/shard_map/all_to_all | solution.py:575
  14.8 30.9 %all-gather.5.cloned.1.call-start = ((), (), s32[]{:S(2)}) async-start(), calls=%async_computation.2 | async-start | bytes 1310720 | tf_op jit(solution)/shard_map/all_gather | solution.py:568
  15.7 17.5 %collective-permute-start = (s32[2,2]{1,0:T(2,128)S(1)}, s32[2,2]{1,0:T(2,128)S(1)}, u32[]{:S(2)}, u32[]{:S(2)}) collective-permute-start(s32[2,2]{1,0:T(2,128)S(1)} %bitcast.21), channel_id=1, source_target_pairs={{0,4},{4,8},{8,12},{12,16},{16,20},{20,24},{24,28},{1,5},{5,9},{9,... | collective-permute-start | bytes 56 | tf_op jit(solution)/shard_map/ppermute | solution.py:27
  33.3 77.6 %copy-start.2 = (s32[23]{0:T(128)}, s32[23]{0:T(128)S(1)}, u32[]{:S(2)}) copy-start(s32[23]{0:T(128)S(1)} %concatenate.3.info_ref.where_ref) | copy-start | bytes 280
  39.7 13.2 %all-to-all-start.1 = ((bf16[8,256,128]{2,1,0:T(8,128)(2,1)}), bf16[8,256,128]{2,1,0:T(8,128)(2,1)S(1)}, u32[]{:S(2)}, u32[]{:S(2)}) async-start(bf16[8,256,128]{2,1,0:T(8,128)(2,1)} %self_attend.1), calls=%async_computation.1 | async-start | bytes 1048576 | tf_op jit(solution)/shard_map/all_to_all | solution.py:577
  44.7 90.0 %all-gather.7.cloned.1.call-start = ((), (), s32[]{:S(2)}) async-start(), calls=%async_computation.3 | async-start | bytes 9437184 | tf_op jit(solution)/shard_map/all_gather | solution.py:582
  58.8 16.5 %collective-permute-start.3 = (bf16[64,4096]{1,0:T(8,128)(2,1)S(1)}, bf16[64,4096]{1,0:T(8,128)(2,1)S(1)}, u32[]{:S(2)}, u32[]{:S(2)}) collective-permute-start(bf16[64,4096]{1,0:T(8,128)(2,1)S(1)} %get-tuple-element.52), channel_id=1, source_target_pairs={{3,2},{4,5},{11,10},{12,13},{19,18},{20,21},{27,26},{28,29}} | collective-permute-start | bytes 1572872 | tf_op jit(solution)/shard_map/ppermute | solution.py:39
  60.1 15.9 %collective-permute-start.1 = (bf16[64,4096]{1,0:T(8,128)(2,1)S(1)}, bf16[64,4096]{1,0:T(8,128)(2,1)S(1)}, u32[]{:S(2)}, u32[]{:S(2)}) collective-permute-start(bf16[64,4096]{1,0:T(8,128)(2,1)S(1)} %get-tuple-element.50), channel_id=1, source_target_pairs={{0,1},{7,6},{8,9},{15,14},{16,17},{23,22},{24,25},{31,30}} | collective-permute-start | bytes 1572872 | tf_op jit(solution)/shard_map/ppermute | solution.py:39
  76.7 16.3 %collective-permute-start.5 = (bf16[64,4096]{1,0:T(8,128)(2,1)S(1)}, bf16[64,4096]{1,0:T(8,128)(2,1)S(1)}, u32[]{:S(2)}, u32[]{:S(2)}) collective-permute-start(bf16[64,4096]{1,0:T(8,128)(2,1)S(1)} %add_step.10), channel_id=1, source_target_pairs={{2,1},{3,2},{4,5},{5,6},{10,9},{11,10},{12,13},{13,14},{18,17},{19... | collective-permute-start | bytes 1572872 | tf_op jit(solution)/shard_map/ppermute | solution.py:39
  78.6 15.1 %collective-permute-start.2 = (bf16[64,4096]{1,0:T(8,128)(2,1)S(1)}, bf16[64,4096]{1,0:T(8,128)(2,1)S(1)}, u32[]{:S(2)}, u32[]{:S(2)}) collective-permute-start(bf16[64,4096]{1,0:T(8,128)(2,1)S(1)} %add_step.8), channel_id=1, source_target_pairs={{0,1},{1,2},{6,5},{7,6},{8,9},{9,10},{14,13},{15,14},{16,17},{17,1... | collective-permute-start | bytes 1572872 | tf_op jit(solution)/shard_map/ppermute | solution.py:39
  93.7 6.6 %copy-start.4 = (bf16[4096]{0:T(1024)(128)(2,1)S(1)}, bf16[4096]{0:T(1024)(128)(2,1)}, u32[]{:S(2)}) copy-start(bf16[4096]{0:T(1024)(128)(2,1)} %param.18) | copy-start | bytes 24580
  93.7 17.2 %copy-start.1 = (bf16[256,4096]{1,0:T(8,128)(2,1)S(1)}, bf16[256,4096]{1,0:T(8,128)(2,1)}, u32[]{:S(2)}) copy-start(bf16[256,4096]{1,0:T(8,128)(2,1)} %hidden_hbm.1) | copy-start | bytes 6291460
  94.4 16.5 %collective-permute-start.6 = (bf16[64,4096]{1,0:T(8,128)(2,1)S(1)}, bf16[64,4096]{1,0:T(8,128)(2,1)S(1)}, u32[]{:S(2)}, u32[]{:S(2)}) collective-permute-start(bf16[64,4096]{1,0:T(8,128)(2,1)S(1)} %add_step.11), channel_id=1, source_target_pairs={{1,0},{2,1},{3,2},{4,5},{5,6},{6,7},{9,8},{10,9},{11,10},{12,13},{... | collective-permute-start | bytes 1572872 | tf_op jit(solution)/shard_map/ppermute | solution.py:39
  96.3 14.6 %collective-permute-start.4 = (bf16[64,4096]{1,0:T(8,128)(2,1)S(1)}, bf16[64,4096]{1,0:T(8,128)(2,1)S(1)}, u32[]{:S(2)}, u32[]{:S(2)}) collective-permute-start(bf16[64,4096]{1,0:T(8,128)(2,1)S(1)} %add_step.9), channel_id=1, source_target_pairs={{0,1},{1,2},{2,3},{5,4},{6,5},{7,6},{8,9},{9,10},{10,11},{13,12},{... | collective-permute-start | bytes 1572872 | tf_op jit(solution)/shard_map/ppermute | solution.py:39
  112.4 15.6 %collective-permute-start.7 = (bf16[64,4096]{1,0:T(8,128)(2,1)S(1)}, bf16[64,4096]{1,0:T(8,128)(2,1)S(1)}, u32[]{:S(2)}, u32[]{:S(2)}) collective-permute-start(bf16[64,4096]{1,0:T(8,128)(2,1)S(1)} %get-tuple-element.59.own_ref), channel_id=1, source_target_pairs={{0,1},{1,2},{2,3},{5,4},{6,5},{7,6},{8,9},{9,10},{10,11},{13,12},{... | collective-permute-start | bytes 1572872 | tf_op jit(solution)/shard_map/ppermute | solution.py:39
  114.3 15.6 %collective-permute-start.8 = (bf16[64,4096]{1,0:T(8,128)(2,1)S(1)}, bf16[64,4096]{1,0:T(8,128)(2,1)S(1)}, u32[]{:S(2)}, u32[]{:S(2)}) collective-permute-start(bf16[64,4096]{1,0:T(8,128)(2,1)S(1)} %get-tuple-element.59.own_ref), channel_id=1, source_target_pairs={{1,0},{2,1},{3,2},{4,5},{5,6},{6,7},{9,8},{10,9},{11,10},{12,13},{... | collective-permute-start | bytes 1572872 | tf_op jit(solution)/shard_map/ppermute | solution.py:39
  128.0 17.2 %collective-permute-start.9 = (bf16[64,4096]{1,0:T(8,128)(2,1)S(1)}, bf16[64,4096]{1,0:T(8,128)(2,1)S(1)}, u32[]{:S(2)}, u32[]{:S(2)}) collective-permute-start(bf16[64,4096]{1,0:T(8,128)(2,1)S(1)} %collective-permute-done.7.refs_0_), channel_id=1, source_target_pairs={{1,2},{2,3},{5,4},{6,5},{9,10},{10,11},{13,12},{14,13},{17,18},{18... | collective-permute-start | bytes 1572872 | tf_op jit(solution)/shard_map/ppermute | solution.py:39
  129.9 15.3 %collective-permute-start.10 = (bf16[64,4096]{1,0:T(8,128)(2,1)S(1)}, bf16[64,4096]{1,0:T(8,128)(2,1)}, u32[]{:S(2)}, u32[]{:S(2)}) collective-permute-start(bf16[64,4096]{1,0:T(8,128)(2,1)S(1)} %collective-permute-done.8.refs_1_), channel_id=1, source_target_pairs={{1,0},{2,1},{5,6},{6,7},{9,8},{10,9},{13,14},{14,15},{17,16},{18,1... | collective-permute-start | bytes 1572872 | tf_op jit(solution)/shard_map/ppermute | solution.py:39
  134.6 23.4 %copy-start.3 = (s32[23]{0:T(128)S(1)}, s32[23]{0:T(128)}, u32[]{:S(2)}) copy-start(s32[23]{0:T(128)} %copy-done.2) | copy-start | bytes 280
  145.2 2.0 collective-permute-start.12
  145.9 12.2 %collective-permute-start.11 = (bf16[64,4096]{1,0:T(8,128)(2,1)S(1)}, bf16[64,4096]{1,0:T(8,128)(2,1)S(1)}, u32[]{:S(2)}, u32[]{:S(2)}) collective-permute-start(bf16[64,4096]{1,0:T(8,128)(2,1)S(1)} %collective-permute-done.9.refs_2_), channel_id=1, source_target_pairs={{2,3},{5,4},{10,11},{13,12},{18,19},{21,20},{26,27},{29,28}} | collective-permute-start | bytes 1572872 | tf_op jit(solution)/shard_map/ppermute | solution.py:39
  170.5 2.0 collective-permute-start.13
  171.2 13.8 %collective-permute-start.15 = (bf16[64,4096]{1,0:T(8,128)(2,1)S(1)}, bf16[64,4096]{1,0:T(8,128)(2,1)S(1)}, u32[]{:S(2)}, u32[]{:S(2)}) collective-permute-start(bf16[64,4096]{1,0:T(8,128)(2,1)S(1)} %get-tuple-element.72), channel_id=1, source_target_pairs={{3,2},{4,5},{11,10},{12,13},{19,18},{20,21},{27,26},{28,29}} | collective-permute-start | bytes 1572872 | tf_op jit(solution)/shard_map/ppermute | solution.py:39
  172.5 1.6 copy-start
  174.8 28.0 %collective-permute-start.14 = (bf16[64,4096]{1,0:T(8,128)(2,1)S(1)}, bf16[64,4096]{1,0:T(8,128)(2,1)S(1)}, u32[]{:S(2)}, u32[]{:S(2)}) collective-permute-start(bf16[64,4096]{1,0:T(8,128)(2,1)S(1)} %add_step.12), channel_id=1, source_target_pairs={{0,1},{1,2},{6,5},{7,6},{8,9},{9,10},{14,13},{15,14},{16,17},{17,1... | collective-permute-start | bytes 1572872 | tf_op jit(solution)/shard_map/ppermute | solution.py:39
  185.6 17.8 %collective-permute-start.17 = (bf16[64,4096]{1,0:T(8,128)(2,1)S(1)}, bf16[64,4096]{1,0:T(8,128)(2,1)S(1)}, u32[]{:S(2)}, u32[]{:S(2)}) collective-permute-start(bf16[64,4096]{1,0:T(8,128)(2,1)S(1)} %add_step.14), channel_id=1, source_target_pairs={{2,1},{3,2},{4,5},{5,6},{10,9},{11,10},{12,13},{13,14},{18,17},{19... | collective-permute-start | bytes 1572872 | tf_op jit(solution)/shard_map/ppermute | solution.py:39
  204.1 16.3 %collective-permute-start.18 = (bf16[64,4096]{1,0:T(8,128)(2,1)S(1)}, bf16[64,4096]{1,0:T(8,128)(2,1)S(1)}, u32[]{:S(2)}, u32[]{:S(2)}) collective-permute-start(bf16[64,4096]{1,0:T(8,128)(2,1)S(1)} %add_step.15), channel_id=1, source_target_pairs={{1,0},{2,1},{3,2},{4,5},{5,6},{6,7},{9,8},{10,9},{11,10},{12,13},{... | collective-permute-start | bytes 1572872 | tf_op jit(solution)/shard_map/ppermute | solution.py:39
  206.0 14.4 %collective-permute-start.16 = (bf16[64,4096]{1,0:T(8,128)(2,1)S(1)}, bf16[64,4096]{1,0:T(8,128)(2,1)S(1)}, u32[]{:S(2)}, u32[]{:S(2)}) collective-permute-start(bf16[64,4096]{1,0:T(8,128)(2,1)S(1)} %add_step.13), channel_id=1, source_target_pairs={{0,1},{1,2},{2,3},{5,4},{6,5},{7,6},{8,9},{9,10},{10,11},{13,12},{... | collective-permute-start | bytes 1572872 | tf_op jit(solution)/shard_map/ppermute | solution.py:39
Sparse Core Ops, SparseCore 0:
  17.2 28.4 all-gather.4
  53.1 54.4 all-gather.6

commit v9 on v8

--- a/solution.py
+++ b/solution.py
@@ -31,7 +31,7 @@
     n_seq, size = lax.axis_size("seq"), lax.axis_size("db")
     route = []
     for row in range(n_seq):
-        up = row % 2 == lead
+        up = lead == 0
         for k in up_from if up else down_from:
             other = k + 1 if up else k - 1
             if 0 <= other < size:
@@ -40,71 +40,66 @@
 
 
 def far_block(blocks_ref, info_ref, lead, far):
-    way = 1 - 2 * (info_ref[2] ^ lead)
+    way = 1 - 2 * lead
     return jnp.clip(info_ref[0] + way * far, 0, blocks_ref.shape[0] - 1)
 
 
-def add_kernel(info_ref, blocks_ref, sum_ref, out_ref, *, lead, far):
-    index = far_block(blocks_ref, info_ref, lead, far)
+def add_kernel(info_ref, blocks_ref, up_ref, down_ref, up_out_ref, down_out_ref, *, far):
     rows = 16
 
     def add(at, carried):
         here = pl.ds(pl.multiple_of(at * rows, rows), rows)
-        out_ref[here, :] = (
-            blocks_ref[index, here, :].astype(jnp.float32) + sum_ref[here, :].astype(jnp.float32)
-        ).astype(jnp.bfloat16)
+        for lead, ref, out_ref in ((0, up_ref, up_out_ref), (1, down_ref, down_out_ref)):
+            index = far_block(blocks_ref, info_ref, lead, far)
+            out_ref[here, :] = (
+                blocks_ref[index, here, :].astype(jnp.float32) + ref[here, :].astype(jnp.float32)
+            ).astype(jnp.bfloat16)
         return carried
 
-    lax.fori_loop(0, sum_ref.shape[0] // rows, add, 0)
-
-
-def add_step(info, blocks, arrived, lead, far):
+    lax.fori_loop(0, up_ref.shape[0] // rows, add, 0)
+
+
+def add_step(info, blocks, up, down, far):
     vmem = pl.BlockSpec(memory_space=pltpu.VMEM)
+    one = jax.ShapeDtypeStruct(up.shape, up.dtype)
     return pl.pallas_call(
-        functools.partial(add_kernel, lead=lead, far=far),
-        out_shape=jax.ShapeDtypeStruct(arrived.shape, arrived.dtype),
-        in_specs=[pl.BlockSpec(memory_space=pltpu.SMEM), vmem, vmem],
-        out_specs=vmem,
+        functools.partial(add_kernel, far=far),
+        out_shape=[one, one],
+        in_specs=[pl.BlockSpec(memory_space=pltpu.SMEM), vmem, vmem, vmem],
+        out_specs=[vmem, vmem],
         compiler_params=pltpu.CompilerParams(vmem_limit_bytes=SMALL_BYTES),
         cost_estimate=pl.CostEstimate(
-            flops=arrived.size, bytes_accessed=6 * arrived.size, transcendentals=0
+            flops=2 * up.size, bytes_accessed=12 * up.size, transcendentals=0
         ),
         name="add_step",
-    )(info, blocks, arrived)
-
-
-def reduce_scatter(info, blocks, first, second):
+    )(info, blocks, up, down)
+
+
+def reduce_scatter(info, blocks, up, down):
     size = lax.axis_size("db")
     for step in range(size - 1):
         senders = (range(step + 1), range(size - 1 - step, size))
         if step:
-            first = add_step(info, blocks, first, 0, size - 1 - step)
-            first, held = lax.optimization_barrier((first, held))
-        first_sent = first
-        first = line_shift(first, 0, *senders)
-        if step:
-            second = add_step(info, blocks, second, 1, size - 1 - step)
-        second, first_sent = lax.optimization_barrier((second, first_sent))
-        held = second
-        second = line_shift(second, 1, *senders)
-    return first, second
+            up, down = add_step(info, blocks, up, down, size - 1 - step)
+        down = line_shift(down, 1, *senders)
+        up = line_shift(up, 0, *senders)
+        down, up = lax.optimization_barrier((down, up))
+    return up, down
 
 
 def gather(block, beside):
     size = lax.axis_size("db")
-    first, second, pieces = block, block, []
+    up, down, pieces = block, block, []
     for step in range(size - 1):
         senders = (range(step, size), range(0, size - step))
-        if step == size // 2:
-            first, held, beside = lax.optimization_barrier((first, held, beside))
-        elif step:
-            first, held = lax.optimization_barrier((first, held))
-        first_sent = first
-        first = line_shift(first, 0, *senders)
-        second, first_sent = lax.optimization_barrier((second, first_sent))
-        held = second
-        second = line_shift(second, 1, *senders)
-        pieces.append((first, second))
+        down = line_shift(down, 1, *senders)
+        up = line_shift(up, 0, *senders)
+        at = step + len(beside) - (size - 1)
+        if at >= 0:
+            up, down, beside[at] = lax.optimization_barrier((up, down, beside[at]))
+        else:
+            up, down = lax.optimization_barrier((up, down))
+        pieces.append((up, down))
     return pieces, beside
 
 
@@ -339,52 +334,51 @@
     )(info, blocks, up, down, gain, hidden)
 
 
-def project_kernel(where_ref, first_ref, second_ref, wk_ref, wv_ref, keys_ref, values_ref):
+def project_kernel(where_ref, first_ref, second_ref, weight_ref, made_ref):
     depth = first_ref.shape[-1]
     rows = jnp.concatenate(
         (first_ref[...].reshape(NLEN, depth), second_ref[...].reshape(NLEN, depth)), axis=0
     )
-    keys_ref[...] = jnp.dot(rows, wk_ref[...], preferred_element_type=jnp.float32).astype(
+    made_ref[...] = jnp.dot(rows, weight_ref[...], preferred_element_type=jnp.float32).astype(
         jnp.bfloat16
     )
-    values_ref[...] = jnp.dot(rows, wv_ref[...], preferred_element_type=jnp.float32).astype(
-        jnp.bfloat16
-    )
-
-
-def project_encodings(where, table, w_cross_k, w_cross_v):
-    groups = (where.shape[0] - 3) // (2 * NEIGH)
+
+
+def project_encodings(where, table, weight):
+    groups = (where.shape[0] - 2) // (2 * NEIGH)
     _, cuts, _, piece, depth = table.shape
-    width = w_cross_k.shape[1]
+    width = weight.shape[1]
 
     def entry(neighbour):
         def index(group, where_ref):
-            at = 3 + 2 * (NEIGH * group + neighbour)
+            at = 2 + 2 * (NEIGH * group + neighbour)
             return (where_ref[at], 0, where_ref[at + 1], 0, 0)
 
         return pl.BlockSpec((1, cuts, 1, piece, depth), index)
 
-    fixed = pl.BlockSpec((depth, width), lambda group, where_ref: (0, 0))
-    made = pl.BlockSpec((GROUP, width), lambda group, where_ref: (group, 0))
     return pl.pallas_call(
         project_kernel,
-        out_shape=[jax.ShapeDtypeStruct((groups * GROUP, width), jnp.bfloat16)] * 2,
+        out_shape=jax.ShapeDtypeStruct((groups * GROUP, width), jnp.bfloat16),
         grid_spec=pltpu.PrefetchScalarGridSpec(
             num_scalar_prefetch=1,
             grid=(groups,),
-            in_specs=[entry(0), entry(1), fixed, fixed],
-            out_specs=[made, made],
+            in_specs=[
+                entry(0),
+                entry(1),
+                pl.BlockSpec((depth, width), lambda group, where_ref: (0, 0)),
+            ],
+            out_specs=pl.BlockSpec((GROUP, width), lambda group, where_ref: (group, 0)),
         ),
         compiler_params=pltpu.CompilerParams(
             vmem_limit_bytes=LARGE_BYTES, dimension_semantics=("arbitrary",)
         ),
         cost_estimate=pl.CostEstimate(
-            flops=4 * groups * GROUP * depth * width,
-            bytes_accessed=2 * (groups * GROUP * (depth + 2 * width) + 2 * depth * width),
+            flops=2 * groups * GROUP * depth * width,
+            bytes_accessed=2 * (groups * GROUP * (depth + width) + depth * width),
             transcendentals=0,
         ),
         name="project_encodings",
-    )(where, table, table, w_cross_k, w_cross_v)
+    )(where, table, table, weight)
 
 
 def apart_heads(query):
@@ -439,7 +433,7 @@
 
     place(own_ref, me)
     for at, source in enumerate(pieces):
-        way = 1 - 2 * (info_ref[2] ^ (at % 2))
+        way = 1 - 2 * (at % 2)
         place(source, me - way * (at // 2 + 1))
     lanes = [slice(2 * pair * HD, 2 * (pair + 1) * HD) for pair in range(pairs)]
     for k, copy in enumerate(wq_copies):
@@ -569,7 +563,7 @@
 
     packed, nb_row, nb_shard = lax.optimization_barrier((packed, nb_row, nb_shard))
     wanted = jnp.stack((nb_row, nb_shard), axis=-1).astype(jnp.int32)
-    place = jnp.stack((db_index, (seq_index > 0).astype(jnp.int32), seq_index % 2)).astype(jnp.int32)
+    place = jnp.stack((db_index, (seq_index > 0).astype(jnp.int32))).astype(jnp.int32)
     info = jnp.concatenate((place, span_before(wanted).reshape(-1), wanted.reshape(-1)))
     if heads == n_seq:
         held = lax.all_to_all(packed, "seq", 0, 0, tiled=True)
@@ -588,7 +582,7 @@
     residual, normed = norm_share(
         info, partial, up, down, norm_gain.reshape(1, features), hidden_in
     )
-    projected = project_encodings(info, table, w_cross_k, w_cross_v)
+    projected = [project_encodings(info, table, weight) for weight in (w_cross_k, w_cross_v)]
     pieces, (keys, values) = gather(normed, projected)
     partial, up, down = cross_block(
         info, normed, pieces, w_cross_q, keys, values, w_cross_out, n_db, scale

time: 230 us -> 221 us (0.961)
  the two profiles are of different devices: /device:TPU:18 before, /device:TPU:0 now
where the time goes in v9:
time: 221 us; the launch traced here: 219 us
  waiting for transfers between devices  100 us (45%)
  starting transfers between devices  53.2 us (24%)
  Pallas kernels  48 us (22%)
  between operations  13.7 us (6%)
  other arithmetic  2.38 us (1%)
    ppermute x18, waiting for transfers between devices, line_shift(): return lax.ppermute(block, ('seq', 'db'), route)  72.5 us
    ppermute x18, starting transfers between devices, line_shift(): return lax.ppermute(block, ('seq', 'db'), route)  42 us
    all_to_all x1, waiting for transfers between devices, per_device(): held = lax.all_to_all(packed, 'seq', 0, 0, tiled=True)  16.7 us
    pallas_call x2, Pallas kernels, project_encodings(): pl.pallas_call(project_kernel, out_shape=jax.ShapeDtypeStruct((groups * G...  15.8 us
    pallas_call x1, Pallas kernels, cross_block(): pl.pallas_call(functools.partial(cross_kernel, scale=scale), out_shape=[j...  12.4 us
    all_to_all x1, waiting for transfers between devices, per_device(): lax.all_to_all(self_attend_head(held, scale), 'seq', 0, 0, tiled=True)  7.68 us
    pallas_call x1, Pallas kernels, self_out(): pl.pallas_call(self_out_kernel, out_shape=[jax.ShapeDtypeStruct((n_db, sh...  5.77 us
    pallas_call x1, Pallas kernels, self_attend_head(): pl.pallas_call(functools.partial(self_kernel, blocks=blocks, rows=rows, s...  5.56 us
  transfers between devices with their start and end apart: 23, of which 16 were waited for; matrix products, arithmetic and copies ran while one was open for 0% of the time, Pallas kernels for 14%

profile of v9, /device:TPU:0, one launch (start us, length us, event | category | flops | bytes accessed | tf_op | source)
XLA Modules:
  0.0 219.5 jit_solution(11857445953493172126)
XLA Ops:
  6.5 3.8 %pack_heads.1 = (bf16[8,3,256,128]{3,2,1,0:T(8,128)(2,1)}, bf16[128,1024]{1,0:T(8,128)(2,1)}) custom-call(s32[1]{0:T(128)} %bitcast.index_ref, bf16[256,1024]{1,0:T(8,128)(2,1)} %query_ref.1, bf16[256,1024]{1,0:T(8,128)(2,1)} %key_ref.1, bf16[256,1024]{1,0:T(8,128)(2,1)} %value_ref.1, bf16[1024,1024]{1,0:T(8,128)(2,1)} %bitcast.16), custom_call_target="tpu_custom_call" | custom-call | bytes 3145728 | tf_op jit(solution)/shard_map/pack_heads/pallas_call | solution.py:160
  10.4 5.3 %all-to-all-start = ((bf16[8,3,256,128]{3,2,1,0:T(8,128)(2,1)}), bf16[8,3,256,128]{3,2,1,0:T(8,128)(2,1)S(1)}, u32[]{:S(2)}, u32[]{:S(2)}) async-start(bf16[8,3,256,128]{3,2,1,0:T(8,128)(2,1)} %get-tuple-element.51), calls=%async_computation | async-start | bytes 3145728 | tf_op jit(solution)/shard_map/all_to_all | solution.py:569
  15.7 0.0 all-gather.5.cloned.1.call-start
  15.7 0.7 all-gather.5.cloned.1.call-update
  16.4 0.1 fusion.2
  16.5 0.1 copy.18
  16.6 2.4 %collective-permute-start = (s32[2,2]{1,0:T(2,128)S(1)}, s32[2,2]{1,0:T(2,128)S(1)}, u32[]{:S(2)}, u32[]{:S(2)}) collective-permute-start(s32[2,2]{1,0:T(2,128)S(1)} %bitcast.22), channel_id=1, source_target_pairs={{0,4},{4,8},{8,12},{12,16},{16,20},{20,24},{24,28},{1,5},{5,9},{9,... | collective-permute-start | bytes 56 | tf_op jit(solution)/shard_map/ppermute | solution.py:27
  19.0 0.1 copy.19
  19.1 0.1 reshape.23
  19.2 0.6 collective-permute-done
  19.8 0.1 reshape.22
  19.9 0.1 pad_add_fusion.1.info_ref.where_ref
  20.0 16.7 %all-to-all-done.qkv_ref = bf16[8,3,256,128]{3,2,1,0:T(8,128)(2,1)S(1)} async-done(((bf16[8,3,256,128]{3,2,1,0:T(8,128)(2,1)}), bf16[8,3,256,128]{3,2,1,0:T(8,128)(2,1)S(1)}, u32[]{:S(2)}, u32[]{:S(2)}) %all-to-all-start) | async-done | bytes 1572896 | tf_op jit(solution)/shard_map/all_to_all | solution.py:569
  36.7 5.6 %self_attend.1 = bf16[8,256,128]{2,1,0:T(8,128)(2,1)} custom-call(bf16[8,3,256,128]{3,2,1,0:T(8,128)(2,1)S(1)} %all-to-all-done.qkv_ref), custom_call_target="tpu_custom_call" | custom-call | flops 1073741824 | bytes 2097152 | tf_op jit(solution)/shard_map/self_attend/pallas_call | solution.py:127
  42.3 3.5 %all-to-all-start.1 = ((bf16[8,256,128]{2,1,0:T(8,128)(2,1)}), bf16[8,256,128]{2,1,0:T(8,128)(2,1)S(1)}, u32[]{:S(2)}, u32[]{:S(2)}) async-start(bf16[8,256,128]{2,1,0:T(8,128)(2,1)} %self_attend.1), calls=%async_computation.1 | async-start | bytes 1048576 | tf_op jit(solution)/shard_map/all_to_all | solution.py:571
  45.8 0.0 all-gather.7.cloned.1.call-start
  45.8 1.9 all-gather.5.cloned.1.call-done
  47.8 7.7 %all-to-all-done.1.attended_ref = bf16[8,256,128]{2,1,0:T(8,128)(2,1)S(1)} async-done(((bf16[8,256,128]{2,1,0:T(8,128)(2,1)}), bf16[8,256,128]{2,1,0:T(8,128)(2,1)S(1)}, u32[]{:S(2)}, u32[]{:S(2)}) %all-to-all-start.1) | async-done | bytes 524320 | tf_op jit(solution)/shard_map/all_to_all | solution.py:571
  55.4 0.0 all-gather.7.cloned.1.call-update
  55.5 5.8 %self_out.1 = (bf16[4,64,4096]{2,1,0:T(8,128)(2,1)S(1)}, bf16[64,4096]{1,0:T(8,128)(2,1)S(1)}, bf16[64,4096]{1,0:T(8,128)(2,1)S(1)}) custom-call(s32[22]{0:T(128)S(1)} %pad_add_fusion.1.info_ref.where_ref, bf16[8,256,128]{2,1,0:T(8,128)(2,1)S(1)} %all-to-all-done.1.attended_ref, bf16[1024,4096]{1,0:T(8,128)(2,1)} %weight_hbm.1), custom_call_target="tpu_custom_call" | custom-call | flops 2147483648 | bytes 11010048 | tf_op jit(solution)/shard_map/self_out/pallas_call | solution.py:265
  61.2 0.7 collective-permute-start.1
  61.9 3.5 %collective-permute-start.2 = (bf16[64,4096]{1,0:T(8,128)(2,1)S(1)}, bf16[64,4096]{1,0:T(8,128)(2,1)S(1)}, u32[]{:S(2)}, u32[]{:S(2)}) collective-permute-start(bf16[64,4096]{1,0:T(8,128)(2,1)S(1)} %get-tuple-element.60), channel_id=1, source_target_pairs={{0,1},{4,5},{8,9},{12,13},{16,17},{20,21},{24,25},{28,29}} | collective-permute-start | bytes 1572872 | tf_op jit(solution)/shard_map/ppermute | solution.py:39
  65.5 0.0 collective-permute-done.1.down_ref
  65.5 8.8 %collective-permute-done.2.up_ref = bf16[64,4096]{1,0:T(8,128)(2,1)S(1)} collective-permute-done((bf16[64,4096]{1,0:T(8,128)(2,1)S(1)}, bf16[64,4096]{1,0:T(8,128)(2,1)S(1)}, u32[]{:S(2)}, u32[]{:S(2)}) %collective-permute-start.2) | collective-permute-done | bytes 524320 | tf_op jit(solution)/shard_map/ppermute | solution.py:39
  74.3 0.8 add_step.4
  75.1 0.0 copy-start.4
  75.1 0.0 copy-start.1
  75.1 0.8 collective-permute-start.3
  75.9 5.0 %collective-permute-start.4 = (bf16[64,4096]{1,0:T(8,128)(2,1)S(1)}, bf16[64,4096]{1,0:T(8,128)(2,1)S(1)}, u32[]{:S(2)}, u32[]{:S(2)}) collective-permute-start(bf16[64,4096]{1,0:T(8,128)(2,1)S(1)} %get-tuple-element.64), channel_id=1, source_target_pairs={{0,1},{1,2},{4,5},{5,6},{8,9},{9,10},{12,13},{13,14},{16,17},{17,1... | collective-permute-start | bytes 1572872 | tf_op jit(solution)/shard_map/ppermute | solution.py:39
  81.0 8.0 %collective-permute-done.4.up_ref = bf16[64,4096]{1,0:T(8,128)(2,1)S(1)} collective-permute-done((bf16[64,4096]{1,0:T(8,128)(2,1)S(1)}, bf16[64,4096]{1,0:T(8,128)(2,1)S(1)}, u32[]{:S(2)}, u32[]{:S(2)}) %collective-permute-start.4) | collective-permute-done | bytes 524320 | tf_op jit(solution)/shard_map/ppermute | solution.py:39
  88.9 0.8 add_step.5
  89.7 1.3 collective-permute-start.5
  91.0 5.0 %collective-permute-start.6 = (bf16[64,4096]{1,0:T(8,128)(2,1)S(1)}, bf16[64,4096]{1,0:T(8,128)(2,1)S(1)}, u32[]{:S(2)}, u32[]{:S(2)}) collective-permute-start(bf16[64,4096]{1,0:T(8,128)(2,1)S(1)} %get-tuple-element.68), channel_id=1, source_target_pairs={{0,1},{1,2},{2,3},{4,5},{5,6},{6,7},{8,9},{9,10},{10,11},{12,13},{... | collective-permute-start | bytes 1572872 | tf_op jit(solution)/shard_map/ppermute | solution.py:39
  96.1 5.9 %collective-permute-done.5.down_ref = bf16[64,4096]{1,0:T(8,128)(2,1)S(1)} collective-permute-done((bf16[64,4096]{1,0:T(8,128)(2,1)S(1)}, bf16[64,4096]{1,0:T(8,128)(2,1)S(1)}, u32[]{:S(2)}, u32[]{:S(2)}) %collective-permute-start.5) | collective-permute-done | bytes 524320 | tf_op jit(solution)/shard_map/ppermute | solution.py:39
  102.0 1.2 collective-permute-done.6.up_ref
  103.2 1.4 norm_share.1
  104.7 1.3 collective-permute-start.8
  106.0 5.0 %collective-permute-start.7 = (bf16[64,4096]{1,0:T(8,128)(2,1)S(1)}, bf16[64,4096]{1,0:T(8,128)(2,1)S(1)}, u32[]{:S(2)}, u32[]{:S(2)}) collective-permute-start(bf16[64,4096]{1,0:T(8,128)(2,1)S(1)} %get-tuple-element.72.own_ref), channel_id=1, source_target_pairs={{0,1},{1,2},{2,3},{4,5},{5,6},{6,7},{8,9},{9,10},{10,11},{12,13},{... | collective-permute-start | bytes 1572872 | tf_op jit(solution)/shard_map/ppermute | solution.py:39
  111.0 5.2 %collective-permute-done.8.refs_1_ = bf16[64,4096]{1,0:T(8,128)(2,1)S(1)} collective-permute-done((bf16[64,4096]{1,0:T(8,128)(2,1)S(1)}, bf16[64,4096]{1,0:T(8,128)(2,1)S(1)}, u32[]{:S(2)}, u32[]{:S(2)}) %collective-permute-start.8) | collective-permute-done | bytes 524320 | tf_op jit(solution)/shard_map/ppermute | solution.py:39
  116.2 1.5 collective-permute-done.7.refs_0_
  117.7 0.7 collective-permute-start.9
  118.4 1.3 collective-permute-start.10
  119.7 0.0 all-gather.7.cloned.1.call-done
  119.7 7.9 %project_encodings.2.refs_7_ = bf16[1280,1024]{1,0:T(8,128)(2,1)} custom-call(s32[22]{0:T(128)} %copy-done.2, bf16[8,1,4,128,1024]{4,3,2,1,0:T(8,128)(2,1)} %bitcast.12, bf16[8,1,4,128,1024]{4,3,2,1,0:T(8,128)(2,1)} %bitcast.13, bf16[1024,1024]{1,0:T(8,128)(2,1)} %weight_ref.2), custom_call_target="tpu_custom_call" | custom-call | flops 2684354560 | bytes 7340032 | tf_op jit(solution)/shard_map/project_encodings/pallas_call | solution.py:359
  127.6 10.8 %collective-permute-done.10.refs_3_ = bf16[64,4096]{1,0:T(8,128)(2,1)} collective-permute-done((bf16[64,4096]{1,0:T(8,128)(2,1)S(1)}, bf16[64,4096]{1,0:T(8,128)(2,1)}, u32[]{:S(2)}, u32[]{:S(2)}) %collective-permute-start.10) | collective-permute-done | bytes 524320 | tf_op jit(solution)/shard_map/ppermute | solution.py:39
  138.4 0.7 collective-permute-start.11
  139.1 1.3 collective-permute-start.12
  140.4 7.9 %project_encodings.3.refs_8_ = bf16[1280,1024]{1,0:T(8,128)(2,1)} custom-call(s32[22]{0:T(128)} %copy-done.2, bf16[8,1,4,128,1024]{4,3,2,1,0:T(8,128)(2,1)} %bitcast.14, bf16[8,1,4,128,1024]{4,3,2,1,0:T(8,128)(2,1)} %bitcast.15, bf16[1024,1024]{1,0:T(8,128)(2,1)} %weight_ref.3), custom_call_target="tpu_custom_call" | custom-call | flops 2684354560 | bytes 7340032 | tf_op jit(solution)/shard_map/project_encodings/pallas_call | solution.py:359
  148.3 2.1 collective-permute-done.12.refs_5_
  150.4 12.4 %cross_block.1 = (bf16[4,64,4096]{2,1,0:T(8,128)(2,1)}, bf16[64,4096]{1,0:T(8,128)(2,1)S(1)}, bf16[64,4096]{1,0:T(8,128)(2,1)S(1)}) custom-call(s32[22]{0:T(128)S(1)} %copy-done.3, bf16[64,4096]{1,0:T(8,128)(2,1)S(1)} %get-tuple-element.72.own_ref, bf16[64,4096]{1,0:T(8,128)(2,1)S(1)} %collective-permute-done.7.refs_0_, ...), custom_call_target="tpu_custom_call" | custom-call | flops 4563402752 | bytes 26214400 | tf_op jit(solution)/shard_map/cross_block/pallas_call | solution.py:508
  162.8 0.7 collective-permute-start.13
  163.5 2.5 %collective-permute-start.14 = (bf16[64,4096]{1,0:T(8,128)(2,1)S(1)}, bf16[64,4096]{1,0:T(8,128)(2,1)S(1)}, u32[]{:S(2)}, u32[]{:S(2)}) collective-permute-start(bf16[64,4096]{1,0:T(8,128)(2,1)S(1)} %get-tuple-element.84), channel_id=1, source_target_pairs={{0,1},{4,5},{8,9},{12,13},{16,17},{20,21},{24,25},{28,29}} | collective-permute-start | bytes 1572872 | tf_op jit(solution)/shard_map/ppermute | solution.py:39
  166.1 10.2 %collective-permute-done.14.up_ref = bf16[64,4096]{1,0:T(8,128)(2,1)S(1)} collective-permute-done((bf16[64,4096]{1,0:T(8,128)(2,1)S(1)}, bf16[64,4096]{1,0:T(8,128)(2,1)S(1)}, u32[]{:S(2)}, u32[]{:S(2)}) %collective-permute-start.14) | collective-permute-done | bytes 524320 | tf_op jit(solution)/shard_map/ppermute | solution.py:39
  176.3 1.6 copy-done
  177.9 0.8 add_step.6
  178.7 0.7 collective-permute-start.15
  179.4 5.0 %collective-permute-start.16 = (bf16[64,4096]{1,0:T(8,128)(2,1)S(1)}, bf16[64,4096]{1,0:T(8,128)(2,1)S(1)}, u32[]{:S(2)}, u32[]{:S(2)}) collective-permute-start(bf16[64,4096]{1,0:T(8,128)(2,1)S(1)} %get-tuple-element.88), channel_id=1, source_target_pairs={{0,1},{1,2},{4,5},{5,6},{8,9},{9,10},{12,13},{13,14},{16,17},{17,1... | collective-permute-start | bytes 1572872 | tf_op jit(solution)/shard_map/ppermute | solution.py:39
  184.4 12.2 %collective-permute-done.16.up_ref = bf16[64,4096]{1,0:T(8,128)(2,1)S(1)} collective-permute-done((bf16[64,4096]{1,0:T(8,128)(2,1)S(1)}, bf16[64,4096]{1,0:T(8,128)(2,1)S(1)}, u32[]{:S(2)}, u32[]{:S(2)}) %collective-permute-start.16) | collective-permute-done | bytes 524320 | tf_op jit(solution)/shard_map/ppermute | solution.py:39
  196.6 0.8 add_step.7
  197.4 1.3 collective-permute-start.17
  198.7 5.0 %collective-permute-start.18 = (bf16[64,4096]{1,0:T(8,128)(2,1)S(1)}, bf16[64,4096]{1,0:T(8,128)(2,1)S(1)}, u32[]{:S(2)}, u32[]{:S(2)}) collective-permute-start(bf16[64,4096]{1,0:T(8,128)(2,1)S(1)} %get-tuple-element.92), channel_id=1, source_target_pairs={{0,1},{1,2},{2,3},{4,5},{5,6},{6,7},{8,9},{9,10},{10,11},{12,13},{... | collective-permute-start | bytes 1572872 | tf_op jit(solution)/shard_map/ppermute | solution.py:39
  203.8 5.2 %collective-permute-done.17 = bf16[64,4096]{1,0:T(8,128)(2,1)S(1)} collective-permute-done((bf16[64,4096]{1,0:T(8,128)(2,1)S(1)}, bf16[64,4096]{1,0:T(8,128)(2,1)S(1)}, u32[]{:S(2)}, u32[]{:S(2)}) %collective-permute-start.17) | collective-permute-done | bytes 524320 | tf_op jit(solution)/shard_map/ppermute | solution.py:39
  209.0 1.5 collective-permute-done.18
  210.4 2.2 %fusion.1 = f32[64,4096]{1,0:T(8,128)} fusion(f32[64,4096]{1,0:T(8,128)S(1)} %get-tuple-element.71, bf16[64,4096]{1,0:T(8,128)(2,1)S(1)} %collective-permute-done.17, bf16[64,4096]{1,0:T(8,128)(2,1)S(1)} %collective-permute-done.18, bf16[4,64,4096]{2,1,0:T(8,128)(2,1)} %get-tuple-element.82.blocks_ref, s32[]{:T(128)S(6)} %select_n.4), kind=kLoop, calls=%fused_computation.2 | loop fusion | flops 1572864 | bytes 3670020 | tf_op jit(solution)/shard_map/add | solution.py:592
  (18 shorter events, 0.1 us)
Async XLA Ops:
  10.4 6.1 %copy-start.5 = (s32[4,2]{0,1:T(2,128)S(1)}, s32[4,2]{0,1:T(2,128)}, u32[]{:S(2)}) copy-start(s32[4,2]{0,1:T(2,128)} %param.24) | copy-start | bytes 100
  10.4 6.1 %copy-start.6 = (s32[4,2]{0,1:T(2,128)S(1)}, s32[4,2]{0,1:T(2,128)}, u32[]{:S(2)}) copy-start(s32[4,2]{0,1:T(2,128)} %param.25) | copy-start | bytes 100
  10.4 26.3 %all-to-all-start = ((bf16[8,3,256,128]{3,2,1,0:T(8,128)(2,1)}), bf16[8,3,256,128]{3,2,1,0:T(8,128)(2,1)S(1)}, u32[]{:S(2)}, u32[]{:S(2)}) async-start(bf16[8,3,256,128]{3,2,1,0:T(8,128)(2,1)} %get-tuple-element.51), calls=%async_computation | async-start | bytes 3145728 | tf_op jit(solution)/shard_map/all_to_all | solution.py:569
  15.7 32.1 %all-gather.5.cloned.1.call-start = ((), (), s32[]{:S(2)}) async-start(), calls=%async_computation.2 | async-start | bytes 1310720 | tf_op jit(solution)/shard_map/all_gather | solution.py:562
  16.6 3.2 %collective-permute-start = (s32[2,2]{1,0:T(2,128)S(1)}, s32[2,2]{1,0:T(2,128)S(1)}, u32[]{:S(2)}, u32[]{:S(2)}) collective-permute-start(s32[2,2]{1,0:T(2,128)S(1)} %bitcast.22), channel_id=1, source_target_pairs={{0,4},{4,8},{8,12},{12,16},{16,20},{20,24},{24,28},{1,5},{5,9},{9,... | collective-permute-start | bytes 56 | tf_op jit(solution)/shard_map/ppermute | solution.py:27
  20.0 83.3 %copy-start.2 = (s32[22]{0:T(128)}, s32[22]{0:T(128)S(1)}, u32[]{:S(2)}) copy-start(s32[22]{0:T(128)S(1)} %pad_add_fusion.1.info_ref.where_ref) | copy-start | bytes 268
  42.3 13.2 %all-to-all-start.1 = ((bf16[8,256,128]{2,1,0:T(8,128)(2,1)}), bf16[8,256,128]{2,1,0:T(8,128)(2,1)S(1)}, u32[]{:S(2)}, u32[]{:S(2)}) async-start(bf16[8,256,128]{2,1,0:T(8,128)(2,1)} %self_attend.1), calls=%async_computation.1 | async-start | bytes 1048576 | tf_op jit(solution)/shard_map/all_to_all | solution.py:571
  45.8 73.9 %all-gather.7.cloned.1.call-start = ((), (), s32[]{:S(2)}) async-start(), calls=%async_computation.3 | async-start | bytes 9437184 | tf_op jit(solution)/shard_map/all_gather | solution.py:576
  61.2 4.2 %collective-permute-start.1 = (bf16[64,4096]{1,0:T(8,128)(2,1)S(1)}, bf16[64,4096]{1,0:T(8,128)(2,1)S(1)}, u32[]{:S(2)}, u32[]{:S(2)}) collective-permute-start(bf16[64,4096]{1,0:T(8,128)(2,1)S(1)} %get-tuple-element.59), channel_id=1, source_target_pairs={{3,2},{7,6},{11,10},{15,14},{19,18},{23,22},{27,26},{31,30}} | collective-permute-start | bytes 1572872 | tf_op jit(solution)/shard_map/ppermute | solution.py:39
  61.9 12.3 %collective-permute-start.2 = (bf16[64,4096]{1,0:T(8,128)(2,1)S(1)}, bf16[64,4096]{1,0:T(8,128)(2,1)S(1)}, u32[]{:S(2)}, u32[]{:S(2)}) collective-permute-start(bf16[64,4096]{1,0:T(8,128)(2,1)S(1)} %get-tuple-element.60), channel_id=1, source_target_pairs={{0,1},{4,5},{8,9},{12,13},{16,17},{20,21},{24,25},{28,29}} | collective-permute-start | bytes 1572872 | tf_op jit(solution)/shard_map/ppermute | solution.py:39
  75.1 21.0 %copy-start.4 = (bf16[4096]{0:T(1024)(128)(2,1)S(1)}, bf16[4096]{0:T(1024)(128)(2,1)}, u32[]{:S(2)}) copy-start(bf16[4096]{0:T(1024)(128)(2,1)} %param.18) | copy-start | bytes 24580
  75.1 28.2 %copy-start.1 = (bf16[256,4096]{1,0:T(8,128)(2,1)S(1)}, bf16[256,4096]{1,0:T(8,128)(2,1)}, u32[]{:S(2)}) copy-start(bf16[256,4096]{1,0:T(8,128)(2,1)} %hidden_hbm.1) | copy-start | bytes 6291460
  75.1 5.9 %collective-permute-start.3 = (bf16[64,4096]{1,0:T(8,128)(2,1)S(1)}, bf16[64,4096]{1,0:T(8,128)(2,1)S(1)}, u32[]{:S(2)}, u32[]{:S(2)}) collective-permute-start(bf16[64,4096]{1,0:T(8,128)(2,1)S(1)} %get-tuple-element.63), channel_id=1, source_target_pairs={{2,1},{3,2},{6,5},{7,6},{10,9},{11,10},{14,13},{15,14},{18,17},{19... | collective-permute-start | bytes 1572872 | tf_op jit(solution)/shard_map/ppermute | solution.py:39
  75.9 13.0 %collective-permute-start.4 = (bf16[64,4096]{1,0:T(8,128)(2,1)S(1)}, bf16[64,4096]{1,0:T(8,128)(2,1)S(1)}, u32[]{:S(2)}, u32[]{:S(2)}) collective-permute-start(bf16[64,4096]{1,0:T(8,128)(2,1)S(1)} %get-tuple-element.64), channel_id=1, source_target_pairs={{0,1},{1,2},{4,5},{5,6},{8,9},{9,10},{12,13},{13,14},{16,17},{17,1... | collective-permute-start | bytes 1572872 | tf_op jit(solution)/shard_map/ppermute | solution.py:39
  89.7 12.3 %collective-permute-start.5 = (bf16[64,4096]{1,0:T(8,128)(2,1)S(1)}, bf16[64,4096]{1,0:T(8,128)(2,1)S(1)}, u32[]{:S(2)}, u32[]{:S(2)}) collective-permute-start(bf16[64,4096]{1,0:T(8,128)(2,1)S(1)} %get-tuple-element.67), channel_id=1, source_target_pairs={{1,0},{2,1},{3,2},{5,4},{6,5},{7,6},{9,8},{10,9},{11,10},{13,12},{... | collective-permute-start | bytes 1572872 | tf_op jit(solution)/shard_map/ppermute | solution.py:39
  91.0 12.2 %collective-permute-start.6 = (bf16[64,4096]{1,0:T(8,128)(2,1)S(1)}, bf16[64,4096]{1,0:T(8,128)(2,1)S(1)}, u32[]{:S(2)}, u32[]{:S(2)}) collective-permute-start(bf16[64,4096]{1,0:T(8,128)(2,1)S(1)} %get-tuple-element.68), channel_id=1, source_target_pairs={{0,1},{1,2},{2,3},{4,5},{5,6},{6,7},{8,9},{9,10},{10,11},{12,13},{... | collective-permute-start | bytes 1572872 | tf_op jit(solution)/shard_map/ppermute | solution.py:39
  104.7 11.5 %collective-permute-start.8 = (bf16[64,4096]{1,0:T(8,128)(2,1)S(1)}, bf16[64,4096]{1,0:T(8,128)(2,1)S(1)}, u32[]{:S(2)}, u32[]{:S(2)}) collective-permute-start(bf16[64,4096]{1,0:T(8,128)(2,1)S(1)} %get-tuple-element.72.own_ref), channel_id=1, source_target_pairs={{1,0},{2,1},{3,2},{5,4},{6,5},{7,6},{9,8},{10,9},{11,10},{13,12},{... | collective-permute-start | bytes 1572872 | tf_op jit(solution)/shard_map/ppermute | solution.py:39
  106.0 11.7 %collective-permute-start.7 = (bf16[64,4096]{1,0:T(8,128)(2,1)S(1)}, bf16[64,4096]{1,0:T(8,128)(2,1)S(1)}, u32[]{:S(2)}, u32[]{:S(2)}) collective-permute-start(bf16[64,4096]{1,0:T(8,128)(2,1)S(1)} %get-tuple-element.72.own_ref), channel_id=1, source_target_pairs={{0,1},{1,2},{2,3},{4,5},{5,6},{6,7},{8,9},{9,10},{10,11},{12,13},{... | collective-permute-start | bytes 1572872 | tf_op jit(solution)/shard_map/ppermute | solution.py:39
  117.7 9.9 %collective-permute-start.9 = (bf16[64,4096]{1,0:T(8,128)(2,1)S(1)}, bf16[64,4096]{1,0:T(8,128)(2,1)S(1)}, u32[]{:S(2)}, u32[]{:S(2)}) collective-permute-start(bf16[64,4096]{1,0:T(8,128)(2,1)S(1)} %collective-permute-done.7.refs_0_), channel_id=1, source_target_pairs={{1,2},{2,3},{5,6},{6,7},{9,10},{10,11},{13,14},{14,15},{17,18},{18... | collective-permute-start | bytes 1572872 | tf_op jit(solution)/shard_map/ppermute | solution.py:39
  118.4 20.1 %collective-permute-start.10 = (bf16[64,4096]{1,0:T(8,128)(2,1)S(1)}, bf16[64,4096]{1,0:T(8,128)(2,1)}, u32[]{:S(2)}, u32[]{:S(2)}) collective-permute-start(bf16[64,4096]{1,0:T(8,128)(2,1)S(1)} %collective-permute-done.8.refs_1_), channel_id=1, source_target_pairs={{1,0},{2,1},{5,4},{6,5},{9,8},{10,9},{13,12},{14,13},{17,16},{18,1... | collective-permute-start | bytes 1572872 | tf_op jit(solution)/shard_map/ppermute | solution.py:39
  127.6 22.8 %copy-start.3 = (s32[22]{0:T(128)S(1)}, s32[22]{0:T(128)}, u32[]{:S(2)}) copy-start(s32[22]{0:T(128)} %copy-done.2) | copy-start | bytes 268
  138.4 9.9 %collective-permute-start.11 = (bf16[64,4096]{1,0:T(8,128)(2,1)S(1)}, bf16[64,4096]{1,0:T(8,128)(2,1)S(1)}, u32[]{:S(2)}, u32[]{:S(2)}) collective-permute-start(bf16[64,4096]{1,0:T(8,128)(2,1)S(1)} %collective-permute-done.9.refs_2_), channel_id=1, source_target_pairs={{2,3},{6,7},{10,11},{14,15},{18,19},{22,23},{26,27},{30,31}} | collective-permute-start | bytes 1572872 | tf_op jit(solution)/shard_map/ppermute | solution.py:39
  139.1 11.3 %collective-permute-start.12 = (bf16[64,4096]{1,0:T(8,128)(2,1)}, bf16[64,4096]{1,0:T(8,128)(2,1)S(1)}, u32[]{:S(2)}, u32[]{:S(2)}) collective-permute-start(bf16[64,4096]{1,0:T(8,128)(2,1)} %collective-permute-done.10.refs_3_), channel_id=1, source_target_pairs={{1,0},{5,4},{9,8},{13,12},{17,16},{21,20},{25,24},{29,28}} | collective-permute-start | bytes 1572872 | tf_op jit(solution)/shard_map/ppermute | solution.py:39
  162.8 3.3 %collective-permute-start.13 = (bf16[64,4096]{1,0:T(8,128)(2,1)S(1)}, bf16[64,4096]{1,0:T(8,128)(2,1)S(1)}, u32[]{:S(2)}, u32[]{:S(2)}) collective-permute-start(bf16[64,4096]{1,0:T(8,128)(2,1)S(1)} %get-tuple-element.83), channel_id=1, source_target_pairs={{3,2},{7,6},{11,10},{15,14},{19,18},{23,22},{27,26},{31,30}} | collective-permute-start | bytes 1572872 | tf_op jit(solution)/shard_map/ppermute | solution.py:39
  163.5 12.8 %collective-permute-start.14 = (bf16[64,4096]{1,0:T(8,128)(2,1)S(1)}, bf16[64,4096]{1,0:T(8,128)(2,1)S(1)}, u32[]{:S(2)}, u32[]{:S(2)}) collective-permute-start(bf16[64,4096]{1,0:T(8,128)(2,1)S(1)} %get-tuple-element.84), channel_id=1, source_target_pairs={{0,1},{4,5},{8,9},{12,13},{16,17},{20,21},{24,25},{28,29}} | collective-permute-start | bytes 1572872 | tf_op jit(solution)/shard_map/ppermute | solution.py:39
  176.3 1.6 copy-start
  178.7 5.7 %collective-permute-start.15 = (bf16[64,4096]{1,0:T(8,128)(2,1)S(1)}, bf16[64,4096]{1,0:T(8,128)(2,1)S(1)}, u32[]{:S(2)}, u32[]{:S(2)}) collective-permute-start(bf16[64,4096]{1,0:T(8,128)(2,1)S(1)} %get-tuple-element.87), channel_id=1, source_target_pairs={{2,1},{3,2},{6,5},{7,6},{10,9},{11,10},{14,13},{15,14},{18,17},{19... | collective-permute-start | bytes 1572872 | tf_op jit(solution)/shard_map/ppermute | solution.py:39
  179.4 17.2 %collective-permute-start.16 = (bf16[64,4096]{1,0:T(8,128)(2,1)S(1)}, bf16[64,4096]{1,0:T(8,128)(2,1)S(1)}, u32[]{:S(2)}, u32[]{:S(2)}) collective-permute-start(bf16[64,4096]{1,0:T(8,128)(2,1)S(1)} %get-tuple-element.88), channel_id=1, source_target_pairs={{0,1},{1,2},{4,5},{5,6},{8,9},{9,10},{12,13},{13,14},{16,17},{17,1... | collective-permute-start | bytes 1572872 | tf_op jit(solution)/shard_map/ppermute | solution.py:39
  197.4 11.5 %collective-permute-start.17 = (bf16[64,4096]{1,0:T(8,128)(2,1)S(1)}, bf16[64,4096]{1,0:T(8,128)(2,1)S(1)}, u32[]{:S(2)}, u32[]{:S(2)}) collective-permute-start(bf16[64,4096]{1,0:T(8,128)(2,1)S(1)} %get-tuple-element.91), channel_id=1, source_target_pairs={{1,0},{2,1},{3,2},{5,4},{6,5},{7,6},{9,8},{10,9},{11,10},{13,12},{... | collective-permute-start | bytes 1572872 | tf_op jit(solution)/shard_map/ppermute | solution.py:39
  198.7 11.7 %collective-permute-start.18 = (bf16[64,4096]{1,0:T(8,128)(2,1)S(1)}, bf16[64,4096]{1,0:T(8,128)(2,1)S(1)}, u32[]{:S(2)}, u32[]{:S(2)}) collective-permute-start(bf16[64,4096]{1,0:T(8,128)(2,1)S(1)} %get-tuple-element.92), channel_id=1, source_target_pairs={{0,1},{1,2},{2,3},{4,5},{5,6},{6,7},{8,9},{9,10},{10,11},{12,13},{... | collective-permute-start | bytes 1572872 | tf_op jit(solution)/shard_map/ppermute | solution.py:39
Sparse Core Ops, SparseCore 0:
  18.1 29.6 all-gather.4
  55.6 53.7 all-gather.6

commit v10 on v9

--- a/solution.py
+++ b/solution.py
@@ -87,20 +87,18 @@
     return up, down
 
 
-def gather(block, beside):
-    size = lax.axis_size("db")
-    up, down, pieces = block, block, []
-    for step in range(size - 1):
-        senders = (range(step, size), range(0, size - step))
-        down = line_shift(down, 1, *senders)
-        up = line_shift(up, 0, *senders)
-        at = step + len(beside) - (size - 1)
-        if at >= 0:
-            up, down, beside[at] = lax.optimization_barrier((up, down, beside[at]))
-        else:
-            up, down = lax.optimization_barrier((up, down))
-        pieces.append((up, down))
-    return pieces, beside
+def plane_swap(block, mask):
+    return lax.ppermute(block, "seq", [(i, i ^ mask) for i in range(8)])
+
+
+def plane_pieces(own):
+    same = lax.optimization_barrier((own,) + tuple(plane_swap(own, mask) for mask in (2, 4, 6)))
+    return same + tuple(plane_swap(one, 1) for one in same)
+
+
+def plane_slot(owner, me):
+    apart = owner ^ me
+    return (apart >> 1) + 4 * (apart & 1)
 
 
 def self_kernel(qkv_ref, out_ref, *, blocks, rows, scale):
@@ -213,10 +211,10 @@
 
 
 def self_out_kernel(
-    info_ref, attended_ref, weight_hbm, out_ref, first_ref, second_ref, rows_ref, weight_ref, sum_ref, sems
+    attended_ref, weight_hbm, out_ref, rows_ref, weight_ref, sum_ref, sems
 ):
     heads, rows, _ = attended_ref.shape
-    n_db, share, features = out_ref.shape
+    features = out_ref.shape[1]
     width = weight_hbm.shape[0]
     cuts = 4
     depth = width // cuts
@@ -241,9 +239,7 @@
         if begin == 0:
             sum_ref[:, here] = product
             return carried
-        product = (product + sum_ref[:, here]).astype(jnp.bfloat16)
-        for owner in range(n_db):
-            out_ref[owner, :, here] = product[owner * share : (owner + 1) * share]
+        out_ref[:, here] = (product + sum_ref[:, here]).astype(jnp.bfloat16)
         return carried
 
     for begin, end in ((0, cuts // 2), (cuts // 2, cuts)):
@@ -252,23 +248,17 @@
         lax.fori_loop(
             0, features // step, functools.partial(columns, begin=begin, end=end), 0, unroll=4
         )
-    first_ref[...] = out_ref[far_block(out_ref, info_ref, 0, n_db - 1)]
-    second_ref[...] = out_ref[far_block(out_ref, info_ref, 1, n_db - 1)]
-
-
-def self_out(info, attended, weight, n_db):
+
+
+def self_out(attended, weight):
     heads, rows, _ = attended.shape
     width, features = weight.shape
-    share = rows // n_db
     vmem = pl.BlockSpec(memory_space=pltpu.VMEM)
-    one = jax.ShapeDtypeStruct((share, features), jnp.bfloat16)
     return pl.pallas_call(
         self_out_kernel,
-        out_shape=[jax.ShapeDtypeStruct((n_db, share, features), jnp.bfloat16), one, one],
-        in_specs=[
-            pl.BlockSpec(memory_space=pltpu.SMEM), vmem, pl.BlockSpec(memory_space=pl.ANY)
-        ],
-        out_specs=[vmem] * 3,
+        out_shape=jax.ShapeDtypeStruct((rows, features), jnp.bfloat16),
+        in_specs=[vmem, pl.BlockSpec(memory_space=pl.ANY)],
+        out_specs=vmem,
         scratch_shapes=[
             pltpu.VMEM((rows, width), jnp.bfloat16),
             pltpu.VMEM((width, features), jnp.bfloat16),
@@ -282,103 +272,85 @@
             transcendentals=0,
         ),
         name="self_out",
-    )(info, attended, weight)
-
-
-def norm_kernel(
-    info_ref, blocks_ref, up_ref, down_ref, gain_ref, hidden_hbm, residual_ref, normed_ref, own_ref, sem
-):
-    me = info_ref[0]
-    share = up_ref.shape[0]
-    bring = pltpu.make_async_copy(
-        hidden_hbm.at[pl.ds(pl.multiple_of(me * share, share), share)], own_ref, sem
-    )
-    bring.start()
-    bring.wait()
-    rows = 16
-
-    def norm(at, carried):
-        here = pl.ds(pl.multiple_of(at * rows, rows), rows)
-        residual = own_ref[here, :].astype(jnp.float32) + blocks_ref[me, here, :].astype(jnp.float32)
-        residual = residual + up_ref[here, :].astype(jnp.float32)
-        residual = residual + down_ref[here, :].astype(jnp.float32)
-        residual_ref[here, :] = residual
-        mean_square = jnp.mean(residual * residual, axis=-1, keepdims=True)
-        normed_ref[here, :] = (
-            residual * lax.rsqrt(mean_square + 1e-05) * gain_ref[...].astype(jnp.float32)
-        ).astype(jnp.bfloat16)
-        return carried
-
-    lax.fori_loop(0, share // rows, norm, 0)
-
-
-def norm_share(info, blocks, up, down, gain, hidden):
-    share, features = up.shape
+    )(attended, weight)
+
+
+def project_kernel(where_ref, *refs, cuts):
+    wk_hbm, wv_hbm, keys_ref, values_ref = refs[-8:-4]
+    rows_ref, wk_ref, wv_ref, sems = refs[-4:]
+    tables = refs[:-8]
+    entries = keys_ref.shape[0] // NLEN
+    piece = NLEN // cuts
+    bring = [
+        pltpu.make_async_copy(source, target, sems.at[entries * cuts + at])
+        for at, (source, target) in enumerate(
+            ((wk_hbm, wk_ref), (wv_hbm, wv_ref))
+        )
+    ]
+    for copy in bring:
+        copy.start()
+
+    def entry_copy(entry, cut, table, first, shard):
+        return pltpu.make_async_copy(
+            table.at[first + cut, shard],
+            rows_ref.at[pl.ds(entry * NLEN + cut * piece, piece)],
+            sems.at[entry * cuts + cut],
+        )
+
+    for entry in range(entries):
+        for slot, table in enumerate(tables):
+
+            @pl.when(where_ref[2 + 3 * entry] == slot)
+            def _(entry=entry, table=table):
+                for cut in range(cuts):
+                    entry_copy(
+                        entry, cut, table, where_ref[3 + 3 * entry], where_ref[4 + 3 * entry]
+                    ).start()
+
+    for copy in bring:
+        copy.wait()
+    width = keys_ref.shape[1]
+    step = math.gcd(width, 512)
+    for group in range(entries // NEIGH):
+        for entry in range(NEIGH * group, NEIGH * (group + 1)):
+            for cut in range(cuts):
+                entry_copy(entry, cut, tables[0], 0, 0).wait()
+        here = slice(group * GROUP, (group + 1) * GROUP)
+        for at in range(0, width, step):
+            lanes = slice(at, at + step)
+            for weight, made in ((wk_ref, keys_ref), (wv_ref, values_ref)):
+                made[here, lanes] = jnp.dot(
+                    rows_ref[here, :], weight[:, lanes], preferred_element_type=jnp.float32
+                ).astype(jnp.bfloat16)
+
+
+def project_encodings(where, tables, w_cross_k, w_cross_v):
+    entries = (where.shape[0] - 2) // 3
+    piece, depth = tables[0].shape[2:]
+    cuts = NLEN // piece
+    width = w_cross_k.shape[1]
     vmem = pl.BlockSpec(memory_space=pltpu.VMEM)
+    anywhere = pl.BlockSpec(memory_space=pl.ANY)
+    made = jax.ShapeDtypeStruct((entries * NLEN, width), jnp.bfloat16)
     return pl.pallas_call(
-        norm_kernel,
-        out_shape=[
-            jax.ShapeDtypeStruct((share, features), jnp.float32),
-            jax.ShapeDtypeStruct((share, features), jnp.bfloat16),
+        functools.partial(project_kernel, cuts=cuts),
+        out_shape=[made, made],
+        in_specs=[pl.BlockSpec(memory_space=pltpu.SMEM)] + [anywhere] * (len(tables) + 2),
+        out_specs=[vmem] * 2,
+        scratch_shapes=[
+            pltpu.VMEM((entries * NLEN, depth), jnp.bfloat16),
+            pltpu.VMEM(w_cross_k.shape, jnp.bfloat16),
+            pltpu.VMEM(w_cross_v.shape, jnp.bfloat16),
+            pltpu.SemaphoreType.DMA((entries * cuts + 2,)),
         ],
-        in_specs=[pl.BlockSpec(memory_space=pltpu.SMEM)]
-        + [vmem] * 4
-        + [pl.BlockSpec(memory_space=pl.ANY)],
-        out_specs=[vmem, vmem],
-        scratch_shapes=[pltpu.VMEM((share, features), jnp.bfloat16), pltpu.SemaphoreType.DMA],
-        compiler_params=pltpu.CompilerParams(vmem_limit_bytes=SMALL_BYTES),
+        compiler_params=pltpu.CompilerParams(vmem_limit_bytes=VMEM_BYTES),
         cost_estimate=pl.CostEstimate(
-            flops=8 * up.size, bytes_accessed=16 * up.size, transcendentals=0
-        ),
-        name="norm_share",
-    )(info, blocks, up, down, gain, hidden)
-
-
-def project_kernel(where_ref, first_ref, second_ref, weight_ref, made_ref):
-    depth = first_ref.shape[-1]
-    rows = jnp.concatenate(
-        (first_ref[...].reshape(NLEN, depth), second_ref[...].reshape(NLEN, depth)), axis=0
-    )
-    made_ref[...] = jnp.dot(rows, weight_ref[...], preferred_element_type=jnp.float32).astype(
-        jnp.bfloat16
-    )
-
-
-def project_encodings(where, table, weight):
-    groups = (where.shape[0] - 2) // (2 * NEIGH)
-    _, cuts, _, piece, depth = table.shape
-    width = weight.shape[1]
-
-    def entry(neighbour):
-        def index(group, where_ref):
-            at = 2 + 2 * (NEIGH * group + neighbour)
-            return (where_ref[at], 0, where_ref[at + 1], 0, 0)
-
-        return pl.BlockSpec((1, cuts, 1, piece, depth), index)
-
-    return pl.pallas_call(
-        project_kernel,
-        out_shape=jax.ShapeDtypeStruct((groups * GROUP, width), jnp.bfloat16),
-        grid_spec=pltpu.PrefetchScalarGridSpec(
-            num_scalar_prefetch=1,
-            grid=(groups,),
-            in_specs=[
-                entry(0),
-                entry(1),
-                pl.BlockSpec((depth, width), lambda group, where_ref: (0, 0)),
-            ],
-            out_specs=pl.BlockSpec((GROUP, width), lambda group, where_ref: (group, 0)),
-        ),
-        compiler_params=pltpu.CompilerParams(
-            vmem_limit_bytes=LARGE_BYTES, dimension_semantics=("arbitrary",)
-        ),
-        cost_estimate=pl.CostEstimate(
-            flops=2 * groups * GROUP * depth * width,
-            bytes_accessed=2 * (groups * GROUP * (depth + width) + depth * width),
+            flops=entries * NLEN * depth,
+            bytes_accessed=2 * entries * NLEN * depth,
             transcendentals=0,
         ),
         name="project_encodings",
-    )(where, table, table, weight)
+    )(where, *tables, w_cross_k, w_cross_v)
 
 
 def apart_heads(query):
@@ -395,13 +367,33 @@
     return jnp.where(first, mixed[:rows], mixed[rows:])
 
 
-def cross_kernel(info_ref, own_ref, *refs, scale):
-    wq_hbm, keys_hbm, values_hbm, wo_hbm, out_ref, first_ref, second_ref = refs[-15:-8]
-    wq_ref, keys_ref, values_ref, wo_ref, rows_ref, query_ref, mixed_ref, sems = refs[-8:]
-    pieces = refs[:-15]
-    share, features = own_ref.shape
+def cross_kernel(
+    info_ref,
+    hidden_ref,
+    total_ref,
+    gain_ref,
+    wq_hbm,
+    keys_hbm,
+    values_hbm,
+    wo_hbm,
+    out_ref,
+    residual_ref,
+    first_ref,
+    second_ref,
+    wq_ref,
+    keys_ref,
+    values_ref,
+    wo_ref,
+    rows_ref,
+    query_ref,
+    mixed_ref,
+    sems,
+    *,
+    scale,
+):
+    rows, features = hidden_ref.shape
+    n_db, share, _ = out_ref.shape
     width = wq_ref.shape[1]
-    n_db = out_ref.shape[0]
     pairs = width // HD // 2
     tail = 16
     cut = features // 4
@@ -423,18 +415,22 @@
     ]
     for copy in wq_copies + other_copies:
         copy.start()
-    me = info_ref[0]
-
-    def place(source, owner):
-        @pl.when((owner >= 0) & (owner < n_db))
-        def _():
-            at = pl.multiple_of(jnp.clip(owner, 0, n_db - 1) * share, share)
-            rows_ref[pl.ds(at, share), :] = source[...]
-
-    place(own_ref, me)
-    for at, source in enumerate(pieces):
-        way = 1 - 2 * (at % 2)
-        place(source, me - way * (at // 2 + 1))
+    block = math.gcd(rows, 32)
+
+    def norm(at, carried):
+        here = pl.ds(pl.multiple_of(at * block, block), block)
+        residual = hidden_ref[here, :].astype(jnp.float32) + total_ref[here, :].astype(jnp.float32)
+        mean_square = jnp.mean(residual * residual, axis=-1, keepdims=True)
+        rows_ref[here, :] = (
+            residual * lax.rsqrt(mean_square + 1e-05) * gain_ref[...].astype(jnp.float32)
+        ).astype(jnp.bfloat16)
+        return carried
+
+    lax.fori_loop(0, rows // block, norm, 0)
+    own = pl.ds(pl.multiple_of(info_ref[0] * share, share), share)
+    residual_ref[...] = hidden_ref[own, :].astype(jnp.float32) + total_ref[own, :].astype(
+        jnp.float32
+    )
     lanes = [slice(2 * pair * HD, 2 * (pair + 1) * HD) for pair in range(pairs)]
     for k, copy in enumerate(wq_copies):
         copy.wait()
@@ -447,7 +443,7 @@
     for copy in other_copies[:2]:
         copy.wait()
     row = lax.broadcasted_iota(jnp.int32, (tail, 2 * HD), 0)
-    spans = n_db * share // SPAN
+    spans = rows // SPAN
     for span in range(spans):
         top = span * SPAN
         here, after = (slice((span + k) * GROUP, (span + k + 1) * GROUP) for k in (0, 1))
@@ -497,21 +493,23 @@
     second_ref[...] = out_ref[far_block(out_ref, info_ref, 1, n_db - 1)]
 
 
-def cross_block(info, normed, pieces, w_cross_q, keys, values, w_cross_out, n_db, scale):
-    share, features = normed.shape
+def cross_block(info, hidden, total, gain, w_cross_q, keys, values, w_cross_out, n_db, scale):
+    rows, features = hidden.shape
+    share = rows // n_db
     width = w_cross_q.shape[1]
-    rows = n_db * share
     vmem = pl.BlockSpec(memory_space=pltpu.VMEM)
     anywhere = pl.BlockSpec(memory_space=pl.ANY)
     one = jax.ShapeDtypeStruct((share, features), jnp.bfloat16)
-    flat = [one for pair in pieces for one in pair]
     return pl.pallas_call(
         functools.partial(cross_kernel, scale=scale),
-        out_shape=[jax.ShapeDtypeStruct((n_db, share, features), jnp.bfloat16), one, one],
-        in_specs=[pl.BlockSpec(memory_space=pltpu.SMEM)]
-        + [vmem] * (1 + len(flat))
-        + [anywhere] * 4,
-        out_specs=[vmem] * 3,
+        out_shape=[
+            jax.ShapeDtypeStruct((n_db, share, features), jnp.bfloat16),
+            jax.ShapeDtypeStruct((share, features), jnp.float32),
+            one,
+            one,
+        ],
+        in_specs=[pl.BlockSpec(memory_space=pltpu.SMEM)] + [vmem] * 3 + [anywhere] * 4,
+        out_specs=[vmem] * 4,
         scratch_shapes=[
             pltpu.VMEM((features, width), jnp.bfloat16),
             pltpu.VMEM(keys.shape, jnp.bfloat16),
@@ -525,11 +523,11 @@
         compiler_params=pltpu.CompilerParams(vmem_limit_bytes=VMEM_BYTES),
         cost_estimate=pl.CostEstimate(
             flops=4 * rows * width * (features + GROUP),
-            bytes_accessed=4 * width * (features + keys.shape[0]) + 4 * rows * features,
+            bytes_accessed=4 * width * (features + keys.shape[0]) + 8 * rows * features,
             transcendentals=rows * GROUP * width // HD,
         ),
         name="cross_block",
-    )(info, normed, *flat, w_cross_q, keys, values, w_cross_out)
+    )(info, hidden, total, gain, w_cross_q, keys, values, w_cross_out)
 
 
 def per_device(
@@ -564,7 +562,14 @@
     packed, nb_row, nb_shard = lax.optimization_barrier((packed, nb_row, nb_shard))
     wanted = jnp.stack((nb_row, nb_shard), axis=-1).astype(jnp.int32)
     place = jnp.stack((db_index, (seq_index > 0).astype(jnp.int32))).astype(jnp.int32)
-    info = jnp.concatenate((place, span_before(wanted).reshape(-1), wanted.reshape(-1)))
+    nearest = jnp.concatenate((span_before(wanted)[None], wanted), axis=0)
+    row, shard = nearest[..., 0], nearest[..., 1]
+    in_plane = n_seq == 8 and piece == NLEN
+    if in_plane:
+        where = jnp.stack((plane_slot(row, seq_index), jnp.zeros_like(row), shard), axis=-1)
+    else:
+        where = jnp.stack((jnp.zeros_like(row), row * (NLEN // piece), shard), axis=-1)
+    info = jnp.concatenate((place, where.reshape(-1))).astype(jnp.int32)
     if heads == n_seq:
         held = lax.all_to_all(packed, "seq", 0, 0, tiled=True)
         held, info = lax.optimization_barrier((held, info))
@@ -573,19 +578,27 @@
         attended = self_attention_gathered(query_rows, key_rows, value_rows, scale)
 
     along_db, attended = lax.optimization_barrier((along_db, attended))
-    table = lax.all_gather(along_db, "seq", axis=0).reshape(
-        rows_shard, NLEN // piece, n_db, piece, depth
-    )
-
-    partial, up, down = self_out(info, attended, w_self_out, n_db)
-    up, down = reduce_scatter(info, partial, up, down)
-    residual, normed = norm_share(
-        info, partial, up, down, norm_gain.reshape(1, features), hidden_in
-    )
-    projected = [project_encodings(info, table, weight) for weight in (w_cross_k, w_cross_v)]
-    pieces, (keys, values) = gather(normed, projected)
-    partial, up, down = cross_block(
-        info, normed, pieces, w_cross_q, keys, values, w_cross_out, n_db, scale
+    partial = self_out(attended, w_self_out)
+    along_db, partial = lax.optimization_barrier((along_db, partial))
+    total = lax.psum(partial, "db")
+    if in_plane:
+        tables = tuple(one[None] for one in plane_pieces(along_db))
+    else:
+        tables = (lax.all_gather(along_db, "seq", axis=0),)
+    projected = project_encodings(info, tables, w_cross_k, w_cross_v)
+    total, (keys, values) = lax.optimization_barrier((total, projected))
+
+    partial, residual, up, down = cross_block(
+        info,
+        hidden_in,
+        total,
+        norm_gain.reshape(1, features),
+        w_cross_q,
+        keys,
+        values,
+        w_cross_out,
+        n_db,
+        scale,
     )
     up, down = reduce_scatter(info, partial, up, down)
     own = lax.dynamic_index_in_dim(partial, db_index, 0, keepdims=False).astype(jnp.float32)

time: 221 us -> 222 us (level)
  waiting for transfers between devices: 100 us -> 130 us
  starting transfers between devices: 53.2 us -> 31.4 us
  Pallas kernels: 48 us -> 42.1 us
    ppermute x0 -> x7, waiting for transfers between devices: none -> 50.8 us  [plane_swap(): return lax.ppermute(block, 'seq', [(i, i ^ mask) for i in range(8)])]
    ppermute x18 -> x6, waiting for transfers between devices: 72.5 us -> 29.5 us  [line_shift(): return lax.ppermute(block, ('seq', 'db'), route)]
    ppermute x18 -> x6, starting transfers between devices: 42 us -> 15.5 us  [line_shift(): return lax.ppermute(block, ('seq', 'db'), route)]
    psum x0 -> x1, waiting for transfers between devices: none -> 21.9 us  [per_device(): total = lax.psum(partial, 'db')]
    pallas_call x4 -> x2, Pallas kernels: 23 us -> 17.8 us  [the longest x1 11.3 us: project_encodings(): pl.pallas_call(functools.partial(project_kernel, cuts=cuts), out_shape=[m...]
    ppermute x0 -> x7, starting transfers between devices: none -> 4.57 us  [plane_swap(): return lax.ppermute(block, 'seq', [(i, i ^ mask) for i in range(8)])]
  transfers between devices with their start and end apart: 23 -> 18, of which waited for: 16 -> 15; matrix products, arithmetic and copies ran while one was open for 0% -> 0% of each run, Pallas kernels for 14% -> 8%
where the time goes in v10:
time: 222 us; the launch traced here: 221 us
  waiting for transfers between devices  130 us (59%)
  Pallas kernels  42.1 us (19%)
  starting transfers between devices  31.4 us (14%)
  between operations  13.6 us (6%)
  other arithmetic  2.73 us (1%)
    ppermute x7, waiting for transfers between devices, plane_swap(): return lax.ppermute(block, 'seq', [(i, i ^ mask) for i in range(8)])  50.8 us
    ppermute x6, waiting for transfers between devices, line_shift(): return lax.ppermute(block, ('seq', 'db'), route)  29.5 us
    psum x1, waiting for transfers between devices, per_device(): total = lax.psum(partial, 'db')  21.9 us
    all_to_all x1, waiting for transfers between devices, per_device(): held = lax.all_to_all(packed, 'seq', 0, 0, tiled=True)  16.4 us
    ppermute x6, starting transfers between devices, line_shift(): return lax.ppermute(block, ('seq', 'db'), route)  15.5 us
    pallas_call x1, Pallas kernels, cross_block(): pl.pallas_call(functools.partial(cross_kernel, scale=scale), out_shape=[j...  12.3 us
    pallas_call x1, Pallas kernels, project_encodings(): pl.pallas_call(functools.partial(project_kernel, cuts=cuts), out_shape=[m...  11.3 us
    all_to_all x1, waiting for transfers between devices, per_device(): lax.all_to_all(self_attend_head(held, scale), 'seq', 0, 0, tiled=True)  7.68 us
  transfers between devices with their start and end apart: 18, of which 15 were waited for; matrix products, arithmetic and copies ran while one was open for 0% of the time, Pallas kernels for 8%

profile of v10, /device:TPU:0, one launch (start us, length us, event | category | flops | bytes accessed | tf_op | source)
XLA Modules:
  0.0 220.8 jit_solution(7962126414693880389)
XLA Ops:
  6.5 3.8 %pack_heads.1 = (bf16[8,3,256,128]{3,2,1,0:T(8,128)(2,1)}, bf16[128,1024]{1,0:T(8,128)(2,1)}) custom-call(s32[1]{0:T(128)} %bitcast.index_ref, bf16[256,1024]{1,0:T(8,128)(2,1)} %query_ref.1, bf16[256,1024]{1,0:T(8,128)(2,1)} %key_ref.1, bf16[256,1024]{1,0:T(8,128)(2,1)} %value_ref.1, bf16[1024,1024]{1,0:T(8,128)(2,1)} %bitcast.28), custom_call_target="tpu_custom_call" | custom-call | bytes 3145728 | tf_op jit(solution)/shard_map/pack_heads/pallas_call | solution.py:158
  10.4 0.0 copy-start.5
  10.4 5.3 %all-to-all-start = ((bf16[8,3,256,128]{3,2,1,0:T(8,128)(2,1)}), bf16[8,3,256,128]{3,2,1,0:T(8,128)(2,1)S(1)}, u32[]{:S(2)}, u32[]{:S(2)}) async-start(bf16[8,3,256,128]{3,2,1,0:T(8,128)(2,1)} %get-tuple-element.40), calls=%async_computation | async-start | bytes 3145728 | tf_op jit(solution)/shard_map/all_to_all | solution.py:574
  15.7 0.0 all-gather.3.cloned.1.call-start
  15.7 0.7 all-gather.3.cloned.1.call-update
  16.4 0.0 copy-done.5
  16.4 0.0 copy-done.6
  16.4 0.1 pad_add_fusion.1
  16.5 0.1 copy.17
  16.6 2.4 %collective-permute-start = (s32[2,2]{1,0:T(2,128)S(1)}, s32[2,2]{1,0:T(2,128)S(1)}, u32[]{:S(2)}, u32[]{:S(2)}) collective-permute-start(s32[2,2]{1,0:T(2,128)S(1)} %bitcast.36), channel_id=1, source_target_pairs={{0,4},{4,8},{8,12},{12,16},{16,20},{20,24},{24,28},{1,5},{5,9},{9,... | collective-permute-start | bytes 56 | tf_op jit(solution)/shard_map/ppermute | solution.py:27
  19.0 0.1 pad.4.clone
  19.1 0.7 collective-permute-done
  19.8 0.1 copy.18
  19.9 0.1 add_add_fusion
  20.0 0.1 pad_add_fusion
  20.1 0.1 copy.19
  20.2 0.1 reshape.16
  20.3 0.1 pad_add_fusion.2.where_ref.info_ref
  20.3 16.4 %all-to-all-done.qkv_ref = bf16[8,3,256,128]{3,2,1,0:T(8,128)(2,1)S(1)} async-done(((bf16[8,3,256,128]{3,2,1,0:T(8,128)(2,1)}), bf16[8,3,256,128]{3,2,1,0:T(8,128)(2,1)S(1)}, u32[]{:S(2)}, u32[]{:S(2)}) %all-to-all-start) | async-done | bytes 1572896 | tf_op jit(solution)/shard_map/all_to_all | solution.py:574
  36.7 5.6 %self_attend.1 = bf16[8,256,128]{2,1,0:T(8,128)(2,1)} custom-call(bf16[8,3,256,128]{3,2,1,0:T(8,128)(2,1)S(1)} %all-to-all-done.qkv_ref), custom_call_target="tpu_custom_call" | custom-call | flops 1073741824 | bytes 2097152 | tf_op jit(solution)/shard_map/self_attend/pallas_call | solution.py:125
  42.3 3.5 %all-to-all-start.1 = ((bf16[8,256,128]{2,1,0:T(8,128)(2,1)}), bf16[8,256,128]{2,1,0:T(8,128)(2,1)S(1)}, u32[]{:S(2)}, u32[]{:S(2)}) async-start(bf16[8,256,128]{2,1,0:T(8,128)(2,1)} %self_attend.1), calls=%async_computation.1 | async-start | bytes 1048576 | tf_op jit(solution)/shard_map/all_to_all | solution.py:576
  45.8 0.0 all-reduce.2.cloned.1.call-start
  45.8 1.9 all-gather.3.cloned.1.call-done
  47.8 7.7 %all-to-all-done.1.attended_ref = bf16[8,256,128]{2,1,0:T(8,128)(2,1)S(1)} async-done(((bf16[8,256,128]{2,1,0:T(8,128)(2,1)}), bf16[8,256,128]{2,1,0:T(8,128)(2,1)S(1)}, u32[]{:S(2)}, u32[]{:S(2)}) %all-to-all-start.1) | async-done | bytes 524320 | tf_op jit(solution)/shard_map/all_to_all | solution.py:576
  55.4 6.6 %self_out.1 = bf16[256,4096]{1,0:T(8,128)(2,1)} custom-call(bf16[8,256,128]{2,1,0:T(8,128)(2,1)S(1)} %all-to-all-done.1.attended_ref, bf16[1024,4096]{1,0:T(8,128)(2,1)} %weight_hbm.1), custom_call_target="tpu_custom_call" | custom-call | flops 2147483648 | bytes 11010048 | tf_op jit(solution)/shard_map/self_out/pallas_call | solution.py:257
  62.0 0.0 copy-start.4
  62.0 0.0 copy-done
  62.1 0.6 collective-permute-start.1
  62.7 0.6 collective-permute-start.2
  63.2 2.4 %collective-permute-start.3 = (bf16[4,128,1024]{2,1,0:T(8,128)(2,1)S(1)}, bf16[4,128,1024]{2,1,0:T(8,128)(2,1)}, u32[]{:S(2)}, u32[]{:S(2)}) collective-permute-start(bf16[4,128,1024]{2,1,0:T(8,128)(2,1)S(1)} %bitcast.23), channel_id=1, source_target_pairs={{0,24},{4,28},{8,16},{12,20},{16,8},{20,12},{24,0},{28,4},{1,25},{... | collective-permute-start | bytes 3145736 | tf_op jit(solution)/shard_map/ppermute | solution.py:91
  65.6 0.0 all-reduce.2.cloned.1.call-update
  65.6 22.6 %collective-permute-done.1 = bf16[4,128,1024]{2,1,0:T(8,128)(2,1)S(1)} collective-permute-done((bf16[4,128,1024]{2,1,0:T(8,128)(2,1)S(1)}, bf16[4,128,1024]{2,1,0:T(8,128)(2,1)S(1)}, u32[]{:S(2)}, u32[]{:S(2)}) %collective-permute-start.1) | collective-permute-done | bytes 1048608 | tf_op jit(solution)/shard_map/ppermute | solution.py:91
  88.2 21.9 %collective-permute-done.2 = bf16[4,128,1024]{2,1,0:T(8,128)(2,1)} collective-permute-done((bf16[4,128,1024]{2,1,0:T(8,128)(2,1)S(1)}, bf16[4,128,1024]{2,1,0:T(8,128)(2,1)}, u32[]{:S(2)}, u32[]{:S(2)}) %collective-permute-start.2) | collective-permute-done | bytes 1048608 | tf_op jit(solution)/shard_map/ppermute | solution.py:91
  110.1 0.0 collective-permute-done.3
  110.1 0.0 collective-permute-start.4
  110.1 0.5 collective-permute-start.5
  110.6 0.0 collective-permute-start.6
  110.6 0.5 collective-permute-start.7
  111.1 0.0 copy-done.4
  111.1 1.6 collective-permute-done.4
  112.8 3.0 %collective-permute-done.5 = bf16[4,128,1024]{2,1,0:T(8,128)(2,1)S(1)} collective-permute-done((bf16[4,128,1024]{2,1,0:T(8,128)(2,1)S(1)}, bf16[4,128,1024]{2,1,0:T(8,128)(2,1)S(1)}, u32[]{:S(2)}, u32[]{:S(2)}) %collective-permute-start.5) | collective-permute-done | bytes 1048608 | tf_op jit(solution)/shard_map/ppermute | solution.py:91
  115.8 0.2 collective-permute-done.6
  116.0 1.5 collective-permute-done.7
  117.5 0.0 copy-done.1
  117.5 0.0 copy-done.2
  117.5 1.0 copy-done.3
  118.5 11.3 %project_encodings.1 = (bf16[1280,1024]{1,0:T(8,128)(2,1)}, bf16[1280,1024]{1,0:T(8,128)(2,1)}) custom-call(s32[32]{0:T(128)S(1)} %pad_add_fusion.2.where_ref.info_ref, bf16[1,4,128,1024]{3,2,1,0:T(8,128)(2,1)S(1)} %bitcast.25, bf16[1,4,128,1024]{3,2,1,0:T(8,128)(2,1)S(1)} %bitcast.26, bf16[1,4,128,1024]{3,2,1,0:T(8,128)(2,1)} %bitcast.11.refs_2_, ...), custom_call_target="tpu_custom_call" | custom-call | flops 1310720 | bytes 2621440 | tf_op jit(solution)/shard_map/project_encodings/pallas_call | solution.py:335
  129.7 21.9 %all-reduce.2.cloned.1.call-done.total_ref = bf16[256,4096]{1,0:T(8,128)(2,1)} async-done(((bf16[256,4096]{1,0:T(8,128)(2,1)}), bf16[256,4096]{1,0:T(8,128)(2,1)}) %all-reduce.2.cloned.1.call-update) | async-done | bytes 2097168 | tf_op jit(solution)/shard_map/psum | solution.py:583
  151.6 12.3 %cross_block.1 = (bf16[4,64,4096]{2,1,0:T(8,128)(2,1)S(1)}, f32[64,4096]{1,0:T(8,128)S(1)}, bf16[64,4096]{1,0:T(8,128)(2,1)S(1)}, bf16[64,4096]{1,0:T(8,128)(2,1)S(1)}) custom-call(s32[32]{0:T(128)S(1)} %pad_add_fusion.2.where_ref.info_ref, bf16[256,4096]{1,0:T(8,128)(2,1)} %hidden_ref.1, bf16[256,4096]{1,0:T(8,128)(2,1)} %all-reduce.2.cloned.1.call-done.total_ref, ...), custom_call_target="tpu_custom_call" | custom-call | flops 4563402752 | bytes 30408704 | tf_op jit(solution)/shard_map/cross_block/pallas_call | solution.py:503
  163.9 0.7 collective-permute-start.8
  164.6 2.0 collective-permute-start.9
  166.7 0.0 collective-permute-done.8.down_ref
  166.7 10.9 %collective-permute-done.9.up_ref = bf16[64,4096]{1,0:T(8,128)(2,1)S(1)} collective-permute-done((bf16[64,4096]{1,0:T(8,128)(2,1)S(1)}, bf16[64,4096]{1,0:T(8,128)(2,1)S(1)}, u32[]{:S(2)}, u32[]{:S(2)}) %collective-permute-start.9) | collective-permute-done | bytes 524320 | tf_op jit(solution)/shard_map/ppermute | solution.py:39
  177.6 0.8 add_step.2
  178.4 0.7 collective-permute-start.10
  179.1 5.0 %collective-permute-start.11 = (bf16[64,4096]{1,0:T(8,128)(2,1)S(1)}, bf16[64,4096]{1,0:T(8,128)(2,1)S(1)}, u32[]{:S(2)}, u32[]{:S(2)}) collective-permute-start(bf16[64,4096]{1,0:T(8,128)(2,1)S(1)} %get-tuple-element.66), channel_id=1, source_target_pairs={{0,1},{1,2},{4,5},{5,6},{8,9},{9,10},{12,13},{13,14},{16,17},{17,1... | collective-permute-start | bytes 1572872 | tf_op jit(solution)/shard_map/ppermute | solution.py:39
  184.1 0.0 collective-permute-done.10.down_ref
  184.1 10.0 %collective-permute-done.11.up_ref = bf16[64,4096]{1,0:T(8,128)(2,1)S(1)} collective-permute-done((bf16[64,4096]{1,0:T(8,128)(2,1)S(1)}, bf16[64,4096]{1,0:T(8,128)(2,1)S(1)}, u32[]{:S(2)}, u32[]{:S(2)}) %collective-permute-start.11) | collective-permute-done | bytes 524320 | tf_op jit(solution)/shard_map/ppermute | solution.py:39
  194.1 1.7 add_step.3
  195.9 1.3 collective-permute-start.12
  197.1 5.8 %collective-permute-start.13 = (bf16[64,4096]{1,0:T(8,128)(2,1)}, bf16[64,4096]{1,0:T(8,128)(2,1)}, u32[]{:S(2)}, u32[]{:S(2)}) collective-permute-start(bf16[64,4096]{1,0:T(8,128)(2,1)} %get-tuple-element.70), channel_id=1, source_target_pairs={{0,1},{1,2},{2,3},{4,5},{5,6},{6,7},{8,9},{9,10},{10,11},{12,13},{... | collective-permute-start | bytes 1572872 | tf_op jit(solution)/shard_map/ppermute | solution.py:39
  203.0 7.4 %collective-permute-done.12 = bf16[64,4096]{1,0:T(8,128)(2,1)} collective-permute-done((bf16[64,4096]{1,0:T(8,128)(2,1)}, bf16[64,4096]{1,0:T(8,128)(2,1)}, u32[]{:S(2)}, u32[]{:S(2)}) %collective-permute-start.12) | collective-permute-done | bytes 524320 | tf_op jit(solution)/shard_map/ppermute | solution.py:39
  210.4 1.2 collective-permute-done.13
  211.6 2.4 %fusion.1 = f32[64,4096]{1,0:T(8,128)} fusion(f32[64,4096]{1,0:T(8,128)S(1)} %get-tuple-element.59, bf16[64,4096]{1,0:T(8,128)(2,1)} %collective-permute-done.12, bf16[64,4096]{1,0:T(8,128)(2,1)} %collective-permute-done.13, bf16[4,64,4096]{2,1,0:T(8,128)(2,1)S(1)} %get-tuple-element.60.blocks_ref, s32[]{:T(128)S(6)} %select_n.4), kind=kLoop, calls=%fused_computation.2 | loop fusion | flops 1572864 | bytes 3670020 | tf_op jit(solution)/shard_map/add | solution.py:605
  (7 shorter events, 0.0 us)
Async XLA Ops:
  10.4 6.1 %copy-start.5 = (s32[4,2]{0,1:T(2,128)S(1)}, s32[4,2]{0,1:T(2,128)}, u32[]{:S(2)}) copy-start(s32[4,2]{0,1:T(2,128)} %param.24) | copy-start | bytes 100
  10.4 6.1 %copy-start.6 = (s32[4,2]{0,1:T(2,128)S(1)}, s32[4,2]{0,1:T(2,128)}, u32[]{:S(2)}) copy-start(s32[4,2]{0,1:T(2,128)} %param.25) | copy-start | bytes 100
  10.4 26.3 %all-to-all-start = ((bf16[8,3,256,128]{3,2,1,0:T(8,128)(2,1)}), bf16[8,3,256,128]{3,2,1,0:T(8,128)(2,1)S(1)}, u32[]{:S(2)}, u32[]{:S(2)}) async-start(bf16[8,3,256,128]{3,2,1,0:T(8,128)(2,1)} %get-tuple-element.40), calls=%async_computation | async-start | bytes 3145728 | tf_op jit(solution)/shard_map/all_to_all | solution.py:574
  15.7 32.1 %all-gather.3.cloned.1.call-start = ((), (), s32[]{:S(2)}) async-start(), calls=%async_computation.3 | async-start | bytes 1310720 | tf_op jit(solution)/shard_map/all_gather | solution.py:560
  16.6 3.2 %collective-permute-start = (s32[2,2]{1,0:T(2,128)S(1)}, s32[2,2]{1,0:T(2,128)S(1)}, u32[]{:S(2)}, u32[]{:S(2)}) collective-permute-start(s32[2,2]{1,0:T(2,128)S(1)} %bitcast.36), channel_id=1, source_target_pairs={{0,4},{4,8},{8,12},{12,16},{16,20},{20,24},{24,28},{1,5},{5,9},{9,... | collective-permute-start | bytes 56 | tf_op jit(solution)/shard_map/ppermute | solution.py:27
  42.3 13.2 %all-to-all-start.1 = ((bf16[8,256,128]{2,1,0:T(8,128)(2,1)}), bf16[8,256,128]{2,1,0:T(8,128)(2,1)S(1)}, u32[]{:S(2)}, u32[]{:S(2)}) async-start(bf16[8,256,128]{2,1,0:T(8,128)(2,1)} %self_attend.1), calls=%async_computation.1 | async-start | bytes 1048576 | tf_op jit(solution)/shard_map/all_to_all | solution.py:576
  45.8 105.9 %all-reduce.2.cloned.1.call-start = ((), (), s32[]{:S(2)}) async-start(), calls=%async_computation.2 | async-start | bytes 4194304 | tf_op jit(solution)/shard_map/psum | solution.py:583
  55.4 6.6 %copy-start = (bf16[512,1024]{1,0:T(8,128)(2,1)S(1)}, bf16[512,1024]{1,0:T(8,128)(2,1)}, u32[]{:S(2)}) copy-start(bf16[512,1024]{1,0:T(8,128)(2,1)} %all-gather.3.cloned.1.call-done) | copy-start | bytes 3145732
  62.0 49.1 %copy-start.4 = (bf16[4096]{0:T(1024)(128)(2,1)S(1)}, bf16[4096]{0:T(1024)(128)(2,1)}, u32[]{:S(2)}) copy-start(bf16[4096]{0:T(1024)(128)(2,1)} %param.18) | copy-start | bytes 24580
  62.1 26.2 %collective-permute-start.1 = (bf16[4,128,1024]{2,1,0:T(8,128)(2,1)S(1)}, bf16[4,128,1024]{2,1,0:T(8,128)(2,1)S(1)}, u32[]{:S(2)}, u32[]{:S(2)}) collective-permute-start(bf16[4,128,1024]{2,1,0:T(8,128)(2,1)S(1)} %bitcast.21), channel_id=1, source_target_pairs={{0,8},{4,12},{8,0},{12,4},{16,24},{20,28},{24,16},{28,20},{1,9},{5... | collective-permute-start | bytes 3145736 | tf_op jit(solution)/shard_map/ppermute | solution.py:91
  62.7 47.4 %collective-permute-start.2 = (bf16[4,128,1024]{2,1,0:T(8,128)(2,1)S(1)}, bf16[4,128,1024]{2,1,0:T(8,128)(2,1)}, u32[]{:S(2)}, u32[]{:S(2)}) collective-permute-start(bf16[4,128,1024]{2,1,0:T(8,128)(2,1)S(1)} %bitcast.22), channel_id=1, source_target_pairs={{0,16},{4,20},{8,24},{12,28},{16,0},{20,4},{24,8},{28,12},{1,17},{... | collective-permute-start | bytes 3145736 | tf_op jit(solution)/shard_map/ppermute | solution.py:91
  63.2 46.9 %collective-permute-start.3 = (bf16[4,128,1024]{2,1,0:T(8,128)(2,1)S(1)}, bf16[4,128,1024]{2,1,0:T(8,128)(2,1)}, u32[]{:S(2)}, u32[]{:S(2)}) collective-permute-start(bf16[4,128,1024]{2,1,0:T(8,128)(2,1)S(1)} %bitcast.23), channel_id=1, source_target_pairs={{0,24},{4,28},{8,16},{12,20},{16,8},{20,12},{24,0},{28,4},{1,25},{... | collective-permute-start | bytes 3145736 | tf_op jit(solution)/shard_map/ppermute | solution.py:91
  110.1 2.7 %collective-permute-start.4 = (bf16[4,128,1024]{2,1,0:T(8,128)(2,1)S(1)}, bf16[4,128,1024]{2,1,0:T(8,128)(2,1)S(1)}, u32[]{:S(2)}, u32[]{:S(2)}) collective-permute-start(bf16[4,128,1024]{2,1,0:T(8,128)(2,1)S(1)} %bitcast.24), channel_id=1, source_target_pairs={{0,4},{4,0},{8,12},{12,8},{16,20},{20,16},{24,28},{28,24},{1,5},{5... | collective-permute-start | bytes 3145736 | tf_op jit(solution)/shard_map/ppermute | solution.py:91
  110.1 5.7 %collective-permute-start.5 = (bf16[4,128,1024]{2,1,0:T(8,128)(2,1)S(1)}, bf16[4,128,1024]{2,1,0:T(8,128)(2,1)S(1)}, u32[]{:S(2)}, u32[]{:S(2)}) collective-permute-start(bf16[4,128,1024]{2,1,0:T(8,128)(2,1)S(1)} %collective-permute-done.1), channel_id=1, source_target_pairs={{0,4},{4,0},{8,12},{12,8},{16,20},{20,16},{24,28},{28,24},{1,5},{5... | collective-permute-start | bytes 3145736 | tf_op jit(solution)/shard_map/ppermute | solution.py:91
  110.6 5.4 %collective-permute-start.6 = (bf16[4,128,1024]{2,1,0:T(8,128)(2,1)}, bf16[4,128,1024]{2,1,0:T(8,128)(2,1)S(1)}, u32[]{:S(2)}, u32[]{:S(2)}) collective-permute-start(bf16[4,128,1024]{2,1,0:T(8,128)(2,1)} %collective-permute-done.2), channel_id=1, source_target_pairs={{0,4},{4,0},{8,12},{12,8},{16,20},{20,16},{24,28},{28,24},{1,5},{5... | collective-permute-start | bytes 3145736 | tf_op jit(solution)/shard_map/ppermute | solution.py:91
  110.6 6.9 %collective-permute-start.7 = (bf16[4,128,1024]{2,1,0:T(8,128)(2,1)}, bf16[4,128,1024]{2,1,0:T(8,128)(2,1)S(1)}, u32[]{:S(2)}, u32[]{:S(2)}) collective-permute-start(bf16[4,128,1024]{2,1,0:T(8,128)(2,1)} %collective-permute-done.3), channel_id=1, source_target_pairs={{0,4},{4,0},{8,12},{12,8},{16,20},{20,16},{24,28},{28,24},{1,5},{5... | collective-permute-start | bytes 3145736 | tf_op jit(solution)/shard_map/ppermute | solution.py:91
  115.8 1.7 copy-start.1
  116.0 1.5 copy-start.2
  117.5 1.0 copy-start.3
  163.9 2.7 %collective-permute-start.8 = (bf16[64,4096]{1,0:T(8,128)(2,1)S(1)}, bf16[64,4096]{1,0:T(8,128)(2,1)S(1)}, u32[]{:S(2)}, u32[]{:S(2)}) collective-permute-start(bf16[64,4096]{1,0:T(8,128)(2,1)S(1)} %get-tuple-element.61), channel_id=1, source_target_pairs={{3,2},{7,6},{11,10},{15,14},{19,18},{23,22},{27,26},{31,30}} | collective-permute-start | bytes 1572872 | tf_op jit(solution)/shard_map/ppermute | solution.py:39
  164.6 12.9 %collective-permute-start.9 = (bf16[64,4096]{1,0:T(8,128)(2,1)S(1)}, bf16[64,4096]{1,0:T(8,128)(2,1)S(1)}, u32[]{:S(2)}, u32[]{:S(2)}) collective-permute-start(bf16[64,4096]{1,0:T(8,128)(2,1)S(1)} %get-tuple-element.62), channel_id=1, source_target_pairs={{0,1},{4,5},{8,9},{12,13},{16,17},{20,21},{24,25},{28,29}} | collective-permute-start | bytes 1572872 | tf_op jit(solution)/shard_map/ppermute | solution.py:39
  178.4 5.7 %collective-permute-start.10 = (bf16[64,4096]{1,0:T(8,128)(2,1)S(1)}, bf16[64,4096]{1,0:T(8,128)(2,1)S(1)}, u32[]{:S(2)}, u32[]{:S(2)}) collective-permute-start(bf16[64,4096]{1,0:T(8,128)(2,1)S(1)} %get-tuple-element.65), channel_id=1, source_target_pairs={{2,1},{3,2},{6,5},{7,6},{10,9},{11,10},{14,13},{15,14},{18,17},{19... | collective-permute-start | bytes 1572872 | tf_op jit(solution)/shard_map/ppermute | solution.py:39
  179.1 15.0 %collective-permute-start.11 = (bf16[64,4096]{1,0:T(8,128)(2,1)S(1)}, bf16[64,4096]{1,0:T(8,128)(2,1)S(1)}, u32[]{:S(2)}, u32[]{:S(2)}) collective-permute-start(bf16[64,4096]{1,0:T(8,128)(2,1)S(1)} %get-tuple-element.66), channel_id=1, source_target_pairs={{0,1},{1,2},{4,5},{5,6},{8,9},{9,10},{12,13},{13,14},{16,17},{17,1... | collective-permute-start | bytes 1572872 | tf_op jit(solution)/shard_map/ppermute | solution.py:39
  195.9 14.6 %collective-permute-start.12 = (bf16[64,4096]{1,0:T(8,128)(2,1)}, bf16[64,4096]{1,0:T(8,128)(2,1)}, u32[]{:S(2)}, u32[]{:S(2)}) collective-permute-start(bf16[64,4096]{1,0:T(8,128)(2,1)} %get-tuple-element.69), channel_id=1, source_target_pairs={{1,0},{2,1},{3,2},{5,4},{6,5},{7,6},{9,8},{10,9},{11,10},{13,12},{... | collective-permute-start | bytes 1572872 | tf_op jit(solution)/shard_map/ppermute | solution.py:39
  197.1 14.4 %collective-permute-start.13 = (bf16[64,4096]{1,0:T(8,128)(2,1)}, bf16[64,4096]{1,0:T(8,128)(2,1)}, u32[]{:S(2)}, u32[]{:S(2)}) collective-permute-start(bf16[64,4096]{1,0:T(8,128)(2,1)} %get-tuple-element.70), channel_id=1, source_target_pairs={{0,1},{1,2},{2,3},{4,5},{5,6},{6,7},{8,9},{9,10},{10,11},{12,13},{... | collective-permute-start | bytes 1572872 | tf_op jit(solution)/shard_map/ppermute | solution.py:39
Sparse Core Ops, SparseCore 0:
  18.1 29.6 all-gather.2
  65.8 85.8 all-reduce.1

commit v11 on v10

--- a/solution.py
+++ b/solution.py
@@ -18,7 +18,6 @@
 LOG2E = 1.4426950408889634
 VMEM_BYTES = 48 * 1024 * 1024
 LARGE_BYTES = 58 * 1024 * 1024
-SMALL_BYTES = 4 * 1024 * 1024
 
 
 def shift(block, axis, distance, senders):
@@ -27,73 +26,14 @@
     return lax.ppermute(block, axis, route)
 
 
-def line_shift(block, lead, up_from, down_from):
-    n_seq, size = lax.axis_size("seq"), lax.axis_size("db")
-    route = []
-    for row in range(n_seq):
-        up = lead == 0
-        for k in up_from if up else down_from:
-            other = k + 1 if up else k - 1
-            if 0 <= other < size:
-                route.append((row * size + k, row * size + other))
-    return lax.ppermute(block, ("seq", "db"), route)
-
-
-def far_block(blocks_ref, info_ref, lead, far):
-    way = 1 - 2 * lead
-    return jnp.clip(info_ref[0] + way * far, 0, blocks_ref.shape[0] - 1)
-
-
-def add_kernel(info_ref, blocks_ref, up_ref, down_ref, up_out_ref, down_out_ref, *, far):
-    rows = 16
-
-    def add(at, carried):
-        here = pl.ds(pl.multiple_of(at * rows, rows), rows)
-        for lead, ref, out_ref in ((0, up_ref, up_out_ref), (1, down_ref, down_out_ref)):
-            index = far_block(blocks_ref, info_ref, lead, far)
-            out_ref[here, :] = (
-                blocks_ref[index, here, :].astype(jnp.float32) + ref[here, :].astype(jnp.float32)
-            ).astype(jnp.bfloat16)
-        return carried
-
-    lax.fori_loop(0, up_ref.shape[0] // rows, add, 0)
-
-
-def add_step(info, blocks, up, down, far):
-    vmem = pl.BlockSpec(memory_space=pltpu.VMEM)
-    one = jax.ShapeDtypeStruct(up.shape, up.dtype)
-    return pl.pallas_call(
-        functools.partial(add_kernel, far=far),
-        out_shape=[one, one],
-        in_specs=[pl.BlockSpec(memory_space=pltpu.SMEM), vmem, vmem, vmem],
-        out_specs=[vmem, vmem],
-        compiler_params=pltpu.CompilerParams(vmem_limit_bytes=SMALL_BYTES),
-        cost_estimate=pl.CostEstimate(
-            flops=2 * up.size, bytes_accessed=12 * up.size, transcendentals=0
-        ),
-        name="add_step",
-    )(info, blocks, up, down)
-
-
-def reduce_scatter(info, blocks, up, down):
-    size = lax.axis_size("db")
-    for step in range(size - 1):
-        senders = (range(step + 1), range(size - 1 - step, size))
-        if step:
-            up, down = add_step(info, blocks, up, down, size - 1 - step)
-        down = line_shift(down, 1, *senders)
-        up = line_shift(up, 0, *senders)
-        down, up = lax.optimization_barrier((down, up))
-    return up, down
-
-
 def plane_swap(block, mask):
     return lax.ppermute(block, "seq", [(i, i ^ mask) for i in range(8)])
 
 
-def plane_pieces(own):
-    same = lax.optimization_barrier((own,) + tuple(plane_swap(own, mask) for mask in (2, 4, 6)))
-    return same + tuple(plane_swap(one, 1) for one in same)
+def plane_pieces(own, after):
+    same = (own,) + tuple(plane_swap(own, mask) for mask in (2, 4, 6))
+    same, after = lax.optimization_barrier((same, after))
+    return same + tuple(plane_swap(one, 1) for one in same), after
 
 
 def plane_slot(owner, me):
@@ -211,10 +151,11 @@
 
 
 def self_out_kernel(
-    attended_ref, weight_hbm, out_ref, rows_ref, weight_ref, sum_ref, sems
+    attended_ref, weight_hbm, first_ref, second_ref, rows_ref, weight_ref, sum_ref, sems, *, n_db
 ):
     heads, rows, _ = attended_ref.shape
-    features = out_ref.shape[1]
+    features = first_ref.shape[1]
+    half = rows // n_db // 2
     width = weight_hbm.shape[0]
     cuts = 4
     depth = width // cuts
@@ -226,8 +167,14 @@
     ]
     for copy in copies:
         copy.start()
-    for head in range(heads):
-        rows_ref[:, head * HD : (head + 1) * HD] = attended_ref[head]
+    for chunk in range(2):
+        for owner in range(n_db):
+            source = (2 * owner + chunk) * half
+            target = (chunk * n_db + owner) * half
+            for head in range(heads):
+                rows_ref[target : target + half, head * HD : (head + 1) * HD] = attended_ref[
+                    head, source : source + half, :
+                ]
     step = math.gcd(features, 512)
 
     def columns(at, carried, begin, end):
@@ -239,7 +186,9 @@
         if begin == 0:
             sum_ref[:, here] = product
             return carried
-        out_ref[:, here] = (product + sum_ref[:, here]).astype(jnp.bfloat16)
+        product = (product + sum_ref[:, here]).astype(jnp.bfloat16)
+        first_ref[:, here] = product[: rows // 2]
+        second_ref[:, here] = product[rows // 2 :]
         return carried
 
     for begin, end in ((0, cuts // 2), (cuts // 2, cuts)):
@@ -250,15 +199,15 @@
         )
 
 
-def self_out(attended, weight):
+def self_out(attended, weight, n_db):
     heads, rows, _ = attended.shape
     width, features = weight.shape
     vmem = pl.BlockSpec(memory_space=pltpu.VMEM)
     return pl.pallas_call(
-        self_out_kernel,
-        out_shape=jax.ShapeDtypeStruct((rows, features), jnp.bfloat16),
+        functools.partial(self_out_kernel, n_db=n_db),
+        out_shape=[jax.ShapeDtypeStruct((rows // 2, features), jnp.bfloat16)] * 2,
         in_specs=[vmem, pl.BlockSpec(memory_space=pl.ANY)],
-        out_specs=vmem,
+        out_specs=[vmem] * 2,
         scratch_shapes=[
             pltpu.VMEM((rows, width), jnp.bfloat16),
             pltpu.VMEM((width, features), jnp.bfloat16),
@@ -369,7 +318,7 @@
 
 def cross_kernel(
     info_ref,
-    hidden_ref,
+    hidden_hbm,
     total_ref,
     gain_ref,
     wq_hbm,
@@ -378,26 +327,35 @@
     wo_hbm,
     out_ref,
     residual_ref,
-    first_ref,
-    second_ref,
     wq_ref,
     keys_ref,
     values_ref,
     wo_ref,
+    hidden_ref,
     rows_ref,
     query_ref,
     mixed_ref,
     sems,
     *,
+    chunk,
+    n_db,
     scale,
 ):
-    rows, features = hidden_ref.shape
-    n_db, share, _ = out_ref.shape
+    rows, features = total_ref.shape
+    half = rows // n_db
     width = wq_ref.shape[1]
     pairs = width // HD // 2
     tail = 16
     cut = features // 4
     low = width // 4
+    hidden_copies = [
+        pltpu.make_async_copy(
+            hidden_hbm.at[pl.ds((2 * owner + chunk) * half, half)],
+            hidden_ref.at[pl.ds(owner * half, half)],
+            sems.at[10 + owner],
+        )
+        for owner in range(n_db)
+    ]
     wq_copies = [
         pltpu.make_async_copy(
             wq_hbm.at[pl.ds(k * cut, cut)], wq_ref.at[pl.ds(k * cut, cut)], sems.at[k]
@@ -413,8 +371,10 @@
         )
         for k in range(4)
     ]
-    for copy in wq_copies + other_copies:
+    for copy in hidden_copies + wq_copies + other_copies:
         copy.start()
+    for copy in hidden_copies:
+        copy.wait()
     block = math.gcd(rows, 32)
 
     def norm(at, carried):
@@ -427,7 +387,7 @@
         return carried
 
     lax.fori_loop(0, rows // block, norm, 0)
-    own = pl.ds(pl.multiple_of(info_ref[0] * share, share), share)
+    own = pl.ds(pl.multiple_of(info_ref[0] * half, half), half)
     residual_ref[...] = hidden_ref[own, :].astype(jnp.float32) + total_ref[own, :].astype(
         jnp.float32
     )
@@ -443,21 +403,28 @@
     for copy in other_copies[:2]:
         copy.wait()
     row = lax.broadcasted_iota(jnp.int32, (tail, 2 * HD), 0)
-    spans = rows // SPAN
-    for span in range(spans):
-        top = span * SPAN
-        here, after = (slice((span + k) * GROUP, (span + k + 1) * GROUP) for k in (0, 1))
-        work = [(slice(top, top + SPAN), here, at) for at in lanes]
-        work += [(slice(top + SPAN - tail, top + SPAN), after, at) for at in lanes]
+    queries = [query_ref[:, at].astype(jnp.bfloat16) for at in lanes]
+    for owner in range(n_db):
+        top = owner * half
+        place = (2 * owner + chunk) * half
+        group = place // SPAN
+        ends = (place + half) % SPAN == 0
+        here, after = (slice((group + k) * GROUP, (group + k + 1) * GROUP) for k in (0, 1))
+        work = [(query[top : top + half], here, at) for query, at in zip(queries, lanes)]
+        if ends:
+            work += [
+                (query[top + half - tail : top + half], after, at)
+                for query, at in zip(queries, lanes)
+            ]
         scores = [
             lax.dot_general(
-                apart_heads(query_ref[of, at].astype(jnp.bfloat16)),
+                apart_heads(query),
                 keys_ref[which, at],
                 (((1,), (1,)), ((), ())),
                 preferred_element_type=jnp.float32,
             )
             * (scale * LOG2E)
-            for of, which, at in work
+            for query, which, at in work
         ]
         tops = [jnp.max(one, axis=-1, keepdims=True) for one in scores]
         weights = [jnp.exp2(one - top_one) for one, top_one in zip(scores, tops)]
@@ -470,12 +437,19 @@
         ]
         mixed = [together_heads(one / total) for one, total in zip(mixed, totals)]
         for pair, at in enumerate(lanes):
-            main, last = mixed[pair], mixed[pairs + pair]
-            if span == 0:
+            main = mixed[pair]
+            if group == 0:
                 main = jnp.where(info_ref[1] > 0, main, 0.0)
-            last = jnp.where(row == tail - 1, last, main[SPAN - tail :])
-            mixed_ref[top : top + SPAN - tail, at] = main[: SPAN - tail].astype(jnp.bfloat16)
-            mixed_ref[top + SPAN - tail : top + SPAN, at] = last.astype(jnp.bfloat16)
+            if ends:
+                last = jnp.where(row == tail - 1, mixed[pairs + pair], main[half - tail :])
+                if half > tail:
+                    mixed_ref[top : top + half - tail, at] = main[: half - tail].astype(
+                        jnp.bfloat16
+                    )
+                mixed_ref[top + half - tail : top + half, at] = last.astype(jnp.bfloat16)
+            else:
+                mixed_ref[top : top + half, at] = main.astype(jnp.bfloat16)
+
     for copy in other_copies[2:]:
         copy.wait()
     step = math.gcd(features, 512)
@@ -483,42 +457,37 @@
     def columns(at, carried):
         here = pl.ds(pl.multiple_of(at * step, step), step)
         product = jnp.dot(mixed_ref[...], wo_ref[:, here], preferred_element_type=jnp.float32)
-        product = product.astype(jnp.bfloat16)
-        for owner in range(n_db):
-            out_ref[owner, :, here] = product[owner * share : (owner + 1) * share]
+        out_ref[:, here] = product.astype(jnp.bfloat16)
         return carried
 
     lax.fori_loop(0, features // step, columns, 0, unroll=4)
-    first_ref[...] = out_ref[far_block(out_ref, info_ref, 0, n_db - 1)]
-    second_ref[...] = out_ref[far_block(out_ref, info_ref, 1, n_db - 1)]
-
-
-def cross_block(info, hidden, total, gain, w_cross_q, keys, values, w_cross_out, n_db, scale):
-    rows, features = hidden.shape
-    share = rows // n_db
+
+
+def cross_block(
+    chunk, info, hidden, total, gain, w_cross_q, keys, values, w_cross_out, n_db, scale
+):
+    rows, features = total.shape
     width = w_cross_q.shape[1]
     vmem = pl.BlockSpec(memory_space=pltpu.VMEM)
     anywhere = pl.BlockSpec(memory_space=pl.ANY)
-    one = jax.ShapeDtypeStruct((share, features), jnp.bfloat16)
     return pl.pallas_call(
-        functools.partial(cross_kernel, scale=scale),
+        functools.partial(cross_kernel, chunk=chunk, n_db=n_db, scale=scale),
         out_shape=[
-            jax.ShapeDtypeStruct((n_db, share, features), jnp.bfloat16),
-            jax.ShapeDtypeStruct((share, features), jnp.float32),
-            one,
-            one,
+            jax.ShapeDtypeStruct((rows, features), jnp.bfloat16),
+            jax.ShapeDtypeStruct((rows // n_db, features), jnp.float32),
         ],
-        in_specs=[pl.BlockSpec(memory_space=pltpu.SMEM)] + [vmem] * 3 + [anywhere] * 4,
-        out_specs=[vmem] * 4,
+        in_specs=[pl.BlockSpec(memory_space=pltpu.SMEM), anywhere, vmem, vmem] + [anywhere] * 4,
+        out_specs=[vmem] * 2,
         scratch_shapes=[
             pltpu.VMEM((features, width), jnp.bfloat16),
             pltpu.VMEM(keys.shape, jnp.bfloat16),
             pltpu.VMEM(values.shape, jnp.bfloat16),
             pltpu.VMEM((width, features), jnp.bfloat16),
             pltpu.VMEM((rows, features), jnp.bfloat16),
+            pltpu.VMEM((rows, features), jnp.bfloat16),
             pltpu.VMEM((rows, width), jnp.float32),
             pltpu.VMEM((rows, width), jnp.bfloat16),
-            pltpu.SemaphoreType.DMA((10,)),
+            pltpu.SemaphoreType.DMA((10 + n_db,)),
         ],
         compiler_params=pltpu.CompilerParams(vmem_limit_bytes=VMEM_BYTES),
         cost_estimate=pl.CostEstimate(
@@ -578,31 +547,28 @@
         attended = self_attention_gathered(query_rows, key_rows, value_rows, scale)
 
     along_db, attended = lax.optimization_barrier((along_db, attended))
-    partial = self_out(attended, w_self_out)
+    partial = self_out(attended, w_self_out, n_db)
     along_db, partial = lax.optimization_barrier((along_db, partial))
-    total = lax.psum(partial, "db")
+    total = lax.psum(partial[0], "db")
     if in_plane:
-        tables = tuple(one[None] for one in plane_pieces(along_db))
+        tables, total = plane_pieces(along_db, total)
+        tables = tuple(one[None] for one in tables)
     else:
         tables = (lax.all_gather(along_db, "seq", axis=0),)
+    total, second = lax.optimization_barrier((total, partial[1]))
+    totals = [total, lax.psum(second, "db")]
     projected = project_encodings(info, tables, w_cross_k, w_cross_v)
-    total, (keys, values) = lax.optimization_barrier((total, projected))
-
-    partial, residual, up, down = cross_block(
-        info,
-        hidden_in,
-        total,
-        norm_gain.reshape(1, features),
-        w_cross_q,
-        keys,
-        values,
-        w_cross_out,
-        n_db,
-        scale,
-    )
-    up, down = reduce_scatter(info, partial, up, down)
-    own = lax.dynamic_index_in_dim(partial, db_index, 0, keepdims=False).astype(jnp.float32)
-    return residual + own + up.astype(jnp.float32) + down.astype(jnp.float32)
+    totals[0], (keys, values) = lax.optimization_barrier((totals[0], projected))
+
+    gain = norm_gain.reshape(1, features)
+    blocks = []
+    for chunk, total in enumerate(totals):
+        out_partial, residual = cross_block(
+            chunk, info, hidden_in, total, gain, w_cross_q, keys, values, w_cross_out, n_db, scale
+        )
+        summed = lax.psum_scatter(out_partial, "db", scatter_dimension=0, tiled=True)
+        blocks.append(residual + summed.astype(jnp.float32))
+    return jnp.concatenate(blocks, axis=0)
 
 
 def solution(mesh):

time: 222 us -> 237 us (1.068)
  waiting for transfers between devices: 130 us -> 149 us
  starting transfers between devices: 31.4 us -> 15.9 us
  Pallas kernels: 42.1 us -> 47.7 us
  local copies, waits for them, and re-layouts: 1.5 us -> 7.09 us
    reduce_scatter x0 -> x2, waiting for transfers between devices: none -> 43.7 us  [per_device(): lax.psum_scatter(out_partial, 'db', scatter_dimension=0, tiled=True)]
    ppermute x6 -> x0, waiting for transfers between devices: 29.5 us -> none  [line_shift(): return lax.ppermute(block, ('seq', 'db'), route)]
    ppermute x6 -> x0, starting transfers between devices: 15.5 us -> none  [line_shift(): return lax.ppermute(block, ('seq', 'db'), route)]
    psum x1 -> x2, waiting for transfers between devices: 21.9 us -> 28.3 us  [the longest x1 21.4 us: per_device(): totals = [total, lax.psum(second, 'db')]]
    unnamed x14 -> x26, local copies, waits for them, and re-layouts: 1.02 us -> 6.61 us
    pallas_call x4 -> x3, Pallas kernels: 21.4 us -> 26.7 us  [the longest x2 21.4 us: cross_block(): pl.pallas_call(functools.partial(cross_kernel, chunk=chunk, n_db=n_db, sc...]
  transfers between devices with their start and end apart: 18 -> 15, of which waited for: 15 -> 14; matrix products, arithmetic and copies ran while one was open for 0% -> 1% of each run, Pallas kernels for 8% -> 16%
where the time goes in v11:
time: 237 us
  waiting for transfers between devices  149 us (63%)
  Pallas kernels  47.7 us (20%)
  starting transfers between devices  15.9 us (7%)
  between operations  13.3 us (6%)
  local copies, waits for them, and re-layouts  7.09 us (3%)
  other arithmetic  3.37 us (1%)
    ppermute x7, waiting for transfers between devices, plane_swap(): return lax.ppermute(block, 'seq', [(i, i ^ mask) for i in range(8)])  49.7 us
    reduce_scatter x2, waiting for transfers between devices, per_device(): lax.psum_scatter(out_partial, 'db', scatter_dimension=0, tiled=True)  43.7 us
    pallas_call x2, Pallas kernels, cross_block(): pl.pallas_call(functools.partial(cross_kernel, chunk=chunk, n_db=n_db, sc...  21.4 us
    psum x1, waiting for transfers between devices, per_device(): totals = [total, lax.psum(second, 'db')]  21.4 us
    all_to_all x1, waiting for transfers between devices, per_device(): held = lax.all_to_all(packed, 'seq', 0, 0, tiled=True)  16.4 us
    pallas_call x1, Pallas kernels, project_encodings(): pl.pallas_call(functools.partial(project_kernel, cuts=cuts), out_shape=[m...  11.7 us
    all_to_all x1, waiting for transfers between devices, per_device(): lax.all_to_all(self_attend_head(held, scale), 'seq', 0, 0, tiled=True)  7.68 us
    psum x1, waiting for transfers between devices, per_device(): total = lax.psum(partial[0], 'db')  6.97 us
  transfers between devices with their start and end apart: 15, of which 14 were waited for; matrix products, arithmetic and copies ran while one was open for 1% of the time, Pallas kernels for 16%

profile of v11, /device:TPU:0, one launch (start us, length us, event | category | flops | bytes accessed | tf_op | source)
XLA Modules:
  0.0 236.6 jit_solution(5677355169290469323)
XLA Ops:
  6.5 3.8 %pack_heads.1 = (bf16[8,3,256,128]{3,2,1,0:T(8,128)(2,1)}, bf16[128,1024]{1,0:T(8,128)(2,1)}) custom-call(s32[1]{0:T(128)} %bitcast.index_ref, bf16[256,1024]{1,0:T(8,128)(2,1)} %query_ref.1, bf16[256,1024]{1,0:T(8,128)(2,1)} %key_ref.1, bf16[256,1024]{1,0:T(8,128)(2,1)} %value_ref.1, bf16[1024,1024]{1,0:T(8,128)(2,1)} %bitcast.25), custom_call_target="tpu_custom_call" | custom-call | bytes 3145728 | tf_op jit(solution)/shard_map/pack_heads/pallas_call | solution.py:98
  10.4 5.3 %all-to-all-start = ((bf16[8,3,256,128]{3,2,1,0:T(8,128)(2,1)}), bf16[8,3,256,128]{3,2,1,0:T(8,128)(2,1)S(1)}, u32[]{:S(2)}, u32[]{:S(2)}) async-start(bf16[8,3,256,128]{3,2,1,0:T(8,128)(2,1)} %get-tuple-element.36), calls=%async_computation | async-start | bytes 3145728 | tf_op jit(solution)/shard_map/all_to_all | solution.py:543
  15.7 0.0 all-gather.3.cloned.1.call-start
  15.7 0.7 all-gather.3.cloned.1.call-update
  16.4 0.0 copy-done.11
  16.4 0.0 copy-done.12
  16.4 0.1 pad_add_fusion.1
  16.5 0.1 copy.17
  16.6 2.4 %collective-permute-start = (s32[2,2]{1,0:T(2,128)S(1)}, s32[2,2]{1,0:T(2,128)S(1)}, u32[]{:S(2)}, u32[]{:S(2)}) collective-permute-start(s32[2,2]{1,0:T(2,128)S(1)} %bitcast.30), channel_id=1, source_target_pairs={{0,4},{4,8},{8,12},{12,16},{16,20},{20,24},{24,28},{1,5},{5,9},{9,... | collective-permute-start | bytes 56 | tf_op jit(solution)/shard_map/ppermute | solution.py:26
  19.0 0.1 pad.6.clone
  19.1 0.7 collective-permute-done
  19.8 0.1 copy.18
  19.9 0.1 add_add_fusion
  20.0 0.1 pad_add_fusion
  20.1 0.1 copy.19
  20.2 0.1 reshape.14
  20.3 0.1 pad_add_fusion.2.where_ref.info_ref
  20.3 16.4 %all-to-all-done.qkv_ref = bf16[8,3,256,128]{3,2,1,0:T(8,128)(2,1)S(1)} async-done(((bf16[8,3,256,128]{3,2,1,0:T(8,128)(2,1)}), bf16[8,3,256,128]{3,2,1,0:T(8,128)(2,1)S(1)}, u32[]{:S(2)}, u32[]{:S(2)}) %all-to-all-start) | async-done | bytes 1572896 | tf_op jit(solution)/shard_map/all_to_all | solution.py:543
  36.7 5.6 %self_attend.1 = bf16[8,256,128]{2,1,0:T(8,128)(2,1)} custom-call(bf16[8,3,256,128]{3,2,1,0:T(8,128)(2,1)S(1)} %all-to-all-done.qkv_ref), custom_call_target="tpu_custom_call" | custom-call | flops 1073741824 | bytes 2097152 | tf_op jit(solution)/shard_map/self_attend/pallas_call | solution.py:65
  42.3 3.5 %all-to-all-start.1 = ((bf16[8,256,128]{2,1,0:T(8,128)(2,1)}), bf16[8,256,128]{2,1,0:T(8,128)(2,1)S(1)}, u32[]{:S(2)}, u32[]{:S(2)}) async-start(bf16[8,256,128]{2,1,0:T(8,128)(2,1)} %self_attend.1), calls=%async_computation.1 | async-start | bytes 1048576 | tf_op jit(solution)/shard_map/all_to_all | solution.py:545
  45.8 0.0 all-reduce.3.cloned.1.call-start
  45.8 1.9 all-gather.3.cloned.1.call-done
  47.8 7.7 %all-to-all-done.1.attended_ref = bf16[8,256,128]{2,1,0:T(8,128)(2,1)S(1)} async-done(((bf16[8,256,128]{2,1,0:T(8,128)(2,1)}), bf16[8,256,128]{2,1,0:T(8,128)(2,1)S(1)}, u32[]{:S(2)}, u32[]{:S(2)}) %all-to-all-start.1) | async-done | bytes 524320 | tf_op jit(solution)/shard_map/all_to_all | solution.py:545
  55.4 5.2 %self_out.1 = (bf16[128,4096]{1,0:T(8,128)(2,1)S(1)}, bf16[128,4096]{1,0:T(8,128)(2,1)S(1)}) custom-call(bf16[8,256,128]{2,1,0:T(8,128)(2,1)S(1)} %all-to-all-done.1.attended_ref, bf16[1024,4096]{1,0:T(8,128)(2,1)} %weight_hbm.1), custom_call_target="tpu_custom_call" | custom-call | flops 2147483648 | bytes 11010048 | tf_op jit(solution)/shard_map/self_out/pallas_call | solution.py:206
  60.7 0.0 copy-start.8
  60.7 1.0 copy-done.8
  61.7 1.0 copy-done.9
  62.7 0.0 copy-done.1
  62.7 0.5 collective-permute-start.1
  63.2 0.6 collective-permute-start.2
  63.8 2.4 %collective-permute-start.3 = (bf16[4,128,1024]{2,1,0:T(8,128)(2,1)S(1)}, bf16[4,128,1024]{2,1,0:T(8,128)(2,1)}, u32[]{:S(2)}, u32[]{:S(2)}) collective-permute-start(bf16[4,128,1024]{2,1,0:T(8,128)(2,1)S(1)} %bitcast.20), channel_id=1, source_target_pairs={{0,24},{4,28},{8,16},{12,20},{16,8},{20,12},{24,0},{28,4},{1,25},{... | collective-permute-start | bytes 3145736 | tf_op jit(solution)/shard_map/ppermute | solution.py:30
  66.1 0.0 all-reduce.3.cloned.1.call-update
  66.2 0.0 all-reduce.5.cloned.1.call-start
  66.2 22.5 %collective-permute-done.1 = bf16[4,128,1024]{2,1,0:T(8,128)(2,1)S(1)} collective-permute-done((bf16[4,128,1024]{2,1,0:T(8,128)(2,1)S(1)}, bf16[4,128,1024]{2,1,0:T(8,128)(2,1)S(1)}, u32[]{:S(2)}, u32[]{:S(2)}) %collective-permute-start.1) | collective-permute-done | bytes 1048608 | tf_op jit(solution)/shard_map/ppermute | solution.py:30
  88.8 21.8 %collective-permute-done.2 = bf16[4,128,1024]{2,1,0:T(8,128)(2,1)S(1)} collective-permute-done((bf16[4,128,1024]{2,1,0:T(8,128)(2,1)S(1)}, bf16[4,128,1024]{2,1,0:T(8,128)(2,1)S(1)}, u32[]{:S(2)}, u32[]{:S(2)}) %collective-permute-start.2) | collective-permute-done | bytes 1048608 | tf_op jit(solution)/shard_map/ppermute | solution.py:30
  110.5 0.0 collective-permute-done.3
  110.5 7.0 %all-reduce.3.cloned.1.call-done.total_ref = bf16[128,4096]{1,0:T(8,128)(2,1)} async-done(((bf16[128,4096]{1,0:T(8,128)(2,1)}), bf16[128,4096]{1,0:T(8,128)(2,1)}) %all-reduce.3.cloned.1.call-update) | async-done | bytes 1048592 | tf_op jit(solution)/shard_map/psum | solution.py:552
  117.5 0.0 collective-permute-start.4
  117.5 0.5 collective-permute-start.5
  118.0 0.0 collective-permute-start.6
  118.1 1.0 copy-done.5
  119.0 0.5 collective-permute-start.7
  119.5 0.0 all-reduce.5.cloned.1.call-update
  119.5 0.0 reduce-scatter.3.cloned.1.call-start
  119.6 0.0 copy-done.10
  119.6 0.7 collective-permute-done.4
  120.3 1.5 collective-permute-done.5
  121.8 3.0 %collective-permute-done.6 = bf16[4,128,1024]{2,1,0:T(8,128)(2,1)} collective-permute-done((bf16[4,128,1024]{2,1,0:T(8,128)(2,1)S(1)}, bf16[4,128,1024]{2,1,0:T(8,128)(2,1)}, u32[]{:S(2)}, u32[]{:S(2)}) %collective-permute-start.6) | collective-permute-done | bytes 1048608 | tf_op jit(solution)/shard_map/ppermute | solution.py:30
  124.8 0.2 collective-permute-done.7
  125.0 1.2 copy-done.4
  126.2 1.2 copy-done.6
  127.5 11.7 %project_encodings.1 = (bf16[1280,1024]{1,0:T(8,128)(2,1)}, bf16[1280,1024]{1,0:T(8,128)(2,1)}) custom-call(s32[32]{0:T(128)S(1)} %pad_add_fusion.2.where_ref.info_ref, bf16[1,4,128,1024]{3,2,1,0:T(8,128)(2,1)S(1)} %bitcast.22, bf16[1,4,128,1024]{3,2,1,0:T(8,128)(2,1)S(1)} %bitcast.23, bf16[1,4,128,1024]{3,2,1,0:T(8,128)(2,1)S(1)} %bitcast.24, ...), custom_call_target="tpu_custom_call" | custom-call | flops 1310720 | bytes 2621440 | tf_op jit(solution)/shard_map/project_encodings/pallas_call | solution.py:284
  139.2 10.7 %cross_block.2 = (bf16[128,4096]{1,0:T(8,128)(2,1)}, f32[32,4096]{1,0:T(8,128)S(1)}) custom-call(s32[32]{0:T(128)S(1)} %pad_add_fusion.2.where_ref.info_ref, bf16[256,4096]{1,0:T(8,128)(2,1)S(1)} %copy-done, bf16[128,4096]{1,0:T(8,128)(2,1)S(1)} %copy-done.2, bf16[1,4096]{1,0:T(2,128)(2,1)S(1)} %reshape.15.gain_ref, bf16[4096,1024]{1,0:T(8,128)(2,1)} %wq_hbm.3, ...), custom_call_target="tpu_custom_call" | custom-call | flops 2281701376 | bytes 26214400 | tf_op jit(solution)/shard_map/cross_block/pallas_call | solution.py:473
  149.9 0.0 reduce-scatter.3.cloned.1.call-update
  149.9 0.0 reduce-scatter.5.cloned.1.call-start
  149.9 21.4 %all-reduce.5.cloned.1.call-done.total_ref = bf16[128,4096]{1,0:T(8,128)(2,1)} async-done(((bf16[128,4096]{1,0:T(8,128)(2,1)}), bf16[128,4096]{1,0:T(8,128)(2,1)}) %all-reduce.5.cloned.1.call-update) | async-done | bytes 1048592 | tf_op jit(solution)/shard_map/psum | solution.py:559
  171.3 1.2 copy-done.7
  172.5 10.7 %cross_block.3 = (bf16[128,4096]{1,0:T(8,128)(2,1)}, f32[32,4096]{1,0:T(8,128)S(1)}) custom-call(s32[32]{0:T(128)S(1)} %pad_add_fusion.2.where_ref.info_ref, bf16[256,4096]{1,0:T(8,128)(2,1)S(1)} %copy-done, bf16[128,4096]{1,0:T(8,128)(2,1)S(1)} %copy-done.7, bf16[1,4096]{1,0:T(2,128)(2,1)S(1)} %reshape.15.gain_ref, bf16[4096,1024]{1,0:T(8,128)(2,1)} %wq_hbm.3, ...), custom_call_target="tpu_custom_call" | custom-call | flops 2281701376 | bytes 26214400 | tf_op jit(solution)/shard_map/cross_block/pallas_call | solution.py:473
  183.3 0.0 reduce-scatter.5.cloned.1.call-update
  183.3 16.7 %reduce-scatter.3.cloned.1.call-done = bf16[32,4096]{1,0:T(8,128)(2,1)} async-done(((bf16[128,4096]{1,0:T(8,128)(2,1)}), bf16[32,4096]{1,0:T(8,128)(2,1)}) %reduce-scatter.3.cloned.1.call-update) | async-done | bytes 262160 | tf_op jit(solution)/shard_map/reduce_scatter | solution.py:569
  200.0 1.0 convert_add_fusion.1
  201.0 27.1 %reduce-scatter.5.cloned.1.call-done = bf16[32,4096]{1,0:T(8,128)(2,1)} async-done(((bf16[128,4096]{1,0:T(8,128)(2,1)}), bf16[32,4096]{1,0:T(8,128)(2,1)}) %reduce-scatter.5.cloned.1.call-update) | async-done | bytes 262160 | tf_op jit(solution)/shard_map/reduce_scatter | solution.py:569
  228.0 1.0 convert_add_fusion
  229.0 1.0 pad_maximum_fusion
  (17 shorter events, 0.0 us)
Async XLA Ops:
  10.4 6.1 %copy-start.11 = (s32[4,2]{0,1:T(2,128)S(1)}, s32[4,2]{0,1:T(2,128)}, u32[]{:S(2)}) copy-start(s32[4,2]{0,1:T(2,128)} %param.24) | copy-start | bytes 100
  10.4 6.1 %copy-start.12 = (s32[4,2]{0,1:T(2,128)S(1)}, s32[4,2]{0,1:T(2,128)}, u32[]{:S(2)}) copy-start(s32[4,2]{0,1:T(2,128)} %param.25) | copy-start | bytes 100
  10.4 26.3 %all-to-all-start = ((bf16[8,3,256,128]{3,2,1,0:T(8,128)(2,1)}), bf16[8,3,256,128]{3,2,1,0:T(8,128)(2,1)S(1)}, u32[]{:S(2)}, u32[]{:S(2)}) async-start(bf16[8,3,256,128]{3,2,1,0:T(8,128)(2,1)} %get-tuple-element.36), calls=%async_computation | async-start | bytes 3145728 | tf_op jit(solution)/shard_map/all_to_all | solution.py:543
  15.7 32.1 %all-gather.3.cloned.1.call-start = ((), (), s32[]{:S(2)}) async-start(), calls=%async_computation.8 | async-start | bytes 1310720 | tf_op jit(solution)/shard_map/all_gather | solution.py:529
  16.6 3.2 %collective-permute-start = (s32[2,2]{1,0:T(2,128)S(1)}, s32[2,2]{1,0:T(2,128)S(1)}, u32[]{:S(2)}, u32[]{:S(2)}) collective-permute-start(s32[2,2]{1,0:T(2,128)S(1)} %bitcast.30), channel_id=1, source_target_pairs={{0,4},{4,8},{8,12},{12,16},{16,20},{20,24},{24,28},{1,5},{5,9},{9,... | collective-permute-start | bytes 56 | tf_op jit(solution)/shard_map/ppermute | solution.py:26
  42.3 13.2 %all-to-all-start.1 = ((bf16[8,256,128]{2,1,0:T(8,128)(2,1)}), bf16[8,256,128]{2,1,0:T(8,128)(2,1)S(1)}, u32[]{:S(2)}, u32[]{:S(2)}) async-start(bf16[8,256,128]{2,1,0:T(8,128)(2,1)} %self_attend.1), calls=%async_computation.1 | async-start | bytes 1048576 | tf_op jit(solution)/shard_map/all_to_all | solution.py:545
  45.8 71.7 %all-reduce.3.cloned.1.call-start = ((), (), s32[]{:S(2)}) async-start(), calls=%async_computation.4 | async-start | bytes 2097152 | tf_op jit(solution)/shard_map/psum | solution.py:552
  55.4 7.2 %copy-start.1 = (bf16[512,1024]{1,0:T(8,128)(2,1)S(1)}, bf16[512,1024]{1,0:T(8,128)(2,1)}, u32[]{:S(2)}) copy-start(bf16[512,1024]{1,0:T(8,128)(2,1)} %all-gather.3.cloned.1.call-done) | copy-start | bytes 3145732
  60.7 1.0 copy-start.8
  61.7 1.0 copy-start.9
  62.7 56.9 %copy-start.10 = (bf16[4096]{0:T(1024)(128)(2,1)S(1)}, bf16[4096]{0:T(1024)(128)(2,1)}, u32[]{:S(2)}) copy-start(bf16[4096]{0:T(1024)(128)(2,1)} %param.18) | copy-start | bytes 24580
  62.7 26.1 %collective-permute-start.1 = (bf16[4,128,1024]{2,1,0:T(8,128)(2,1)S(1)}, bf16[4,128,1024]{2,1,0:T(8,128)(2,1)S(1)}, u32[]{:S(2)}, u32[]{:S(2)}) collective-permute-start(bf16[4,128,1024]{2,1,0:T(8,128)(2,1)S(1)} %bitcast.18), channel_id=1, source_target_pairs={{0,8},{4,12},{8,0},{12,4},{16,24},{20,28},{24,16},{28,20},{1,9},{5... | collective-permute-start | bytes 3145736 | tf_op jit(solution)/shard_map/ppermute | solution.py:30
  63.2 47.3 %collective-permute-start.2 = (bf16[4,128,1024]{2,1,0:T(8,128)(2,1)S(1)}, bf16[4,128,1024]{2,1,0:T(8,128)(2,1)S(1)}, u32[]{:S(2)}, u32[]{:S(2)}) collective-permute-start(bf16[4,128,1024]{2,1,0:T(8,128)(2,1)S(1)} %bitcast.19), channel_id=1, source_target_pairs={{0,16},{4,20},{8,24},{12,28},{16,0},{20,4},{24,8},{28,12},{1,17},{... | collective-permute-start | bytes 3145736 | tf_op jit(solution)/shard_map/ppermute | solution.py:30
  63.8 46.8 %collective-permute-start.3 = (bf16[4,128,1024]{2,1,0:T(8,128)(2,1)S(1)}, bf16[4,128,1024]{2,1,0:T(8,128)(2,1)}, u32[]{:S(2)}, u32[]{:S(2)}) collective-permute-start(bf16[4,128,1024]{2,1,0:T(8,128)(2,1)S(1)} %bitcast.20), channel_id=1, source_target_pairs={{0,24},{4,28},{8,16},{12,20},{16,8},{20,12},{24,0},{28,4},{1,25},{... | collective-permute-start | bytes 3145736 | tf_op jit(solution)/shard_map/ppermute | solution.py:30
  66.2 105.1 %all-reduce.5.cloned.1.call-start = ((), (), s32[]{:S(2)}) async-start(), calls=%async_computation.6 | async-start | bytes 2097152 | tf_op jit(solution)/shard_map/psum | solution.py:559
  88.8 36.2 %copy-start.3 = (bf16[4,128,1024]{2,1,0:T(8,128)(2,1)}, bf16[4,128,1024]{2,1,0:T(8,128)(2,1)S(1)}, u32[]{:S(2)}) copy-start(bf16[4,128,1024]{2,1,0:T(8,128)(2,1)S(1)} %collective-permute-done.1) | copy-start | bytes 3145732
  117.5 2.8 %collective-permute-start.4 = (bf16[4,128,1024]{2,1,0:T(8,128)(2,1)S(1)}, bf16[4,128,1024]{2,1,0:T(8,128)(2,1)}, u32[]{:S(2)}, u32[]{:S(2)}) collective-permute-start(bf16[4,128,1024]{2,1,0:T(8,128)(2,1)S(1)} %bitcast.21), channel_id=1, source_target_pairs={{0,4},{4,0},{8,12},{12,8},{16,20},{20,16},{24,28},{28,24},{1,5},{5... | collective-permute-start | bytes 3145736 | tf_op jit(solution)/shard_map/ppermute | solution.py:30
  117.5 4.2 %collective-permute-start.5 = (bf16[4,128,1024]{2,1,0:T(8,128)(2,1)S(1)}, bf16[4,128,1024]{2,1,0:T(8,128)(2,1)}, u32[]{:S(2)}, u32[]{:S(2)}) collective-permute-start(bf16[4,128,1024]{2,1,0:T(8,128)(2,1)S(1)} %collective-permute-done.1), channel_id=1, source_target_pairs={{0,4},{4,0},{8,12},{12,8},{16,20},{20,16},{24,28},{28,24},{1,5},{5... | collective-permute-start | bytes 3145736 | tf_op jit(solution)/shard_map/ppermute | solution.py:30
  118.0 6.8 %collective-permute-start.6 = (bf16[4,128,1024]{2,1,0:T(8,128)(2,1)S(1)}, bf16[4,128,1024]{2,1,0:T(8,128)(2,1)}, u32[]{:S(2)}, u32[]{:S(2)}) collective-permute-start(bf16[4,128,1024]{2,1,0:T(8,128)(2,1)S(1)} %collective-permute-done.2), channel_id=1, source_target_pairs={{0,4},{4,0},{8,12},{12,8},{16,20},{20,16},{24,28},{28,24},{1,5},{5... | collective-permute-start | bytes 3145736 | tf_op jit(solution)/shard_map/ppermute | solution.py:30
  118.1 1.0 copy-start.5
  119.0 6.0 %collective-permute-start.7 = (bf16[4,128,1024]{2,1,0:T(8,128)(2,1)}, bf16[4,128,1024]{2,1,0:T(8,128)(2,1)}, u32[]{:S(2)}, u32[]{:S(2)}) collective-permute-start(bf16[4,128,1024]{2,1,0:T(8,128)(2,1)} %collective-permute-done.3), channel_id=1, source_target_pairs={{0,4},{4,0},{8,12},{12,8},{16,20},{20,16},{24,28},{28,24},{1,5},{5... | collective-permute-start | bytes 3145736 | tf_op jit(solution)/shard_map/ppermute | solution.py:30
  119.5 80.5 %reduce-scatter.3.cloned.1.call-start = ((), (), s32[]{:S(2)}) async-start(), calls=%async_computation.5 | async-start | bytes 1310720 | tf_op jit(solution)/shard_map/reduce_scatter | solution.py:569
  125.0 1.2 copy-start.4
  126.2 1.2 copy-start.6
  127.5 11.7 %copy-start = (bf16[256,4096]{1,0:T(8,128)(2,1)S(1)}, bf16[256,4096]{1,0:T(8,128)(2,1)}, u32[]{:S(2)}) copy-start(bf16[256,4096]{1,0:T(8,128)(2,1)} %hidden_hbm.3) | copy-start | bytes 6291460
  127.5 11.7 %copy-start.2 = (bf16[128,4096]{1,0:T(8,128)(2,1)S(1)}, bf16[128,4096]{1,0:T(8,128)(2,1)}, u32[]{:S(2)}) copy-start(bf16[128,4096]{1,0:T(8,128)(2,1)} %all-reduce.3.cloned.1.call-done.total_ref) | copy-start | bytes 3145732
  149.9 78.2 %reduce-scatter.5.cloned.1.call-start = ((), (), s32[]{:S(2)}) async-start(), calls=%async_computation.7 | async-start | bytes 1310720 | tf_op jit(solution)/shard_map/reduce_scatter | solution.py:569
  171.3 1.2 copy-start.7
Sparse Core Ops, SparseCore 0:
  18.1 29.6 all-gather.2
  66.3 51.1 all-reduce.2
  120.0 51.2 all-reduce.4
  173.4 26.4 reduce-scatter.2
  202.2 25.7 reduce-scatter.4

commit v12 on v10

--- a/solution.py
+++ b/solution.py
@@ -18,73 +18,12 @@
 LOG2E = 1.4426950408889634
 VMEM_BYTES = 48 * 1024 * 1024
 LARGE_BYTES = 58 * 1024 * 1024
-SMALL_BYTES = 4 * 1024 * 1024
 
 
 def shift(block, axis, distance, senders):
     size = lax.axis_size(axis)
     route = [(k, k + distance) for k in senders if 0 <= k + distance < size]
     return lax.ppermute(block, axis, route)
-
-
-def line_shift(block, lead, up_from, down_from):
-    n_seq, size = lax.axis_size("seq"), lax.axis_size("db")
-    route = []
-    for row in range(n_seq):
-        up = lead == 0
-        for k in up_from if up else down_from:
-            other = k + 1 if up else k - 1
-            if 0 <= other < size:
-                route.append((row * size + k, row * size + other))
-    return lax.ppermute(block, ("seq", "db"), route)
-
-
-def far_block(blocks_ref, info_ref, lead, far):
-    way = 1 - 2 * lead
-    return jnp.clip(info_ref[0] + way * far, 0, blocks_ref.shape[0] - 1)
-
-
-def add_kernel(info_ref, blocks_ref, up_ref, down_ref, up_out_ref, down_out_ref, *, far):
-    rows = 16
-
-    def add(at, carried):
-        here = pl.ds(pl.multiple_of(at * rows, rows), rows)
-        for lead, ref, out_ref in ((0, up_ref, up_out_ref), (1, down_ref, down_out_ref)):
-            index = far_block(blocks_ref, info_ref, lead, far)
-            out_ref[here, :] = (
-                blocks_ref[index, here, :].astype(jnp.float32) + ref[here, :].astype(jnp.float32)
-            ).astype(jnp.bfloat16)
-        return carried
-
-    lax.fori_loop(0, up_ref.shape[0] // rows, add, 0)
-
-
-def add_step(info, blocks, up, down, far):
-    vmem = pl.BlockSpec(memory_space=pltpu.VMEM)
-    one = jax.ShapeDtypeStruct(up.shape, up.dtype)
-    return pl.pallas_call(
-        functools.partial(add_kernel, far=far),
-        out_shape=[one, one],
-        in_specs=[pl.BlockSpec(memory_space=pltpu.SMEM), vmem, vmem, vmem],
-        out_specs=[vmem, vmem],
-        compiler_params=pltpu.CompilerParams(vmem_limit_bytes=SMALL_BYTES),
-        cost_estimate=pl.CostEstimate(
-            flops=2 * up.size, bytes_accessed=12 * up.size, transcendentals=0
-        ),
-        name="add_step",
-    )(info, blocks, up, down)
-
-
-def reduce_scatter(info, blocks, up, down):
-    size = lax.axis_size("db")
-    for step in range(size - 1):
-        senders = (range(step + 1), range(size - 1 - step, size))
-        if step:
-            up, down = add_step(info, blocks, up, down, size - 1 - step)
-        down = line_shift(down, 1, *senders)
-        up = line_shift(up, 0, *senders)
-        down, up = lax.optimization_barrier((down, up))
-    return up, down
 
 
 def plane_swap(block, mask):
@@ -378,8 +317,6 @@
     wo_hbm,
     out_ref,
     residual_ref,
-    first_ref,
-    second_ref,
     wq_ref,
     keys_ref,
     values_ref,
@@ -396,22 +333,22 @@
     width = wq_ref.shape[1]
     pairs = width // HD // 2
     tail = 16
-    cut = features // 4
-    low = width // 4
+    parts = 8
+    cut, low = features // parts, width // parts
     wq_copies = [
         pltpu.make_async_copy(
             wq_hbm.at[pl.ds(k * cut, cut)], wq_ref.at[pl.ds(k * cut, cut)], sems.at[k]
         )
-        for k in range(4)
+        for k in range(parts)
     ]
     other_copies = [
-        pltpu.make_async_copy(keys_hbm, keys_ref, sems.at[4]),
-        pltpu.make_async_copy(values_hbm, values_ref, sems.at[5]),
+        pltpu.make_async_copy(keys_hbm, keys_ref, sems.at[2 * parts]),
+        pltpu.make_async_copy(values_hbm, values_ref, sems.at[2 * parts + 1]),
     ] + [
         pltpu.make_async_copy(
-            wo_hbm.at[pl.ds(k * low, low)], wo_ref.at[pl.ds(k * low, low)], sems.at[6 + k]
-        )
-        for k in range(4)
+            wo_hbm.at[pl.ds(k * low, low)], wo_ref.at[pl.ds(k * low, low)], sems.at[parts + k]
+        )
+        for k in range(parts)
     ]
     for copy in wq_copies + other_copies:
         copy.start()
@@ -432,9 +369,10 @@
         jnp.float32
     )
     lanes = [slice(2 * pair * HD, 2 * (pair + 1) * HD) for pair in range(pairs)]
-    for k, copy in enumerate(wq_copies):
-        copy.wait()
-        inner = slice(k * cut, (k + 1) * cut)
+    for k in range(0, parts, 2):
+        for copy in wq_copies[k : k + 2]:
+            copy.wait()
+        inner = slice(k * cut, (k + 2) * cut)
         for at in lanes:
             part = jnp.dot(
                 rows_ref[:, inner], wq_ref[inner, at], preferred_element_type=jnp.float32
@@ -489,8 +427,6 @@
         return carried
 
     lax.fori_loop(0, features // step, columns, 0, unroll=4)
-    first_ref[...] = out_ref[far_block(out_ref, info_ref, 0, n_db - 1)]
-    second_ref[...] = out_ref[far_block(out_ref, info_ref, 1, n_db - 1)]
 
 
 def cross_block(info, hidden, total, gain, w_cross_q, keys, values, w_cross_out, n_db, scale):
@@ -499,17 +435,14 @@
     width = w_cross_q.shape[1]
     vmem = pl.BlockSpec(memory_space=pltpu.VMEM)
     anywhere = pl.BlockSpec(memory_space=pl.ANY)
-    one = jax.ShapeDtypeStruct((share, features), jnp.bfloat16)
     return pl.pallas_call(
         functools.partial(cross_kernel, scale=scale),
         out_shape=[
             jax.ShapeDtypeStruct((n_db, share, features), jnp.bfloat16),
             jax.ShapeDtypeStruct((share, features), jnp.float32),
-            one,
-            one,
         ],
         in_specs=[pl.BlockSpec(memory_space=pltpu.SMEM)] + [vmem] * 3 + [anywhere] * 4,
-        out_specs=[vmem] * 4,
+        out_specs=[vmem] * 2,
         scratch_shapes=[
             pltpu.VMEM((features, width), jnp.bfloat16),
             pltpu.VMEM(keys.shape, jnp.bfloat16),
@@ -518,7 +451,7 @@
             pltpu.VMEM((rows, features), jnp.bfloat16),
             pltpu.VMEM((rows, width), jnp.float32),
             pltpu.VMEM((rows, width), jnp.bfloat16),
-            pltpu.SemaphoreType.DMA((10,)),
+            pltpu.SemaphoreType.DMA((18,)),
         ],
         compiler_params=pltpu.CompilerParams(vmem_limit_bytes=VMEM_BYTES),
         cost_estimate=pl.CostEstimate(
@@ -588,7 +521,7 @@
     projected = project_encodings(info, tables, w_cross_k, w_cross_v)
     total, (keys, values) = lax.optimization_barrier((total, projected))
 
-    partial, residual, up, down = cross_block(
+    partial, residual = cross_block(
         info,
         hidden_in,
         total,
@@ -600,9 +533,11 @@
         n_db,
         scale,
     )
-    up, down = reduce_scatter(info, partial, up, down)
-    own = lax.dynamic_index_in_dim(partial, db_index, 0, keepdims=False).astype(jnp.float32)
-    return residual + own + up.astype(jnp.float32) + down.astype(jnp.float32)
+    rows = hidden_in.shape[0]
+    summed = lax.psum_scatter(
+        partial.reshape(rows, features), "db", scatter_dimension=0, tiled=True
+    )
+    return residual + summed.astype(jnp.float32)
 
 
 def solution(mesh):

time: 222 us -> 217 us (0.977)
  starting transfers between devices: 31.4 us -> 15.9 us
  waiting for transfers between devices: 130 us -> 138 us
  local copies, waits for them, and re-layouts: 1.5 us -> 7.44 us
  Pallas kernels: 42.1 us -> 39 us
    reduce_scatter x0 -> x1, waiting for transfers between devices: none -> 43 us  [per_device(): lax.psum_scatter(partial.reshape(rows, features), 'db', scatter_dimension...]
    ppermute x6 -> x0, waiting for transfers between devices: 29.5 us -> none  [line_shift(): return lax.ppermute(block, ('seq', 'db'), route)]
    ppermute x6 -> x0, starting transfers between devices: 15.5 us -> none  [line_shift(): return lax.ppermute(block, ('seq', 'db'), route)]
    unnamed x14 -> x26, local copies, waits for them, and re-layouts: 1.02 us -> 6.97 us
    psum x1, waiting for transfers between devices: 21.9 us -> 19.3 us  [per_device(): total = lax.psum(partial, 'db')]
    pallas_call x2 -> x0, Pallas kernels: 2.56 us -> none  [add_step(): pl.pallas_call(functools.partial(add_kernel, far=far), out_shape=[one, on...]
  transfers between devices with their start and end apart: 18 -> 13, of which waited for: 15 -> 11; matrix products, arithmetic and copies ran while one was open for 0% -> 0% of each run, Pallas kernels for 8% -> 8%
where the time goes in v12:
time: 217 us; the launch traced here: 216 us
  waiting for transfers between devices  138 us (64%)
  Pallas kernels  39 us (18%)
  starting transfers between devices  15.9 us (7%)
  between operations  13.2 us (6%)
  local copies, waits for them, and re-layouts  7.44 us (3%)
  other arithmetic  2.44 us (1%)
    ppermute x7, waiting for transfers between devices, plane_swap(): return lax.ppermute(block, 'seq', [(i, i ^ mask) for i in range(8)])  48.7 us
    reduce_scatter x1, waiting for transfers between devices, per_device(): lax.psum_scatter(partial.reshape(rows, features), 'db', scatter_dimension...  43 us
    psum x1, waiting for transfers between devices, per_device(): total = lax.psum(partial, 'db')  19.3 us
    all_to_all x1, waiting for transfers between devices, per_device(): held = lax.all_to_all(packed, 'seq', 0, 0, tiled=True)  16.4 us
    pallas_call x1, Pallas kernels, cross_block(): pl.pallas_call(functools.partial(cross_kernel, scale=scale), out_shape=[j...  11.7 us
    pallas_call x1, Pallas kernels, project_encodings(): pl.pallas_call(functools.partial(project_kernel, cuts=cuts), out_shape=[m...  11.4 us
    all_to_all x1, waiting for transfers between devices, per_device(): lax.all_to_all(self_attend_head(held, scale), 'seq', 0, 0, tiled=True)  7.68 us
    unnamed x26, local copies, waits for them, and re-layouts  6.97 us
  transfers between devices with their start and end apart: 13, of which 11 were waited for; matrix products, arithmetic and copies ran while one was open for 0% of the time, Pallas kernels for 8%

profile of v12, /device:TPU:0, one launch (start us, length us, event | category | flops | bytes accessed | tf_op | source)
XLA Modules:
  0.0 216.3 jit_solution(17322571921372993199)
XLA Ops:
  6.5 3.8 %pack_heads.1 = (bf16[8,3,256,128]{3,2,1,0:T(8,128)(2,1)}, bf16[128,1024]{1,0:T(8,128)(2,1)}) custom-call(s32[1]{0:T(128)} %bitcast.index_ref, bf16[256,1024]{1,0:T(8,128)(2,1)} %query_ref.1, bf16[256,1024]{1,0:T(8,128)(2,1)} %key_ref.1, bf16[256,1024]{1,0:T(8,128)(2,1)} %value_ref.1, bf16[1024,1024]{1,0:T(8,128)(2,1)} %bitcast.28), custom_call_target="tpu_custom_call" | custom-call | bytes 3145728 | tf_op jit(solution)/shard_map/pack_heads/pallas_call | solution.py:97
  10.3 0.0 copy-start.11
  10.3 0.0 copy-start.12
  10.3 5.3 %all-to-all-start = ((bf16[8,3,256,128]{3,2,1,0:T(8,128)(2,1)}), bf16[8,3,256,128]{3,2,1,0:T(8,128)(2,1)S(1)}, u32[]{:S(2)}, u32[]{:S(2)}) async-start(bf16[8,3,256,128]{3,2,1,0:T(8,128)(2,1)} %get-tuple-element.28), calls=%async_computation | async-start | bytes 3145728 | tf_op jit(solution)/shard_map/all_to_all | solution.py:507
  15.7 0.0 all-gather.3.cloned.1.call-start
  15.7 0.7 all-gather.3.cloned.1.call-update
  16.4 0.0 copy-done.11
  16.4 0.0 copy-done.12
  16.4 0.1 pad_add_fusion.1
  16.5 0.1 copy.17
  16.6 2.4 %collective-permute-start = (s32[2,2]{1,0:T(2,128)S(1)}, s32[2,2]{1,0:T(2,128)S(1)}, u32[]{:S(2)}, u32[]{:S(2)}) collective-permute-start(s32[2,2]{1,0:T(2,128)S(1)} %bitcast.36), channel_id=1, source_target_pairs={{0,4},{4,8},{8,12},{12,16},{16,20},{20,24},{24,28},{1,5},{5,9},{9,... | collective-permute-start | bytes 56 | tf_op jit(solution)/shard_map/ppermute | solution.py:26
  19.0 0.1 pad.4.clone
  19.1 0.7 collective-permute-done
  19.8 0.1 copy.18
  19.9 0.1 add_add_fusion
  20.0 0.1 pad_add_fusion
  20.0 0.1 copy.19
  20.1 0.1 reshape.17
  20.2 0.1 pad_add_fusion.2.where_ref.info_ref
  20.3 16.4 %all-to-all-done.qkv_ref = bf16[8,3,256,128]{3,2,1,0:T(8,128)(2,1)S(1)} async-done(((bf16[8,3,256,128]{3,2,1,0:T(8,128)(2,1)}), bf16[8,3,256,128]{3,2,1,0:T(8,128)(2,1)S(1)}, u32[]{:S(2)}, u32[]{:S(2)}) %all-to-all-start) | async-done | bytes 1572896 | tf_op jit(solution)/shard_map/all_to_all | solution.py:507
  36.7 5.6 %self_attend.1 = bf16[8,256,128]{2,1,0:T(8,128)(2,1)} custom-call(bf16[8,3,256,128]{3,2,1,0:T(8,128)(2,1)S(1)} %all-to-all-done.qkv_ref), custom_call_target="tpu_custom_call" | custom-call | flops 1073741824 | bytes 2097152 | tf_op jit(solution)/shard_map/self_attend/pallas_call | solution.py:64
  42.2 3.5 %all-to-all-start.1 = ((bf16[8,256,128]{2,1,0:T(8,128)(2,1)}), bf16[8,256,128]{2,1,0:T(8,128)(2,1)S(1)}, u32[]{:S(2)}, u32[]{:S(2)}) async-start(bf16[8,256,128]{2,1,0:T(8,128)(2,1)} %self_attend.1), calls=%async_computation.1 | async-start | bytes 1048576 | tf_op jit(solution)/shard_map/all_to_all | solution.py:509
  45.7 0.0 all-reduce.2.cloned.1.call-start
  45.8 1.9 all-gather.3.cloned.1.call-done
  47.7 7.7 %all-to-all-done.1.attended_ref = bf16[8,256,128]{2,1,0:T(8,128)(2,1)S(1)} async-done(((bf16[8,256,128]{2,1,0:T(8,128)(2,1)}), bf16[8,256,128]{2,1,0:T(8,128)(2,1)S(1)}, u32[]{:S(2)}, u32[]{:S(2)}) %all-to-all-start.1) | async-done | bytes 524320 | tf_op jit(solution)/shard_map/all_to_all | solution.py:509
  55.4 0.0 copy-start.2
  55.4 6.6 %self_out.1 = bf16[256,4096]{1,0:T(8,128)(2,1)} custom-call(bf16[8,256,128]{2,1,0:T(8,128)(2,1)S(1)} %all-to-all-done.1.attended_ref, bf16[1024,4096]{1,0:T(8,128)(2,1)} %weight_hbm.1), custom_call_target="tpu_custom_call" | custom-call | flops 2147483648 | bytes 11010048 | tf_op jit(solution)/shard_map/self_out/pallas_call | solution.py:196
  62.0 0.0 copy-start.10
  62.0 0.0 copy-done.2
  62.0 0.6 collective-permute-start.1
  62.6 0.6 collective-permute-start.2
  63.2 2.4 %collective-permute-start.3 = (bf16[4,128,1024]{2,1,0:T(8,128)(2,1)S(1)}, bf16[4,128,1024]{2,1,0:T(8,128)(2,1)}, u32[]{:S(2)}, u32[]{:S(2)}) collective-permute-start(bf16[4,128,1024]{2,1,0:T(8,128)(2,1)S(1)} %bitcast.22), channel_id=1, source_target_pairs={{0,24},{4,28},{8,16},{12,20},{16,8},{20,12},{24,0},{28,4},{1,25},{... | collective-permute-start | bytes 3145736 | tf_op jit(solution)/shard_map/ppermute | solution.py:30
  65.6 0.0 all-reduce.2.cloned.1.call-update
  65.6 0.0 reduce-scatter.2.cloned.1.call-start
  65.6 22.5 %collective-permute-done.1 = bf16[4,128,1024]{2,1,0:T(8,128)(2,1)S(1)} collective-permute-done((bf16[4,128,1024]{2,1,0:T(8,128)(2,1)S(1)}, bf16[4,128,1024]{2,1,0:T(8,128)(2,1)S(1)}, u32[]{:S(2)}, u32[]{:S(2)}) %collective-permute-start.1) | collective-permute-done | bytes 1048608 | tf_op jit(solution)/shard_map/ppermute | solution.py:30
  88.2 21.8 %collective-permute-done.2 = bf16[4,128,1024]{2,1,0:T(8,128)(2,1)S(1)} collective-permute-done((bf16[4,128,1024]{2,1,0:T(8,128)(2,1)S(1)}, bf16[4,128,1024]{2,1,0:T(8,128)(2,1)S(1)}, u32[]{:S(2)}, u32[]{:S(2)}) %collective-permute-start.2) | collective-permute-done | bytes 1048608 | tf_op jit(solution)/shard_map/ppermute | solution.py:30
  109.9 0.0 collective-permute-done.3
  110.0 0.0 collective-permute-start.4
  110.0 0.5 collective-permute-start.5
  110.5 0.0 copy-start.3
  110.5 1.0 copy-done.3
  111.4 0.0 collective-permute-start.6
  111.4 0.0 copy-start.5
  111.4 1.0 copy-done.5
  112.4 0.5 collective-permute-start.7
  112.9 0.0 copy-done.10
  112.9 0.0 collective-permute-done.4
  112.9 1.2 collective-permute-done.5
  114.1 3.0 %collective-permute-done.6 = bf16[4,128,1024]{2,1,0:T(8,128)(2,1)S(1)} collective-permute-done((bf16[4,128,1024]{2,1,0:T(8,128)(2,1)S(1)}, bf16[4,128,1024]{2,1,0:T(8,128)(2,1)S(1)}, u32[]{:S(2)}, u32[]{:S(2)}) %collective-permute-start.6) | collective-permute-done | bytes 1048608 | tf_op jit(solution)/shard_map/ppermute | solution.py:30
  117.1 0.2 collective-permute-done.7
  117.3 0.0 copy-done.7
  117.3 0.8 copy-done.8
  118.1 0.4 copy-done.9
  118.5 1.2 copy-done.4
  119.7 1.2 copy-done.6
  121.0 11.4 %project_encodings.1 = (bf16[1280,1024]{1,0:T(8,128)(2,1)}, bf16[1280,1024]{1,0:T(8,128)(2,1)}) custom-call(s32[32]{0:T(128)S(1)} %pad_add_fusion.2.where_ref.info_ref, bf16[1,4,128,1024]{3,2,1,0:T(8,128)(2,1)S(1)} %bitcast.24, bf16[1,4,128,1024]{3,2,1,0:T(8,128)(2,1)S(1)} %bitcast.25, bf16[1,4,128,1024]{3,2,1,0:T(8,128)(2,1)S(1)} %bitcast.26, ...), custom_call_target="tpu_custom_call" | custom-call | flops 1310720 | bytes 2621440 | tf_op jit(solution)/shard_map/project_encodings/pallas_call | solution.py:274
  132.3 19.3 %all-reduce.2.cloned.1.call-done.total_ref = bf16[256,4096]{1,0:T(8,128)(2,1)} async-done(((bf16[256,4096]{1,0:T(8,128)(2,1)}), bf16[256,4096]{1,0:T(8,128)(2,1)}) %all-reduce.2.cloned.1.call-update) | async-done | bytes 2097168 | tf_op jit(solution)/shard_map/psum | solution.py:516
  151.6 0.0 copy-done
  151.6 11.7 %cross_block.1 = (bf16[4,64,4096]{2,1,0:T(8,128)(2,1)S(1)}, f32[64,4096]{1,0:T(8,128)S(1)}) custom-call(s32[32]{0:T(128)S(1)} %pad_add_fusion.2.where_ref.info_ref, bf16[256,4096]{1,0:T(8,128)(2,1)S(1)} %copy-done, bf16[256,4096]{1,0:T(8,128)(2,1)} %all-reduce.2.cloned.1.call-done.total_ref, bf16[1,4096]{1,0:T(2,128)(2,1)S(1)} %reshape.18.gain_ref, ...), custom_call_target="tpu_custom_call" | custom-call | flops 4563402752 | bytes 30408704 | tf_op jit(solution)/shard_map/cross_block/pallas_call | solution.py:438
  163.3 0.0 copy-start.1
  163.3 1.4 copy-done.1
  164.7 0.0 reduce-scatter.2.cloned.1.call-update
  164.7 43.0 %reduce-scatter.2.cloned.1.call-done = bf16[64,4096]{1,0:T(8,128)(2,1)} async-done(((bf16[256,4096]{1,0:T(8,128)(2,1)}), bf16[64,4096]{1,0:T(8,128)(2,1)}) %reduce-scatter.2.cloned.1.call-update) | async-done | bytes 524304 | tf_op jit(solution)/shard_map/reduce_scatter | solution.py:537
  207.7 2.1 convert_add_fusion
  (8 shorter events, 0.0 us)
Async XLA Ops:
  10.3 6.1 %copy-start.11 = (s32[4,2]{0,1:T(2,128)S(1)}, s32[4,2]{0,1:T(2,128)}, u32[]{:S(2)}) copy-start(s32[4,2]{0,1:T(2,128)} %param.24) | copy-start | bytes 100
  10.3 6.1 %copy-start.12 = (s32[4,2]{0,1:T(2,128)S(1)}, s32[4,2]{0,1:T(2,128)}, u32[]{:S(2)}) copy-start(s32[4,2]{0,1:T(2,128)} %param.25) | copy-start | bytes 100
  10.3 26.3 %all-to-all-start = ((bf16[8,3,256,128]{3,2,1,0:T(8,128)(2,1)}), bf16[8,3,256,128]{3,2,1,0:T(8,128)(2,1)S(1)}, u32[]{:S(2)}, u32[]{:S(2)}) async-start(bf16[8,3,256,128]{3,2,1,0:T(8,128)(2,1)} %get-tuple-element.28), calls=%async_computation | async-start | bytes 3145728 | tf_op jit(solution)/shard_map/all_to_all | solution.py:507
  15.7 32.1 %all-gather.3.cloned.1.call-start = ((), (), s32[]{:S(2)}) async-start(), calls=%async_computation.5 | async-start | bytes 1310720 | tf_op jit(solution)/shard_map/all_gather | solution.py:493
  16.6 3.2 %collective-permute-start = (s32[2,2]{1,0:T(2,128)S(1)}, s32[2,2]{1,0:T(2,128)S(1)}, u32[]{:S(2)}, u32[]{:S(2)}) collective-permute-start(s32[2,2]{1,0:T(2,128)S(1)} %bitcast.36), channel_id=1, source_target_pairs={{0,4},{4,8},{8,12},{12,16},{16,20},{20,24},{24,28},{1,5},{5,9},{9,... | collective-permute-start | bytes 56 | tf_op jit(solution)/shard_map/ppermute | solution.py:26
  42.2 13.2 %all-to-all-start.1 = ((bf16[8,256,128]{2,1,0:T(8,128)(2,1)}), bf16[8,256,128]{2,1,0:T(8,128)(2,1)S(1)}, u32[]{:S(2)}, u32[]{:S(2)}) async-start(bf16[8,256,128]{2,1,0:T(8,128)(2,1)} %self_attend.1), calls=%async_computation.1 | async-start | bytes 1048576 | tf_op jit(solution)/shard_map/all_to_all | solution.py:509
  45.7 105.9 %all-reduce.2.cloned.1.call-start = ((), (), s32[]{:S(2)}) async-start(), calls=%async_computation.3 | async-start | bytes 4194304 | tf_op jit(solution)/shard_map/psum | solution.py:516
  55.4 6.6 %copy-start.2 = (bf16[512,1024]{1,0:T(8,128)(2,1)S(1)}, bf16[512,1024]{1,0:T(8,128)(2,1)}, u32[]{:S(2)}) copy-start(bf16[512,1024]{1,0:T(8,128)(2,1)} %all-gather.3.cloned.1.call-done) | copy-start | bytes 3145732
  62.0 50.9 %copy-start.10 = (bf16[4096]{0:T(1024)(128)(2,1)S(1)}, bf16[4096]{0:T(1024)(128)(2,1)}, u32[]{:S(2)}) copy-start(bf16[4096]{0:T(1024)(128)(2,1)} %param.18) | copy-start | bytes 24580
  62.0 26.2 %collective-permute-start.1 = (bf16[4,128,1024]{2,1,0:T(8,128)(2,1)S(1)}, bf16[4,128,1024]{2,1,0:T(8,128)(2,1)S(1)}, u32[]{:S(2)}, u32[]{:S(2)}) collective-permute-start(bf16[4,128,1024]{2,1,0:T(8,128)(2,1)S(1)} %bitcast.20), channel_id=1, source_target_pairs={{0,8},{4,12},{8,0},{12,4},{16,24},{20,28},{24,16},{28,20},{1,9},{5... | collective-permute-start | bytes 3145736 | tf_op jit(solution)/shard_map/ppermute | solution.py:30
  62.6 47.3 %collective-permute-start.2 = (bf16[4,128,1024]{2,1,0:T(8,128)(2,1)S(1)}, bf16[4,128,1024]{2,1,0:T(8,128)(2,1)S(1)}, u32[]{:S(2)}, u32[]{:S(2)}) collective-permute-start(bf16[4,128,1024]{2,1,0:T(8,128)(2,1)S(1)} %bitcast.21), channel_id=1, source_target_pairs={{0,16},{4,20},{8,24},{12,28},{16,0},{20,4},{24,8},{28,12},{1,17},{... | collective-permute-start | bytes 3145736 | tf_op jit(solution)/shard_map/ppermute | solution.py:30
  63.2 46.8 %collective-permute-start.3 = (bf16[4,128,1024]{2,1,0:T(8,128)(2,1)S(1)}, bf16[4,128,1024]{2,1,0:T(8,128)(2,1)}, u32[]{:S(2)}, u32[]{:S(2)}) collective-permute-start(bf16[4,128,1024]{2,1,0:T(8,128)(2,1)S(1)} %bitcast.22), channel_id=1, source_target_pairs={{0,24},{4,28},{8,16},{12,20},{16,8},{20,12},{24,0},{28,4},{1,25},{... | collective-permute-start | bytes 3145736 | tf_op jit(solution)/shard_map/ppermute | solution.py:30
  65.6 142.1 %reduce-scatter.2.cloned.1.call-start = ((), (), s32[]{:S(2)}) async-start(), calls=%async_computation.4 | async-start | bytes 2621440 | tf_op jit(solution)/shard_map/reduce_scatter | solution.py:537
  110.0 3.0 %collective-permute-start.4 = (bf16[4,128,1024]{2,1,0:T(8,128)(2,1)S(1)}, bf16[4,128,1024]{2,1,0:T(8,128)(2,1)S(1)}, u32[]{:S(2)}, u32[]{:S(2)}) collective-permute-start(bf16[4,128,1024]{2,1,0:T(8,128)(2,1)S(1)} %bitcast.23), channel_id=1, source_target_pairs={{0,4},{4,0},{8,12},{12,8},{16,20},{20,16},{24,28},{28,24},{1,5},{5... | collective-permute-start | bytes 3145736 | tf_op jit(solution)/shard_map/ppermute | solution.py:30
  110.0 4.2 %collective-permute-start.5 = (bf16[4,128,1024]{2,1,0:T(8,128)(2,1)S(1)}, bf16[4,128,1024]{2,1,0:T(8,128)(2,1)S(1)}, u32[]{:S(2)}, u32[]{:S(2)}) collective-permute-start(bf16[4,128,1024]{2,1,0:T(8,128)(2,1)S(1)} %collective-permute-done.1), channel_id=1, source_target_pairs={{0,4},{4,0},{8,12},{12,8},{16,20},{20,16},{24,28},{28,24},{1,5},{5... | collective-permute-start | bytes 3145736 | tf_op jit(solution)/shard_map/ppermute | solution.py:30
  110.5 1.0 copy-start.3
  111.4 5.7 %collective-permute-start.6 = (bf16[4,128,1024]{2,1,0:T(8,128)(2,1)S(1)}, bf16[4,128,1024]{2,1,0:T(8,128)(2,1)S(1)}, u32[]{:S(2)}, u32[]{:S(2)}) collective-permute-start(bf16[4,128,1024]{2,1,0:T(8,128)(2,1)S(1)} %collective-permute-done.2), channel_id=1, source_target_pairs={{0,4},{4,0},{8,12},{12,8},{16,20},{20,16},{24,28},{28,24},{1,5},{5... | collective-permute-start | bytes 3145736 | tf_op jit(solution)/shard_map/ppermute | solution.py:30
  111.4 1.0 copy-start.5
  112.4 4.9 %collective-permute-start.7 = (bf16[4,128,1024]{2,1,0:T(8,128)(2,1)}, bf16[4,128,1024]{2,1,0:T(8,128)(2,1)S(1)}, u32[]{:S(2)}, u32[]{:S(2)}) collective-permute-start(bf16[4,128,1024]{2,1,0:T(8,128)(2,1)} %collective-permute-done.3), channel_id=1, source_target_pairs={{0,4},{4,0},{8,12},{12,8},{16,20},{20,16},{24,28},{28,24},{1,5},{5... | collective-permute-start | bytes 3145736 | tf_op jit(solution)/shard_map/ppermute | solution.py:30
  114.1 3.2 %copy-start.7 = (bf16[4,128,1024]{2,1,0:T(8,128)(2,1)}, bf16[4,128,1024]{2,1,0:T(8,128)(2,1)S(1)}, u32[]{:S(2)}) copy-start(bf16[4,128,1024]{2,1,0:T(8,128)(2,1)S(1)} %collective-permute-done.5) | copy-start | bytes 3145732
  117.1 1.0 copy-start.8
  117.3 1.2 copy-start.9
  118.5 1.2 copy-start.4
  119.7 1.2 copy-start.6
  121.0 30.7 %copy-start = (bf16[256,4096]{1,0:T(8,128)(2,1)S(1)}, bf16[256,4096]{1,0:T(8,128)(2,1)}, u32[]{:S(2)}) copy-start(bf16[256,4096]{1,0:T(8,128)(2,1)} %hidden_ref.1) | copy-start | bytes 6291460
  163.3 1.4 copy-start.1
Sparse Core Ops, SparseCore 0:
  18.1 29.6 all-gather.2
  65.7 85.8 all-reduce.1
  164.8 42.7 reduce-scatter.1

commit v13 on v12

--- a/solution.py
+++ b/solution.py
@@ -316,7 +316,7 @@
     values_hbm,
     wo_hbm,
     out_ref,
-    residual_ref,
+    residual_hbm,
     wq_ref,
     keys_ref,
     values_ref,
@@ -324,6 +324,7 @@
     rows_ref,
     query_ref,
     mixed_ref,
+    residual_ref,
     sems,
     *,
     scale,
@@ -368,6 +369,8 @@
     residual_ref[...] = hidden_ref[own, :].astype(jnp.float32) + total_ref[own, :].astype(
         jnp.float32
     )
+    residual_copy = pltpu.make_async_copy(residual_ref, residual_hbm, sems.at[18])
+    residual_copy.start()
     lanes = [slice(2 * pair * HD, 2 * (pair + 1) * HD) for pair in range(pairs)]
     for k in range(0, parts, 2):
         for copy in wq_copies[k : k + 2]:
@@ -427,6 +430,7 @@
         return carried
 
     lax.fori_loop(0, features // step, columns, 0, unroll=4)
+    residual_copy.wait()
 
 
 def cross_block(info, hidden, total, gain, w_cross_q, keys, values, w_cross_out, n_db, scale):
@@ -442,7 +446,7 @@
             jax.ShapeDtypeStruct((share, features), jnp.float32),
         ],
         in_specs=[pl.BlockSpec(memory_space=pltpu.SMEM)] + [vmem] * 3 + [anywhere] * 4,
-        out_specs=[vmem] * 2,
+        out_specs=[vmem, anywhere],
         scratch_shapes=[
             pltpu.VMEM((features, width), jnp.bfloat16),
             pltpu.VMEM(keys.shape, jnp.bfloat16),
@@ -451,7 +455,8 @@
             pltpu.VMEM((rows, features), jnp.bfloat16),
             pltpu.VMEM((rows, width), jnp.float32),
             pltpu.VMEM((rows, width), jnp.bfloat16),
-            pltpu.SemaphoreType.DMA((18,)),
+            pltpu.VMEM((share, features), jnp.float32),
+            pltpu.SemaphoreType.DMA((19,)),
         ],
         compiler_params=pltpu.CompilerParams(vmem_limit_bytes=VMEM_BYTES),
         cost_estimate=pl.CostEstimate(

time: 217 us -> 217 us (level)
  no operation moved by 1% of the time
where the time goes in v13:
time: 217 us; the launch traced here: 216 us
  waiting for transfers between devices  138 us (64%)
  Pallas kernels  39 us (18%)
  starting transfers between devices  15.9 us (7%)
  between operations  13.2 us (6%)
  local copies, waits for them, and re-layouts  7.44 us (3%)
  other arithmetic  2.44 us (1%)
    ppermute x7, waiting for transfers between devices, plane_swap(): return lax.ppermute(block, 'seq', [(i, i ^ mask) for i in range(8)])  48.7 us
    reduce_scatter x1, waiting for transfers between devices, per_device(): lax.psum_scatter(partial.reshape(rows, features), 'db', scatter_dimension...  43 us
    psum x1, waiting for transfers between devices, per_device(): total = lax.psum(partial, 'db')  19.3 us
    all_to_all x1, waiting for transfers between devices, per_device(): held = lax.all_to_all(packed, 'seq', 0, 0, tiled=True)  16.4 us
    pallas_call x1, Pallas kernels, cross_block(): pl.pallas_call(functools.partial(cross_kernel, scale=scale), out_shape=[j...  11.7 us
    pallas_call x1, Pallas kernels, project_encodings(): pl.pallas_call(functools.partial(project_kernel, cuts=cuts), out_shape=[m...  11.4 us
    all_to_all x1, waiting for transfers between devices, per_device(): lax.all_to_all(self_attend_head(held, scale), 'seq', 0, 0, tiled=True)  7.68 us
    unnamed x26, local copies, waits for them, and re-layouts  6.97 us
  transfers between devices with their start and end apart: 13, of which 11 were waited for; matrix products, arithmetic and copies ran while one was open for 0% of the time, Pallas kernels for 8%

profile of v13, /device:TPU:0, one launch (start us, length us, event | category | flops | bytes accessed | tf_op | source)
XLA Modules:
  0.0 216.3 jit_solution(5161412832367114109)
XLA Ops:
  6.5 3.8 %pack_heads.1 = (bf16[8,3,256,128]{3,2,1,0:T(8,128)(2,1)}, bf16[128,1024]{1,0:T(8,128)(2,1)}) custom-call(s32[1]{0:T(128)} %bitcast.index_ref, bf16[256,1024]{1,0:T(8,128)(2,1)} %query_ref.1, bf16[256,1024]{1,0:T(8,128)(2,1)} %key_ref.1, bf16[256,1024]{1,0:T(8,128)(2,1)} %value_ref.1, bf16[1024,1024]{1,0:T(8,128)(2,1)} %bitcast.28), custom_call_target="tpu_custom_call" | custom-call | bytes 3145728 | tf_op jit(solution)/shard_map/pack_heads/pallas_call | solution.py:97
  10.3 0.0 copy-start.11
  10.3 0.0 copy-start.12
  10.3 5.3 %all-to-all-start = ((bf16[8,3,256,128]{3,2,1,0:T(8,128)(2,1)}), bf16[8,3,256,128]{3,2,1,0:T(8,128)(2,1)S(1)}, u32[]{:S(2)}, u32[]{:S(2)}) async-start(bf16[8,3,256,128]{3,2,1,0:T(8,128)(2,1)} %get-tuple-element.28), calls=%async_computation | async-start | bytes 3145728 | tf_op jit(solution)/shard_map/all_to_all | solution.py:512
  15.7 0.0 all-gather.3.cloned.1.call-start
  15.7 0.7 all-gather.3.cloned.1.call-update
  16.4 0.0 copy-done.11
  16.4 0.0 copy-done.12
  16.4 0.1 pad_add_fusion.1
  16.5 0.1 copy.17
  16.6 2.4 %collective-permute-start = (s32[2,2]{1,0:T(2,128)S(1)}, s32[2,2]{1,0:T(2,128)S(1)}, u32[]{:S(2)}, u32[]{:S(2)}) collective-permute-start(s32[2,2]{1,0:T(2,128)S(1)} %bitcast.36), channel_id=1, source_target_pairs={{0,4},{4,8},{8,12},{12,16},{16,20},{20,24},{24,28},{1,5},{5,9},{9,... | collective-permute-start | bytes 56 | tf_op jit(solution)/shard_map/ppermute | solution.py:26
  19.0 0.1 pad.4.clone
  19.1 0.7 collective-permute-done
  19.8 0.1 copy.18
  19.9 0.1 add_add_fusion
  20.0 0.1 pad_add_fusion
  20.0 0.1 copy.19
  20.1 0.1 reshape.17
  20.2 0.1 pad_add_fusion.2.where_ref.info_ref
  20.3 16.4 %all-to-all-done.qkv_ref = bf16[8,3,256,128]{3,2,1,0:T(8,128)(2,1)S(1)} async-done(((bf16[8,3,256,128]{3,2,1,0:T(8,128)(2,1)}), bf16[8,3,256,128]{3,2,1,0:T(8,128)(2,1)S(1)}, u32[]{:S(2)}, u32[]{:S(2)}) %all-to-all-start) | async-done | bytes 1572896 | tf_op jit(solution)/shard_map/all_to_all | solution.py:512
  36.7 5.6 %self_attend.1 = bf16[8,256,128]{2,1,0:T(8,128)(2,1)} custom-call(bf16[8,3,256,128]{3,2,1,0:T(8,128)(2,1)S(1)} %all-to-all-done.qkv_ref), custom_call_target="tpu_custom_call" | custom-call | flops 1073741824 | bytes 2097152 | tf_op jit(solution)/shard_map/self_attend/pallas_call | solution.py:64
  42.2 3.5 %all-to-all-start.1 = ((bf16[8,256,128]{2,1,0:T(8,128)(2,1)}), bf16[8,256,128]{2,1,0:T(8,128)(2,1)S(1)}, u32[]{:S(2)}, u32[]{:S(2)}) async-start(bf16[8,256,128]{2,1,0:T(8,128)(2,1)} %self_attend.1), calls=%async_computation.1 | async-start | bytes 1048576 | tf_op jit(solution)/shard_map/all_to_all | solution.py:514
  45.7 0.0 all-reduce.2.cloned.1.call-start
  45.8 1.9 all-gather.3.cloned.1.call-done
  47.7 7.7 %all-to-all-done.1.attended_ref = bf16[8,256,128]{2,1,0:T(8,128)(2,1)S(1)} async-done(((bf16[8,256,128]{2,1,0:T(8,128)(2,1)}), bf16[8,256,128]{2,1,0:T(8,128)(2,1)S(1)}, u32[]{:S(2)}, u32[]{:S(2)}) %all-to-all-start.1) | async-done | bytes 524320 | tf_op jit(solution)/shard_map/all_to_all | solution.py:514
  55.4 0.0 copy-start.2
  55.4 6.6 %self_out.1 = bf16[256,4096]{1,0:T(8,128)(2,1)} custom-call(bf16[8,256,128]{2,1,0:T(8,128)(2,1)S(1)} %all-to-all-done.1.attended_ref, bf16[1024,4096]{1,0:T(8,128)(2,1)} %weight_hbm.1), custom_call_target="tpu_custom_call" | custom-call | flops 2147483648 | bytes 11010048 | tf_op jit(solution)/shard_map/self_out/pallas_call | solution.py:196
  62.0 0.0 copy-start.10
  62.0 0.0 copy-done.2
  62.0 0.6 collective-permute-start.1
  62.6 0.6 collective-permute-start.2
  63.2 2.4 %collective-permute-start.3 = (bf16[4,128,1024]{2,1,0:T(8,128)(2,1)S(1)}, bf16[4,128,1024]{2,1,0:T(8,128)(2,1)}, u32[]{:S(2)}, u32[]{:S(2)}) collective-permute-start(bf16[4,128,1024]{2,1,0:T(8,128)(2,1)S(1)} %bitcast.22), channel_id=1, source_target_pairs={{0,24},{4,28},{8,16},{12,20},{16,8},{20,12},{24,0},{28,4},{1,25},{... | collective-permute-start | bytes 3145736 | tf_op jit(solution)/shard_map/ppermute | solution.py:30
  65.6 0.0 all-reduce.2.cloned.1.call-update
  65.6 0.0 reduce-scatter.2.cloned.1.call-start
  65.6 22.5 %collective-permute-done.1 = bf16[4,128,1024]{2,1,0:T(8,128)(2,1)S(1)} collective-permute-done((bf16[4,128,1024]{2,1,0:T(8,128)(2,1)S(1)}, bf16[4,128,1024]{2,1,0:T(8,128)(2,1)S(1)}, u32[]{:S(2)}, u32[]{:S(2)}) %collective-permute-start.1) | collective-permute-done | bytes 1048608 | tf_op jit(solution)/shard_map/ppermute | solution.py:30
  88.2 21.8 %collective-permute-done.2 = bf16[4,128,1024]{2,1,0:T(8,128)(2,1)S(1)} collective-permute-done((bf16[4,128,1024]{2,1,0:T(8,128)(2,1)S(1)}, bf16[4,128,1024]{2,1,0:T(8,128)(2,1)S(1)}, u32[]{:S(2)}, u32[]{:S(2)}) %collective-permute-start.2) | collective-permute-done | bytes 1048608 | tf_op jit(solution)/shard_map/ppermute | solution.py:30
  109.9 0.0 collective-permute-done.3
  110.0 0.0 collective-permute-start.4
  110.0 0.5 collective-permute-start.5
  110.5 0.0 copy-start.3
  110.5 1.0 copy-done.3
  111.4 0.0 collective-permute-start.6
  111.4 0.0 copy-start.5
  111.4 1.0 copy-done.5
  112.4 0.5 collective-permute-start.7
  112.9 0.0 copy-done.10
  112.9 0.0 collective-permute-done.4
  112.9 1.2 collective-permute-done.5
  114.1 3.0 %collective-permute-done.6 = bf16[4,128,1024]{2,1,0:T(8,128)(2,1)S(1)} collective-permute-done((bf16[4,128,1024]{2,1,0:T(8,128)(2,1)S(1)}, bf16[4,128,1024]{2,1,0:T(8,128)(2,1)S(1)}, u32[]{:S(2)}, u32[]{:S(2)}) %collective-permute-start.6) | collective-permute-done | bytes 1048608 | tf_op jit(solution)/shard_map/ppermute | solution.py:30
  117.1 0.2 collective-permute-done.7
  117.3 0.0 copy-done.7
  117.3 0.8 copy-done.8
  118.1 0.4 copy-done.9
  118.5 1.2 copy-done.4
  119.7 1.2 copy-done.6
  121.0 11.4 %project_encodings.1 = (bf16[1280,1024]{1,0:T(8,128)(2,1)}, bf16[1280,1024]{1,0:T(8,128)(2,1)}) custom-call(s32[32]{0:T(128)S(1)} %pad_add_fusion.2.where_ref.info_ref, bf16[1,4,128,1024]{3,2,1,0:T(8,128)(2,1)S(1)} %bitcast.24, bf16[1,4,128,1024]{3,2,1,0:T(8,128)(2,1)S(1)} %bitcast.25, bf16[1,4,128,1024]{3,2,1,0:T(8,128)(2,1)S(1)} %bitcast.26, ...), custom_call_target="tpu_custom_call" | custom-call | flops 1310720 | bytes 2621440 | tf_op jit(solution)/shard_map/project_encodings/pallas_call | solution.py:274
  132.3 19.3 %all-reduce.2.cloned.1.call-done.total_ref = bf16[256,4096]{1,0:T(8,128)(2,1)} async-done(((bf16[256,4096]{1,0:T(8,128)(2,1)}), bf16[256,4096]{1,0:T(8,128)(2,1)}) %all-reduce.2.cloned.1.call-update) | async-done | bytes 2097168 | tf_op jit(solution)/shard_map/psum | solution.py:521
  151.6 0.0 copy-done
  151.6 11.7 %cross_block.1 = (bf16[4,64,4096]{2,1,0:T(8,128)(2,1)S(1)}, f32[64,4096]{1,0:T(8,128)S(1)}) custom-call(s32[32]{0:T(128)S(1)} %pad_add_fusion.2.where_ref.info_ref, bf16[256,4096]{1,0:T(8,128)(2,1)S(1)} %copy-done, bf16[256,4096]{1,0:T(8,128)(2,1)} %all-reduce.2.cloned.1.call-done.total_ref, bf16[1,4096]{1,0:T(2,128)(2,1)S(1)} %reshape.18.gain_ref, ...), custom_call_target="tpu_custom_call" | custom-call | flops 4563402752 | bytes 30408704 | tf_op jit(solution)/shard_map/cross_block/pallas_call | solution.py:442
  163.3 0.0 copy-start.1
  163.3 1.4 copy-done.1
  164.7 0.0 reduce-scatter.2.cloned.1.call-update
  164.7 43.0 %reduce-scatter.2.cloned.1.call-done = bf16[64,4096]{1,0:T(8,128)(2,1)} async-done(((bf16[256,4096]{1,0:T(8,128)(2,1)}), bf16[64,4096]{1,0:T(8,128)(2,1)}) %reduce-scatter.2.cloned.1.call-update) | async-done | bytes 524304 | tf_op jit(solution)/shard_map/reduce_scatter | solution.py:542
  207.7 2.1 convert_add_fusion
  (8 shorter events, 0.0 us)
Async XLA Ops:
  10.3 6.1 %copy-start.11 = (s32[4,2]{0,1:T(2,128)S(1)}, s32[4,2]{0,1:T(2,128)}, u32[]{:S(2)}) copy-start(s32[4,2]{0,1:T(2,128)} %param.24) | copy-start | bytes 100
  10.3 6.1 %copy-start.12 = (s32[4,2]{0,1:T(2,128)S(1)}, s32[4,2]{0,1:T(2,128)}, u32[]{:S(2)}) copy-start(s32[4,2]{0,1:T(2,128)} %param.25) | copy-start | bytes 100
  10.3 26.3 %all-to-all-start = ((bf16[8,3,256,128]{3,2,1,0:T(8,128)(2,1)}), bf16[8,3,256,128]{3,2,1,0:T(8,128)(2,1)S(1)}, u32[]{:S(2)}, u32[]{:S(2)}) async-start(bf16[8,3,256,128]{3,2,1,0:T(8,128)(2,1)} %get-tuple-element.28), calls=%async_computation | async-start | bytes 3145728 | tf_op jit(solution)/shard_map/all_to_all | solution.py:512
  15.7 32.1 %all-gather.3.cloned.1.call-start = ((), (), s32[]{:S(2)}) async-start(), calls=%async_computation.5 | async-start | bytes 1310720 | tf_op jit(solution)/shard_map/all_gather | solution.py:498
  16.6 3.2 %collective-permute-start = (s32[2,2]{1,0:T(2,128)S(1)}, s32[2,2]{1,0:T(2,128)S(1)}, u32[]{:S(2)}, u32[]{:S(2)}) collective-permute-start(s32[2,2]{1,0:T(2,128)S(1)} %bitcast.36), channel_id=1, source_target_pairs={{0,4},{4,8},{8,12},{12,16},{16,20},{20,24},{24,28},{1,5},{5,9},{9,... | collective-permute-start | bytes 56 | tf_op jit(solution)/shard_map/ppermute | solution.py:26
  42.2 13.2 %all-to-all-start.1 = ((bf16[8,256,128]{2,1,0:T(8,128)(2,1)}), bf16[8,256,128]{2,1,0:T(8,128)(2,1)S(1)}, u32[]{:S(2)}, u32[]{:S(2)}) async-start(bf16[8,256,128]{2,1,0:T(8,128)(2,1)} %self_attend.1), calls=%async_computation.1 | async-start | bytes 1048576 | tf_op jit(solution)/shard_map/all_to_all | solution.py:514
  45.7 105.9 %all-reduce.2.cloned.1.call-start = ((), (), s32[]{:S(2)}) async-start(), calls=%async_computation.3 | async-start | bytes 4194304 | tf_op jit(solution)/shard_map/psum | solution.py:521
  55.4 6.6 %copy-start.2 = (bf16[512,1024]{1,0:T(8,128)(2,1)S(1)}, bf16[512,1024]{1,0:T(8,128)(2,1)}, u32[]{:S(2)}) copy-start(bf16[512,1024]{1,0:T(8,128)(2,1)} %all-gather.3.cloned.1.call-done) | copy-start | bytes 3145732
  62.0 50.9 %copy-start.10 = (bf16[4096]{0:T(1024)(128)(2,1)S(1)}, bf16[4096]{0:T(1024)(128)(2,1)}, u32[]{:S(2)}) copy-start(bf16[4096]{0:T(1024)(128)(2,1)} %param.18) | copy-start | bytes 24580
  62.0 26.2 %collective-permute-start.1 = (bf16[4,128,1024]{2,1,0:T(8,128)(2,1)S(1)}, bf16[4,128,1024]{2,1,0:T(8,128)(2,1)S(1)}, u32[]{:S(2)}, u32[]{:S(2)}) collective-permute-start(bf16[4,128,1024]{2,1,0:T(8,128)(2,1)S(1)} %bitcast.20), channel_id=1, source_target_pairs={{0,8},{4,12},{8,0},{12,4},{16,24},{20,28},{24,16},{28,20},{1,9},{5... | collective-permute-start | bytes 3145736 | tf_op jit(solution)/shard_map/ppermute | solution.py:30
  62.6 47.3 %collective-permute-start.2 = (bf16[4,128,1024]{2,1,0:T(8,128)(2,1)S(1)}, bf16[4,128,1024]{2,1,0:T(8,128)(2,1)S(1)}, u32[]{:S(2)}, u32[]{:S(2)}) collective-permute-start(bf16[4,128,1024]{2,1,0:T(8,128)(2,1)S(1)} %bitcast.21), channel_id=1, source_target_pairs={{0,16},{4,20},{8,24},{12,28},{16,0},{20,4},{24,8},{28,12},{1,17},{... | collective-permute-start | bytes 3145736 | tf_op jit(solution)/shard_map/ppermute | solution.py:30
  63.2 46.8 %collective-permute-start.3 = (bf16[4,128,1024]{2,1,0:T(8,128)(2,1)S(1)}, bf16[4,128,1024]{2,1,0:T(8,128)(2,1)}, u32[]{:S(2)}, u32[]{:S(2)}) collective-permute-start(bf16[4,128,1024]{2,1,0:T(8,128)(2,1)S(1)} %bitcast.22), channel_id=1, source_target_pairs={{0,24},{4,28},{8,16},{12,20},{16,8},{20,12},{24,0},{28,4},{1,25},{... | collective-permute-start | bytes 3145736 | tf_op jit(solution)/shard_map/ppermute | solution.py:30
  65.6 142.1 %reduce-scatter.2.cloned.1.call-start = ((), (), s32[]{:S(2)}) async-start(), calls=%async_computation.4 | async-start | bytes 2621440 | tf_op jit(solution)/shard_map/reduce_scatter | solution.py:542
  110.0 3.0 %collective-permute-start.4 = (bf16[4,128,1024]{2,1,0:T(8,128)(2,1)S(1)}, bf16[4,128,1024]{2,1,0:T(8,128)(2,1)S(1)}, u32[]{:S(2)}, u32[]{:S(2)}) collective-permute-start(bf16[4,128,1024]{2,1,0:T(8,128)(2,1)S(1)} %bitcast.23), channel_id=1, source_target_pairs={{0,4},{4,0},{8,12},{12,8},{16,20},{20,16},{24,28},{28,24},{1,5},{5... | collective-permute-start | bytes 3145736 | tf_op jit(solution)/shard_map/ppermute | solution.py:30
  110.0 4.2 %collective-permute-start.5 = (bf16[4,128,1024]{2,1,0:T(8,128)(2,1)S(1)}, bf16[4,128,1024]{2,1,0:T(8,128)(2,1)S(1)}, u32[]{:S(2)}, u32[]{:S(2)}) collective-permute-start(bf16[4,128,1024]{2,1,0:T(8,128)(2,1)S(1)} %collective-permute-done.1), channel_id=1, source_target_pairs={{0,4},{4,0},{8,12},{12,8},{16,20},{20,16},{24,28},{28,24},{1,5},{5... | collective-permute-start | bytes 3145736 | tf_op jit(solution)/shard_map/ppermute | solution.py:30
  110.5 1.0 copy-start.3
  111.4 5.7 %collective-permute-start.6 = (bf16[4,128,1024]{2,1,0:T(8,128)(2,1)S(1)}, bf16[4,128,1024]{2,1,0:T(8,128)(2,1)S(1)}, u32[]{:S(2)}, u32[]{:S(2)}) collective-permute-start(bf16[4,128,1024]{2,1,0:T(8,128)(2,1)S(1)} %collective-permute-done.2), channel_id=1, source_target_pairs={{0,4},{4,0},{8,12},{12,8},{16,20},{20,16},{24,28},{28,24},{1,5},{5... | collective-permute-start | bytes 3145736 | tf_op jit(solution)/shard_map/ppermute | solution.py:30
  111.4 1.0 copy-start.5
  112.4 4.9 %collective-permute-start.7 = (bf16[4,128,1024]{2,1,0:T(8,128)(2,1)}, bf16[4,128,1024]{2,1,0:T(8,128)(2,1)S(1)}, u32[]{:S(2)}, u32[]{:S(2)}) collective-permute-start(bf16[4,128,1024]{2,1,0:T(8,128)(2,1)} %collective-permute-done.3), channel_id=1, source_target_pairs={{0,4},{4,0},{8,12},{12,8},{16,20},{20,16},{24,28},{28,24},{1,5},{5... | collective-permute-start | bytes 3145736 | tf_op jit(solution)/shard_map/ppermute | solution.py:30
  114.1 3.2 %copy-start.7 = (bf16[4,128,1024]{2,1,0:T(8,128)(2,1)}, bf16[4,128,1024]{2,1,0:T(8,128)(2,1)S(1)}, u32[]{:S(2)}) copy-start(bf16[4,128,1024]{2,1,0:T(8,128)(2,1)S(1)} %collective-permute-done.5) | copy-start | bytes 3145732
  117.1 1.0 copy-start.8
  117.3 1.2 copy-start.9
  118.5 1.2 copy-start.4
  119.7 1.2 copy-start.6
  121.0 30.7 %copy-start = (bf16[256,4096]{1,0:T(8,128)(2,1)S(1)}, bf16[256,4096]{1,0:T(8,128)(2,1)}, u32[]{:S(2)}) copy-start(bf16[256,4096]{1,0:T(8,128)(2,1)} %hidden_ref.1) | copy-start | bytes 6291460
  163.3 1.4 copy-start.1
Sparse Core Ops, SparseCore 0:
  18.1 29.6 all-gather.2
  65.7 85.8 all-reduce.1
  164.8 42.7 reduce-scatter.1
